TPU v7x, 32 devices: a whole 2x2x4 slice. The times are simulated.
32 devices in a mesh: image: 4 (over y, core), space: 8 (over z, x).
Axes of the slice: x: 2, y: 2, z: 4, core: 2. Of those that a mesh axis runs over, the one named last changes fastest.
Arguments:
- positions: float32 [4, 3, 163840], P('image', None, 'space'), may hold values from -1 to 2, as said below
- strength: float32 [163840], P('space'), may hold values from 0.5 to 2
- charge: float32 [163840], P('space'), may hold values from -4 to 4
- rest_scale: float32 [4], P('image'), may hold values from 0.3 to 1
- cell_order: int32 [4, 8, 20480], P('image', 'space'), may hold values from 0 to 20479, each once within a row
- ghost_index: int32 [4, 8, 20480], P('image', 'space'), may hold values from 0 to 20479, each once within a row
- tile_atoms: int32 [4, 1280, 256], P('image', 'space'), may hold values from 0 to 40959
Outputs:
- new_positions: float32 [4, 3, 163840], P('image', None, 'space')
Inputs may be any that keep to these rules, and one draw needn't show every extreme that they name: `positions`: the solute displaced from image to image along a path. `cell_order`: each row lists every atom of the domain once. `ghost_index`: each row lists every atom of the domain once; the first 10240 are the shell for the lower domain, the rest the shell for the upper domain. `tile_atoms`: entries below 10240 are ghosts from the lower domain, the next 20480 own atoms, the rest ghosts from the upper domain; an own atom listed against itself adds nothing.
All inputs are finite; a program needn't handle non-finite values.
Results may differ from a plain program's by a relative error of at most 0.0003.
Values sent between devices are 32-bit elements; how exact they have to be, the bound alone decides.
No kernel may reach another device: no remote copies, remote signals or barrier semaphores. Data moves between devices by JAX's collectives and lax.ppermute only.
A program may use at most 128 MiB of HBM per device.

v0:
```python
import math

import jax
import jax.numpy as jnp
from jax import lax
from jax.sharding import PartitionSpec as P

SOL_DEV = 1024
TILE = 128


LJ_COEF = 0.5
CHARGE_COEF = 0.1
SOFT_CORE = 0.09
SLAB_WIDTH = 1.0
STEP_SIZE = 0.2
SPRING_COEF = 1.0
EPSILON = 1e-06


def extended_2(array, sides, width):
    for axis, dim in sides:
        count, length = (lax.axis_size(axis), array.shape[dim])
        up = [(i, (i + 1) % count) for i in range(count)]
        down = [(j, i) for i, j in up]
        last = lax.slice_in_dim(array, length - width, length, axis=dim)
        initial = lax.slice_in_dim(array, 0, width, axis=dim)
        before = lax.ppermute(last, axis, up)
        after = lax.ppermute(initial, axis, down)
        array = jnp.concatenate([before, array, after], axis=dim)
    return array


def shifted_2(array, axis, by):
    count = lax.axis_size(axis)
    pairs = [(i, i + by) for i in range(count) if 0 <= i + by < count]
    return lax.ppermute(array, axis, pairs)


def carried_in(array, axis, combine, identity):
    count, index = (lax.axis_size(axis), lax.axis_index(axis))
    everything = lax.all_gather(array, axis)
    start = jnp.broadcast_to(jnp.asarray(identity, array.dtype), array.shape)

    def step(k, before):
        reached = k < index
        new = combine(before, everything[k])
        return jnp.where(reached, new, before)

    return lax.fori_loop(0, count, step, start)


def pair_tile(own_atoms, extended, rows_i, rows_j):
    near_atoms = jnp.take(own_atoms, rows_i, axis=1)
    far_atoms = jnp.take(extended, rows_j, axis=1)
    delta_x = near_atoms[0][:, None] - far_atoms[0][None, :]
    delta_y = near_atoms[1][:, None] - far_atoms[1][None, :]
    delta_z = near_atoms[2][:, None] - far_atoms[2][None, :]
    radius_sq = delta_x * delta_x + delta_y * delta_y + delta_z * delta_z
    inside = jnp.maximum(1.0 - radius_sq, 0.0)
    shifted = radius_sq + SOFT_CORE
    coupling = (
        inside
        * inside
        * (
            LJ_COEF * near_atoms[3][:, None] * far_atoms[3][None, :]
            + CHARGE_COEF
            * near_atoms[4][:, None]
            * far_atoms[4][None, :]
            / (shifted * jnp.sqrt(shifted))
        )
    )
    return jnp.stack(
        [
            jnp.sum(coupling * delta_x, axis=1),
            jnp.sum(coupling * delta_y, axis=1),
            jnp.sum(coupling * delta_z, axis=1),
        ],
        axis=0,
    )


def add_scalars(earlier, later):
    return earlier + later


def per_device(positions, strength, charge, rest_scale, cell_order, ghost_index, tile_atoms):
    atom_count = positions.shape[2]
    half_count = atom_count // 2
    own_coords = positions[0]
    row_index = jnp.arange(atom_count)
    factor = jnp.where(row_index < SOL_DEV, jnp.sqrt(rest_scale[0]), 1.0)
    own_atoms = jnp.concatenate(
        [own_coords, (strength * factor)[None], (charge * factor)[None]], axis=0
    )
    offset = jnp.array([SLAB_WIDTH, 0.0, 0.0, 0.0, 0.0], jnp.float32)[:, None]
    shell_list = ghost_index[0, 0]
    widened = extended_2(own_atoms, (("space", 1),), atom_count)
    wide_index = extended_2(shell_list, (("space", 0),), half_count)
    lower_ghosts = jnp.take(widened[:, :atom_count], wide_index[:half_count], axis=1) - offset
    upper_ghosts = (
        jnp.take(widened[:, 2 * atom_count :], wide_index[half_count + atom_count :], axis=1)
        + offset
    )
    extended = jnp.concatenate([lower_ghosts, own_atoms, upper_ghosts], axis=1)
    tile_count = atom_count // TILE
    block_size = math.gcd(tile_count, 16)
    tile_order = cell_order[0, 0]
    order_blocks = tile_order.reshape(tile_count // block_size, block_size, TILE)
    partner_blocks = tile_atoms[0].reshape(
        tile_count // block_size, block_size, tile_atoms.shape[2]
    )

    def block_forces(block_rows):
        return jax.vmap(pair_tile, in_axes=(None, None, 0, 0))(
            own_atoms, extended, block_rows[0], block_rows[1]
        )

    per_tile = lax.map(block_forces, (order_blocks, partner_blocks))
    flat_forces = per_tile.reshape(tile_count, 3, TILE).transpose(1, 0, 2).reshape(3, atom_count)
    forces = jnp.zeros((3, atom_count), jnp.float32).at[:, tile_order].set(flat_forces)
    solute_path = own_coords[:, :SOL_DEV]
    solute_force = forces[:, :SOL_DEV]
    image_index = lax.axis_index("image")
    image_count = lax.axis_size("image")
    has_before = image_index > 0
    has_after = image_index < image_count - 1
    before_path = shifted_2(solute_path, "image", 1)
    after_path = shifted_2(solute_path, "image", -1)
    lower_path = jnp.where(has_before, before_path, solute_path)
    upper_path = jnp.where(has_after, after_path, solute_path)
    tangent = upper_path - lower_path
    tangent_sq, along_sum, ahead_sq, behind_sq = lax.psum(
        (
            jnp.sum(tangent * tangent),
            jnp.sum(solute_force * tangent),
            jnp.sum((upper_path - solute_path) ** 2),
            jnp.sum((solute_path - lower_path) ** 2),
        ),
        "space",
    )
    tangent_norm = jnp.sqrt(tangent_sq + EPSILON)
    perpendicular = solute_force - along_sum / (tangent_sq + EPSILON) * tangent
    spring = (
        SPRING_COEF
        * (jnp.sqrt(ahead_sq + EPSILON) - jnp.sqrt(behind_sq + EPSILON))
        / tangent_norm
        * tangent
    )
    interior = has_before & has_after
    moved = solute_path + STEP_SIZE * (perpendicular + jnp.where(interior, spring, 0.0))
    before_moved = shifted_2(moved, "image", 1)
    after_moved = shifted_2(moved, "image", -1)
    back_diff = moved - before_moved
    fore_diff = after_moved - moved
    back_sq, fore_sq = lax.psum(
        (jnp.sum(back_diff * back_diff), jnp.sum(fore_diff * fore_diff)), "space"
    )
    below = jnp.where(has_before, jnp.sqrt(back_sq + EPSILON), 0.0)
    above = jnp.where(has_after, jnp.sqrt(fore_sq + EPSILON), 0.0)
    halfway = (0.5 * (below + above)).reshape(1)
    earlier_sum = carried_in(halfway, "image", add_scalars, jnp.zeros((1,), jnp.float32))
    own_knot = (earlier_sum + 0.5 * below)[0]
    knot_values = lax.all_gather(earlier_sum + 0.5 * below, "image", axis=0, tiled=True)
    total = knot_values[image_count - 1]
    target = total * (image_index.astype(jnp.float32) / (image_count - 1))
    back = jnp.where(
        has_before, jnp.clip((own_knot - target) / jnp.where(has_before, below, 1.0), 0.0, 1.0), 0.0
    )
    ahead = jnp.where(
        has_after, jnp.clip((target - own_knot) / jnp.where(has_after, above, 1.0), 0.0, 1.0), 0.0
    )
    blended = moved + back * (before_moved - moved) + ahead * (after_moved - moved)
    relaxed = own_coords + STEP_SIZE * forces
    relaxed = relaxed.at[:, :SOL_DEV].set(blended)
    return relaxed[None]


def solution(mesh):
    placed = (
        P("image", None, "space"),
        P("space"),
        P("space"),
        P("image"),
        P("image", "space", None),
        P("image", "space", None),
        P("image", "space", None),
    )
    return jax.shard_map(
        per_device, mesh=mesh, in_specs=placed, out_specs=P("image", None, "space"), check_vma=False
    )
```

profile of v0, /device:TPU:0, one launch (start us, length us, event | category | flops | bytes accessed | tf_op | source)
XLA Modules:
  0.0 677.8 jit_solution(2080113493291674400)
XLA Ops:
  0.0 6.4 copy.57
  6.4 6.0 copy.58
  13.4 6.0 collective-permute-start.2
  26.3 4.7 collective-permute-start.3
  31.8 5.3 copy.63
  38.3 7.7 %collective-permute-done.3 = s32[10240]{0:T(1024)S(1)} collective-permute-done((s32[10240]{0:T(1024)}, s32[10240]{0:T(1024)S(1)}, u32[]{:S(2)}, u32[]{:S(2)}) %collective-permute-start.3) | collective-permute-done | bytes 40992 | tf_op jit(solution)/shard_map/ppermute | solution.py:29
  47.3 5.7 collective-permute-done.1
  53.6 5.5 copy.61
  59.1 41.5 %gather_fusion.3 = f32[10240,5]{1,0:T(8,128)} fusion(f32[5,20480]{0,1:T(8,128)} %copy.61, s32[10240]{0:T(1024)} %fusion.23), kind=kCustom, calls=%fused_computation.3.clone | custom fusion | bytes 450560 | tf_op jit(solution)/shard_map/jit(_take)/gather | solution.py:102
  103.9 5.5 copy.59
  109.4 38.2 %gather_fusion.2 = f32[10240,5]{1,0:T(8,128)} fusion(f32[5,20480]{0,1:T(8,128)} %copy.59, s32[10240]{0:T(1024)S(1)} %fusion.22), kind=kCustom, calls=%fused_computation.clone | custom fusion | bytes 450560 | tf_op jit(solution)/shard_map/jit(_take)/gather | solution.py:100
  151.4 10.0 %copy.64 = f32[5,40960]{0,1:T(8,128)} copy(f32[5,40960]{1,0:T(8,128)S(1)} %pad_maximum_fusion) | data formatting | bytes 1638400 | tf_op jit(solution)/shard_map/while | solution.py:119
  161.5 353.5 %while.24 = (s32[]{:T(128)}, f32[10,16,3,128]{3,1,0,2:T(8,128)S(1)}, s32[10,16,128]{2,1,0:T(8,128)}, f32[5,20480]{0,1:T(8,128)}, s32[10,16,256]{2,1,0:T(8,128)}, /*index=5*/f32[5,40960]{0,1:T(8,128)}, s32[]{:T(128)}) while((s32[]{:T(128)}, f32[10,16,3,128]{3,1,0,2:T(8,128)S(1)}, s32[10,16,128]{2,1,0:T(8,128)}, f32[5,20480]{0,1:T(8,128)}, ...), condition=%wide.region_4.6_spmd, body=%wide.region_0.5_spmd.sunk | while | flops 12685314 | bytes 1355873 | solution.py:119
  162.2 17.7 %gather_fusion = f32[4096,5]{1,0:T(8,128)S(1)} fusion(f32[5,40960]{0,1:T(8,128)} %get-tuple-element.316, s32[4096]{0:T(1024)S(1)} %broadcast_clamp_fusion.2), kind=kCustom, calls=%fused_computation.2.clone.1 | custom fusion | bytes 180224 | tf_op jit(solution)/shard_map/while/body/eval_jaxpr/vmap(jit(_take))/gather | solution.py:55
  182.0 9.4 %gather_fusion.1 = f32[2048,5]{1,0:T(8,128)S(1)} fusion(f32[5,20480]{0,1:T(8,128)} %get-tuple-element.314, s32[2048]{0:T(1024)S(1)} %fusion.30), kind=kCustom, calls=%fused_computation.1.clone.1 | custom fusion | bytes 90112 | tf_op jit(solution)/shard_map/while/body/eval_jaxpr/vmap(jit(_take))/gather | solution.py:54
  192.6 4.2 fusion.31
  197.5 17.7 %gather_fusion = f32[4096,5]{1,0:T(8,128)S(1)} fusion(f32[5,40960]{0,1:T(8,128)} %get-tuple-element.316, s32[4096]{0:T(1024)S(1)} %broadcast_clamp_fusion.2), kind=kCustom, calls=%fused_computation.2.clone.1 | custom fusion | bytes 180224 | tf_op jit(solution)/shard_map/while/body/eval_jaxpr/vmap(jit(_take))/gather | solution.py:55
  217.4 9.4 %gather_fusion.1 = f32[2048,5]{1,0:T(8,128)S(1)} fusion(f32[5,20480]{0,1:T(8,128)} %get-tuple-element.314, s32[2048]{0:T(1024)S(1)} %fusion.30), kind=kCustom, calls=%fused_computation.1.clone.1 | custom fusion | bytes 90112 | tf_op jit(solution)/shard_map/while/body/eval_jaxpr/vmap(jit(_take))/gather | solution.py:54
  227.9 4.2 fusion.31
  232.9 17.7 %gather_fusion = f32[4096,5]{1,0:T(8,128)S(1)} fusion(f32[5,40960]{0,1:T(8,128)} %get-tuple-element.316, s32[4096]{0:T(1024)S(1)} %broadcast_clamp_fusion.2), kind=kCustom, calls=%fused_computation.2.clone.1 | custom fusion | bytes 180224 | tf_op jit(solution)/shard_map/while/body/eval_jaxpr/vmap(jit(_take))/gather | solution.py:55
  252.7 9.4 %gather_fusion.1 = f32[2048,5]{1,0:T(8,128)S(1)} fusion(f32[5,20480]{0,1:T(8,128)} %get-tuple-element.314, s32[2048]{0:T(1024)S(1)} %fusion.30), kind=kCustom, calls=%fused_computation.1.clone.1 | custom fusion | bytes 90112 | tf_op jit(solution)/shard_map/while/body/eval_jaxpr/vmap(jit(_take))/gather | solution.py:54
  263.3 4.2 fusion.31
  268.2 17.7 %gather_fusion = f32[4096,5]{1,0:T(8,128)S(1)} fusion(f32[5,40960]{0,1:T(8,128)} %get-tuple-element.316, s32[4096]{0:T(1024)S(1)} %broadcast_clamp_fusion.2), kind=kCustom, calls=%fused_computation.2.clone.1 | custom fusion | bytes 180224 | tf_op jit(solution)/shard_map/while/body/eval_jaxpr/vmap(jit(_take))/gather | solution.py:55
  288.1 9.4 %gather_fusion.1 = f32[2048,5]{1,0:T(8,128)S(1)} fusion(f32[5,20480]{0,1:T(8,128)} %get-tuple-element.314, s32[2048]{0:T(1024)S(1)} %fusion.30), kind=kCustom, calls=%fused_computation.1.clone.1 | custom fusion | bytes 90112 | tf_op jit(solution)/shard_map/while/body/eval_jaxpr/vmap(jit(_take))/gather | solution.py:54
  303.6 17.7 %gather_fusion = f32[4096,5]{1,0:T(8,128)S(1)} fusion(f32[5,40960]{0,1:T(8,128)} %get-tuple-element.316, s32[4096]{0:T(1024)S(1)} %broadcast_clamp_fusion.2), kind=kCustom, calls=%fused_computation.2.clone.1 | custom fusion | bytes 180224 | tf_op jit(solution)/shard_map/while/body/eval_jaxpr/vmap(jit(_take))/gather | solution.py:55
  323.4 9.4 %gather_fusion.1 = f32[2048,5]{1,0:T(8,128)S(1)} fusion(f32[5,20480]{0,1:T(8,128)} %get-tuple-element.314, s32[2048]{0:T(1024)S(1)} %fusion.30), kind=kCustom, calls=%fused_computation.1.clone.1 | custom fusion | bytes 90112 | tf_op jit(solution)/shard_map/while/body/eval_jaxpr/vmap(jit(_take))/gather | solution.py:54
  334.0 4.2 fusion.31
  338.9 17.7 %gather_fusion = f32[4096,5]{1,0:T(8,128)S(1)} fusion(f32[5,40960]{0,1:T(8,128)} %get-tuple-element.316, s32[4096]{0:T(1024)S(1)} %broadcast_clamp_fusion.2), kind=kCustom, calls=%fused_computation.2.clone.1 | custom fusion | bytes 180224 | tf_op jit(solution)/shard_map/while/body/eval_jaxpr/vmap(jit(_take))/gather | solution.py:55
  358.8 9.4 %gather_fusion.1 = f32[2048,5]{1,0:T(8,128)S(1)} fusion(f32[5,20480]{0,1:T(8,128)} %get-tuple-element.314, s32[2048]{0:T(1024)S(1)} %fusion.30), kind=kCustom, calls=%fused_computation.1.clone.1 | custom fusion | bytes 90112 | tf_op jit(solution)/shard_map/while/body/eval_jaxpr/vmap(jit(_take))/gather | solution.py:54
  374.3 17.7 %gather_fusion = f32[4096,5]{1,0:T(8,128)S(1)} fusion(f32[5,40960]{0,1:T(8,128)} %get-tuple-element.316, s32[4096]{0:T(1024)S(1)} %broadcast_clamp_fusion.2), kind=kCustom, calls=%fused_computation.2.clone.1 | custom fusion | bytes 180224 | tf_op jit(solution)/shard_map/while/body/eval_jaxpr/vmap(jit(_take))/gather | solution.py:55
  394.1 9.4 %gather_fusion.1 = f32[2048,5]{1,0:T(8,128)S(1)} fusion(f32[5,20480]{0,1:T(8,128)} %get-tuple-element.314, s32[2048]{0:T(1024)S(1)} %fusion.30), kind=kCustom, calls=%fused_computation.1.clone.1 | custom fusion | bytes 90112 | tf_op jit(solution)/shard_map/while/body/eval_jaxpr/vmap(jit(_take))/gather | solution.py:54
  409.6 17.7 %gather_fusion = f32[4096,5]{1,0:T(8,128)S(1)} fusion(f32[5,40960]{0,1:T(8,128)} %get-tuple-element.316, s32[4096]{0:T(1024)S(1)} %broadcast_clamp_fusion.2), kind=kCustom, calls=%fused_computation.2.clone.1 | custom fusion | bytes 180224 | tf_op jit(solution)/shard_map/while/body/eval_jaxpr/vmap(jit(_take))/gather | solution.py:55
  429.5 9.4 %gather_fusion.1 = f32[2048,5]{1,0:T(8,128)S(1)} fusion(f32[5,20480]{0,1:T(8,128)} %get-tuple-element.314, s32[2048]{0:T(1024)S(1)} %fusion.30), kind=kCustom, calls=%fused_computation.1.clone.1 | custom fusion | bytes 90112 | tf_op jit(solution)/shard_map/while/body/eval_jaxpr/vmap(jit(_take))/gather | solution.py:54
  445.0 17.7 %gather_fusion = f32[4096,5]{1,0:T(8,128)S(1)} fusion(f32[5,40960]{0,1:T(8,128)} %get-tuple-element.316, s32[4096]{0:T(1024)S(1)} %broadcast_clamp_fusion.2), kind=kCustom, calls=%fused_computation.2.clone.1 | custom fusion | bytes 180224 | tf_op jit(solution)/shard_map/while/body/eval_jaxpr/vmap(jit(_take))/gather | solution.py:55
  464.8 9.4 %gather_fusion.1 = f32[2048,5]{1,0:T(8,128)S(1)} fusion(f32[5,20480]{0,1:T(8,128)} %get-tuple-element.314, s32[2048]{0:T(1024)S(1)} %fusion.30), kind=kCustom, calls=%fused_computation.1.clone.1 | custom fusion | bytes 90112 | tf_op jit(solution)/shard_map/while/body/eval_jaxpr/vmap(jit(_take))/gather | solution.py:54
  475.4 4.2 fusion.31
  480.3 17.7 %gather_fusion = f32[4096,5]{1,0:T(8,128)S(1)} fusion(f32[5,40960]{0,1:T(8,128)} %get-tuple-element.316, s32[4096]{0:T(1024)S(1)} %broadcast_clamp_fusion.2), kind=kCustom, calls=%fused_computation.2.clone.1 | custom fusion | bytes 180224 | tf_op jit(solution)/shard_map/while/body/eval_jaxpr/vmap(jit(_take))/gather | solution.py:55
  500.2 9.4 %gather_fusion.1 = f32[2048,5]{1,0:T(8,128)S(1)} fusion(f32[5,20480]{0,1:T(8,128)} %get-tuple-element.314, s32[2048]{0:T(1024)S(1)} %fusion.30), kind=kCustom, calls=%fused_computation.1.clone.1 | custom fusion | bytes 90112 | tf_op jit(solution)/shard_map/while/body/eval_jaxpr/vmap(jit(_take))/gather | solution.py:54
  514.9 5.4 copy.68
  520.4 55.2 %scatter_custom_fusion = f32[3,20480]{0,1:T(8,128)} fusion(s32[20480]{0:T(1024)} %bitcast.149, f32[20480,3]{1,0:T(8,128)} %bitcast.137, f32[]{:T(128)} %constant.133.clone.1), kind=kCustom, calls=%fused_computation.52 | custom fusion | bytes 246272 | tf_op jit(solution)/shard_map/scatter | solution.py:121
  577.8 18.4 %all-reduce.3 = (f32[]{:T(128)}, f32[]{:T(128)}, f32[]{:T(128)}, f32[]{:T(128)}) all-reduce(f32[]{:T(128)} %get-tuple-element.159, f32[]{:T(128)} %get-tuple-element.158, f32[]{:T(128)} %get-tuple-element.201, f32[]{:T(128)} %get-tuple-element.202), channel_id=1, replica_groups=mesh['image'=4,'space'=8] {'space'}, use_global_device_ids=true, to_apply=%region_12.14 | all-reduce | flops 4 | bytes 32 | tf_op jit(solution)/shard_map/psum | solution.py:133
  602.8 11.9 %multiply_add_fusion = f32[3,20480]{0,1:T(8,128)} fusion(f32[3,20480]{0,1:T(8,128)} %scatter_custom_fusion, f32[1,3,20480]{1,2,0:T(8,128)} %copy.57), kind=kLoop, calls=%fused_computation.51 | loop fusion | flops 122880 | bytes 737280 | tf_op jit(solution)/shard_map/add | solution.py:174
  615.6 19.2 %all-reduce.2 = (f32[]{:T(128)}, f32[]{:T(128)}) all-reduce(f32[]{:T(128)} %get-tuple-element.204, f32[]{:T(128)} %get-tuple-element.188), channel_id=1, replica_groups=mesh['image'=4,'space'=8] {'space'}, use_global_device_ids=true, to_apply=%region_16.18 | all-reduce | flops 2 | bytes 16 | tf_op jit(solution)/shard_map/psum | solution.py:156
  636.8 8.4 %all-reduce = f32[4]{0:T(128)S(1)} all-reduce(f32[4]{0:T(128)S(1)} %dynamic-update-slice.4), channel_id=1, replica_groups=mesh['image'=4,'space'=8] {'image'}, use_global_device_ids=true, to_apply=%add | all-reduce | flops 4 | bytes 32
  645.2 5.3 while.25
  651.2 8.8 %copy.105 = f32[1,3,20480]{1,2,0:T(8,128)} copy(f32[1,3,20480]{1,2,0:T(8,128)} %bitcast.135) | data formatting | bytes 491520
  660.0 7.2 %all-reduce.1 = f32[4]{0:T(128)S(1)} all-reduce(f32[4]{0:T(128)S(1)} %dynamic-update-slice.5), channel_id=1, replica_groups=mesh['image'=4,'space'=8] {'image'}, use_global_device_ids=true, to_apply=%add.1 | all-reduce | flops 4 | bytes 32
  671.1 6.7 copy.67
  (197 shorter events, 92.2 us)
Async XLA Ops:
  6.4 6.8 %copy-start.2 = (f32[20480]{0:T(1024)S(1)}, f32[20480]{0:T(1024)}, u32[]{:S(2)}) copy-start(f32[20480]{0:T(1024)} %param.18) | copy-start | bytes 245764
  6.4 6.8 %copy-start.3 = (f32[20480]{0:T(1024)S(1)}, f32[20480]{0:T(1024)}, u32[]{:S(2)}) copy-start(f32[20480]{0:T(1024)} %param.17) | copy-start | bytes 245764
  12.4 13.3 %copy-start.4 = (s32[1,1,20480]{2,1,0:T(1,128)S(1)}, s32[1,1,20480]{2,1,0:T(1,128)}, u32[]{:S(2)}) copy-start(s32[1,1,20480]{2,1,0:T(1,128)} %param.21) | copy-start | bytes 245764
  12.4 18.6 %copy-start = (s32[1,1,20480]{2,1,0:T(1,128)S(1)}, s32[1,1,20480]{2,1,0:T(1,128)}, u32[]{:S(2)}) copy-start(s32[1,1,20480]{2,1,0:T(1,128)} %param.20) | copy-start | bytes 245764
  13.4 40.2 %collective-permute-start.2 = (f32[5,20480]{1,0:T(8,128)S(1)}, f32[5,20480]{1,0:T(8,128)S(1)}, u32[]{:S(2)}, u32[]{:S(2)}) collective-permute-start(f32[5,20480]{1,0:T(8,128)S(1)} %pad_maximum_fusion.1), channel_id=1, source_target_pairs={{1,0},{2,1},{3,2},{4,3},{5,4},{6,5},{7,6},{0,7},{9,8},{10,9},{11,1... | collective-permute-start | bytes 1228808 | tf_op jit(solution)/shard_map/ppermute | solution.py:29
  19.5 84.4 %collective-permute-start = (f32[5,20480]{1,0:T(8,128)S(1)}, f32[5,20480]{1,0:T(8,128)S(1)}, u32[]{:S(2)}, u32[]{:S(2)}) collective-permute-start(f32[5,20480]{1,0:T(8,128)S(1)} %pad_maximum_fusion.1), channel_id=1, source_target_pairs={{0,1},{1,2},{2,3},{3,4},{4,5},{5,6},{6,7},{7,0},{8,9},{9,10},{10,1... | collective-permute-start | bytes 1228808 | tf_op jit(solution)/shard_map/ppermute | solution.py:28
  20.6 555.0 %collective-permute-start.4 = (f32[3,1024]{0,1:T(8,128)S(1)}, f32[3,1024]{0,1:T(8,128)S(1)}, u32[]{:S(2)}, u32[]{:S(2)}) collective-permute-start(f32[3,1024]{0,1:T(8,128)S(1)} %slice.96), channel_id=1, source_target_pairs={{8,0},{16,8},{24,16},{9,1},{17,9},{25,17},{10,2},{18,10},{26,18},{... | collective-permute-start | bytes 36872 | tf_op jit(solution)/shard_map/ppermute | solution.py:37
  21.9 553.7 %collective-permute-start.5 = (f32[3,1024]{0,1:T(8,128)S(1)}, f32[3,1024]{0,1:T(8,128)}, u32[]{:S(2)}, u32[]{:S(2)}) collective-permute-start(f32[3,1024]{0,1:T(8,128)S(1)} %slice.96), channel_id=1, source_target_pairs={{0,8},{8,16},{16,24},{1,9},{9,17},{17,25},{2,10},{10,18},{18,26},{... | collective-permute-start | bytes 36872 | tf_op jit(solution)/shard_map/ppermute | solution.py:37
  26.3 19.7 %collective-permute-start.3 = (s32[10240]{0:T(1024)}, s32[10240]{0:T(1024)S(1)}, u32[]{:S(2)}, u32[]{:S(2)}) collective-permute-start(s32[10240]{0:T(1024)} %bitcast.37), channel_id=1, source_target_pairs={{1,0},{2,1},{3,2},{4,3},{5,4},{6,5},{7,6},{0,7},{9,8},{10,9},{11,1... | collective-permute-start | bytes 122888 | tf_op jit(solution)/shard_map/ppermute | solution.py:29
  31.8 5.3 copy-start.9
  46.1 6.9 %collective-permute-start.1 = (s32[10240]{0:T(1024)}, s32[10240]{0:T(1024)S(1)}, u32[]{:S(2)}, u32[]{:S(2)}) collective-permute-start(s32[10240]{0:T(1024)} %bitcast.150), channel_id=1, source_target_pairs={{0,1},{1,2},{2,3},{3,4},{4,5},{5,6},{6,7},{7,0},{8,9},{9,10},{10,1... | collective-permute-start | bytes 122888 | tf_op jit(solution)/shard_map/ppermute | solution.py:28
  147.6 3.4 copy-start.5
  147.6 3.4 copy-start.8
  147.6 3.5 copy-start.6
  147.6 3.5 copy-start.7
  151.4 10.0 %copy-start.1 = (f32[10,16,3,128]{3,1,0,2:T(8,128)S(1)}, f32[10,16,3,128]{3,1,0,2:T(8,128)}, u32[]{:S(2)}) copy-start(f32[10,16,3,128]{3,1,0,2:T(8,128)} %custom-call.8) | copy-start | bytes 737284
  600.2 14.6 %collective-permute-start.6 = (f32[3,1024]{0,1:T(8,128)S(1)}, f32[3,1024]{0,1:T(8,128)S(1)}, u32[]{:S(2)}, u32[]{:S(2)}) collective-permute-start(f32[3,1024]{0,1:T(8,128)S(1)} %multiply_add_fusion.1), channel_id=1, source_target_pairs={{0,8},{8,16},{16,24},{1,9},{9,17},{17,25},{2,10},{10,18},{18,26},{... | collective-permute-start | bytes 36872 | tf_op jit(solution)/shard_map/ppermute | solution.py:37
  601.5 13.2 %collective-permute-start.7 = (f32[3,1024]{0,1:T(8,128)S(1)}, f32[3,1024]{0,1:T(8,128)S(1)}, u32[]{:S(2)}, u32[]{:S(2)}) collective-permute-start(f32[3,1024]{0,1:T(8,128)S(1)} %multiply_add_fusion.1), channel_id=1, source_target_pairs={{8,0},{16,8},{24,16},{9,1},{17,9},{25,17},{10,2},{18,10},{26,18},{... | collective-permute-start | bytes 36872 | tf_op jit(solution)/shard_map/ppermute | solution.py:37
where the time goes:
time: 682 us; the launch traced here: 678 us
  local copies, waits for them, and re-layouts  490 us (72%)
  other arithmetic  94 us (14%)
  blocking collectives  53.2 us (8%)
  starting transfers between devices  18.5 us (3%)
  waiting for transfers between devices  13.4 us (2%)
    gather x20, local copies, waits for them, and re-layouts, pair_tile(): far_atoms = jnp.take(extended, rows_j, axis=1)  184 us
    gather x20, local copies, waits for them, and re-layouts, pair_tile(): near_atoms = jnp.take(own_atoms, rows_i, axis=1)  97.7 us
    scatter x1, local copies, waits for them, and re-layouts, per_device(): jnp.zeros((3, atom_count), jnp.float32).at[:, tile_order].set(flat_forces)  55.2 us
    gather x2, local copies, waits for them, and re-layouts, per_device(): jnp.take(widened[:, 2 * atom_count:], wide_index[half_count + atom_count:...  44.8 us
    reduce_sum x10, other arithmetic, pair_tile(): jnp.sum(coupling * delta_x, axis=1)  42 us
    gather x2, local copies, waits for them, and re-layouts, per_device(): jnp.take(widened[:, :atom_count], wide_index[:half_count], axis=1) - offset  41.5 us
    psum x1, blocking collectives, per_device(): lax.psum((jnp.sum(back_diff * back_diff), jnp.sum(fore_diff * fore_diff))...  19.2 us
    psum x1, blocking collectives, per_device(): lax.psum((jnp.sum(tangent * tangent), jnp.sum(solute_force * tangent), jn...  18.4 us
  transfers between devices with their start and end apart: 8, of which 2 were waited for; matrix products, arithmetic and copies ran while one was open for 80% of the time, Pallas kernels for 0%

commit v1 on v0

v1 whole, which is shorter than its diff:
```python
import functools

import jax
import jax.numpy as jnp
from jax import lax
from jax.experimental import pallas as pl
from jax.experimental.pallas import tpu as pltpu
from jax.sharding import PartitionSpec as P

SOL_DEV = 1024
TILE = 128
ROW = 256
FIELDS = 5

LJ_COEF = 0.5
CHARGE_COEF = 0.1
SOFT_CORE = 0.09
SLAB_WIDTH = 1.0
STEP_SIZE = 0.2
SPRING_COEF = 1.0
EPSILON = 1e-06

F32 = jnp.float32
BF16 = jnp.bfloat16
VMEM_LIMIT = 48 * 1024 * 1024


def two_pieces(values):
    high = values.astype(BF16)
    low = (values - high.astype(F32)).astype(BF16)
    return jnp.concatenate([high, low], axis=1)


def one_hot(entries):
    width = entries.shape[1]
    column = jnp.bitwise_and(entries, ROW - 1)
    grid = lax.broadcasted_iota(jnp.int32, (ROW, width), 0)
    return jnp.where(grid == column, 1.0, 0.0).astype(BF16)


def pick(table, hot, row_masks):
    rows = 8 * len(row_masks)
    width = hot.shape[1]
    picked = jnp.dot(table, jnp.concatenate([hot, hot], axis=0), preferred_element_type=F32)
    result = []
    for field in range(table.shape[0] // rows):
        found = jnp.zeros((8, width), F32)
        for block, mask in enumerate(row_masks):
            start = field * rows + block * 8
            found = jnp.where(mask, picked[start : start + 8], found)
        result.append(jnp.sum(found, axis=0, keepdims=True))
    return result


def masks_of(row_entries, starts):
    width = row_entries.shape[1]
    grid = lax.broadcasted_iota(jnp.int32, (8, width), 0)
    relative = row_entries - grid
    return [relative == start for start in starts]


def shell_kernel(rows, scale_ref, pos_ref, strength_ref, charge_ref, ghost_ref, table_ref, down_ref, up_ref, plain):
    root = jnp.sqrt(jnp.full((1, ROW), scale_ref[0], F32))
    for row in range(rows):
        span = slice(row * ROW, (row + 1) * ROW)
        for axis in range(3):
            plain[axis * rows + row : axis * rows + row + 1, :] = pos_ref[0, axis : axis + 1, span]
        a = strength_ref[0:1, span]
        q = charge_ref[0:1, span]
        if row < SOL_DEV // ROW:
            a, q = a * root, q * root
        plain[3 * rows + row : 3 * rows + row + 1, :] = a
        plain[4 * rows + row : 4 * rows + row + 1, :] = q
    table_ref[...] = two_pieces(plain[...])
    half = rows // 2

    def send(out_ref, first, shift):
        def step(block, carry):
            entries = ghost_ref[0:1, pl.ds(pl.multiple_of((first + block) * ROW, ROW), ROW)]
            masks = masks_of(lax.shift_right_logical(entries, 8), range(0, rows, 8))
            found = pick(table_ref[...], one_hot(entries), masks)
            found[0] = found[0] + shift
            for field in range(FIELDS):
                out_ref[field, pl.ds(block, 1), :] = found[field]
            return carry

        lax.fori_loop(0, half, step, 0)

    send(down_ref, 0, SLAB_WIDTH)
    send(up_ref, half, -SLAB_WIDTH)


def own_kernel(rows, order_ref, partner_ref, table_ref, near_ref, far_ref):
    half = rows // 2

    def step(pair, carry):
        entries = order_ref[0:1, pl.ds(pl.multiple_of(pair * ROW, ROW), ROW)]
        masks = masks_of(lax.shift_right_logical(entries, 8), range(0, rows, 8))
        found = pick(table_ref[...], one_hot(entries), masks)
        for field in range(FIELDS):
            near_ref[pair, field : field + 1, :] = found[field]
        for side in range(ROW // TILE):
            tile = pair * (ROW // TILE) + side
            entries = partner_ref[0, pl.ds(tile, 1), :]
            masks = masks_of(lax.shift_right_logical(entries, 8), range(half, half + rows, 8))
            found = pick(table_ref[...], one_hot(entries), masks)
            for field in range(FIELDS):
                far_ref[tile, field : field + 1, :] = found[field]
        return carry

    lax.fori_loop(0, near_ref.shape[0], step, 0)


def tile_forces(near, far_columns, width):
    near = [jnp.broadcast_to(row, (8, TILE)) for row in near]
    sums = [jnp.zeros((8, TILE), F32) for _ in range(3)]
    for block in range(width // 8):
        far = far_columns[block * 8 : block * 8 + 8]
        part = [jnp.broadcast_to(far[:, f : f + 1], (8, TILE)) for f in range(FIELDS)]
        dx, dy, dz = (near[f] - part[f] for f in range(3))
        radius_sq = dx * dx + dy * dy + dz * dz
        inside = jnp.maximum(1.0 - radius_sq, 0.0)
        root = lax.rsqrt(radius_sq + SOFT_CORE)
        strength = near[3] * part[3] + near[4] * part[4] * (root * root * root)
        coupling = inside * inside * strength
        sums = [total + coupling * delta for total, delta in zip(sums, (dx, dy, dz))]
    return [jnp.sum(total, axis=0, keepdims=True) for total in sums]


def force_kernel(
    rows, order_ref, partner_ref, near_ref, far_ref, lower_ref, upper_ref, pos_ref, out_ref, solute_ref, table, total
):
    half = rows // 2
    for side, ref in enumerate((lower_ref, upper_ref)):
        for field in range(FIELDS):
            start = field * rows + side * half
            table[start : start + half, :] = two_pieces(ref[field])
    total[...] = jnp.zeros_like(total)
    starts = list(range(0, half, 8)) + list(range(half + rows, 2 * rows, 8))

    def step(pair, carry):
        forces = [[], [], []]
        for side in range(ROW // TILE):
            tile = pair * (ROW // TILE) + side
            entries = partner_ref[0, pl.ds(tile, 1), :]
            masks = masks_of(lax.shift_right_logical(entries, 8), starts)
            found = pick(table[...], one_hot(entries), masks)
            width = entries.shape[1]
            far = [found[f] + far_ref[tile, f : f + 1, :] for f in range(FIELDS)]
            far_rows = jnp.concatenate(far + [jnp.zeros((8 - FIELDS, width), F32)], axis=0)
            span = slice(side * TILE, (side + 1) * TILE)
            near = [near_ref[pair, f : f + 1, span] for f in range(FIELDS)]
            near[3] = near[3] * LJ_COEF
            near[4] = near[4] * CHARGE_COEF
            for axis, row in enumerate(tile_forces(near, far_rows.T, width)):
                forces[axis].append(row)
        entries = order_ref[0:1, pl.ds(pl.multiple_of(pair * ROW, ROW), ROW)]
        hot = one_hot(entries)
        grid = lax.broadcasted_iota(jnp.int32, (rows, ROW), 0)
        mask = grid == lax.shift_right_logical(entries, 8)
        spread = jnp.concatenate(
            [jnp.where(mask, jnp.concatenate(forces[axis], axis=1), 0.0) for axis in range(3)], axis=0
        )
        total[...] += lax.dot_general(
            two_pieces(spread),
            jnp.concatenate([hot, hot], axis=1),
            (((1,), (1,)), ((), ())),
            preferred_element_type=F32,
        )
        return carry

    lax.fori_loop(0, near_ref.shape[0], step, 0)
    for row in range(rows):
        span = slice(row * ROW, (row + 1) * ROW)
        for axis in range(3):
            force = total[axis * rows + row : axis * rows + row + 1, :]
            out_ref[0, axis : axis + 1, span] = pos_ref[0, axis : axis + 1, span] + STEP_SIZE * force
    solute_ref[...] = out_ref[:, :, 0:SOL_DEV]


def whole(*shape, dtype=F32):
    return jax.ShapeDtypeStruct(shape, dtype)


def kernel_call(body, outs, scratch=(), scalar=0, **more):
    return functools.partial(_call, body, outs, scratch, scalar, more)


def _call(body, outs, scratch, scalar, more, *args):
    in_specs = [pl.BlockSpec(memory_space=pltpu.SMEM)] * scalar
    in_specs += [pl.BlockSpec(memory_space=pltpu.VMEM)] * (len(args) - scalar)
    return pl.pallas_call(
        body,
        out_shape=outs,
        in_specs=in_specs,
        out_specs=[pl.BlockSpec(memory_space=pltpu.VMEM)] * len(outs),
        scratch_shapes=list(scratch),
        compiler_params=pltpu.CompilerParams(vmem_limit_bytes=VMEM_LIMIT),
        **more,
    )(*args)


def turned(array, axis, by):
    count = lax.axis_size(axis)
    return lax.ppermute(array, axis, [(i, (i + by) % count) for i in range(count)])


def round_trip(array, axis):
    count, index = lax.axis_size(axis), lax.axis_index(axis)
    result = jnp.zeros((count,) + array.shape, array.dtype)
    for by in range(count):
        piece = turned(array, axis, by) if by else array
        result = lax.dynamic_update_index_in_dim(result, piece, (index + count - by) % count, 0)
    return result


def inner(left, right):
    return jnp.sum(left * right, axis=(1, 2))


def per_device(positions, strength, charge, rest_scale, cell_order, ghost_index, tile_atoms):
    atoms = positions.shape[2]
    rows = atoms // ROW
    tiles = atoms // TILE
    partners = tile_atoms.shape[2]
    order = cell_order.reshape(1, atoms)
    paths = round_trip(positions[0, :, :SOL_DEV], "image")

    table, down, up = kernel_call(
        functools.partial(shell_kernel, rows),
        [
            whole(FIELDS * rows, 2 * ROW, dtype=BF16),
            whole(FIELDS, rows // 2, ROW),
            whole(FIELDS, rows // 2, ROW),
        ],
        [pltpu.VMEM((FIELDS * rows, ROW), F32)],
        scalar=1,
        cost_estimate=pl.CostEstimate(flops=8 * 10**9, bytes_accessed=10**6, transcendentals=0),
    )(rest_scale, positions, strength.reshape(1, atoms), charge.reshape(1, atoms), ghost_index.reshape(1, atoms))
    upper = turned(down, "space", -1)
    lower = turned(up, "space", 1)
    near, far = kernel_call(
        functools.partial(own_kernel, rows),
        [whole(atoms // ROW, 8, ROW), whole(tiles, 8, partners)],
        cost_estimate=pl.CostEstimate(flops=25 * 10**9, bytes_accessed=10**6, transcendentals=0),
    )(order, tile_atoms, table)
    out, solute = kernel_call(
        functools.partial(force_kernel, rows),
        [whole(1, 3, atoms), whole(1, 3, SOL_DEV)],
        [pltpu.VMEM((FIELDS * rows, 2 * ROW), BF16), pltpu.VMEM((3 * rows, ROW), F32)],
        cost_estimate=pl.CostEstimate(flops=25 * 10**9, bytes_accessed=10**6, transcendentals=0),
    )(order, tile_atoms, near, far, lower, upper, positions)

    pushed = round_trip(solute[0], "image")
    images = lax.axis_size("image")
    index = lax.axis_index("image")
    steps = paths[1:] - paths[:-1]
    upper_path = jnp.concatenate([paths[1:], paths[-1:]])
    lower_path = jnp.concatenate([paths[:1], paths[:-1]])
    tangents = upper_path - lower_path
    gaps = pushed[1:] - pushed[:-1]
    none = jnp.zeros((1,), F32)
    sums = lax.psum(
        jnp.stack(
            [
                inner(tangents, tangents),
                inner(pushed - paths, tangents),
                jnp.concatenate([inner(steps, steps), none]),
                jnp.concatenate([inner(gaps, gaps), none]),
                jnp.concatenate([inner(gaps, tangents[1:]), none]),
                jnp.concatenate([inner(gaps, tangents[:-1]), none]),
                jnp.concatenate([inner(tangents[1:], tangents[:-1]), none]),
            ]
        ),
        "space",
    )
    tangent_sq, along = sums[0], sums[1]
    step_sq, gap_sq, gap_next, gap_this, cross = (sums[i, :-1] for i in range(2, 7))
    step_root = jnp.sqrt(step_sq + EPSILON)
    spring = SPRING_COEF * (step_root[1:] - step_root[:-1]) / jnp.sqrt(tangent_sq[1:-1] + EPSILON)
    spring = jnp.concatenate([none, spring, none])
    shift = STEP_SIZE * spring - along / (tangent_sq + EPSILON)
    ahead_shift, here_shift = shift[1:], shift[:-1]
    length_sq = (
        gap_sq
        + ahead_shift * ahead_shift * tangent_sq[1:]
        + here_shift * here_shift * tangent_sq[:-1]
        + 2.0 * (ahead_shift * gap_next - here_shift * gap_this - ahead_shift * here_shift * cross)
    )
    lengths = jnp.sqrt(jnp.maximum(length_sq, 0.0) + EPSILON)
    knots = jnp.concatenate([none, jnp.cumsum(lengths)])
    targets = knots[-1] * (jnp.arange(images, dtype=F32) / (images - 1))
    back = jnp.concatenate([none, jnp.clip((knots - targets)[1:] / lengths, 0.0, 1.0)])
    ahead = jnp.concatenate([jnp.clip((targets - knots)[:-1] / lengths, 0.0, 1.0), none])
    moved = pushed + shift[:, None, None] * tangents

    def at(array, place):
        return lax.dynamic_index_in_dim(array, jnp.clip(place, 0, images - 1), 0, keepdims=False)

    here = at(moved, index)
    blended = (
        here
        + at(back, index) * (at(moved, index - 1) - here)
        + at(ahead, index) * (at(moved, index + 1) - here)
    )
    return lax.dynamic_update_slice(out, blended[None], (0, 0, 0))


def solution(mesh):
    placed = (
        P("image", None, "space"),
        P("space"),
        P("space"),
        P("image"),
        P("image", "space", None),
        P("image", "space", None),
        P("image", "space", None),
    )
    return jax.shard_map(
        per_device, mesh=mesh, in_specs=placed, out_specs=P("image", None, "space"), check_vma=False
    )
```

time: 682 us -> 224 us (0.33)
  local copies, waits for them, and re-layouts: 490 us -> 6.73 us
  Pallas kernels: 0 us -> 181 us
  other arithmetic: 94 us -> 2.92 us
  blocking collectives: 53.2 us -> 19 us
  waiting for transfers between devices: 13.4 us -> 1.93 us
  starting transfers between devices: 18.5 us -> 11.2 us
    gather x44 -> x0, local copies, waits for them, and re-layouts: 368 us -> none  [the longest x20 184 us: pair_tile(): far_atoms = jnp.take(extended, rows_j, axis=1)]
    pallas_call x0 -> x3, Pallas kernels: none -> 181 us  [_call(): pl.pallas_call(body, out_shape=outs, in_specs=in_specs, out_specs=[pl.Blo...]
    scatter x2 -> x0, local copies, waits for them, and re-layouts: 61.9 us -> none  [the longest x1 55.2 us: per_device(): jnp.zeros((3, atom_count), jnp.float32).at[:, tile_order].set(flat_forces)]
    reduce_sum x12 -> x3, other arithmetic: 45.1 us -> 0.43 us  [inner(): return jnp.sum(left * right, axis=(1, 2))]
    psum x2 -> x1, blocking collectives: 37.6 us -> 19 us  [per_device(): lax.psum(jnp.stack([inner(tangents, tangents), inner(pushed - paths, tang...]
    and x22 -> x0, other arithmetic: 15.7 us -> none  [the longest x10 7.34 us: pair_tile(): far_atoms = jnp.take(extended, rows_j, axis=1)]
    unnamed x2 -> x0, blocking collectives: 15.6 us -> none
    while x12 -> x0, local copies, waits for them, and re-layouts: 15.5 us -> none  [the longest x2 15.4 us: per_device(): per_tile = lax.map(block_forces, (order_blocks, partner_blocks))]
  transfers between devices with their start and end apart: 8 -> 8, of which waited for: 2 -> 2; matrix products, arithmetic and copies ran while one was open for 80% -> 0% of each run, Pallas kernels for 0% -> 29%
where the time goes in v1:
time: 224 us
  Pallas kernels  181 us (81%)
  blocking collectives  19 us (8%)
  starting transfers between devices  11.2 us (5%)
  local copies, waits for them, and re-layouts  6.73 us (3%)
  other arithmetic  2.92 us (1%)
    pallas_call x3, Pallas kernels, _call(): pl.pallas_call(body, out_shape=outs, in_specs=in_specs, out_specs=[pl.Blo...  181 us
    psum x1, blocking collectives, per_device(): lax.psum(jnp.stack([inner(tangents, tangents), inner(pushed - paths, tang...  19 us
    ppermute x8, starting transfers between devices, turned(): lax.ppermute(array, axis, [(i, (i + by) % count) for i in range(count)])  11.2 us
  transfers between devices with their start and end apart: 8, of which 2 were waited for; matrix products, arithmetic and copies ran while one was open for 0% of the time, Pallas kernels for 29%

profile of v1, /device:TPU:0, one launch (start us, length us, event | category | flops | bytes accessed | tf_op | source)
XLA Modules:
  0.0 224.1 jit_solution(3727267995011281320)
XLA Ops:
  0.0 1.1 copy.8.pos_ref
  1.2 0.5 collective-permute-start.5
  1.7 2.6 %collective-permute-start.6 = (f32[3,1024]{1,0:T(4,128)S(1)}, f32[3,1024]{1,0:T(4,128)S(1)}, u32[]{:S(2)}, u32[]{:S(2)}) collective-permute-start(f32[3,1024]{1,0:T(4,128)S(1)} %get-tuple-element.26), channel_id=1, source_target_pairs={{0,16},{8,24},{16,0},{24,8},{1,17},{9,25},{17,1},{25,9},{2,18},{10... | collective-permute-start | bytes 36872 | tf_op jit(solution)/shard_map/ppermute | solution.py:205
  4.3 1.4 collective-permute-start.7
  6.3 0.0 copy-start.1
  6.3 0.9 copy-done.1
  7.2 0.9 copy-done.2
  8.1 0.9 copy-done.3
  9.0 23.1 %shard_map.73 = (bf16[400,512]{1,0:T(8,128)(2,1)S(1)}, f32[5,40,256]{2,1,0:T(8,128)S(1)}, f32[5,40,256]{2,1,0:T(8,128)S(1)}) custom-call(f32[1]{0:T(128)S(6)} %copy.22.scale_ref, f32[1,3,20480]{2,1,0:T(4,128)S(1)} %copy.8.pos_ref, f32[1,20480]{1,0:T(1,128)S(1)} %bitcast.87, f32[1,20480]{1,0:T(1,128)S(1)} %bitcast.88, s32[1,20480]{1,0:T(1,128)S(1)} %bitcast.89), custom_call_target="tpu_custom_call" | custom-call | flops 8000000000 | bytes 1000000 | tf_op jit(solution)/shard_map/pallas_call | solution.py:192
  32.1 1.5 collective-permute-start
  33.6 3.3 %collective-permute-start.1 = (f32[5,40,256]{2,1,0:T(8,128)S(1)}, f32[5,40,256]{2,1,0:T(8,128)S(1)}, u32[]{:S(2)}, u32[]{:S(2)}) collective-permute-start(f32[5,40,256]{2,1,0:T(8,128)S(1)} %get-tuple-element.16), channel_id=1, source_target_pairs={{0,7},{1,0},{2,1},{3,2},{4,3},{5,4},{6,5},{7,6},{8,15},{9,8},{10,9... | collective-permute-start | bytes 614408 | tf_op jit(solution)/shard_map/ppermute | solution.py:205
  36.9 0.0 copy-done
  36.9 0.0 copy-done.4
  36.9 42.5 %shard_map.74 = (f32[80,8,256]{2,1,0:T(8,128)S(1)}, f32[160,8,256]{2,1,0:T(8,128)S(1)}) custom-call(s32[1,20480]{1,0:T(1,128)S(1)} %bitcast.90, s32[1,160,256]{2,1,0:T(8,128)S(1)} %copy-done, bf16[400,512]{1,0:T(8,128)(2,1)S(1)} %get-tuple-element.12.table_ref), custom_call_target="tpu_custom_call" | custom-call | flops 24999999488 | bytes 1000000 | tf_op jit(solution)/shard_map/pallas_call | solution.py:192
  79.4 0.0 collective-permute-done.5
  79.5 0.0 collective-permute-done.6
  79.5 0.0 collective-permute-done.7
  79.5 0.1 multiply_reduce_fusion.6
  79.7 0.1 fusion
  79.8 0.0 collective-permute-done.lower_ref
  79.8 0.0 collective-permute-done.1.upper_ref
  79.8 115.2 %shard_map.75 = (f32[1,3,20480]{2,1,0:T(4,128)S(1)}, f32[1,3,1024]{2,1,0:T(4,128)S(1)}) custom-call(s32[1,20480]{1,0:T(1,128)S(1)} %bitcast.91, s32[1,160,256]{2,1,0:T(8,128)S(1)} %copy-done, f32[80,8,256]{2,1,0:T(8,128)S(1)} %get-tuple-element.13.near_ref, f32[160,8,256]{2,1,0:T(8,128)S(1)} %get-tuple-element.14.far_ref, ...), custom_call_target="tpu_custom_call" | custom-call | flops 24999999488 | bytes 1000000 | tf_op jit(solution)/shard_map/pallas_call | solution.py:192
  195.0 0.1 collective-permute-start.2
  195.1 0.4 collective-permute-start.3
  195.5 1.4 collective-permute-start.4
  197.0 1.3 collective-permute-done.2
  198.2 0.6 collective-permute-done.3
  198.9 0.0 collective-permute-done.4
  198.9 0.2 multiply_reduce_fusion
  199.1 0.2 multiply_reduce_fusion.3
  199.2 0.1 fusion.1
  199.3 0.1 fusion.2
  199.4 0.1 fusion.3
  199.5 0.1 fusion.4
  199.6 19.0 %psum.7 = f32[7,4]{1,0:T(8,128)S(1)} all-reduce(f32[7,4]{1,0:T(8,128)S(1)} %stack.31), channel_id=1, replica_groups=mesh['image'=4,'space'=8] {'space'}, use_global_device_ids=true, to_apply=%region_7.8 | all-reduce | flops 28 | bytes 224 | tf_op jit(solution)/shard_map/psum | solution.py:263
  218.5 0.1 multiply_bitcast_fusion
  218.6 0.1 fusion.6
  218.7 0.1 multiply_add_fusion
  218.8 0.1 add_sqrt_fusion
  218.9 0.2 reduce-window.4
  219.1 0.6 slice.120
  220.3 0.1 fusion.14
  220.4 0.1 fusion.15
  220.4 0.1 pad_maximum_fusion
  220.5 0.6 dynamic_slice.20
  221.1 0.7 dynamic_slice.18
  221.8 1.4 add_dynamic-update-slice_fusion
  223.1 0.9 copy.11
  (17 shorter events, 0.2 us)
Async XLA Ops:
  1.2 78.3 %collective-permute-start.5 = (f32[3,1024]{1,0:T(4,128)S(1)}, f32[3,1024]{1,0:T(4,128)S(1)}, u32[]{:S(2)}, u32[]{:S(2)}) collective-permute-start(f32[3,1024]{1,0:T(4,128)S(1)} %get-tuple-element.26), channel_id=1, source_target_pairs={{0,8},{8,16},{16,24},{24,0},{1,9},{9,17},{17,25},{25,1},{2,10},{10... | collective-permute-start | bytes 36872 | tf_op jit(solution)/shard_map/ppermute | solution.py:205
  1.7 77.8 %collective-permute-start.6 = (f32[3,1024]{1,0:T(4,128)S(1)}, f32[3,1024]{1,0:T(4,128)S(1)}, u32[]{:S(2)}, u32[]{:S(2)}) collective-permute-start(f32[3,1024]{1,0:T(4,128)S(1)} %get-tuple-element.26), channel_id=1, source_target_pairs={{0,16},{8,24},{16,0},{24,8},{1,17},{9,25},{17,1},{25,9},{2,18},{10... | collective-permute-start | bytes 36872 | tf_op jit(solution)/shard_map/ppermute | solution.py:205
  4.3 75.3 %collective-permute-start.7 = (f32[3,1024]{1,0:T(4,128)S(1)}, f32[3,1024]{1,0:T(4,128)S(1)}, u32[]{:S(2)}, u32[]{:S(2)}) collective-permute-start(f32[3,1024]{1,0:T(4,128)S(1)} %get-tuple-element.26), channel_id=1, source_target_pairs={{0,24},{8,0},{16,8},{24,16},{1,25},{9,1},{17,9},{25,17},{2,26},{10... | collective-permute-start | bytes 36872 | tf_op jit(solution)/shard_map/ppermute | solution.py:205
  6.3 0.9 copy-start.1
  7.2 0.9 copy-start.2
  8.1 0.9 copy-start.3
  9.0 27.9 %copy-start = (s32[1,160,256]{2,1,0:T(8,128)S(1)}, s32[1,160,256]{2,1,0:T(8,128)}, u32[]{:S(2)}) copy-start(s32[1,160,256]{2,1,0:T(8,128)} %partner_ref.3) | copy-start | bytes 491524
  9.0 27.9 %copy-start.4 = (s32[1,1,20480]{2,1,0:T(1,128)S(1)}, s32[1,1,20480]{2,1,0:T(1,128)}, u32[]{:S(2)}) copy-start(s32[1,1,20480]{2,1,0:T(1,128)} %param.11) | copy-start | bytes 245764
  32.1 47.7 %collective-permute-start = (f32[5,40,256]{2,1,0:T(8,128)S(1)}, f32[5,40,256]{2,1,0:T(8,128)S(1)}, u32[]{:S(2)}, u32[]{:S(2)}) collective-permute-start(f32[5,40,256]{2,1,0:T(8,128)S(1)} %get-tuple-element.15), channel_id=1, source_target_pairs={{0,1},{1,2},{2,3},{3,4},{4,5},{5,6},{6,7},{7,0},{8,9},{9,10},{10,1... | collective-permute-start | bytes 614408 | tf_op jit(solution)/shard_map/ppermute | solution.py:205
  33.6 46.2 %collective-permute-start.1 = (f32[5,40,256]{2,1,0:T(8,128)S(1)}, f32[5,40,256]{2,1,0:T(8,128)S(1)}, u32[]{:S(2)}, u32[]{:S(2)}) collective-permute-start(f32[5,40,256]{2,1,0:T(8,128)S(1)} %get-tuple-element.16), channel_id=1, source_target_pairs={{0,7},{1,0},{2,1},{3,2},{4,3},{5,4},{6,5},{7,6},{8,15},{9,8},{10,9... | collective-permute-start | bytes 614408 | tf_op jit(solution)/shard_map/ppermute | solution.py:205
  195.0 3.2 %collective-permute-start.2 = (f32[3,1024]{1,0:T(4,128)S(1)}, f32[3,1024]{1,0:T(4,128)S(1)}, u32[]{:S(2)}, u32[]{:S(2)}) collective-permute-start(f32[3,1024]{1,0:T(4,128)S(1)} %bitcast.84), channel_id=1, source_target_pairs={{0,8},{8,16},{16,24},{24,0},{1,9},{9,17},{17,25},{25,1},{2,10},{10... | collective-permute-start | bytes 36872 | tf_op jit(solution)/shard_map/ppermute | solution.py:205
  195.1 3.8 %collective-permute-start.3 = (f32[3,1024]{1,0:T(4,128)S(1)}, f32[3,1024]{1,0:T(4,128)S(1)}, u32[]{:S(2)}, u32[]{:S(2)}) collective-permute-start(f32[3,1024]{1,0:T(4,128)S(1)} %bitcast.85), channel_id=1, source_target_pairs={{0,16},{8,24},{16,0},{24,8},{1,17},{9,25},{17,1},{25,9},{2,18},{10... | collective-permute-start | bytes 36872 | tf_op jit(solution)/shard_map/ppermute | solution.py:205
  195.5 3.4 %collective-permute-start.4 = (f32[3,1024]{1,0:T(4,128)S(1)}, f32[3,1024]{1,0:T(4,128)S(1)}, u32[]{:S(2)}, u32[]{:S(2)}) collective-permute-start(f32[3,1024]{1,0:T(4,128)S(1)} %bitcast.86), channel_id=1, source_target_pairs={{0,24},{8,0},{16,8},{24,16},{1,25},{9,1},{17,9},{25,17},{2,26},{10... | collective-permute-start | bytes 36872 | tf_op jit(solution)/shard_map/ppermute | solution.py:205

commit v2 on v1

v2 whole, which is shorter than its diff:
```python
import functools

import jax
import jax.numpy as jnp
from jax import lax
from jax.experimental import pallas as pl
from jax.experimental.pallas import tpu as pltpu
from jax.sharding import PartitionSpec as P

SOL_DEV = 1024
TILE = 128
LANES = 128
ROW = 256
FIELDS = 5
WORDS = 3
FEATURES = 32

LJ_COEF = 0.5
CHARGE_COEF = 0.1
SOFT_CORE = 0.09
SLAB_WIDTH = 1.0
STEP_SIZE = 0.2
SPRING_COEF = 1.0
EPSILON = 1e-06

POS_LOW, POS_SCALE = -1.0, (2**19 - 1) / 3.0
A_SCALE = (2**19 - 1) / 2.0
Q_LOW, Q_SCALE = -4.0, (2**20 - 1) / 8.0
CENTRE = 0.5

F32 = jnp.float32
BF16 = jnp.bfloat16
I32 = jnp.int32
VMEM_LIMIT = 48 * 1024 * 1024


def packed(fields):
    def level(value, low, scale):
        return jnp.floor((value - low) * scale + 0.5).astype(I32)

    x, y, z = (level(fields[axis], POS_LOW, POS_SCALE) for axis in range(3))
    a = level(fields[3], 0.0, A_SCALE)
    q = level(fields[4], Q_LOW, Q_SCALE)
    return [
        (x << 13) | (a >> 6),
        (y << 13) | (q >> 7),
        (z << 13) | ((a & 63) << 7) | (q & 127),
    ]


def unpacked(words):
    def value(level, low, scale):
        return level.astype(F32) * (1.0 / scale) + low

    x, y, z = (value(lax.shift_right_logical(word, 13), POS_LOW, POS_SCALE) for word in words)
    a = ((words[0] & 8191) << 6) | ((words[2] >> 7) & 63)
    q = ((words[1] & 8191) << 7) | (words[2] & 127)
    return [x, y, z, value(a, 0.0, A_SCALE), value(q, Q_LOW, Q_SCALE)]


def lane_pick(source, lanes):
    numbers = lax.GatherDimensionNumbers(
        offset_dims=(),
        collapsed_slice_dims=(1,),
        start_index_map=(1,),
        operand_batching_dims=(0,),
        start_indices_batching_dims=(0,),
    )
    return lax.gather(
        source, lanes[:, :, None], numbers, (1, 1), mode=lax.GatherScatterMode.PROMISE_IN_BOUNDS
    )


def spread(words, store, rows):
    for word in range(WORDS):
        for row in range(rows):
            store[word, row * 8 : row * 8 + 8, :] = jnp.broadcast_to(
                words[word][row : row + 1, :], (8, LANES)
            )


def lookup(store, count, entries):
    lanes = [entry & (LANES - 1) for entry in entries]
    places = [entry >> 7 for entry in entries]
    unroll = 4

    def step(turn, found):
        found = list(found)
        for sub in range(unroll):
            row = turn * unroll + sub
            sources = [store[word, pl.ds(pl.multiple_of(row * 8, 8), 8), :] for word in range(WORDS)]
            for i in range(len(entries)):
                here = places[i] == row
                for word in range(WORDS):
                    at = i * WORDS + word
                    found[at] = jnp.where(here, lane_pick(sources[word], lanes[i]), found[at])
        return tuple(found)

    start = tuple(jnp.zeros((8, LANES), I32) for _ in range(WORDS * len(entries)))
    found = lax.fori_loop(0, count // unroll, step, start)
    return [found[i * WORDS : (i + 1) * WORDS] for i in range(len(entries))]


def shell_kernel(rows, scale_ref, pos_ref, strength_ref, charge_ref, ghost_ref, words_ref, down_ref, up_ref, plain, store):
    root = jnp.sqrt(jnp.full((SOL_DEV // LANES, LANES), scale_ref[0], F32))
    for row in range(rows):
        span = slice(row * LANES, (row + 1) * LANES)
        for axis in range(3):
            plain[axis, row : row + 1, :] = pos_ref[0, axis : axis + 1, span]
    plain[3] = strength_ref[...]
    plain[4] = charge_ref[...]
    solute = slice(0, SOL_DEV // LANES)
    plain[3, solute, :] = strength_ref[solute, :] * root
    plain[4, solute, :] = charge_ref[solute, :] * root
    words = packed([plain[field] for field in range(FIELDS)])
    for word in range(WORDS):
        words_ref[word] = words[word]
    spread([words_ref.at[word] for word in range(WORDS)], store, rows)
    half = rows // 2
    batch = 5 if half % 40 == 0 else 1
    for ref, first, shift in ((down_ref, 0, SLAB_WIDTH), (up_ref, half, -SLAB_WIDTH)):

        def step(turn, carry, ref=ref, first=first, shift=shift):
            base = turn * batch * 8
            entries = [
                ghost_ref[pl.ds(pl.multiple_of(first + base + i * 8, 8), 8), :] for i in range(batch)
            ]
            for i, found in enumerate(lookup(store, rows, entries)):
                fields = unpacked(found)
                fields[0] = fields[0] + shift
                for field in range(FIELDS):
                    ref[field, pl.ds(pl.multiple_of(base + i * 8, 8), 8), :] = fields[field]
            return carry

        lax.fori_loop(0, half // (8 * batch), step, 0)


def own_kernel(rows, order_ref, partner_ref, words_ref, near_ref, far_ref, store):
    spread([words_ref.at[word] for word in range(WORDS)], store, rows)
    half = rows // 2

    def near_step(turn, carry):
        base = turn * 32
        entries = [order_ref[pl.ds(pl.multiple_of(base + i * 8, 8), 8), :] for i in range(4)]
        for i, found in enumerate(lookup(store, rows, entries)):
            fields = unpacked(found)
            for field in range(FIELDS):
                near_ref[field, pl.ds(pl.multiple_of(base + i * 8, 8), 8), :] = fields[field]
        return carry

    lax.fori_loop(0, rows // 32, near_step, 0)
    sides = partner_ref.shape[2] // LANES

    def far_step(turn, carry):
        base = turn * 32
        spots = [
            (pl.ds(pl.multiple_of(base + i * 8, 8), 8), slice(side * LANES, (side + 1) * LANES))
            for i in range(4)
            for side in range(sides)
        ]
        entries = [partner_ref[0, rows_, span] - half * LANES for rows_, span in spots]
        for spot, found in zip(spots, lookup(store, rows, entries)):
            for word in range(WORDS):
                far_ref[word, spot[0], spot[1]] = found[word]
        return carry

    lax.fori_loop(0, rows // 32, far_step, 0)


def pieces(value, count):
    result = []
    for _ in range(count - 1):
        part = value.astype(BF16).astype(F32)
        result.append(part)
        value = value - part
    return result + [value]


def features(fields, near):
    rows = []
    coords = [pieces(fields[axis], 3) for axis in range(3)]
    for high, middle, low in coords:
        if near:
            rows += [2.0 * part for part in (high, high, middle, high, low, middle)]
        else:
            rows += [high, middle, high, low, high, middle]
    norm = -(fields[0] * fields[0] + fields[1] * fields[1] + fields[2] * fields[2])
    norm = pieces(norm + 1.0 if near else norm, 3)
    one = jnp.ones_like(fields[0])
    if near:
        rows += norm + [one] * 3
    else:
        rows += [one] * 3 + norm
    for value, coef in ((fields[3], LJ_COEF), (fields[4], CHARGE_COEF)):
        high, low = pieces(value * coef if near else value, 2)
        rows += [high, high, low, low] if near else [high, low, high, low]
    return rows


def one_hot(entries):
    width = entries.shape[1]
    grid = lax.broadcasted_iota(I32, (ROW, width), 0)
    return jnp.where(grid == (entries & (ROW - 1)), 1.0, 0.0).astype(BF16)


def two_pieces(values):
    high = values.astype(BF16)
    low = (values - high.astype(F32)).astype(BF16)
    return high, low


def joined(ref, spot):
    return jnp.concatenate([ref[plane, spot, :].astype(BF16) for plane in range(ref.shape[0])], axis=1)


def force_kernel(
    rows, order_ref, partner_ref, near_ref, far_ref, lower_ref, upper_ref, pos_ref, out_ref, solute_ref,
    store, near_rows, far_rows, shifted, total,
):
    half = rows // 2
    sides = partner_ref.shape[2] // LANES
    shell = []
    for field in range(FIELDS):
        both = [lower_ref[field], upper_ref[field]]
        if field == 0:
            both = [both[0] + SLAB_WIDTH, both[1] - SLAB_WIDTH]
        shell.append(jnp.concatenate(both, axis=0))
    words = packed(shell)
    spread(words, store, rows)
    total[...] = jnp.zeros_like(total)
    near_rows[...] = jnp.zeros_like(near_rows)
    shifted[...] = jnp.zeros_like(shifted)
    batch = 32

    def group(turn, carry):
        base = turn * batch
        spots = [(i, side) for i in range(batch // 8) for side in range(sides)]
        entries = []
        for i, side in spots:
            entry = partner_ref[0, pl.ds(pl.multiple_of(base + i * 8, 8), 8), side * LANES : (side + 1) * LANES]
            upper = entry - rows * LANES
            own = jnp.logical_and(entry >= half * LANES, upper < half * LANES)
            entries.append(jnp.where(own, 2 * rows * LANES, jnp.where(upper >= half * LANES, upper, entry)))
        for (i, side), found in zip(spots, lookup(store, rows, entries)):
            span = slice(side * LANES, (side + 1) * LANES)
            place = pl.ds(pl.multiple_of(base + i * 8, 8), 8)
            entry = partner_ref[0, place, span]
            fields = unpacked([found[word] | far_ref[word, place, span] for word in range(WORDS)])
            fields[0] = (
                fields[0]
                + jnp.where(entry >= (half + rows) * LANES, SLAB_WIDTH, 0.0)
                - jnp.where(entry < half * LANES, SLAB_WIDTH, 0.0)
            )
            for axis in range(3):
                fields[axis] = fields[axis] - CENTRE
            for k, row in enumerate(features(fields, False)):
                far_rows[side, pl.ds(i * 8 * FEATURES + k, 8, stride=FEATURES), :] = row
            for axis in range(3):
                high, low = pieces(fields[axis], 2)
                shifted[side, pl.ds(i * 128 + axis, 8, stride=16), :] = high
                shifted[side, pl.ds(i * 128 + 8 + axis, 8, stride=16), :] = low
            shifted[side, pl.ds(i * 128 + 3, 8, stride=16), :] = jnp.ones((8, LANES), F32)
        for i in range(batch // 8):
            place = pl.ds(pl.multiple_of(base + i * 8, 8), 8)
            fields = [near_ref[field, place, :] for field in range(FIELDS)]
            for axis in range(3):
                fields[axis] = fields[axis] - CENTRE
            for k, row in enumerate(features(fields, True)):
                group_of = 0 if k < 24 else (1 if k < 28 else 2)
                near_rows[group_of, pl.ds(i * 8 * FEATURES + k, 8, stride=FEATURES), :] = row

        def pair(turn, carry):
            forces = [[], [], []]
            numbers = []
            for side in range(ROW // TILE):
                local = turn * (ROW // TILE) + side
                spot = pl.ds(pl.multiple_of(local * FEATURES, FEATURES), FEATURES)
                grams = lax.dot_general(
                    joined(far_rows, spot),
                    joined(near_rows, spot),
                    (((0,), (0,)), ((), ())),
                    preferred_element_type=F32,
                )
                window = grams[:, 0:LANES]
                inside = jnp.maximum(window, 0.0)
                root = lax.rsqrt((1.0 + SOFT_CORE) - window)
                strength = grams[:, LANES : 2 * LANES] + grams[:, 2 * LANES :] * (root * root * root)
                high, low = two_pieces(inside * inside * strength)
                left = joined(shifted, pl.ds(pl.multiple_of(local * 16, 16), 16))
                sums = jnp.dot(left, high, preferred_element_type=F32) + jnp.dot(
                    left, low, preferred_element_type=F32
                )
                whole_sum = sums[3:4]
                for axis in range(3):
                    near = near_ref[axis, pl.ds(base + local, 1), :] - CENTRE
                    forces[axis].append(near * whole_sum - sums[axis : axis + 1] - sums[8 + axis : 9 + axis])
                numbers.append(order_ref[pl.ds(base + local, 1), :])
            entries = jnp.concatenate(numbers, axis=1)
            hot = one_hot(entries)
            grid = lax.broadcasted_iota(I32, (total.shape[0] // 3, ROW), 0)
            mask = grid == (entries >> 8)
            parts = [
                jnp.where(mask, jnp.concatenate(forces[axis], axis=1), 0.0) for axis in range(3)
            ]
            high, low = two_pieces(jnp.concatenate(parts, axis=0))
            total[...] += lax.dot_general(
                jnp.concatenate([high, low], axis=1),
                jnp.concatenate([hot, hot], axis=1),
                (((1,), (1,)), ((), ())),
                preferred_element_type=F32,
            )
            return carry

        lax.fori_loop(0, batch * TILE // ROW, pair, 0)
        return carry

    lax.fori_loop(0, rows // batch, group, 0)
    table_rows = total.shape[0] // 3
    for row in range(table_rows):
        span = slice(row * ROW, (row + 1) * ROW)
        for axis in range(3):
            force = total[axis * table_rows + row : axis * table_rows + row + 1, :]
            out_ref[0, axis : axis + 1, span] = pos_ref[0, axis : axis + 1, span] + STEP_SIZE * force
    solute_ref[...] = out_ref[:, :, 0:SOL_DEV]


def whole(*shape, dtype=F32):
    return jax.ShapeDtypeStruct(shape, dtype)


def kernel_call(body, outs, scratch=(), scalar=0, **more):
    return functools.partial(_call, body, outs, scratch, scalar, more)


def _call(body, outs, scratch, scalar, more, *args):
    in_specs = [pl.BlockSpec(memory_space=pltpu.SMEM)] * scalar
    in_specs += [pl.BlockSpec(memory_space=pltpu.VMEM)] * (len(args) - scalar)
    return pl.pallas_call(
        body,
        out_shape=outs,
        in_specs=in_specs,
        out_specs=[pl.BlockSpec(memory_space=pltpu.VMEM)] * len(outs),
        scratch_shapes=list(scratch),
        compiler_params=pltpu.CompilerParams(vmem_limit_bytes=VMEM_LIMIT),
        **more,
    )(*args)


def turned(array, axis, by):
    count = lax.axis_size(axis)
    return lax.ppermute(array, axis, [(i, (i + by) % count) for i in range(count)])


def round_trip(array, axis):
    count, index = lax.axis_size(axis), lax.axis_index(axis)
    result = jnp.zeros((count,) + array.shape, array.dtype)
    for by in range(count):
        piece = turned(array, axis, by) if by else array
        result = lax.dynamic_update_index_in_dim(result, piece, (index + count - by) % count, 0)
    return result


def inner(left, right):
    return jnp.sum(left * right, axis=(1, 2))


def per_device(positions, strength, charge, rest_scale, cell_order, ghost_index, tile_atoms):
    atoms = positions.shape[2]
    rows = atoms // LANES
    partners = tile_atoms.shape[2]
    order = cell_order.reshape(rows, LANES)
    paths = round_trip(positions[0, :, :SOL_DEV], "image")
    store = pltpu.VMEM((WORDS, rows * 8, LANES), I32)
    words, down, up = kernel_call(
        functools.partial(shell_kernel, rows),
        [
            whole(WORDS, rows, LANES, dtype=I32),
            whole(FIELDS, rows // 2, LANES),
            whole(FIELDS, rows // 2, LANES),
        ],
        [pltpu.VMEM((FIELDS, rows, LANES), F32), store],
        scalar=1,
        cost_estimate=pl.CostEstimate(flops=8 * 10**9, bytes_accessed=10**6, transcendentals=0),
    )(
        rest_scale,
        positions,
        strength.reshape(rows, LANES),
        charge.reshape(rows, LANES),
        ghost_index.reshape(rows, LANES),
    )
    upper = turned(down, "space", -1)
    lower = turned(up, "space", 1)
    near, far = kernel_call(
        functools.partial(own_kernel, rows),
        [whole(FIELDS, rows, LANES), whole(WORDS, rows, partners, dtype=I32)],
        [store],
        cost_estimate=pl.CostEstimate(flops=25 * 10**9, bytes_accessed=10**6, transcendentals=0),
    )(order, tile_atoms, words)
    out, solute = kernel_call(
        functools.partial(force_kernel, rows),
        [whole(1, 3, atoms), whole(1, 3, SOL_DEV)],
        [
            store,
            pltpu.VMEM((3, 32 * FEATURES, LANES), F32),
            pltpu.VMEM((partners // LANES, 32 * FEATURES, LANES), F32),
            pltpu.VMEM((partners // LANES, 32 * 16, LANES), F32),
            pltpu.VMEM((3 * (atoms // ROW), ROW), F32),
        ],
        cost_estimate=pl.CostEstimate(flops=25 * 10**9, bytes_accessed=10**6, transcendentals=0),
    )(order, tile_atoms, near, far, lower, upper, positions)

    pushed = round_trip(solute[0], "image")
    images = lax.axis_size("image")
    index = lax.axis_index("image")
    steps = paths[1:] - paths[:-1]
    upper_path = jnp.concatenate([paths[1:], paths[-1:]])
    lower_path = jnp.concatenate([paths[:1], paths[:-1]])
    tangents = upper_path - lower_path
    gaps = pushed[1:] - pushed[:-1]
    none = jnp.zeros((1,), F32)
    sums = lax.psum(
        jnp.stack(
            [
                inner(tangents, tangents),
                inner(pushed - paths, tangents),
                jnp.concatenate([inner(steps, steps), none]),
                jnp.concatenate([inner(gaps, gaps), none]),
                jnp.concatenate([inner(gaps, tangents[1:]), none]),
                jnp.concatenate([inner(gaps, tangents[:-1]), none]),
                jnp.concatenate([inner(tangents[1:], tangents[:-1]), none]),
            ]
        ),
        "space",
    )
    tangent_sq, along = sums[0], sums[1]
    step_sq, gap_sq, gap_next, gap_this, cross = (sums[i, :-1] for i in range(2, 7))
    step_root = jnp.sqrt(step_sq + EPSILON)
    spring = SPRING_COEF * (step_root[1:] - step_root[:-1]) / jnp.sqrt(tangent_sq[1:-1] + EPSILON)
    spring = jnp.concatenate([none, spring, none])
    shift = STEP_SIZE * spring - along / (tangent_sq + EPSILON)
    ahead_shift, here_shift = shift[1:], shift[:-1]
    length_sq = (
        gap_sq
        + ahead_shift * ahead_shift * tangent_sq[1:]
        + here_shift * here_shift * tangent_sq[:-1]
        + 2.0 * (ahead_shift * gap_next - here_shift * gap_this - ahead_shift * here_shift * cross)
    )
    lengths = jnp.sqrt(jnp.maximum(length_sq, 0.0) + EPSILON)
    knots = jnp.concatenate([none, jnp.cumsum(lengths)])
    targets = knots[-1] * (jnp.arange(images, dtype=F32) / (images - 1))
    back = jnp.concatenate([none, jnp.clip((knots - targets)[1:] / lengths, 0.0, 1.0)])
    ahead = jnp.concatenate([jnp.clip((targets - knots)[:-1] / lengths, 0.0, 1.0), none])
    moved = pushed + shift[:, None, None] * tangents

    def at(array, place):
        return lax.dynamic_index_in_dim(array, jnp.clip(place, 0, images - 1), 0, keepdims=False)

    here = at(moved, index)
    blended = (
        here
        + at(back, index) * (at(moved, index - 1) - here)
        + at(ahead, index) * (at(moved, index + 1) - here)
    )
    return lax.dynamic_update_slice(out, blended[None], (0, 0, 0))


def solution(mesh):
    placed = (
        P("image", None, "space"),
        P("space"),
        P("space"),
        P("image"),
        P("image", "space", None),
        P("image", "space", None),
        P("image", "space", None),
    )
    return jax.shard_map(
        per_device, mesh=mesh, in_specs=placed, out_specs=P("image", None, "space"), check_vma=False
    )
```

time: 224 us -> 286 us (1.28)
  Pallas kernels: 181 us -> 245 us
    pallas_call x3, Pallas kernels: 181 us -> 245 us  [_call(): pl.pallas_call(body, out_shape=outs, in_specs=in_specs, out_specs=[pl.Blo...]
  transfers between devices with their start and end apart: 8 -> 8, of which waited for: 2 -> 2; matrix products, arithmetic and copies ran while one was open for 0% -> 0% of each run, Pallas kernels for 29% -> 41%
where the time goes in v2:
time: 286 us
  Pallas kernels  245 us (86%)
  blocking collectives  19 us (7%)
  starting transfers between devices  11.2 us (4%)
  local copies, waits for them, and re-layouts  4.13 us (1%)
  other arithmetic  2.92 us (1%)
    pallas_call x3, Pallas kernels, _call(): pl.pallas_call(body, out_shape=outs, in_specs=in_specs, out_specs=[pl.Blo...  245 us
    psum x1, blocking collectives, per_device(): lax.psum(jnp.stack([inner(tangents, tangents), inner(pushed - paths, tang...  19 us
    ppermute x8, starting transfers between devices, turned(): lax.ppermute(array, axis, [(i, (i + by) % count) for i in range(count)])  11.2 us
  transfers between devices with their start and end apart: 8, of which 2 were waited for; matrix products, arithmetic and copies ran while one was open for 0% of the time, Pallas kernels for 41%

profile of v2, /device:TPU:0, one launch (start us, length us, event | category | flops | bytes accessed | tf_op | source)
XLA Modules:
  0.0 285.6 jit_solution(13915412384372985302)
XLA Ops:
  0.0 1.2 copy.8.pos_ref
  1.2 0.0 copy-start.1
  1.2 0.5 collective-permute-start.5
  1.7 2.6 collective-permute-start.6
  4.3 1.4 collective-permute-start.7
  6.4 0.0 copy-done.2
  6.4 0.0 copy-done.3
  6.4 0.0 copy-done.1
  6.4 0.0 copy-start
  6.4 0.0 copy-start.4
  6.4 31.0 %shard_map.73 = (s32[3,160,128]{2,1,0:T(8,128)S(1)}, f32[5,80,128]{2,1,0:T(8,128)S(1)}, f32[5,80,128]{2,1,0:T(8,128)S(1)}) custom-call(f32[1]{0:T(128)S(6)} %copy.22.scale_ref, f32[1,3,20480]{2,1,0:T(4,128)S(1)} %copy.8.pos_ref, f32[160,128]{1,0:T(8,128)S(1)} %bitcast.87, f32[160,128]{1,0:T(8,128)S(1)} %bitcast.88, s32[160,128]{1,0:T(8,128)S(1)} %bitcast.89), custom_call_target="tpu_custom_call" | custom-call | flops 8000000000 | bytes 1000000 | tf_op jit(solution)/shard_map/pallas_call | solution.py:338
  37.5 1.5 collective-permute-start
  39.0 3.2 %collective-permute-start.1 = (f32[5,80,128]{2,1,0:T(8,128)S(1)}, f32[5,80,128]{2,1,0:T(8,128)S(1)}, u32[]{:S(2)}, u32[]{:S(2)}) collective-permute-start(f32[5,80,128]{2,1,0:T(8,128)S(1)} %get-tuple-element.16), channel_id=1, source_target_pairs={{0,7},{1,0},{2,1},{3,2},{4,3},{5,4},{6,5},{7,6},{8,15},{9,8},{10,9... | collective-permute-start | bytes 614408 | tf_op jit(solution)/shard_map/ppermute | solution.py:351
  42.2 86.6 %shard_map.74 = (f32[5,160,128]{2,1,0:T(8,128)S(1)}, s32[3,160,256]{2,1,0:T(8,128)S(1)}) custom-call(s32[160,128]{1,0:T(8,128)S(1)} %bitcast.90, s32[1,160,256]{2,1,0:T(8,128)S(1)} %copy-done, s32[3,160,128]{2,1,0:T(8,128)S(1)} %get-tuple-element.12.words_ref), custom_call_target="tpu_custom_call" | custom-call | flops 24999999488 | bytes 1000000 | tf_op jit(solution)/shard_map/pallas_call | solution.py:338
  128.9 0.0 collective-permute-done.5
  129.0 0.0 collective-permute-done.6
  129.0 0.0 collective-permute-done.7
  129.0 0.1 multiply_reduce_fusion.6
  129.1 0.1 fusion
  129.2 0.0 collective-permute-done.lower_ref
  129.2 0.0 collective-permute-done.1.upper_ref
  129.2 127.2 %shard_map.75 = (f32[1,3,20480]{2,1,0:T(4,128)S(1)}, f32[1,3,1024]{2,1,0:T(4,128)S(1)}) custom-call(s32[160,128]{1,0:T(8,128)S(1)} %bitcast.91, s32[1,160,256]{2,1,0:T(8,128)S(1)} %copy-done, f32[5,160,128]{2,1,0:T(8,128)S(1)} %get-tuple-element.13.near_ref, s32[3,160,256]{2,1,0:T(8,128)S(1)} %get-tuple-element.14.far_ref, ...), custom_call_target="tpu_custom_call" | custom-call | flops 24999999488 | bytes 1000000 | tf_op jit(solution)/shard_map/pallas_call | solution.py:338
  256.5 0.1 collective-permute-start.2
  256.6 0.4 collective-permute-start.3
  257.0 1.4 collective-permute-start.4
  258.4 1.3 collective-permute-done.2
  259.7 0.6 collective-permute-done.3
  260.4 0.0 collective-permute-done.4
  260.4 0.2 multiply_reduce_fusion
  260.5 0.2 multiply_reduce_fusion.3
  260.7 0.1 fusion.1
  260.8 0.1 fusion.2
  260.9 0.1 fusion.3
  260.9 0.1 fusion.4
  261.0 19.0 %psum.7 = f32[7,4]{1,0:T(8,128)S(1)} all-reduce(f32[7,4]{1,0:T(8,128)S(1)} %stack.31), channel_id=1, replica_groups=mesh['image'=4,'space'=8] {'space'}, use_global_device_ids=true, to_apply=%region_7.8 | all-reduce | flops 28 | bytes 224 | tf_op jit(solution)/shard_map/psum | solution.py:421
  280.0 0.1 multiply_bitcast_fusion
  280.1 0.1 fusion.6
  280.2 0.1 multiply_add_fusion
  280.3 0.1 add_sqrt_fusion
  280.3 0.2 reduce-window.4
  280.5 0.6 slice.120
  281.8 0.1 fusion.14
  281.8 0.1 fusion.15
  281.9 0.1 pad_maximum_fusion
  282.0 0.6 dynamic_slice.20
  282.6 0.7 dynamic_slice.18
  283.2 1.4 add_dynamic-update-slice_fusion
  284.6 0.9 copy.11
  (17 shorter events, 0.2 us)
Async XLA Ops:
  0.0 6.4 %copy-start.2 = (f32[20480]{0:T(1024)S(1)}, f32[20480]{0:T(1024)}, u32[]{:S(2)}) copy-start(f32[20480]{0:T(1024)} %param.9) | copy-start | bytes 245764
  0.0 6.4 %copy-start.3 = (s32[1,1,20480]{2,1,0:T(1,128)S(1)}, s32[1,1,20480]{2,1,0:T(1,128)}, u32[]{:S(2)}) copy-start(s32[1,1,20480]{2,1,0:T(1,128)} %param.12) | copy-start | bytes 245764
  1.2 5.2 %copy-start.1 = (f32[20480]{0:T(1024)S(1)}, f32[20480]{0:T(1024)}, u32[]{:S(2)}) copy-start(f32[20480]{0:T(1024)} %param.8) | copy-start | bytes 245764
  1.2 127.7 %collective-permute-start.5 = (f32[3,1024]{1,0:T(4,128)S(1)}, f32[3,1024]{1,0:T(4,128)S(1)}, u32[]{:S(2)}, u32[]{:S(2)}) collective-permute-start(f32[3,1024]{1,0:T(4,128)S(1)} %get-tuple-element.26), channel_id=1, source_target_pairs={{0,8},{8,16},{16,24},{24,0},{1,9},{9,17},{17,25},{25,1},{2,10},{10... | collective-permute-start | bytes 36872 | tf_op jit(solution)/shard_map/ppermute | solution.py:351
  1.7 127.2 %collective-permute-start.6 = (f32[3,1024]{1,0:T(4,128)S(1)}, f32[3,1024]{1,0:T(4,128)S(1)}, u32[]{:S(2)}, u32[]{:S(2)}) collective-permute-start(f32[3,1024]{1,0:T(4,128)S(1)} %get-tuple-element.26), channel_id=1, source_target_pairs={{0,16},{8,24},{16,0},{24,8},{1,17},{9,25},{17,1},{25,9},{2,18},{10... | collective-permute-start | bytes 36872 | tf_op jit(solution)/shard_map/ppermute | solution.py:351
  4.3 124.7 %collective-permute-start.7 = (f32[3,1024]{1,0:T(4,128)S(1)}, f32[3,1024]{1,0:T(4,128)S(1)}, u32[]{:S(2)}, u32[]{:S(2)}) collective-permute-start(f32[3,1024]{1,0:T(4,128)S(1)} %get-tuple-element.26), channel_id=1, source_target_pairs={{0,24},{8,0},{16,8},{24,16},{1,25},{9,1},{17,9},{25,17},{2,26},{10... | collective-permute-start | bytes 36872 | tf_op jit(solution)/shard_map/ppermute | solution.py:351
  6.4 35.8 %copy-start = (s32[1,160,256]{2,1,0:T(8,128)S(1)}, s32[1,160,256]{2,1,0:T(8,128)}, u32[]{:S(2)}) copy-start(s32[1,160,256]{2,1,0:T(8,128)} %partner_ref.3) | copy-start | bytes 491524
  6.4 35.8 %copy-start.4 = (s32[1,1,20480]{2,1,0:T(1,128)S(1)}, s32[1,1,20480]{2,1,0:T(1,128)}, u32[]{:S(2)}) copy-start(s32[1,1,20480]{2,1,0:T(1,128)} %param.11) | copy-start | bytes 245764
  37.5 91.8 %collective-permute-start = (f32[5,80,128]{2,1,0:T(8,128)S(1)}, f32[5,80,128]{2,1,0:T(8,128)S(1)}, u32[]{:S(2)}, u32[]{:S(2)}) collective-permute-start(f32[5,80,128]{2,1,0:T(8,128)S(1)} %get-tuple-element.15), channel_id=1, source_target_pairs={{0,1},{1,2},{2,3},{3,4},{4,5},{5,6},{6,7},{7,0},{8,9},{9,10},{10,1... | collective-permute-start | bytes 614408 | tf_op jit(solution)/shard_map/ppermute | solution.py:351
  39.0 90.2 %collective-permute-start.1 = (f32[5,80,128]{2,1,0:T(8,128)S(1)}, f32[5,80,128]{2,1,0:T(8,128)S(1)}, u32[]{:S(2)}, u32[]{:S(2)}) collective-permute-start(f32[5,80,128]{2,1,0:T(8,128)S(1)} %get-tuple-element.16), channel_id=1, source_target_pairs={{0,7},{1,0},{2,1},{3,2},{4,3},{5,4},{6,5},{7,6},{8,15},{9,8},{10,9... | collective-permute-start | bytes 614408 | tf_op jit(solution)/shard_map/ppermute | solution.py:351
  256.5 3.2 %collective-permute-start.2 = (f32[3,1024]{1,0:T(4,128)S(1)}, f32[3,1024]{1,0:T(4,128)S(1)}, u32[]{:S(2)}, u32[]{:S(2)}) collective-permute-start(f32[3,1024]{1,0:T(4,128)S(1)} %bitcast.84), channel_id=1, source_target_pairs={{0,8},{8,16},{16,24},{24,0},{1,9},{9,17},{17,25},{25,1},{2,10},{10... | collective-permute-start | bytes 36872 | tf_op jit(solution)/shard_map/ppermute | solution.py:351
  256.6 3.8 %collective-permute-start.3 = (f32[3,1024]{1,0:T(4,128)S(1)}, f32[3,1024]{1,0:T(4,128)S(1)}, u32[]{:S(2)}, u32[]{:S(2)}) collective-permute-start(f32[3,1024]{1,0:T(4,128)S(1)} %bitcast.85), channel_id=1, source_target_pairs={{0,16},{8,24},{16,0},{24,8},{1,17},{9,25},{17,1},{25,9},{2,18},{10... | collective-permute-start | bytes 36872 | tf_op jit(solution)/shard_map/ppermute | solution.py:351
  257.0 3.4 %collective-permute-start.4 = (f32[3,1024]{1,0:T(4,128)S(1)}, f32[3,1024]{1,0:T(4,128)S(1)}, u32[]{:S(2)}, u32[]{:S(2)}) collective-permute-start(f32[3,1024]{1,0:T(4,128)S(1)} %bitcast.86), channel_id=1, source_target_pairs={{0,24},{8,0},{16,8},{24,16},{1,25},{9,1},{17,9},{25,17},{2,26},{10... | collective-permute-start | bytes 36872 | tf_op jit(solution)/shard_map/ppermute | solution.py:351

commit v3 on v1

v3 whole, which is shorter than its diff:
```python
import functools

import jax
import jax.numpy as jnp
import numpy as np
from jax import lax
from jax.experimental import pallas as pl
from jax.experimental.pallas import tpu as pltpu
from jax.sharding import PartitionSpec as P

SOL_DEV = 1024
TILE = 128
LANES = 128
FIELDS = 5
STRIDE = 48

LJ_COEF = 0.5
CHARGE_COEF = 0.1
SOFT_CORE = 0.09
SLAB_WIDTH = 1.0
STEP_SIZE = 0.2
SPRING_COEF = 1.0
EPSILON = 1e-06
CENTRE = 0.5

F32 = jnp.float32
BF16 = jnp.bfloat16
I32 = jnp.int32
VMEM_LIMIT = 58 * 1024 * 1024

ONES = 18
NORM = 21
DEPTH = 24
CHARGE = 28
LAST = 32


def near_selector():
    chosen = np.zeros((LANES, 3 * LANES), np.float32)
    for axis in range(3):
        high, middle, low = 6 * axis, 6 * axis + 1, 6 * axis + 3
        for k, source in enumerate((high, high, middle, high, low, middle)):
            chosen[source, 6 * axis + k] = 2.0
    for k in range(3):
        chosen[NORM + k, ONES + k] = 1.0
        chosen[ONES, NORM + k] = 1.0
    chosen[ONES, LAST] = 1.0
    for block, first in ((1, DEPTH), (2, CHARGE)):
        for k, source in enumerate((first, first, first + 1, first + 1)):
            chosen[source, block * LANES + first + k] = 1.0
    return jnp.asarray(chosen, BF16)


def pieces(value, count):
    result = []
    for _ in range(count - 1):
        part = value.astype(BF16).astype(F32)
        result.append(part)
        value = value - part
    return result + [value]


def features(fields):
    rows = []
    for axis in range(3):
        high, middle, low = pieces(fields[axis], 3)
        rows += [high, middle, high, low, high, middle]
    one = jnp.ones_like(fields[0])
    rows += [one] * 3
    rows += pieces(-(fields[0] * fields[0] + fields[1] * fields[1] + fields[2] * fields[2]), 3)
    for value in fields[3:]:
        high, low = pieces(value, 2)
        rows += [high, low, high, low]
    return rows + [one]


def two_pieces(values):
    high = values.astype(BF16)
    low = (values - high.astype(F32)).astype(BF16)
    return high, low


def nt_dot(left, right):
    return lax.dot_general(left, right, (((1,), (1,)), ((), ())), preferred_element_type=F32)


def fill_table(rows, fields_ref, eye_ref, table, planes):
    planes[...] = jnp.zeros_like(planes)
    groups = rows // 8

    def step(turn, carry):
        domain = turn // groups
        first = pl.multiple_of((turn % groups) * 8, 8)
        fields = [fields_ref[domain, field, pl.ds(first, 8), :] for field in range(FIELDS)]
        shift = (domain - 1).astype(F32) * SLAB_WIDTH
        fields[0] = fields[0] + shift
        for axis in range(3):
            fields[axis] = fields[axis] - CENTRE
        fields[3] = fields[3] * LJ_COEF**0.5
        fields[4] = fields[4] * CHARGE_COEF**0.5
        for k, row in enumerate(features(fields)):
            planes[pl.ds(k, 8, stride=STRIDE), :] = row
        for block in range(8):
            part = planes[block * STRIDE : (block + 1) * STRIDE, :].astype(BF16)
            part = jnp.concatenate([part, jnp.zeros((LANES - STRIDE, LANES), BF16)], axis=0)
            start = pl.multiple_of((turn * 8 + block) * LANES, LANES)
            table[pl.ds(start, LANES), :] = nt_dot(eye_ref[...], part)
        return carry

    lax.fori_loop(0, 3 * groups, step, 0)


def force_kernel(
    rows, partner_ref, entry_ref, order_ref, fields_ref, select_ref, eye_ref, out_ref, solute_ref,
    table, forces, planes, far_a, far_b, near_a, near_b, sum_a, sum_b,
):
    fill_table(rows, fields_ref, eye_ref, table, planes)
    partners = far_a.shape[0]
    own = rows * LANES

    def load(tile, far, near):
        for k in range(partners):
            entry = entry_ref[partner_ref[tile * partners + k]]
            far[k : k + 1, :] = table[pl.ds(entry, 1), :]
        for k in range(TILE):
            entry = order_ref[tile * TILE + k] + own
            near[k : k + 1, :] = table[pl.ds(entry, 1), :]

    def compute(far, near, sums):
        others = far[...].astype(BF16)
        left = jnp.dot(near[...].astype(BF16), select_ref[...], preferred_element_type=F32).astype(BF16)
        left = jnp.concatenate([left[:, k * LANES : (k + 1) * LANES] for k in range(3)], axis=0)
        grams = nt_dot(left, others)
        window = grams[0:TILE]
        inside = jnp.maximum(window, 0.0)
        root = lax.rsqrt((1.0 + SOFT_CORE) - window)
        strength = grams[TILE : 2 * TILE] + grams[2 * TILE :] * (root * root * root)
        high, low = two_pieces(inside * inside * strength)
        both = jnp.dot(jnp.concatenate([high, low], axis=0), others, preferred_element_type=F32)
        sums[...] = both[0:TILE] + both[TILE:]

    def save(tile, sums):
        for k in range(TILE):
            forces[pl.ds(order_ref[tile * TILE + k], 1), :] = sums[k : k + 1, :]

    load(0, far_a, near_a)

    def step(turn, carry):
        tile = turn * 2
        load(tile + 1, far_b, near_b)
        compute(far_a, near_a, sum_a)
        save(tile, sum_a)
        load(jnp.minimum(tile + 2, rows - 1), far_a, near_a)
        compute(far_b, near_b, sum_b)
        save(tile + 1, sum_b)
        return carry

    lax.fori_loop(0, rows // 2, step, 0)

    def finish(row, carry):
        turned_sums = forces[pl.ds(pl.multiple_of(row * LANES, LANES), LANES), :].T
        for axis in range(3):
            first = 6 * axis
            moment = (
                turned_sums[first : first + 1] + turned_sums[first + 1 : first + 2] + turned_sums[first + 3 : first + 4]
            )
            place = fields_ref[1, axis, pl.ds(row, 1), :]
            force = (place - CENTRE) * turned_sums[ONES : ONES + 1] - moment
            out_ref[axis, pl.ds(row, 1), :] = place + STEP_SIZE * force
        return carry

    lax.fori_loop(0, rows, finish, 0)
    solute_ref[...] = out_ref[:, 0 : SOL_DEV // LANES, :]


def whole(*shape, dtype=F32):
    return jax.ShapeDtypeStruct(shape, dtype)


def kernel_call(body, outs, scratch=(), scalar=0, **more):
    return functools.partial(_call, body, outs, scratch, scalar, more)


def _call(body, outs, scratch, scalar, more, *args):
    in_specs = [pl.BlockSpec(memory_space=pltpu.SMEM)] * scalar
    in_specs += [pl.BlockSpec(memory_space=pltpu.VMEM)] * (len(args) - scalar)
    return pl.pallas_call(
        body,
        out_shape=outs,
        in_specs=in_specs,
        out_specs=[pl.BlockSpec(memory_space=pltpu.VMEM)] * len(outs),
        scratch_shapes=list(scratch),
        compiler_params=pltpu.CompilerParams(vmem_limit_bytes=VMEM_LIMIT),
        **more,
    )(*args)


def turned(array, axis, by):
    count = lax.axis_size(axis)
    return lax.ppermute(array, axis, [(i, (i + by) % count) for i in range(count)])


def round_trip(array, axis):
    count, index = lax.axis_size(axis), lax.axis_index(axis)
    result = jnp.zeros((count,) + array.shape, array.dtype)
    for by in range(count):
        piece = turned(array, axis, by) if by else array
        result = lax.dynamic_update_index_in_dim(result, piece, (index + count - by) % count, 0)
    return result


def inner(left, right):
    return jnp.sum(left * right, axis=(1, 2))


def per_device(positions, strength, charge, rest_scale, cell_order, ghost_index, tile_atoms):
    atoms = positions.shape[2]
    rows = atoms // LANES
    half = atoms // 2
    partners = tile_atoms.shape[2]
    paths = round_trip(positions[0, :, :SOL_DEV], "image")

    factor = jnp.where(jnp.arange(atoms) < SOL_DEV, jnp.sqrt(rest_scale[0]), 1.0)
    scaled = jnp.stack([strength * factor, charge * factor])
    fields = jnp.concatenate([positions[0], scaled]).reshape(FIELDS, rows, LANES)
    fields = jnp.stack([turned(fields, "space", 1), fields, turned(fields, "space", -1)])
    shell = ghost_index.reshape(atoms)
    entries = jnp.concatenate(
        [
            turned(shell[half:], "space", 1),
            jnp.arange(atoms, 2 * atoms, dtype=I32),
            turned(shell[:half], "space", -1) + 2 * atoms,
        ]
    )
    out, solute = kernel_call(
        functools.partial(force_kernel, rows),
        [whole(3, rows, LANES), whole(3, SOL_DEV // LANES, LANES)],
        [
            pltpu.VMEM((3 * atoms, LANES), F32),
            pltpu.VMEM((atoms, LANES), F32),
            pltpu.VMEM((8 * STRIDE, LANES), F32),
            pltpu.VMEM((partners, LANES), F32),
            pltpu.VMEM((partners, LANES), F32),
            pltpu.VMEM((TILE, LANES), F32),
            pltpu.VMEM((TILE, LANES), F32),
            pltpu.VMEM((TILE, LANES), F32),
            pltpu.VMEM((TILE, LANES), F32),
        ],
        scalar=3,
        cost_estimate=pl.CostEstimate(flops=25 * 10**9, bytes_accessed=10**6, transcendentals=0),
    )(
        tile_atoms.reshape(rows * partners),
        entries,
        cell_order.reshape(atoms),
        fields,
        near_selector(),
        jnp.eye(LANES, dtype=BF16),
    )
    out = out.reshape(1, 3, atoms)
    solute = solute.reshape(1, 3, SOL_DEV)

    pushed = round_trip(solute[0], "image")
    images = lax.axis_size("image")
    index = lax.axis_index("image")
    steps = paths[1:] - paths[:-1]
    upper_path = jnp.concatenate([paths[1:], paths[-1:]])
    lower_path = jnp.concatenate([paths[:1], paths[:-1]])
    tangents = upper_path - lower_path
    gaps = pushed[1:] - pushed[:-1]
    none = jnp.zeros((1,), F32)
    sums = lax.psum(
        jnp.stack(
            [
                inner(tangents, tangents),
                inner(pushed - paths, tangents),
                jnp.concatenate([inner(steps, steps), none]),
                jnp.concatenate([inner(gaps, gaps), none]),
                jnp.concatenate([inner(gaps, tangents[1:]), none]),
                jnp.concatenate([inner(gaps, tangents[:-1]), none]),
                jnp.concatenate([inner(tangents[1:], tangents[:-1]), none]),
            ]
        ),
        "space",
    )
    tangent_sq, along = sums[0], sums[1]
    step_sq, gap_sq, gap_next, gap_this, cross = (sums[i, :-1] for i in range(2, 7))
    step_root = jnp.sqrt(step_sq + EPSILON)
    spring = SPRING_COEF * (step_root[1:] - step_root[:-1]) / jnp.sqrt(tangent_sq[1:-1] + EPSILON)
    spring = jnp.concatenate([none, spring, none])
    shift = STEP_SIZE * spring - along / (tangent_sq + EPSILON)
    ahead_shift, here_shift = shift[1:], shift[:-1]
    length_sq = (
        gap_sq
        + ahead_shift * ahead_shift * tangent_sq[1:]
        + here_shift * here_shift * tangent_sq[:-1]
        + 2.0 * (ahead_shift * gap_next - here_shift * gap_this - ahead_shift * here_shift * cross)
    )
    lengths = jnp.sqrt(jnp.maximum(length_sq, 0.0) + EPSILON)
    knots = jnp.concatenate([none, jnp.cumsum(lengths)])
    targets = knots[-1] * (jnp.arange(images, dtype=F32) / (images - 1))
    back = jnp.concatenate([none, jnp.clip((knots - targets)[1:] / lengths, 0.0, 1.0)])
    ahead = jnp.concatenate([jnp.clip((targets - knots)[:-1] / lengths, 0.0, 1.0), none])
    moved = pushed + shift[:, None, None] * tangents

    def at(array, place):
        return lax.dynamic_index_in_dim(array, jnp.clip(place, 0, images - 1), 0, keepdims=False)

    here = at(moved, index)
    blended = (
        here
        + at(back, index) * (at(moved, index - 1) - here)
        + at(ahead, index) * (at(moved, index + 1) - here)
    )
    return lax.dynamic_update_slice(out, blended[None], (0, 0, 0))


def solution(mesh):
    placed = (
        P("image", None, "space"),
        P("space"),
        P("space"),
        P("image"),
        P("image", "space", None),
        P("image", "space", None),
        P("image", "space", None),
    )
    return jax.shard_map(
        per_device, mesh=mesh, in_specs=placed, out_specs=P("image", None, "space"), check_vma=False
    )
```

time: 224 us -> 213 us (0.951)
  Pallas kernels: 181 us -> 151 us
  waiting for transfers between devices: 1.93 us -> 7.85 us
  starting transfers between devices: 11.2 us -> 16.9 us
  other arithmetic: 2.92 us -> 7.36 us
  blocking collectives: 19 us -> 21.9 us
    pallas_call x3 -> x1, Pallas kernels: 181 us -> 151 us  [_call(): pl.pallas_call(body, out_shape=outs, in_specs=in_specs, out_specs=[pl.Blo...]
    ppermute x8 -> x10, waiting for transfers between devices: 1.93 us -> 7.85 us  [turned(): lax.ppermute(array, axis, [(i, (i + by) % count) for i in range(count)])]
    ppermute x8 -> x10, starting transfers between devices: 11.2 us -> 16.9 us  [turned(): lax.ppermute(array, axis, [(i, (i + by) % count) for i in range(count)])]
    psum x1, blocking collectives: 19 us -> 21.9 us  [per_device(): lax.psum(jnp.stack([inner(tangents, tangents), inner(pushed - paths, tang...]
    concatenate x0 -> x4, other arithmetic: none -> 2.7 us  [the longest x2 1.93 us: per_device(): jnp.concatenate([positions[0], scaled]).reshape(FIELDS, rows, LANES)]
    unnamed x11 -> x8, local copies, waits for them, and re-layouts: 3.78 us -> 1.48 us
  transfers between devices with their start and end apart: 8 -> 10, of which waited for: 2 -> 3; matrix products, arithmetic and copies ran while one was open for 0% -> 2% of each run, Pallas kernels for 29% -> 0%
where the time goes in v3:
time: 213 us
  Pallas kernels  151 us (71%)
  blocking collectives  21.9 us (10%)
  starting transfers between devices  16.9 us (8%)
  waiting for transfers between devices  7.85 us (4%)
  other arithmetic  7.36 us (3%)
  local copies, waits for them, and re-layouts  6.21 us (3%)
    pallas_call x1, Pallas kernels, _call(): pl.pallas_call(body, out_shape=outs, in_specs=in_specs, out_specs=[pl.Blo...  151 us
    psum x1, blocking collectives, per_device(): lax.psum(jnp.stack([inner(tangents, tangents), inner(pushed - paths, tang...  21.9 us
    ppermute x10, starting transfers between devices, turned(): lax.ppermute(array, axis, [(i, (i + by) % count) for i in range(count)])  16.9 us
    ppermute x10, waiting for transfers between devices, turned(): lax.ppermute(array, axis, [(i, (i + by) % count) for i in range(count)])  7.85 us
  transfers between devices with their start and end apart: 10, of which 3 were waited for; matrix products, arithmetic and copies ran while one was open for 2% of the time, Pallas kernels for 0%

profile of v3, /device:TPU:0, one launch (start us, length us, event | category | flops | bytes accessed | tf_op | source)
XLA Modules:
  0.0 212.7 jit_solution(9734943519508473829)
XLA Ops:
  0.8 1.0 fusion
  1.7 1.0 pad_maximum_fusion.1
  2.7 6.0 %collective-permute-start.3 = (f32[5,160,128]{2,1,0:T(8,128)S(1)}, f32[5,160,128]{2,1,0:T(8,128)S(1)}, u32[]{:S(2)}, u32[]{:S(2)}) collective-permute-start(f32[5,160,128]{2,1,0:T(8,128)S(1)} %pad_maximum_fusion.1), channel_id=1, source_target_pairs={{0,7},{1,0},{2,1},{3,2},{4,3},{5,4},{6,5},{7,6},{8,15},{9,8},{10,9... | collective-permute-start | bytes 1228808 | tf_op jit(solution)/shard_map/ppermute | solution.py:200
  8.8 0.1 collective-permute-start.7
  8.8 1.6 collective-permute-start.8
  10.4 1.4 collective-permute-start.9
  11.9 0.6 fusion.4.eye_ref
  12.5 0.8 copy.20
  13.2 0.0 collective-permute-done.7
  13.2 4.7 %collective-permute-start.1 = (s32[10240]{0:T(1024)S(1)}, s32[10240]{0:T(1024)S(1)}, u32[]{:S(2)}, u32[]{:S(2)}) collective-permute-start(s32[10240]{0:T(1024)S(1)} %bitcast.109), channel_id=1, source_target_pairs={{0,7},{1,0},{2,1},{3,2},{4,3},{5,4},{6,5},{7,6},{8,15},{9,8},{10,9... | collective-permute-start | bytes 122888 | tf_op jit(solution)/shard_map/ppermute | solution.py:200
  17.9 0.0 collective-permute-done.8
  18.0 0.1 collective-permute-start
  18.0 0.0 collective-permute-done.9
  18.1 0.1 multiply_reduce_fusion.6
  18.2 0.1 fusion.5
  18.3 7.4 %collective-permute-done.1 = s32[10240]{0:T(1024)S(1)} collective-permute-done((s32[10240]{0:T(1024)S(1)}, s32[10240]{0:T(1024)S(1)}, u32[]{:S(2)}, u32[]{:S(2)}) %collective-permute-start.1) | collective-permute-done | bytes 40992 | tf_op jit(solution)/shard_map/ppermute | solution.py:200
  25.7 0.2 collective-permute-done
  25.8 0.7 pad_add_fusion.entry_ref
  26.5 1.1 pad_maximum_fusion.fields_ref
  27.7 150.9 %shard_map.82 = (f32[3,160,128]{2,1,0:T(8,128)}, f32[3,8,128]{2,1,0:T(8,128)}) custom-call(s32[40960]{0:T(1024)} %bitcast.106, s32[40960]{0:T(1024)} %pad_add_fusion.entry_ref, s32[20480]{0:T(1024)} %bitcast.117, f32[3,5,160,128]{3,2,1,0:T(8,128)} %pad_maximum_fusion.fields_ref, bf16[128,384]{1,0:T(8,128)(2,1)} %constant.122.clone.select_ref, ...), custom_call_target="tpu_custom_call" | custom-call | flops 24999999488 | bytes 1000000 | tf_op jit(solution)/shard_map/pallas_call | solution.py:187
  178.5 0.7 broadcast_in_dim.35
  179.2 0.7 copy.25
  179.9 0.0 collective-permute-start.4
  180.0 1.6 collective-permute-start.5
  181.6 1.4 collective-permute-start.6
  183.1 1.1 reshape.86
  184.2 0.3 collective-permute-done.6
  184.5 0.2 multiply_reduce_fusion
  184.7 0.2 multiply_reduce_fusion.3
  184.8 0.1 fusion.6
  184.9 0.1 fusion.7
  185.0 0.1 fusion.8
  185.1 0.1 fusion.9
  185.2 21.9 %psum.7 = f32[7,4]{1,0:T(8,128)S(1)} all-reduce(f32[7,4]{1,0:T(8,128)S(1)} %stack.45), channel_id=1, replica_groups=mesh['image'=4,'space'=8] {'space'}, use_global_device_ids=true, to_apply=%region_7.8 | all-reduce | flops 28 | bytes 224 | tf_op jit(solution)/shard_map/psum | solution.py:271
  207.1 0.1 multiply_bitcast_fusion
  207.1 0.1 fusion.11
  207.2 0.1 add_sqrt_fusion
  207.3 0.1 multiply_add_fusion
  207.4 0.2 reduce-window.4
  207.6 0.6 slice.136
  208.8 0.1 fusion.19
  208.9 0.1 fusion.20
  209.0 0.1 pad_maximum_fusion.10
  209.0 0.1 pad_maximum_fusion.2
  209.1 0.7 dynamic_slice.18
  209.8 0.6 dynamic_slice.20
  210.4 1.4 add_dynamic-update-slice_fusion
  211.7 0.9 copy.18
  (28 shorter events, 0.2 us)
Async XLA Ops:
  0.0 8.7 %copy-start = (f32[1,3,20480]{2,0,1:T(1,128)S(1)}, f32[1,3,20480]{2,0,1:T(1,128)}, u32[]{:S(2)}) copy-start(f32[1,3,20480]{2,0,1:T(1,128)} %param.8) | copy-start | bytes 737284
  0.0 11.8 %copy-start.2 = (s32[1,1,20480]{2,1,0:T(1,128)S(1)}, s32[1,1,20480]{2,1,0:T(1,128)}, u32[]{:S(2)}) copy-start(s32[1,1,20480]{2,1,0:T(1,128)} %param.13) | copy-start | bytes 245764
  0.0 12.5 %copy-start.1 = (s32[1,160,256]{2,1,0:T(8,128)S(1)}, s32[1,160,256]{2,1,0:T(8,128)}, u32[]{:S(2)}) copy-start(s32[1,160,256]{2,1,0:T(8,128)} %param.14) | copy-start | bytes 491524
  2.7 23.8 %collective-permute-start.3 = (f32[5,160,128]{2,1,0:T(8,128)S(1)}, f32[5,160,128]{2,1,0:T(8,128)S(1)}, u32[]{:S(2)}, u32[]{:S(2)}) collective-permute-start(f32[5,160,128]{2,1,0:T(8,128)S(1)} %pad_maximum_fusion.1), channel_id=1, source_target_pairs={{0,7},{1,0},{2,1},{3,2},{4,3},{5,4},{6,5},{7,6},{8,15},{9,8},{10,9... | collective-permute-start | bytes 1228808 | tf_op jit(solution)/shard_map/ppermute | solution.py:200
  8.7 17.8 %collective-permute-start.2 = (f32[5,160,128]{2,1,0:T(8,128)S(1)}, f32[5,160,128]{2,1,0:T(8,128)S(1)}, u32[]{:S(2)}, u32[]{:S(2)}) collective-permute-start(f32[5,160,128]{2,1,0:T(8,128)S(1)} %pad_maximum_fusion.1), channel_id=1, source_target_pairs={{0,1},{1,2},{2,3},{3,4},{4,5},{5,6},{6,7},{7,0},{8,9},{9,10},{10,1... | collective-permute-start | bytes 1228808 | tf_op jit(solution)/shard_map/ppermute | solution.py:200
  8.8 4.5 %collective-permute-start.7 = (f32[3,1024]{1,0:T(4,128)S(1)}, f32[3,1024]{1,0:T(4,128)S(1)}, u32[]{:S(2)}, u32[]{:S(2)}) collective-permute-start(f32[3,1024]{1,0:T(4,128)S(1)} %get-tuple-element.27), channel_id=1, source_target_pairs={{0,8},{8,16},{16,24},{24,0},{1,9},{9,17},{17,25},{25,1},{2,10},{10... | collective-permute-start | bytes 36872 | tf_op jit(solution)/shard_map/ppermute | solution.py:200
  8.8 9.1 %collective-permute-start.8 = (f32[3,1024]{1,0:T(4,128)S(1)}, f32[3,1024]{1,0:T(4,128)S(1)}, u32[]{:S(2)}, u32[]{:S(2)}) collective-permute-start(f32[3,1024]{1,0:T(4,128)S(1)} %get-tuple-element.27), channel_id=1, source_target_pairs={{0,16},{8,24},{16,0},{24,8},{1,17},{9,25},{17,1},{25,9},{2,18},{10... | collective-permute-start | bytes 36872 | tf_op jit(solution)/shard_map/ppermute | solution.py:200
  10.4 7.6 %collective-permute-start.9 = (f32[3,1024]{1,0:T(4,128)S(1)}, f32[3,1024]{1,0:T(4,128)S(1)}, u32[]{:S(2)}, u32[]{:S(2)}) collective-permute-start(f32[3,1024]{1,0:T(4,128)S(1)} %get-tuple-element.27), channel_id=1, source_target_pairs={{0,24},{8,0},{16,8},{24,16},{1,25},{9,1},{17,9},{25,17},{2,26},{10... | collective-permute-start | bytes 36872 | tf_op jit(solution)/shard_map/ppermute | solution.py:200
  13.2 12.4 %collective-permute-start.1 = (s32[10240]{0:T(1024)S(1)}, s32[10240]{0:T(1024)S(1)}, u32[]{:S(2)}, u32[]{:S(2)}) collective-permute-start(s32[10240]{0:T(1024)S(1)} %bitcast.109), channel_id=1, source_target_pairs={{0,7},{1,0},{2,1},{3,2},{4,3},{5,4},{6,5},{7,6},{8,15},{9,8},{10,9... | collective-permute-start | bytes 122888 | tf_op jit(solution)/shard_map/ppermute | solution.py:200
  18.0 7.9 %collective-permute-start = (s32[10240]{0:T(1024)S(1)}, s32[10240]{0:T(1024)S(1)}, u32[]{:S(2)}, u32[]{:S(2)}) collective-permute-start(s32[10240]{0:T(1024)S(1)} %bitcast.108), channel_id=1, source_target_pairs={{0,1},{1,2},{2,3},{3,4},{4,5},{5,6},{6,7},{7,0},{8,9},{9,10},{10,1... | collective-permute-start | bytes 122888 | tf_op jit(solution)/shard_map/ppermute | solution.py:200
  179.9 4.2 %collective-permute-start.4 = (f32[3,1024]{1,0:T(4,128)S(1)}, f32[3,1024]{1,0:T(4,128)S(1)}, u32[]{:S(2)}, u32[]{:S(2)}) collective-permute-start(f32[3,1024]{1,0:T(4,128)S(1)} %bitcast.110), channel_id=1, source_target_pairs={{0,8},{8,16},{16,24},{24,0},{1,9},{9,17},{17,25},{25,1},{2,10},{10... | collective-permute-start | bytes 36872 | tf_op jit(solution)/shard_map/ppermute | solution.py:200
  180.0 4.2 %collective-permute-start.5 = (f32[3,1024]{1,0:T(4,128)S(1)}, f32[3,1024]{1,0:T(4,128)S(1)}, u32[]{:S(2)}, u32[]{:S(2)}) collective-permute-start(f32[3,1024]{1,0:T(4,128)S(1)} %bitcast.111), channel_id=1, source_target_pairs={{0,16},{8,24},{16,0},{24,8},{1,17},{9,25},{17,1},{25,9},{2,18},{10... | collective-permute-start | bytes 36872 | tf_op jit(solution)/shard_map/ppermute | solution.py:200
  181.6 2.9 %collective-permute-start.6 = (f32[3,1024]{1,0:T(4,128)S(1)}, f32[3,1024]{1,0:T(4,128)S(1)}, u32[]{:S(2)}, u32[]{:S(2)}) collective-permute-start(f32[3,1024]{1,0:T(4,128)S(1)} %bitcast.112), channel_id=1, source_target_pairs={{0,24},{8,0},{16,8},{24,16},{1,25},{9,1},{17,9},{25,17},{2,26},{10... | collective-permute-start | bytes 36872 | tf_op jit(solution)/shard_map/ppermute | solution.py:200

commit v4 on v3

--- a/solution.py
+++ b/solution.py
@@ -84,120 +84,173 @@
     return lax.dot_general(left, right, (((1,), (1,)), ((), ())), preferred_element_type=F32)
 
 
-def fill_table(rows, fields_ref, eye_ref, table, planes):
-    planes[...] = jnp.zeros_like(planes)
-    groups = rows // 8
-
-    def step(turn, carry):
-        domain = turn // groups
-        first = pl.multiple_of((turn % groups) * 8, 8)
-        fields = [fields_ref[domain, field, pl.ds(first, 8), :] for field in range(FIELDS)]
-        shift = (domain - 1).astype(F32) * SLAB_WIDTH
-        fields[0] = fields[0] + shift
-        for axis in range(3):
-            fields[axis] = fields[axis] - CENTRE
-        fields[3] = fields[3] * LJ_COEF**0.5
-        fields[4] = fields[4] * CHARGE_COEF**0.5
-        for k, row in enumerate(features(fields)):
-            planes[pl.ds(k, 8, stride=STRIDE), :] = row
-        for block in range(8):
-            part = planes[block * STRIDE : (block + 1) * STRIDE, :].astype(BF16)
-            part = jnp.concatenate([part, jnp.zeros((LANES - STRIDE, LANES), BF16)], axis=0)
-            start = pl.multiple_of((turn * 8 + block) * LANES, LANES)
-            table[pl.ds(start, LANES), :] = nt_dot(eye_ref[...], part)
+def fill_blocks(fields, eye, planes, table, first):
+    fields = [field - CENTRE for field in fields[:3]] + fields[3:]
+    fields[3] = fields[3] * LJ_COEF**0.5
+    fields[4] = fields[4] * CHARGE_COEF**0.5
+    for k, row in enumerate(features(fields)):
+        planes[pl.ds(k, 8, stride=STRIDE), :] = row
+    blank = jnp.zeros((LANES - STRIDE, LANES), BF16)
+    for block in range(0, 8, 2):
+        parts = []
+        for side in range(2):
+            start = (block + side) * STRIDE
+            parts += [planes[start : start + STRIDE, :].astype(BF16), blank]
+        both = nt_dot(eye, jnp.concatenate(parts, axis=0))
+        for side in range(2):
+            start = pl.multiple_of(first + (block + side) * LANES, LANES)
+            table[pl.ds(start, LANES), :] = both[:, side * LANES : (side + 1) * LANES]
+
+
+def near_kernel(rows, order_ref, fields_ref, select_ref, eye_ref, table_ref, left_ref, table, planes, stage):
+    turn = pl.program_id(0)
+
+    @pl.when(turn == 0)
+    def _():
+        planes[...] = jnp.zeros_like(planes)
+
+        def fill(group, carry):
+            spot = pl.ds(pl.multiple_of(group * 8, 8), 8)
+            fields = [fields_ref[field, spot, :] for field in range(FIELDS)]
+            fill_blocks(fields, eye_ref[...], planes, table, group * 8 * LANES)
+            return carry
+
+        lax.fori_loop(0, rows // 8, fill, 0)
+
+    def tile_step(local, carry):
+        for side in range(2):
+            tile = turn * 8 + local * 2 + side
+            for k in range(TILE):
+                stage[side, k : k + 1, :] = table[pl.ds(order_ref[tile * TILE + k], 1), :]
+        for side in range(2):
+            left = jnp.dot(stage[side].astype(BF16), select_ref[...], preferred_element_type=F32).astype(BF16)
+            for block in range(3):
+                left_ref[local * 2 + side, block * TILE : (block + 1) * TILE, :] = left[
+                    :, block * LANES : (block + 1) * LANES
+                ]
         return carry
 
-    lax.fori_loop(0, 3 * groups, step, 0)
+    lax.fori_loop(0, 4, tile_step, 0)
+    table_ref[...] = table[pl.ds(pl.multiple_of(turn * 8 * LANES, 8 * LANES), 8 * LANES), :]
+
+
+def tile_sums(left_ref, place, far, sums):
+    others = far[...].astype(BF16)
+    yield
+    grams = nt_dot(left_ref[place], others)
+    yield
+    chunk = 32
+    high, low = [], []
+    for start in range(0, TILE, chunk):
+        window = grams[start : start + chunk]
+        inside = jnp.maximum(window, 0.0)
+        root = lax.rsqrt((1.0 + SOFT_CORE) - window)
+        depth = grams[TILE + start : TILE + start + chunk]
+        charge = grams[2 * TILE + start : 2 * TILE + start + chunk]
+        parts = two_pieces(inside * inside * (depth + charge * (root * root * root)))
+        high.append(parts[0])
+        low.append(parts[1])
+        yield
+    both = jnp.dot(jnp.concatenate(high + low, axis=0), others, preferred_element_type=F32)
+    yield
+    sums[...] = both[0:TILE] + both[TILE:]
+
+
+def weave(stages, copies, parts):
+    size = -(-len(copies) // parts)
+    for turn, _ in enumerate(stages):
+        for copy in copies[turn * size : (turn + 1) * size]:
+            copy()
+    for copy in copies[parts * size :]:
+        copy()
 
 
 def force_kernel(
-    rows, partner_ref, entry_ref, order_ref, fields_ref, select_ref, eye_ref, out_ref, solute_ref,
-    table, forces, planes, far_a, far_b, near_a, near_b, sum_a, sum_b,
+    rows, partner_ref, entry_ref, order_ref, lower_ref, upper_ref, place_ref, eye_ref, left_ref, own_ref,
+    out_ref, solute_ref, table, forces, planes, far_a, far_b, sum_a, sum_b, arrival,
 ):
-    fill_table(rows, fields_ref, eye_ref, table, planes)
+    turn = pl.program_id(0)
     partners = far_a.shape[0]
     own = rows * LANES
 
-    def load(tile, far, near):
-        for k in range(partners):
-            entry = entry_ref[partner_ref[tile * partners + k]]
-            far[k : k + 1, :] = table[pl.ds(entry, 1), :]
-        for k in range(TILE):
-            entry = order_ref[tile * TILE + k] + own
-            near[k : k + 1, :] = table[pl.ds(entry, 1), :]
-
-    def compute(far, near, sums):
-        others = far[...].astype(BF16)
-        left = jnp.dot(near[...].astype(BF16), select_ref[...], preferred_element_type=F32).astype(BF16)
-        left = jnp.concatenate([left[:, k * LANES : (k + 1) * LANES] for k in range(3)], axis=0)
-        grams = nt_dot(left, others)
-        window = grams[0:TILE]
-        inside = jnp.maximum(window, 0.0)
-        root = lax.rsqrt((1.0 + SOFT_CORE) - window)
-        strength = grams[TILE : 2 * TILE] + grams[2 * TILE :] * (root * root * root)
-        high, low = two_pieces(inside * inside * strength)
-        both = jnp.dot(jnp.concatenate([high, low], axis=0), others, preferred_element_type=F32)
-        sums[...] = both[0:TILE] + both[TILE:]
+    def load(tile, far):
+        def copy(k):
+            far[k : k + 1, :] = table[pl.ds(entry_ref[partner_ref[tile * partners + k]], 1), :]
+
+        return [functools.partial(copy, k) for k in range(partners)]
 
     def save(tile, sums):
-        for k in range(TILE):
+        def copy(k):
             forces[pl.ds(order_ref[tile * TILE + k], 1), :] = sums[k : k + 1, :]
 
-    load(0, far_a, near_a)
-
-    def step(turn, carry):
-        tile = turn * 2
-        load(tile + 1, far_b, near_b)
-        compute(far_a, near_a, sum_a)
-        save(tile, sum_a)
-        load(jnp.minimum(tile + 2, rows - 1), far_a, near_a)
-        compute(far_b, near_b, sum_b)
-        save(tile + 1, sum_b)
+        return [functools.partial(copy, k) for k in range(TILE)]
+
+    @pl.when(turn == 0)
+    def _():
+        own_copy = pltpu.make_async_copy(own_ref, table.at[pl.ds(own, own), :], arrival)
+        own_copy.start()
+        planes[...] = jnp.zeros_like(planes)
+
+        def fill(group, carry):
+            spot = pl.ds(pl.multiple_of(group * 8, 8), 8)
+            for ref, first, shift in ((lower_ref, 0, -SLAB_WIDTH), (upper_ref, 2 * own, SLAB_WIDTH)):
+                fields = [ref[field, spot, :] for field in range(FIELDS)]
+                fields[0] = fields[0] + shift
+                fill_blocks(fields, eye_ref[...], planes, table, first + group * 8 * LANES)
+            return carry
+
+        lax.fori_loop(0, rows // 8, fill, 0)
+        own_copy.wait()
+        sum_b[...] = jnp.zeros_like(sum_b)
+        for copy in load(0, far_a):
+            copy()
+
+    def step(pair, carry):
+        tile = turn * 8 + pair * 2
+        copies = save(jnp.maximum(tile - 1, 0), sum_b) + load(tile + 1, far_b)
+        weave(tile_sums(left_ref, pair * 2, far_a, sum_a), copies, 7)
+        copies = save(tile, sum_a) + load(jnp.minimum(tile + 2, rows - 1), far_a)
+        weave(tile_sums(left_ref, pair * 2 + 1, far_b, sum_b), copies, 7)
         return carry
 
-    lax.fori_loop(0, rows // 2, step, 0)
-
-    def finish(row, carry):
-        turned_sums = forces[pl.ds(pl.multiple_of(row * LANES, LANES), LANES), :].T
-        for axis in range(3):
-            first = 6 * axis
-            moment = (
-                turned_sums[first : first + 1] + turned_sums[first + 1 : first + 2] + turned_sums[first + 3 : first + 4]
-            )
-            place = fields_ref[1, axis, pl.ds(row, 1), :]
-            force = (place - CENTRE) * turned_sums[ONES : ONES + 1] - moment
-            out_ref[axis, pl.ds(row, 1), :] = place + STEP_SIZE * force
-        return carry
-
-    lax.fori_loop(0, rows, finish, 0)
-    solute_ref[...] = out_ref[:, 0 : SOL_DEV // LANES, :]
+    lax.fori_loop(0, 4, step, 0)
+
+    @pl.when(turn == pl.num_programs(0) - 1)
+    def _():
+        for copy in save(rows - 1, sum_b):
+            copy()
+
+        def finish(group, carry):
+            for local in range(4):
+                row = group * 4 + local
+                turned_sums = forces[pl.ds(pl.multiple_of(row * LANES, LANES), LANES), :].T
+                for axis in range(3):
+                    first = 6 * axis
+                    moment = (
+                        turned_sums[first : first + 1]
+                        + turned_sums[first + 1 : first + 2]
+                        + turned_sums[first + 3 : first + 4]
+                    )
+                    place = place_ref[axis, pl.ds(row, 1), :]
+                    force = (place - CENTRE) * turned_sums[ONES : ONES + 1] - moment
+                    out_ref[axis, pl.ds(row, 1), :] = place + STEP_SIZE * force
+            return carry
+
+        lax.fori_loop(0, rows // 4, finish, 0)
+        solute_ref[...] = out_ref[:, 0 : SOL_DEV // LANES, :]
 
 
 def whole(*shape, dtype=F32):
     return jax.ShapeDtypeStruct(shape, dtype)
-
-
-def kernel_call(body, outs, scratch=(), scalar=0, **more):
-    return functools.partial(_call, body, outs, scratch, scalar, more)
-
-
-def _call(body, outs, scratch, scalar, more, *args):
-    in_specs = [pl.BlockSpec(memory_space=pltpu.SMEM)] * scalar
-    in_specs += [pl.BlockSpec(memory_space=pltpu.VMEM)] * (len(args) - scalar)
-    return pl.pallas_call(
-        body,
-        out_shape=outs,
-        in_specs=in_specs,
-        out_specs=[pl.BlockSpec(memory_space=pltpu.VMEM)] * len(outs),
-        scratch_shapes=list(scratch),
-        compiler_params=pltpu.CompilerParams(vmem_limit_bytes=VMEM_LIMIT),
-        **more,
-    )(*args)
 
 
 def turned(array, axis, by):
     count = lax.axis_size(axis)
     return lax.ppermute(array, axis, [(i, (i + by) % count) for i in range(count)])
+
+
+def summed(array, axis):
+    return sum((turned(array, axis, by) for by in range(1, lax.axis_size(axis))), array)
 
 
 def round_trip(array, axis):
@@ -223,7 +276,7 @@
     factor = jnp.where(jnp.arange(atoms) < SOL_DEV, jnp.sqrt(rest_scale[0]), 1.0)
     scaled = jnp.stack([strength * factor, charge * factor])
     fields = jnp.concatenate([positions[0], scaled]).reshape(FIELDS, rows, LANES)
-    fields = jnp.stack([turned(fields, "space", 1), fields, turned(fields, "space", -1)])
+    lower, upper = turned(fields, "space", 1), turned(fields, "space", -1)
     shell = ghost_index.reshape(atoms)
     entries = jnp.concatenate(
         [
@@ -232,10 +285,37 @@
             turned(shell[:half], "space", -1) + 2 * atoms,
         ]
     )
-    out, solute = kernel_call(
+    order = cell_order.reshape(atoms)
+    eye = jnp.eye(LANES, dtype=BF16)
+    scalar = pl.BlockSpec(memory_space=pltpu.SMEM)
+    vector = pl.BlockSpec(memory_space=pltpu.VMEM)
+    params = pltpu.CompilerParams(vmem_limit_bytes=VMEM_LIMIT)
+    table, left = pl.pallas_call(
+        functools.partial(near_kernel, rows),
+        grid=(rows // 8,),
+        out_shape=[whole(atoms, LANES), whole(rows, 3 * TILE, LANES, dtype=BF16)],
+        in_specs=[scalar] + [vector] * 3,
+        out_specs=[
+            pl.BlockSpec((8 * LANES, LANES), lambda i: (i, 0)),
+            pl.BlockSpec((8, 3 * TILE, LANES), lambda i: (i, 0, 0)),
+        ],
+        scratch_shapes=[
+            pltpu.VMEM((atoms, LANES), F32),
+            pltpu.VMEM((8 * STRIDE, LANES), F32),
+            pltpu.VMEM((2, TILE, LANES), F32),
+        ],
+        compiler_params=params,
+        cost_estimate=pl.CostEstimate(flops=25 * 10**9, bytes_accessed=3 * 10**7, transcendentals=0),
+    )(order, fields, near_selector(), eye)
+    out, solute = pl.pallas_call(
         functools.partial(force_kernel, rows),
-        [whole(3, rows, LANES), whole(3, SOL_DEV // LANES, LANES)],
-        [
+        grid=(rows // 8,),
+        out_shape=[whole(3, rows, LANES), whole(3, SOL_DEV // LANES, LANES)],
+        in_specs=[scalar] * 3
+        + [vector] * 4
+        + [pl.BlockSpec((8, 3 * TILE, LANES), lambda i: (i, 0, 0)), pl.BlockSpec(memory_space=pl.ANY)],
+        out_specs=[vector] * 2,
+        scratch_shapes=[
             pltpu.VMEM((3 * atoms, LANES), F32),
             pltpu.VMEM((atoms, LANES), F32),
             pltpu.VMEM((8 * STRIDE, LANES), F32),
@@ -243,19 +323,11 @@
             pltpu.VMEM((partners, LANES), F32),
             pltpu.VMEM((TILE, LANES), F32),
             pltpu.VMEM((TILE, LANES), F32),
-            pltpu.VMEM((TILE, LANES), F32),
-            pltpu.VMEM((TILE, LANES), F32),
+            pltpu.SemaphoreType.DMA,
         ],
-        scalar=3,
-        cost_estimate=pl.CostEstimate(flops=25 * 10**9, bytes_accessed=10**6, transcendentals=0),
-    )(
-        tile_atoms.reshape(rows * partners),
-        entries,
-        cell_order.reshape(atoms),
-        fields,
-        near_selector(),
-        jnp.eye(LANES, dtype=BF16),
-    )
+        compiler_params=params,
+        cost_estimate=pl.CostEstimate(flops=25 * 10**9, bytes_accessed=3 * 10**7, transcendentals=0),
+    )(tile_atoms.reshape(rows * partners), entries, order, lower, upper, fields, eye, left, table)
     out = out.reshape(1, 3, atoms)
     solute = solute.reshape(1, 3, SOL_DEV)
 
@@ -268,7 +340,7 @@
     tangents = upper_path - lower_path
     gaps = pushed[1:] - pushed[:-1]
     none = jnp.zeros((1,), F32)
-    sums = lax.psum(
+    sums = summed(
         jnp.stack(
             [
                 inner(tangents, tangents),

time: 213 us -> 194 us (0.911)
  blocking collectives: 21.9 us -> 0 us
  Pallas kernels: 151 us -> 144 us
  starting transfers between devices: 16.9 us -> 21.2 us
  waiting for transfers between devices: 7.85 us -> 11.8 us
  local copies, waits for them, and re-layouts: 6.21 us -> 8.59 us
    psum x1 -> x0, blocking collectives: 21.9 us -> none  [per_device(): lax.psum(jnp.stack([inner(tangents, tangents), inner(pushed - paths, tang...]
    pallas_call x1 -> x2, Pallas kernels: 151 us -> 144 us  [the longest x1 103 us: per_device(): pl.pallas_call(functools.partial(force_kernel, rows), grid=(rows // 8,),...]
    ppermute x10 -> x17, starting transfers between devices: 16.9 us -> 21.2 us  [turned(): lax.ppermute(array, axis, [(i, (i + by) % count) for i in range(count)])]
    ppermute x10 -> x17, waiting for transfers between devices: 7.85 us -> 11.8 us  [turned(): lax.ppermute(array, axis, [(i, (i + by) % count) for i in range(count)])]
  transfers between devices with their start and end apart: 10 -> 17, of which waited for: 3 -> 7; matrix products, arithmetic and copies ran while one was open for 2% -> 3% of each run, Pallas kernels for 0% -> 21%
where the time goes in v4:
time: 194 us; the launch traced here: 193 us
  Pallas kernels  144 us (74%)
  starting transfers between devices  21.2 us (11%)
  waiting for transfers between devices  11.8 us (6%)
  local copies, waits for them, and re-layouts  8.59 us (4%)
  other arithmetic  6.21 us (3%)
    pallas_call x1, Pallas kernels, per_device(): pl.pallas_call(functools.partial(force_kernel, rows), grid=(rows // 8,),...  103 us
    pallas_call x1, Pallas kernels, per_device(): pl.pallas_call(functools.partial(near_kernel, rows), grid=(rows // 8,), o...  40.7 us
    ppermute x17, starting transfers between devices, turned(): lax.ppermute(array, axis, [(i, (i + by) % count) for i in range(count)])  21.2 us
    ppermute x17, waiting for transfers between devices, turned(): lax.ppermute(array, axis, [(i, (i + by) % count) for i in range(count)])  11.8 us
  transfers between devices with their start and end apart: 17, of which 7 were waited for; matrix products, arithmetic and copies ran while one was open for 3% of the time, Pallas kernels for 21%

profile of v4, /device:TPU:0, one launch (start us, length us, event | category | flops | bytes accessed | tf_op | source)
XLA Modules:
  0.0 193.2 jit_solution(16665682658825100340)
XLA Ops:
  0.7 0.9 fusion
  1.6 1.0 pad_maximum_fusion.fields_ref.place_ref
  2.6 3.0 %collective-permute-start.2 = (f32[5,160,128]{2,1,0:T(8,128)S(1)}, f32[5,160,128]{2,1,0:T(8,128)S(1)}, u32[]{:S(2)}, u32[]{:S(2)}) collective-permute-start(f32[5,160,128]{2,1,0:T(8,128)S(1)} %pad_maximum_fusion.fields_ref.place_ref), channel_id=1, source_target_pairs={{0,1},{1,2},{2,3},{3,4},{4,5},{5,6},{6,7},{7,0},{8,9},{9,10},{10,1... | collective-permute-start | bytes 1228808 | tf_op jit(solution)/shard_map/ppermute | solution.py:249
  5.6 3.1 %collective-permute-start.3 = (f32[5,160,128]{2,1,0:T(8,128)S(1)}, f32[5,160,128]{2,1,0:T(8,128)S(1)}, u32[]{:S(2)}, u32[]{:S(2)}) collective-permute-start(f32[5,160,128]{2,1,0:T(8,128)S(1)} %pad_maximum_fusion.fields_ref.place_ref), channel_id=1, source_target_pairs={{0,7},{1,0},{2,1},{3,2},{4,3},{5,4},{6,5},{7,6},{8,15},{9,8},{10,9... | collective-permute-start | bytes 1228808 | tf_op jit(solution)/shard_map/ppermute | solution.py:249
  8.7 0.7 slice.111
  9.5 1.7 collective-permute-start.8
  11.3 1.4 collective-permute-start.9
  12.6 0.6 fusion.2.eye_ref
  13.2 0.8 fusion.20
  14.1 40.7 %shard_map.82 = (f32[20480,128]{1,0:T(8,128)}, bf16[160,384,128]{2,1,0:T(8,128)(2,1)}) custom-call(s32[20480]{0:T(1024)} %bitcast.107, f32[5,160,128]{2,1,0:T(8,128)} %copy-done, bf16[128,384]{1,0:T(8,128)(2,1)} %constant.122.clone.select_ref, bf16[128,128]{1,0:T(8,128)(2,1)} %fusion.2.eye_ref), custom_call_target="tpu_custom_call" | custom-call | flops 24999999488 | bytes 30000000 | tf_op jit(solution)/shard_map/pallas_call | solution.py:293
  54.8 0.8 copy.20
  55.6 1.8 collective-permute-start.1
  57.4 0.3 collective-permute-start
  57.7 0.1 multiply_reduce_fusion.6
  57.9 0.1 fusion.3
  57.9 1.7 collective-permute-done.1
  59.6 4.6 %collective-permute-done = s32[10240]{0:T(1024)S(1)} collective-permute-done((s32[10240]{0:T(1024)S(1)}, s32[10240]{0:T(1024)S(1)}, u32[]{:S(2)}, u32[]{:S(2)}) %collective-permute-start) | collective-permute-done | bytes 40992 | tf_op jit(solution)/shard_map/ppermute | solution.py:249
  64.2 0.7 pad_add_fusion.entry_ref
  64.9 0.7 copy-done.2
  65.6 0.1 copy-done.3
  65.8 103.1 %shard_map.83 = (f32[3,160,128]{2,1,0:T(8,128)}, f32[3,8,128]{2,1,0:T(8,128)}) custom-call(s32[40960]{0:T(1024)} %bitcast.96, s32[40960]{0:T(1024)} %pad_add_fusion.entry_ref, s32[20480]{0:T(1024)} %bitcast.108, f32[5,160,128]{2,1,0:T(8,128)} %copy-done.2, f32[5,160,128]{2,1,0:T(8,128)} %copy-done.3, f32[5,160,128]{2,1,0:T(8,128)} %copy-done, ...), custom_call_target="tpu_custom_call" | custom-call | flops 24999999488 | bytes 30000000 | tf_op jit(solution)/shard_map/pallas_call | solution.py:310
  168.9 0.7 broadcast_in_dim.35
  169.6 0.7 copy.25
  170.3 0.6 collective-permute-start.5
  170.9 1.4 collective-permute-start.6
  172.4 1.1 reshape.80
  173.5 0.6 collective-permute-done.5
  174.1 0.2 multiply_reduce_fusion
  174.3 0.2 multiply_reduce_fusion.3
  174.5 0.1 fusion.4
  174.5 0.1 fusion.5
  175.0 4.2 %collective-permute-start.13 = (f32[7,4]{1,0:T(8,128)S(1)}, f32[7,4]{1,0:T(8,128)S(1)}, u32[]{:S(2)}, u32[]{:S(2)}) collective-permute-start(f32[7,4]{1,0:T(8,128)S(1)} %stack.33), channel_id=1, source_target_pairs={{0,4},{1,5},{2,6},{3,7},{4,0},{5,1},{6,2},{7,3},{8,12},{9,13},{10,... | collective-permute-start | bytes 344 | tf_op jit(solution)/shard_map/ppermute | solution.py:249
  179.2 2.0 %collective-permute-start.11 = (f32[7,4]{1,0:T(8,128)S(1)}, f32[7,4]{1,0:T(8,128)S(1)}, u32[]{:S(2)}, u32[]{:S(2)}) collective-permute-start(f32[7,4]{1,0:T(8,128)S(1)} %stack.33), channel_id=1, source_target_pairs={{0,2},{1,3},{2,4},{3,5},{4,6},{5,7},{6,0},{7,1},{8,10},{9,11},{10,... | collective-permute-start | bytes 344 | tf_op jit(solution)/shard_map/ppermute | solution.py:249
  181.3 1.5 collective-permute-start.10
  182.8 1.9 collective-permute-done.12
  184.7 0.1 collective-permute-done.11
  184.8 2.8 %collective-permute-done.10 = f32[7,4]{1,0:T(8,128)S(1)} collective-permute-done((f32[7,4]{1,0:T(8,128)S(1)}, f32[7,4]{1,0:T(8,128)S(1)}, u32[]{:S(2)}, u32[]{:S(2)}) %collective-permute-start.10) | collective-permute-done | bytes 144 | tf_op jit(solution)/shard_map/ppermute | solution.py:249
  187.6 0.1 multiply_bitcast_fusion
  187.7 0.1 fusion.9
  187.8 0.1 multiply_add_fusion
  187.9 0.1 add_sqrt_fusion
  187.9 0.2 reduce-window.4
  188.1 0.6 slice.136
  189.4 0.1 fusion.17
  189.7 0.6 dynamic_slice.20
  190.3 0.7 dynamic_slice.18
  190.9 1.4 add_dynamic-update-slice_fusion
  192.3 0.9 copy.18
  (44 shorter events, 0.9 us)
Async XLA Ops:
  2.6 11.4 %copy-start = (f32[5,160,128]{2,1,0:T(8,128)}, f32[5,160,128]{2,1,0:T(8,128)S(1)}, u32[]{:S(2)}) copy-start(f32[5,160,128]{2,1,0:T(8,128)S(1)} %pad_maximum_fusion.fields_ref.place_ref) | copy-start | bytes 1228804
  2.6 62.2 %collective-permute-start.2 = (f32[5,160,128]{2,1,0:T(8,128)S(1)}, f32[5,160,128]{2,1,0:T(8,128)S(1)}, u32[]{:S(2)}, u32[]{:S(2)}) collective-permute-start(f32[5,160,128]{2,1,0:T(8,128)S(1)} %pad_maximum_fusion.fields_ref.place_ref), channel_id=1, source_target_pairs={{0,1},{1,2},{2,3},{3,4},{4,5},{5,6},{6,7},{7,0},{8,9},{9,10},{10,1... | collective-permute-start | bytes 1228808 | tf_op jit(solution)/shard_map/ppermute | solution.py:249
  5.6 59.3 %collective-permute-start.3 = (f32[5,160,128]{2,1,0:T(8,128)S(1)}, f32[5,160,128]{2,1,0:T(8,128)S(1)}, u32[]{:S(2)}, u32[]{:S(2)}) collective-permute-start(f32[5,160,128]{2,1,0:T(8,128)S(1)} %pad_maximum_fusion.fields_ref.place_ref), channel_id=1, source_target_pairs={{0,7},{1,0},{2,1},{3,2},{4,3},{5,4},{6,5},{7,6},{8,15},{9,8},{10,9... | collective-permute-start | bytes 1228808 | tf_op jit(solution)/shard_map/ppermute | solution.py:249
  9.5 46.1 %collective-permute-start.7 = (f32[3,1024]{1,0:T(4,128)S(1)}, f32[3,1024]{1,0:T(4,128)S(1)}, u32[]{:S(2)}, u32[]{:S(2)}) collective-permute-start(f32[3,1024]{1,0:T(4,128)S(1)} %get-tuple-element.27), channel_id=1, source_target_pairs={{0,8},{8,16},{16,24},{24,0},{1,9},{9,17},{17,25},{25,1},{2,10},{10... | collective-permute-start | bytes 36872 | tf_op jit(solution)/shard_map/ppermute | solution.py:249
  9.5 47.9 %collective-permute-start.8 = (f32[3,1024]{1,0:T(4,128)S(1)}, f32[3,1024]{1,0:T(4,128)S(1)}, u32[]{:S(2)}, u32[]{:S(2)}) collective-permute-start(f32[3,1024]{1,0:T(4,128)S(1)} %get-tuple-element.27), channel_id=1, source_target_pairs={{0,16},{8,24},{16,0},{24,8},{1,17},{9,25},{17,1},{25,9},{2,18},{10... | collective-permute-start | bytes 36872 | tf_op jit(solution)/shard_map/ppermute | solution.py:249
  11.3 46.5 %collective-permute-start.9 = (f32[3,1024]{1,0:T(4,128)S(1)}, f32[3,1024]{1,0:T(4,128)S(1)}, u32[]{:S(2)}, u32[]{:S(2)}) collective-permute-start(f32[3,1024]{1,0:T(4,128)S(1)} %get-tuple-element.27), channel_id=1, source_target_pairs={{0,24},{8,0},{16,8},{24,16},{1,25},{9,1},{17,9},{25,17},{2,26},{10... | collective-permute-start | bytes 36872 | tf_op jit(solution)/shard_map/ppermute | solution.py:249
  14.1 40.8 %copy-start.1 = (s32[1,160,256]{2,1,0:T(8,128)S(1)}, s32[1,160,256]{2,1,0:T(8,128)}, u32[]{:S(2)}) copy-start(s32[1,160,256]{2,1,0:T(8,128)} %param.14) | copy-start | bytes 491524
  55.6 4.0 %collective-permute-start.1 = (s32[10240]{0:T(1024)S(1)}, s32[10240]{0:T(1024)S(1)}, u32[]{:S(2)}, u32[]{:S(2)}) collective-permute-start(s32[10240]{0:T(1024)S(1)} %bitcast.99), channel_id=1, source_target_pairs={{0,7},{1,0},{2,1},{3,2},{4,3},{5,4},{6,5},{7,6},{8,15},{9,8},{10,9... | collective-permute-start | bytes 122888 | tf_op jit(solution)/shard_map/ppermute | solution.py:249
  57.4 6.8 %collective-permute-start = (s32[10240]{0:T(1024)S(1)}, s32[10240]{0:T(1024)S(1)}, u32[]{:S(2)}, u32[]{:S(2)}) collective-permute-start(s32[10240]{0:T(1024)S(1)} %bitcast.98), channel_id=1, source_target_pairs={{0,1},{1,2},{2,3},{3,4},{4,5},{5,6},{6,7},{7,0},{8,9},{9,10},{10,1... | collective-permute-start | bytes 122888 | tf_op jit(solution)/shard_map/ppermute | solution.py:249
  64.9 0.8 copy-start.2
  64.9 0.9 copy-start.3
  170.3 3.2 %collective-permute-start.4 = (f32[3,1024]{1,0:T(4,128)S(1)}, f32[3,1024]{1,0:T(4,128)S(1)}, u32[]{:S(2)}, u32[]{:S(2)}) collective-permute-start(f32[3,1024]{1,0:T(4,128)S(1)} %bitcast.100), channel_id=1, source_target_pairs={{0,8},{8,16},{16,24},{24,0},{1,9},{9,17},{17,25},{25,1},{2,10},{10... | collective-permute-start | bytes 36872 | tf_op jit(solution)/shard_map/ppermute | solution.py:249
  170.3 3.8 %collective-permute-start.5 = (f32[3,1024]{1,0:T(4,128)S(1)}, f32[3,1024]{1,0:T(4,128)S(1)}, u32[]{:S(2)}, u32[]{:S(2)}) collective-permute-start(f32[3,1024]{1,0:T(4,128)S(1)} %bitcast.101), channel_id=1, source_target_pairs={{0,16},{8,24},{16,0},{24,8},{1,17},{9,25},{17,1},{25,9},{2,18},{10... | collective-permute-start | bytes 36872 | tf_op jit(solution)/shard_map/ppermute | solution.py:249
  170.9 3.2 %collective-permute-start.6 = (f32[3,1024]{1,0:T(4,128)S(1)}, f32[3,1024]{1,0:T(4,128)S(1)}, u32[]{:S(2)}, u32[]{:S(2)}) collective-permute-start(f32[3,1024]{1,0:T(4,128)S(1)} %bitcast.102), channel_id=1, source_target_pairs={{0,24},{8,0},{16,8},{24,16},{1,25},{9,1},{17,9},{25,17},{2,26},{10... | collective-permute-start | bytes 36872 | tf_op jit(solution)/shard_map/ppermute | solution.py:249
  174.8 4.4 %collective-permute-start.16 = (f32[7,4]{1,0:T(8,128)S(1)}, f32[7,4]{1,0:T(8,128)S(1)}, u32[]{:S(2)}, u32[]{:S(2)}) collective-permute-start(f32[7,4]{1,0:T(8,128)S(1)} %stack.33), channel_id=1, source_target_pairs={{0,7},{1,0},{2,1},{3,2},{4,3},{5,4},{6,5},{7,6},{8,15},{9,8},{10,9... | collective-permute-start | bytes 344 | tf_op jit(solution)/shard_map/ppermute | solution.py:249
  174.8 6.4 %collective-permute-start.15 = (f32[7,4]{1,0:T(8,128)S(1)}, f32[7,4]{1,0:T(8,128)S(1)}, u32[]{:S(2)}, u32[]{:S(2)}) collective-permute-start(f32[7,4]{1,0:T(8,128)S(1)} %stack.33), channel_id=1, source_target_pairs={{0,6},{1,7},{2,0},{3,1},{4,2},{5,3},{6,4},{7,5},{8,14},{9,15},{10,... | collective-permute-start | bytes 344 | tf_op jit(solution)/shard_map/ppermute | solution.py:249
  174.9 7.8 %collective-permute-start.14 = (f32[7,4]{1,0:T(8,128)S(1)}, f32[7,4]{1,0:T(8,128)S(1)}, u32[]{:S(2)}, u32[]{:S(2)}) collective-permute-start(f32[7,4]{1,0:T(8,128)S(1)} %stack.33), channel_id=1, source_target_pairs={{0,5},{1,6},{2,7},{3,0},{4,1},{5,2},{6,3},{7,4},{8,13},{9,14},{10,... | collective-permute-start | bytes 344 | tf_op jit(solution)/shard_map/ppermute | solution.py:249
  175.0 7.8 %collective-permute-start.13 = (f32[7,4]{1,0:T(8,128)S(1)}, f32[7,4]{1,0:T(8,128)S(1)}, u32[]{:S(2)}, u32[]{:S(2)}) collective-permute-start(f32[7,4]{1,0:T(8,128)S(1)} %stack.33), channel_id=1, source_target_pairs={{0,4},{1,5},{2,6},{3,7},{4,0},{5,1},{6,2},{7,3},{8,12},{9,13},{10,... | collective-permute-start | bytes 344 | tf_op jit(solution)/shard_map/ppermute | solution.py:249
  179.2 5.4 %collective-permute-start.12 = (f32[7,4]{1,0:T(8,128)S(1)}, f32[7,4]{1,0:T(8,128)S(1)}, u32[]{:S(2)}, u32[]{:S(2)}) collective-permute-start(f32[7,4]{1,0:T(8,128)S(1)} %stack.33), channel_id=1, source_target_pairs={{0,3},{1,4},{2,5},{3,6},{4,7},{5,0},{6,1},{7,2},{8,11},{9,12},{10,... | collective-permute-start | bytes 344 | tf_op jit(solution)/shard_map/ppermute | solution.py:249
  179.2 5.5 %collective-permute-start.11 = (f32[7,4]{1,0:T(8,128)S(1)}, f32[7,4]{1,0:T(8,128)S(1)}, u32[]{:S(2)}, u32[]{:S(2)}) collective-permute-start(f32[7,4]{1,0:T(8,128)S(1)} %stack.33), channel_id=1, source_target_pairs={{0,2},{1,3},{2,4},{3,5},{4,6},{5,7},{6,0},{7,1},{8,10},{9,11},{10,... | collective-permute-start | bytes 344 | tf_op jit(solution)/shard_map/ppermute | solution.py:249
  181.3 6.3 %collective-permute-start.10 = (f32[7,4]{1,0:T(8,128)S(1)}, f32[7,4]{1,0:T(8,128)S(1)}, u32[]{:S(2)}, u32[]{:S(2)}) collective-permute-start(f32[7,4]{1,0:T(8,128)S(1)} %stack.33), channel_id=1, source_target_pairs={{0,1},{1,2},{2,3},{3,4},{4,5},{5,6},{6,7},{7,0},{8,9},{9,10},{10,1... | collective-permute-start | bytes 344 | tf_op jit(solution)/shard_map/ppermute | solution.py:249

commit v5 on v4

--- a/solution.py
+++ b/solution.py
@@ -13,6 +13,7 @@
 LANES = 128
 FIELDS = 5
 STRIDE = 48
+PAD = 8
 
 LJ_COEF = 0.5
 CHARGE_COEF = 0.1
@@ -98,8 +99,25 @@
             parts += [planes[start : start + STRIDE, :].astype(BF16), blank]
         both = nt_dot(eye, jnp.concatenate(parts, axis=0))
         for side in range(2):
-            start = pl.multiple_of(first + (block + side) * LANES, LANES)
+            start = pl.multiple_of(first + (block + side) * LANES + PAD, PAD)
             table[pl.ds(start, LANES), :] = both[:, side * LANES : (side + 1) * LANES]
+
+
+def sublane_masks():
+    sublane = lax.broadcasted_iota(I32, (8, LANES), 0)
+    return [sublane == k for k in range(8)]
+
+
+def merged(table, entries, masks):
+    result = table[pl.ds(entries[0] + PAD, 8), :]
+    for k in range(1, 8):
+        result = jnp.where(masks[k], table[pl.ds(entries[k] + (PAD - k), 8), :], result)
+    return result
+
+
+def copy_rows(table, entry_of, stage, start, masks):
+    parts = [merged(table, [entry_of(start + half + k) for k in range(8)], masks) for half in (0, 8)]
+    stage[start : start + 16, :] = jnp.concatenate(parts, axis=0).astype(BF16)
 
 
 def near_kernel(rows, order_ref, fields_ref, select_ref, eye_ref, table_ref, left_ref, table, planes, stage):
@@ -117,13 +135,15 @@
 
         lax.fori_loop(0, rows // 8, fill, 0)
 
+    masks = sublane_masks()
+
     def tile_step(local, carry):
         for side in range(2):
             tile = turn * 8 + local * 2 + side
-            for k in range(TILE):
-                stage[side, k : k + 1, :] = table[pl.ds(order_ref[tile * TILE + k], 1), :]
+            for start in range(0, TILE, 16):
+                copy_rows(table, lambda k: order_ref[tile * TILE + k], stage.at[side], start, masks)
         for side in range(2):
-            left = jnp.dot(stage[side].astype(BF16), select_ref[...], preferred_element_type=F32).astype(BF16)
+            left = jnp.dot(stage[side], select_ref[...], preferred_element_type=F32).astype(BF16)
             for block in range(3):
                 left_ref[local * 2 + side, block * TILE : (block + 1) * TILE, :] = left[
                     :, block * LANES : (block + 1) * LANES
@@ -131,11 +151,11 @@
         return carry
 
     lax.fori_loop(0, 4, tile_step, 0)
-    table_ref[...] = table[pl.ds(pl.multiple_of(turn * 8 * LANES, 8 * LANES), 8 * LANES), :]
+    table_ref[...] = table[pl.ds(pl.multiple_of(turn * 8 * LANES + PAD, PAD), 8 * LANES), :]
 
 
 def tile_sums(left_ref, place, far, sums):
-    others = far[...].astype(BF16)
+    others = far[...]
     yield
     grams = nt_dot(left_ref[place], others)
     yield
@@ -173,28 +193,37 @@
     partners = far_a.shape[0]
     own = rows * LANES
 
+    masks = sublane_masks()
+
     def load(tile, far):
-        def copy(k):
-            far[k : k + 1, :] = table[pl.ds(entry_ref[partner_ref[tile * partners + k]], 1), :]
-
-        return [functools.partial(copy, k) for k in range(partners)]
+        def entry_of(k):
+            return entry_ref[partner_ref[tile * partners + k]]
+
+        return [
+            functools.partial(copy_rows, table, entry_of, far, start, masks)
+            for start in range(0, partners, 16)
+        ]
 
     def save(tile, sums):
-        def copy(k):
-            forces[pl.ds(order_ref[tile * TILE + k], 1), :] = sums[k : k + 1, :]
-
-        return [functools.partial(copy, k) for k in range(TILE)]
+        def copy(block):
+            value = sums[block * 8 : block * 8 + 8, :]
+            for k in range(8):
+                place = order_ref[tile * TILE + block * 8 + k] + (PAD - k)
+                pltpu.store(forces.at[pl.ds(place, 8), :], value, mask=masks[k])
+
+        return [functools.partial(copy, block) for block in range(TILE // 8)]
 
     @pl.when(turn == 0)
     def _():
-        own_copy = pltpu.make_async_copy(own_ref, table.at[pl.ds(own, own), :], arrival)
+        own_copy = pltpu.make_async_copy(own_ref, table.at[pl.ds(own + PAD, own), :], arrival)
         own_copy.start()
         planes[...] = jnp.zeros_like(planes)
 
         def fill(group, carry):
-            spot = pl.ds(pl.multiple_of(group * 8, 8), 8)
             for ref, first, shift in ((lower_ref, 0, -SLAB_WIDTH), (upper_ref, 2 * own, SLAB_WIDTH)):
-                fields = [ref[field, spot, :] for field in range(FIELDS)]
+                fields = [
+                    ref[pl.ds(pl.multiple_of(field * rows + group * 8, 8), 8), :] for field in range(FIELDS)
+                ]
                 fields[0] = fields[0] + shift
                 fill_blocks(fields, eye_ref[...], planes, table, first + group * 8 * LANES)
             return carry
@@ -223,7 +252,7 @@
         def finish(group, carry):
             for local in range(4):
                 row = group * 4 + local
-                turned_sums = forces[pl.ds(pl.multiple_of(row * LANES, LANES), LANES), :].T
+                turned_sums = forces[pl.ds(pl.multiple_of(row * LANES + PAD, PAD), LANES), :].T
                 for axis in range(3):
                     first = 6 * axis
                     moment = (
@@ -276,13 +305,15 @@
     factor = jnp.where(jnp.arange(atoms) < SOL_DEV, jnp.sqrt(rest_scale[0]), 1.0)
     scaled = jnp.stack([strength * factor, charge * factor])
     fields = jnp.concatenate([positions[0], scaled]).reshape(FIELDS, rows, LANES)
-    lower, upper = turned(fields, "space", 1), turned(fields, "space", -1)
-    shell = ghost_index.reshape(atoms)
+    shell = ghost_index.reshape(2, rows // 2, LANES).astype(F32)
+    planes = fields.reshape(FIELDS * rows, LANES)
+    lower = turned(jnp.concatenate([planes, shell[1]]), "space", 1)
+    upper = turned(jnp.concatenate([planes, shell[0]]), "space", -1)
     entries = jnp.concatenate(
         [
-            turned(shell[half:], "space", 1),
+            lower[FIELDS * rows :].astype(I32).reshape(half),
             jnp.arange(atoms, 2 * atoms, dtype=I32),
-            turned(shell[:half], "space", -1) + 2 * atoms,
+            upper[FIELDS * rows :].astype(I32).reshape(half) + 2 * atoms,
         ]
     )
     order = cell_order.reshape(atoms)
@@ -300,9 +331,9 @@
             pl.BlockSpec((8, 3 * TILE, LANES), lambda i: (i, 0, 0)),
         ],
         scratch_shapes=[
-            pltpu.VMEM((atoms, LANES), F32),
+            pltpu.VMEM((atoms + 2 * PAD, LANES), F32),
             pltpu.VMEM((8 * STRIDE, LANES), F32),
-            pltpu.VMEM((2, TILE, LANES), F32),
+            pltpu.VMEM((2, TILE, LANES), BF16),
         ],
         compiler_params=params,
         cost_estimate=pl.CostEstimate(flops=25 * 10**9, bytes_accessed=3 * 10**7, transcendentals=0),
@@ -316,11 +347,11 @@
         + [pl.BlockSpec((8, 3 * TILE, LANES), lambda i: (i, 0, 0)), pl.BlockSpec(memory_space=pl.ANY)],
         out_specs=[vector] * 2,
         scratch_shapes=[
-            pltpu.VMEM((3 * atoms, LANES), F32),
-            pltpu.VMEM((atoms, LANES), F32),
+            pltpu.VMEM((3 * atoms + 2 * PAD, LANES), F32),
+            pltpu.VMEM((atoms + 2 * PAD, LANES), F32),
             pltpu.VMEM((8 * STRIDE, LANES), F32),
-            pltpu.VMEM((partners, LANES), F32),
-            pltpu.VMEM((partners, LANES), F32),
+            pltpu.VMEM((partners, LANES), BF16),
+            pltpu.VMEM((partners, LANES), BF16),
             pltpu.VMEM((TILE, LANES), F32),
             pltpu.VMEM((TILE, LANES), F32),
             pltpu.SemaphoreType.DMA,

time: 194 us -> 188 us (0.969)
  waiting for transfers between devices: 11.8 us -> 5.53 us
  Pallas kernels: 144 us -> 141 us
  other arithmetic: 6.21 us -> 8.35 us
    ppermute x17 -> x15, waiting for transfers between devices: 11.8 us -> 5.53 us  [turned(): lax.ppermute(array, axis, [(i, (i + by) % count) for i in range(count)])]
    pallas_call x1, Pallas kernels: 40.7 us -> 38.3 us  [per_device(): pl.pallas_call(functools.partial(near_kernel, rows), grid=(rows // 8,), o...]
    ppermute x17 -> x15, starting transfers between devices: 21.2 us -> 22.3 us  [turned(): lax.ppermute(array, axis, [(i, (i + by) % count) for i in range(count)])]
  transfers between devices with their start and end apart: 17 -> 15, of which waited for: 7 -> 5; matrix products, arithmetic and copies ran while one was open for 3% -> 4% of each run, Pallas kernels for 21% -> 20%
where the time goes in v5:
time: 188 us; the launch traced here: 187 us
  Pallas kernels  141 us (75%)
  starting transfers between devices  22.3 us (12%)
  local copies, waits for them, and re-layouts  8.43 us (4%)
  other arithmetic  8.35 us (4%)
  waiting for transfers between devices  5.53 us (3%)
    pallas_call x1, Pallas kernels, per_device(): pl.pallas_call(functools.partial(force_kernel, rows), grid=(rows // 8,),...  103 us
    pallas_call x1, Pallas kernels, per_device(): pl.pallas_call(functools.partial(near_kernel, rows), grid=(rows // 8,), o...  38.3 us
    ppermute x15, starting transfers between devices, turned(): lax.ppermute(array, axis, [(i, (i + by) % count) for i in range(count)])  22.3 us
    ppermute x15, waiting for transfers between devices, turned(): lax.ppermute(array, axis, [(i, (i + by) % count) for i in range(count)])  5.53 us
  transfers between devices with their start and end apart: 15, of which 5 were waited for; matrix products, arithmetic and copies ran while one was open for 4% of the time, Pallas kernels for 20%

profile of v5, /device:TPU:0, one launch (start us, length us, event | category | flops | bytes accessed | tf_op | source)
XLA Modules:
  0.0 187.2 jit_solution(8660321263264613498)
XLA Ops:
  0.0 0.7 slice.113
  0.7 0.5 collective-permute-start.5
  1.3 2.6 %collective-permute-start.6 = (f32[3,1024]{1,0:T(4,128)S(1)}, f32[3,1024]{1,0:T(4,128)S(1)}, u32[]{:S(2)}, u32[]{:S(2)}) collective-permute-start(f32[3,1024]{1,0:T(4,128)S(1)} %get-tuple-element.29), channel_id=1, source_target_pairs={{0,16},{8,24},{16,0},{24,8},{1,17},{9,25},{17,1},{25,9},{2,18},{10... | collective-permute-start | bytes 36872 | tf_op jit(solution)/shard_map/ppermute | solution.py:278
  3.8 1.4 collective-permute-start.7
  5.2 1.1 copy.27
  6.4 0.9 convert_element_type.15
  8.0 0.9 select_multiply_fusion
  9.0 0.2 pad_maximum_fusion
  9.2 0.2 reshape_reshape.3
  9.5 4.6 %collective-permute-start.1 = (f32[880,128]{1,0:T(8,128)S(1)}, f32[880,128]{1,0:T(8,128)S(1)}, u32[]{:S(2)}, u32[]{:S(2)}) collective-permute-start(f32[880,128]{1,0:T(8,128)S(1)} %get-tuple-element.21), channel_id=1, source_target_pairs={{0,7},{1,0},{2,1},{3,2},{4,3},{5,4},{6,5},{7,6},{8,15},{9,8},{10,9... | collective-permute-start | bytes 1351688 | tf_op jit(solution)/shard_map/ppermute | solution.py:278
  14.0 0.6 fusion.eye_ref
  14.7 1.8 pad_maximum_fusion.3.fields_ref.place_ref
  16.4 38.3 %shard_map.82 = (f32[20480,128]{1,0:T(8,128)}, bf16[160,384,128]{2,1,0:T(8,128)(2,1)}) custom-call(s32[20480]{0:T(1024)} %bitcast.119, f32[5,160,128]{2,1,0:T(8,128)} %pad_maximum_fusion.3.fields_ref.place_ref, bf16[128,384]{1,0:T(8,128)(2,1)} %constant.122.clone.select_ref, bf16[128,128]{1,0:T(8,128)(2,1)} %fusion.eye_ref), custom_call_target="tpu_custom_call" | custom-call | flops 24999999488 | bytes 30000000 | tf_op jit(solution)/shard_map/pallas_call | solution.py:324
  54.8 0.8 copy.21
  55.6 0.1 multiply_reduce_fusion.6
  55.7 0.1 fusion.4
  55.9 0.8 pad_add_fusion.entry_ref
  56.6 0.2 copy-done.2
  56.8 102.8 %shard_map.83 = (f32[3,160,128]{2,1,0:T(8,128)}, f32[3,8,128]{2,1,0:T(8,128)}) custom-call(s32[40960]{0:T(1024)} %bitcast.110, s32[40960]{0:T(1024)} %pad_add_fusion.entry_ref, s32[20480]{0:T(1024)} %bitcast.120, f32[880,128]{1,0:T(8,128)} %copy-done.2, f32[880,128]{1,0:T(8,128)} %copy-done.1, f32[5,160,128]{2,1,0:T(8,128)} %pad_maximum_fusion.3.fields_ref.place_ref, ...), custom_call_target="tpu_custom_call" | custom-call | flops 24999999488 | bytes 30000000 | tf_op jit(solution)/shard_map/pallas_call | solution.py:341
  159.6 0.7 broadcast_in_dim.35
  160.3 0.7 copy.28
  161.0 0.5 collective-permute-start.3
  161.6 1.4 collective-permute-start.4
  163.1 1.1 reshape.90
  164.1 0.1 collective-permute-done.2
  164.2 0.6 collective-permute-done.3
  164.8 0.2 multiply_reduce_fusion
  165.0 0.2 multiply_reduce_fusion.3
  165.2 0.1 fusion.5
  165.2 0.1 fusion.6
  165.5 4.8 %collective-permute-start.14 = (f32[7,4]{1,0:T(8,128)S(1)}, f32[7,4]{1,0:T(8,128)S(1)}, u32[]{:S(2)}, u32[]{:S(2)}) collective-permute-start(f32[7,4]{1,0:T(8,128)S(1)} %stack.39), channel_id=1, source_target_pairs={{0,7},{1,0},{2,1},{3,2},{4,3},{5,4},{6,5},{7,6},{8,15},{9,8},{10,9... | collective-permute-start | bytes 344 | tf_op jit(solution)/shard_map/ppermute | solution.py:278
  170.3 3.0 %collective-permute-start.11 = (f32[7,4]{1,0:T(8,128)S(1)}, f32[7,4]{1,0:T(8,128)S(1)}, u32[]{:S(2)}, u32[]{:S(2)}) collective-permute-start(f32[7,4]{1,0:T(8,128)S(1)} %stack.39), channel_id=1, source_target_pairs={{0,4},{1,5},{2,6},{3,7},{4,0},{5,1},{6,2},{7,3},{8,12},{9,13},{10,... | collective-permute-start | bytes 344 | tf_op jit(solution)/shard_map/ppermute | solution.py:278
  173.3 2.0 %collective-permute-start.9 = (f32[7,4]{1,0:T(8,128)S(1)}, f32[7,4]{1,0:T(8,128)S(1)}, u32[]{:S(2)}, u32[]{:S(2)}) collective-permute-start(f32[7,4]{1,0:T(8,128)S(1)} %stack.39), channel_id=1, source_target_pairs={{0,2},{1,3},{2,4},{3,5},{4,6},{5,7},{6,0},{7,1},{8,10},{9,11},{10,... | collective-permute-start | bytes 344 | tf_op jit(solution)/shard_map/ppermute | solution.py:278
  175.3 1.5 collective-permute-start.8
  176.8 2.0 %collective-permute-done.10 = f32[7,4]{1,0:T(8,128)S(1)} collective-permute-done((f32[7,4]{1,0:T(8,128)S(1)}, f32[7,4]{1,0:T(8,128)S(1)}, u32[]{:S(2)}, u32[]{:S(2)}) %collective-permute-start.10) | collective-permute-done | bytes 144 | tf_op jit(solution)/shard_map/ppermute | solution.py:278
  178.7 1.4 collective-permute-done.9
  180.2 1.4 collective-permute-done.8
  181.6 0.1 multiply_bitcast_fusion
  181.7 0.1 fusion.10
  181.8 0.1 multiply_add_fusion
  181.9 0.1 add_sqrt_fusion
  182.0 0.2 reduce-window.4
  182.1 0.6 slice.138
  183.4 0.1 fusion.18
  183.7 0.6 dynamic_slice.20
  184.3 0.7 dynamic_slice.18
  184.9 1.4 add_dynamic-update-slice_fusion
  186.3 0.9 copy.18
  (44 shorter events, 0.7 us)
Async XLA Ops:
  0.7 54.8 %collective-permute-start.5 = (f32[3,1024]{1,0:T(4,128)S(1)}, f32[3,1024]{1,0:T(4,128)S(1)}, u32[]{:S(2)}, u32[]{:S(2)}) collective-permute-start(f32[3,1024]{1,0:T(4,128)S(1)} %get-tuple-element.29), channel_id=1, source_target_pairs={{0,8},{8,16},{16,24},{24,0},{1,9},{9,17},{17,25},{25,1},{2,10},{10... | collective-permute-start | bytes 36872 | tf_op jit(solution)/shard_map/ppermute | solution.py:278
  1.3 54.3 %collective-permute-start.6 = (f32[3,1024]{1,0:T(4,128)S(1)}, f32[3,1024]{1,0:T(4,128)S(1)}, u32[]{:S(2)}, u32[]{:S(2)}) collective-permute-start(f32[3,1024]{1,0:T(4,128)S(1)} %get-tuple-element.29), channel_id=1, source_target_pairs={{0,16},{8,24},{16,0},{24,8},{1,17},{9,25},{17,1},{25,9},{2,18},{10... | collective-permute-start | bytes 36872 | tf_op jit(solution)/shard_map/ppermute | solution.py:278
  3.8 51.7 %collective-permute-start.7 = (f32[3,1024]{1,0:T(4,128)S(1)}, f32[3,1024]{1,0:T(4,128)S(1)}, u32[]{:S(2)}, u32[]{:S(2)}) collective-permute-start(f32[3,1024]{1,0:T(4,128)S(1)} %get-tuple-element.29), channel_id=1, source_target_pairs={{0,24},{8,0},{16,8},{24,16},{1,25},{9,1},{17,9},{25,17},{2,26},{10... | collective-permute-start | bytes 36872 | tf_op jit(solution)/shard_map/ppermute | solution.py:278
  9.5 46.4 %collective-permute-start.1 = (f32[880,128]{1,0:T(8,128)S(1)}, f32[880,128]{1,0:T(8,128)S(1)}, u32[]{:S(2)}, u32[]{:S(2)}) collective-permute-start(f32[880,128]{1,0:T(8,128)S(1)} %get-tuple-element.21), channel_id=1, source_target_pairs={{0,7},{1,0},{2,1},{3,2},{4,3},{5,4},{6,5},{7,6},{8,15},{9,8},{10,9... | collective-permute-start | bytes 1351688 | tf_op jit(solution)/shard_map/ppermute | solution.py:278
  14.0 41.8 %collective-permute-start = (f32[880,128]{1,0:T(8,128)S(1)}, f32[880,128]{1,0:T(8,128)S(1)}, u32[]{:S(2)}, u32[]{:S(2)}) collective-permute-start(f32[880,128]{1,0:T(8,128)S(1)} %get-tuple-element.20), channel_id=1, source_target_pairs={{0,1},{1,2},{2,3},{3,4},{4,5},{5,6},{6,7},{7,0},{8,9},{9,10},{10,1... | collective-permute-start | bytes 1351688 | tf_op jit(solution)/shard_map/ppermute | solution.py:278
  16.4 38.3 %copy-start = (s32[1,160,256]{2,1,0:T(8,128)S(1)}, s32[1,160,256]{2,1,0:T(8,128)}, u32[]{:S(2)}) copy-start(s32[1,160,256]{2,1,0:T(8,128)} %param.14) | copy-start | bytes 491524
  55.8 0.8 copy-start.1
  55.9 1.0 copy-start.2
  161.0 3.2 %collective-permute-start.2 = (f32[3,1024]{1,0:T(4,128)S(1)}, f32[3,1024]{1,0:T(4,128)S(1)}, u32[]{:S(2)}, u32[]{:S(2)}) collective-permute-start(f32[3,1024]{1,0:T(4,128)S(1)} %bitcast.112), channel_id=1, source_target_pairs={{0,8},{8,16},{16,24},{24,0},{1,9},{9,17},{17,25},{25,1},{2,10},{10... | collective-permute-start | bytes 36872 | tf_op jit(solution)/shard_map/ppermute | solution.py:278
  161.0 3.8 %collective-permute-start.3 = (f32[3,1024]{1,0:T(4,128)S(1)}, f32[3,1024]{1,0:T(4,128)S(1)}, u32[]{:S(2)}, u32[]{:S(2)}) collective-permute-start(f32[3,1024]{1,0:T(4,128)S(1)} %bitcast.113), channel_id=1, source_target_pairs={{0,16},{8,24},{16,0},{24,8},{1,17},{9,25},{17,1},{25,9},{2,18},{10... | collective-permute-start | bytes 36872 | tf_op jit(solution)/shard_map/ppermute | solution.py:278
  161.6 3.2 %collective-permute-start.4 = (f32[3,1024]{1,0:T(4,128)S(1)}, f32[3,1024]{1,0:T(4,128)S(1)}, u32[]{:S(2)}, u32[]{:S(2)}) collective-permute-start(f32[3,1024]{1,0:T(4,128)S(1)} %bitcast.114), channel_id=1, source_target_pairs={{0,24},{8,0},{16,8},{24,16},{1,25},{9,1},{17,9},{25,17},{2,26},{10... | collective-permute-start | bytes 36872 | tf_op jit(solution)/shard_map/ppermute | solution.py:278
  165.5 7.8 %collective-permute-start.14 = (f32[7,4]{1,0:T(8,128)S(1)}, f32[7,4]{1,0:T(8,128)S(1)}, u32[]{:S(2)}, u32[]{:S(2)}) collective-permute-start(f32[7,4]{1,0:T(8,128)S(1)} %stack.39), channel_id=1, source_target_pairs={{0,7},{1,0},{2,1},{3,2},{4,3},{5,4},{6,5},{7,6},{8,15},{9,8},{10,9... | collective-permute-start | bytes 344 | tf_op jit(solution)/shard_map/ppermute | solution.py:278
  170.3 5.0 %collective-permute-start.13 = (f32[7,4]{1,0:T(8,128)S(1)}, f32[7,4]{1,0:T(8,128)S(1)}, u32[]{:S(2)}, u32[]{:S(2)}) collective-permute-start(f32[7,4]{1,0:T(8,128)S(1)} %stack.39), channel_id=1, source_target_pairs={{0,6},{1,7},{2,0},{3,1},{4,2},{5,3},{6,4},{7,5},{8,14},{9,15},{10,... | collective-permute-start | bytes 344 | tf_op jit(solution)/shard_map/ppermute | solution.py:278
  170.3 6.5 %collective-permute-start.12 = (f32[7,4]{1,0:T(8,128)S(1)}, f32[7,4]{1,0:T(8,128)S(1)}, u32[]{:S(2)}, u32[]{:S(2)}) collective-permute-start(f32[7,4]{1,0:T(8,128)S(1)} %stack.39), channel_id=1, source_target_pairs={{0,5},{1,6},{2,7},{3,0},{4,1},{5,2},{6,3},{7,4},{8,13},{9,14},{10,... | collective-permute-start | bytes 344 | tf_op jit(solution)/shard_map/ppermute | solution.py:278
  170.3 6.5 %collective-permute-start.11 = (f32[7,4]{1,0:T(8,128)S(1)}, f32[7,4]{1,0:T(8,128)S(1)}, u32[]{:S(2)}, u32[]{:S(2)}) collective-permute-start(f32[7,4]{1,0:T(8,128)S(1)} %stack.39), channel_id=1, source_target_pairs={{0,4},{1,5},{2,6},{3,7},{4,0},{5,1},{6,2},{7,3},{8,12},{9,13},{10,... | collective-permute-start | bytes 344 | tf_op jit(solution)/shard_map/ppermute | solution.py:278
  173.3 5.4 %collective-permute-start.10 = (f32[7,4]{1,0:T(8,128)S(1)}, f32[7,4]{1,0:T(8,128)S(1)}, u32[]{:S(2)}, u32[]{:S(2)}) collective-permute-start(f32[7,4]{1,0:T(8,128)S(1)} %stack.39), channel_id=1, source_target_pairs={{0,3},{1,4},{2,5},{3,6},{4,7},{5,0},{6,1},{7,2},{8,11},{9,12},{10,... | collective-permute-start | bytes 344 | tf_op jit(solution)/shard_map/ppermute | solution.py:278
  173.3 6.9 %collective-permute-start.9 = (f32[7,4]{1,0:T(8,128)S(1)}, f32[7,4]{1,0:T(8,128)S(1)}, u32[]{:S(2)}, u32[]{:S(2)}) collective-permute-start(f32[7,4]{1,0:T(8,128)S(1)} %stack.39), channel_id=1, source_target_pairs={{0,2},{1,3},{2,4},{3,5},{4,6},{5,7},{6,0},{7,1},{8,10},{9,11},{10,... | collective-permute-start | bytes 344 | tf_op jit(solution)/shard_map/ppermute | solution.py:278
  175.3 6.3 %collective-permute-start.8 = (f32[7,4]{1,0:T(8,128)S(1)}, f32[7,4]{1,0:T(8,128)S(1)}, u32[]{:S(2)}, u32[]{:S(2)}) collective-permute-start(f32[7,4]{1,0:T(8,128)S(1)} %stack.39), channel_id=1, source_target_pairs={{0,1},{1,2},{2,3},{3,4},{4,5},{5,6},{6,7},{7,0},{8,9},{9,10},{10,1... | collective-permute-start | bytes 344 | tf_op jit(solution)/shard_map/ppermute | solution.py:278

commit v6 on v5

--- a/solution.py
+++ b/solution.py
@@ -13,6 +13,7 @@
 LANES = 128
 FIELDS = 5
 STRIDE = 48
+FORCE_PAD = 1024
 PAD = 8
 
 LJ_COEF = 0.5
@@ -127,13 +128,15 @@
     def _():
         planes[...] = jnp.zeros_like(planes)
 
-        def fill(group, carry):
-            spot = pl.ds(pl.multiple_of(group * 8, 8), 8)
-            fields = [fields_ref[field, spot, :] for field in range(FIELDS)]
-            fill_blocks(fields, eye_ref[...], planes, table, group * 8 * LANES)
+        def fill(turn, carry):
+            for side in range(2):
+                group = turn * 2 + side
+                spot = pl.ds(pl.multiple_of(group * 8, 8), 8)
+                fields = [fields_ref[field, spot, :] for field in range(FIELDS)]
+                fill_blocks(fields, eye_ref[...], planes.at[side], table, group * 8 * LANES)
             return carry
 
-        lax.fori_loop(0, rows // 8, fill, 0)
+        lax.fori_loop(0, rows // 16, fill, 0)
 
     masks = sublane_masks()
 
@@ -187,7 +190,7 @@
 
 def force_kernel(
     rows, partner_ref, entry_ref, order_ref, lower_ref, upper_ref, place_ref, eye_ref, left_ref, own_ref,
-    out_ref, solute_ref, table, forces, planes, far_a, far_b, sum_a, sum_b, arrival,
+    force_ref, solute_ref, table, forces, planes, far_a, far_b, sum_a, sum_b, arrival,
 ):
     turn = pl.program_id(0)
     partners = far_a.shape[0]
@@ -208,7 +211,7 @@
         def copy(block):
             value = sums[block * 8 : block * 8 + 8, :]
             for k in range(8):
-                place = order_ref[tile * TILE + block * 8 + k] + (PAD - k)
+                place = order_ref[tile * TILE + block * 8 + k] + (FORCE_PAD - k)
                 pltpu.store(forces.at[pl.ds(place, 8), :], value, mask=masks[k])
 
         return [functools.partial(copy, block) for block in range(TILE // 8)]
@@ -220,12 +223,12 @@
         planes[...] = jnp.zeros_like(planes)
 
         def fill(group, carry):
-            for ref, first, shift in ((lower_ref, 0, -SLAB_WIDTH), (upper_ref, 2 * own, SLAB_WIDTH)):
+            for side, ref, first, shift in ((0, lower_ref, 0, -SLAB_WIDTH), (1, upper_ref, 2 * own, SLAB_WIDTH)):
                 fields = [
                     ref[pl.ds(pl.multiple_of(field * rows + group * 8, 8), 8), :] for field in range(FIELDS)
                 ]
                 fields[0] = fields[0] + shift
-                fill_blocks(fields, eye_ref[...], planes, table, first + group * 8 * LANES)
+                fill_blocks(fields, eye_ref[...], planes.at[side], table, first + group * 8 * LANES)
             return carry
 
         lax.fori_loop(0, rows // 8, fill, 0)
@@ -249,24 +252,115 @@
         for copy in save(rows - 1, sum_b):
             copy()
 
-        def finish(group, carry):
-            for local in range(4):
-                row = group * 4 + local
-                turned_sums = forces[pl.ds(pl.multiple_of(row * LANES + PAD, PAD), LANES), :].T
-                for axis in range(3):
-                    first = 6 * axis
-                    moment = (
-                        turned_sums[first : first + 1]
-                        + turned_sums[first + 1 : first + 2]
-                        + turned_sums[first + 3 : first + 4]
-                    )
-                    place = place_ref[axis, pl.ds(row, 1), :]
-                    force = (place - CENTRE) * turned_sums[ONES : ONES + 1] - moment
-                    out_ref[axis, pl.ds(row, 1), :] = place + STEP_SIZE * force
-            return carry
-
-        lax.fori_loop(0, rows // 4, finish, 0)
-        solute_ref[...] = out_ref[:, 0 : SOL_DEV // LANES, :]
+        send = pltpu.make_async_copy(forces, force_ref, arrival)
+        send.start()
+        for row in range(SOL_DEV // LANES):
+            start = FORCE_PAD + row * LANES
+            force = row_forces(forces[start : start + LANES, :], [place_ref[axis, row : row + 1, :] for axis in range(3)])
+            for axis in range(3):
+                solute_ref[axis, row : row + 1, :] = place_ref[axis, row : row + 1, :] + STEP_SIZE * force[axis]
+        send.wait()
+
+
+def row_forces(sums, places):
+    across = sums.T
+    result = []
+    for axis, place in enumerate(places):
+        first = 6 * axis
+        moment = across[first : first + 1] + across[first + 1 : first + 2] + across[first + 3 : first + 4]
+        result.append((place - CENTRE) * across[ONES : ONES + 1] - moment)
+    return result
+
+
+def relax_kernel(place_ref, force_ref, out_ref):
+    for row in range(8):
+        places = [place_ref[axis, row : row + 1, :] for axis in range(3)]
+        for axis, force in enumerate(row_forces(force_ref[row * LANES : (row + 1) * LANES, :], places)):
+            out_ref[axis, row : row + 1, :] = places[axis] + STEP_SIZE * force
+
+
+def product_kernel(images, index_ref, *refs):
+    pushed_refs, path_refs = refs[:images], refs[images : 2 * images]
+    sums_ref, pushed, path = refs[2 * images :]
+    index = index_ref[0]
+    for by in range(images):
+        place = lax.rem(index + images - by, images)
+        pushed[place] = pushed_refs[by][...]
+        path[place] = path_refs[by][...]
+    sums_ref[...] = jnp.zeros_like(sums_ref)
+    last = images - 1
+    tangents = [path[min(k + 1, last)] - path[max(k - 1, 0)] for k in range(images)]
+
+    def put(kind, image, left, right):
+        total = jnp.sum(left * right, axis=0)
+        sums_ref[kind * images + image : kind * images + image + 1, :] = jnp.sum(total, axis=0, keepdims=True)
+
+    for k in range(images):
+        put(0, k, tangents[k], tangents[k])
+        put(1, k, pushed[k] - path[k], tangents[k])
+        if k < last:
+            step = path[k + 1] - path[k]
+            gap = pushed[k + 1] - pushed[k]
+            put(2, k, step, step)
+            put(3, k, gap, gap)
+            put(4, k, gap, tangents[k + 1])
+            put(5, k, gap, tangents[k])
+            put(6, k, tangents[k + 1], tangents[k])
+
+
+def blend_kernel(images, index_ref, sums_ref, pushed, path, out_in, out_ref):
+    del out_in
+    index = index_ref[0]
+    last = images - 1
+    totals = jnp.sum(sums_ref[...], axis=1, keepdims=True)
+
+    def total(kind, image):
+        row = kind * images + image
+        return totals[row : row + 1, :]
+
+    step_root = [jnp.sqrt(total(2, k) + EPSILON) for k in range(last)]
+    shift = []
+    for k in range(images):
+        tangent_sq = total(0, k)
+        value = -total(1, k) / (tangent_sq + EPSILON)
+        if 0 < k < last:
+            spring = SPRING_COEF * (step_root[k] - step_root[k - 1]) / jnp.sqrt(tangent_sq + EPSILON)
+            value = value + STEP_SIZE * spring
+        shift.append(value)
+    lengths = []
+    for k in range(last):
+        there, here = shift[k + 1], shift[k]
+        length_sq = (
+            total(3, k)
+            + there * there * total(0, k + 1)
+            + here * here * total(0, k)
+            + 2.0 * (there * total(4, k) - here * total(5, k) - there * here * total(6, k))
+        )
+        lengths.append(jnp.sqrt(jnp.maximum(length_sq, 0.0) + EPSILON))
+    knots = [jnp.zeros_like(lengths[0])]
+    for length in lengths:
+        knots.append(knots[-1] + length)
+
+    def pick(values):
+        result = values[0]
+        for k in range(1, images):
+            result = jnp.where(index == k, values[k], result)
+        return result
+
+    none = jnp.zeros_like(lengths[0])
+    excess = [knots[k] - knots[last] * (k / last) for k in range(images)]
+    back = pick([none] + [jnp.clip(excess[k] / lengths[k - 1], 0.0, 1.0) for k in range(1, images)])
+    ahead = pick([jnp.clip(-excess[k] / lengths[k], 0.0, 1.0) for k in range(last)] + [none])
+    shifts = [pick([shift[min(max(k + by, 0), last)] for k in range(images)]) for by in (-1, 0, 1)]
+
+    def moved(by):
+        place = jnp.clip(index + by, 0, last)
+        tangent = path[jnp.minimum(place + 1, last)] - path[jnp.maximum(place - 1, 0)]
+        return pushed[place] + shifts[by + 1] * tangent
+
+    here = moved(0)
+    blended = here + back * (moved(-1) - here) + ahead * (moved(1) - here)
+    out_ref[...] = blended
 
 
 def whole(*shape, dtype=F32):
@@ -279,20 +373,18 @@
 
 
 def summed(array, axis):
-    return sum((turned(array, axis, by) for by in range(1, lax.axis_size(axis))), array)
+    count = lax.axis_size(axis)
+    if count & (count - 1):
+        return lax.psum(array, axis)
+    by = 1
+    while by < count:
+        array = array + lax.ppermute(array, axis, [(i, i ^ by) for i in range(count)])
+        by *= 2
+    return array
 
 
 def round_trip(array, axis):
-    count, index = lax.axis_size(axis), lax.axis_index(axis)
-    result = jnp.zeros((count,) + array.shape, array.dtype)
-    for by in range(count):
-        piece = turned(array, axis, by) if by else array
-        result = lax.dynamic_update_index_in_dim(result, piece, (index + count - by) % count, 0)
-    return result
-
-
-def inner(left, right):
-    return jnp.sum(left * right, axis=(1, 2))
+    return [array] + [turned(array, axis, by) for by in range(1, lax.axis_size(axis))]
 
 
 def per_device(positions, strength, charge, rest_scale, cell_order, ghost_index, tile_atoms):
@@ -300,11 +392,14 @@
     rows = atoms // LANES
     half = atoms // 2
     partners = tile_atoms.shape[2]
-    paths = round_trip(positions[0, :, :SOL_DEV], "image")
+    images = lax.axis_size("image")
+    index = lax.axis_index("image").reshape(1)
 
     factor = jnp.where(jnp.arange(atoms) < SOL_DEV, jnp.sqrt(rest_scale[0]), 1.0)
-    scaled = jnp.stack([strength * factor, charge * factor])
-    fields = jnp.concatenate([positions[0], scaled]).reshape(FIELDS, rows, LANES)
+    scaled = jnp.stack([strength * factor, charge * factor]).reshape(2, rows, LANES)
+    places = positions.reshape(3, rows, LANES)
+    fields = jnp.concatenate([places, scaled])
+    paths = round_trip(places[:, : SOL_DEV // LANES], "image")
     shell = ghost_index.reshape(2, rows // 2, LANES).astype(F32)
     planes = fields.reshape(FIELDS * rows, LANES)
     lower = turned(jnp.concatenate([planes, shell[1]]), "space", 1)
@@ -332,24 +427,24 @@
         ],
         scratch_shapes=[
             pltpu.VMEM((atoms + 2 * PAD, LANES), F32),
-            pltpu.VMEM((8 * STRIDE, LANES), F32),
+            pltpu.VMEM((2, 8 * STRIDE, LANES), F32),
             pltpu.VMEM((2, TILE, LANES), BF16),
         ],
         compiler_params=params,
         cost_estimate=pl.CostEstimate(flops=25 * 10**9, bytes_accessed=3 * 10**7, transcendentals=0),
     )(order, fields, near_selector(), eye)
-    out, solute = pl.pallas_call(
+    forces, solute = pl.pallas_call(
         functools.partial(force_kernel, rows),
         grid=(rows // 8,),
-        out_shape=[whole(3, rows, LANES), whole(3, SOL_DEV // LANES, LANES)],
+        out_shape=[whole(atoms + 2 * FORCE_PAD, LANES), whole(3, SOL_DEV // LANES, LANES)],
         in_specs=[scalar] * 3
         + [vector] * 4
         + [pl.BlockSpec((8, 3 * TILE, LANES), lambda i: (i, 0, 0)), pl.BlockSpec(memory_space=pl.ANY)],
-        out_specs=[vector] * 2,
+        out_specs=[pl.BlockSpec(memory_space=pl.ANY), vector],
         scratch_shapes=[
             pltpu.VMEM((3 * atoms + 2 * PAD, LANES), F32),
-            pltpu.VMEM((atoms + 2 * PAD, LANES), F32),
-            pltpu.VMEM((8 * STRIDE, LANES), F32),
+            pltpu.VMEM((atoms + 2 * FORCE_PAD, LANES), F32),
+            pltpu.VMEM((2, 8 * STRIDE, LANES), F32),
             pltpu.VMEM((partners, LANES), BF16),
             pltpu.VMEM((partners, LANES), BF16),
             pltpu.VMEM((TILE, LANES), F32),
@@ -358,63 +453,37 @@
         ],
         compiler_params=params,
         cost_estimate=pl.CostEstimate(flops=25 * 10**9, bytes_accessed=3 * 10**7, transcendentals=0),
-    )(tile_atoms.reshape(rows * partners), entries, order, lower, upper, fields, eye, left, table)
-    out = out.reshape(1, 3, atoms)
-    solute = solute.reshape(1, 3, SOL_DEV)
-
-    pushed = round_trip(solute[0], "image")
-    images = lax.axis_size("image")
-    index = lax.axis_index("image")
-    steps = paths[1:] - paths[:-1]
-    upper_path = jnp.concatenate([paths[1:], paths[-1:]])
-    lower_path = jnp.concatenate([paths[:1], paths[:-1]])
-    tangents = upper_path - lower_path
-    gaps = pushed[1:] - pushed[:-1]
-    none = jnp.zeros((1,), F32)
-    sums = summed(
-        jnp.stack(
-            [
-                inner(tangents, tangents),
-                inner(pushed - paths, tangents),
-                jnp.concatenate([inner(steps, steps), none]),
-                jnp.concatenate([inner(gaps, gaps), none]),
-                jnp.concatenate([inner(gaps, tangents[1:]), none]),
-                jnp.concatenate([inner(gaps, tangents[:-1]), none]),
-                jnp.concatenate([inner(tangents[1:], tangents[:-1]), none]),
-            ]
-        ),
-        "space",
-    )
-    tangent_sq, along = sums[0], sums[1]
-    step_sq, gap_sq, gap_next, gap_this, cross = (sums[i, :-1] for i in range(2, 7))
-    step_root = jnp.sqrt(step_sq + EPSILON)
-    spring = SPRING_COEF * (step_root[1:] - step_root[:-1]) / jnp.sqrt(tangent_sq[1:-1] + EPSILON)
-    spring = jnp.concatenate([none, spring, none])
-    shift = STEP_SIZE * spring - along / (tangent_sq + EPSILON)
-    ahead_shift, here_shift = shift[1:], shift[:-1]
-    length_sq = (
-        gap_sq
-        + ahead_shift * ahead_shift * tangent_sq[1:]
-        + here_shift * here_shift * tangent_sq[:-1]
-        + 2.0 * (ahead_shift * gap_next - here_shift * gap_this - ahead_shift * here_shift * cross)
-    )
-    lengths = jnp.sqrt(jnp.maximum(length_sq, 0.0) + EPSILON)
-    knots = jnp.concatenate([none, jnp.cumsum(lengths)])
-    targets = knots[-1] * (jnp.arange(images, dtype=F32) / (images - 1))
-    back = jnp.concatenate([none, jnp.clip((knots - targets)[1:] / lengths, 0.0, 1.0)])
-    ahead = jnp.concatenate([jnp.clip((targets - knots)[:-1] / lengths, 0.0, 1.0), none])
-    moved = pushed + shift[:, None, None] * tangents
-
-    def at(array, place):
-        return lax.dynamic_index_in_dim(array, jnp.clip(place, 0, images - 1), 0, keepdims=False)
-
-    here = at(moved, index)
-    blended = (
-        here
-        + at(back, index) * (at(moved, index - 1) - here)
-        + at(ahead, index) * (at(moved, index + 1) - here)
-    )
-    return lax.dynamic_update_slice(out, blended[None], (0, 0, 0))
+    )(tile_atoms.reshape(rows * partners), entries, order, lower, upper, places, eye, left, table)
+    solutes = round_trip(solute, "image")
+    block = pl.BlockSpec((3, 8, LANES), lambda i: (0, i, 0))
+    small = pltpu.CompilerParams(vmem_limit_bytes=8 * 1024 * 1024)
+    out = pl.pallas_call(
+        relax_kernel,
+        grid=(rows // 8,),
+        out_shape=whole(3, rows, LANES),
+        in_specs=[block, pl.BlockSpec((8 * LANES, LANES), lambda i: (i + FORCE_PAD // (8 * LANES), 0))],
+        out_specs=block,
+        compiler_params=small,
+        cost_estimate=pl.CostEstimate(flops=10**9, bytes_accessed=2 * 10**7, transcendentals=0),
+    )(places, forces)
+    solute_shape = whole(images, 3, SOL_DEV // LANES, LANES)
+    sums, pushed, path = pl.pallas_call(
+        functools.partial(product_kernel, images),
+        out_shape=[whole(-(-7 * images // 8) * 8, LANES), solute_shape, solute_shape],
+        in_specs=[scalar] + [vector] * (2 * images),
+        out_specs=[vector] * 3,
+        compiler_params=small,
+    )(index, *solutes, *paths)
+    out = pl.pallas_call(
+        functools.partial(blend_kernel, images),
+        grid=(1,),
+        out_shape=whole(3, rows, LANES),
+        in_specs=[scalar] + [vector] * 3 + [pl.BlockSpec(memory_space=pl.ANY)],
+        out_specs=pl.BlockSpec((3, SOL_DEV // LANES, LANES), lambda i: (0, 0, 0)),
+        input_output_aliases={4: 0},
+        compiler_params=small,
+    )(index, summed(sums, "space"), pushed, path, out)
+    return out.reshape(1, 3, atoms)
 
 
 def solution(mesh):

time: 188 us -> 182 us (0.968)
  starting transfers between devices: 22.3 us -> 13.3 us
  Pallas kernels: 141 us -> 148 us
  other arithmetic: 8.35 us -> 4.38 us
  waiting for transfers between devices: 5.53 us -> 9.26 us
    ppermute x15 -> x8, starting transfers between devices: 22.3 us -> 11.2 us  [turned(): lax.ppermute(array, axis, [(i, (i + by) % count) for i in range(count)])]
    pallas_call x0 -> x3, Pallas kernels: none -> 8.83 us  [the longest x1 8 us: per_device(): pl.pallas_call(relax_kernel, grid=(rows // 8,), out_shape=whole(3, rows,...]
    ppermute x0 -> x3, waiting for transfers between devices: none -> 7.4 us  [summed(): lax.ppermute(array, axis, [(i, i ^ by) for i in range(count)])]
    ppermute x15 -> x8, waiting for transfers between devices: 5.53 us -> 1.86 us  [turned(): lax.ppermute(array, axis, [(i, (i + by) % count) for i in range(count)])]
    unnamed x9 -> x15, local copies, waits for them, and re-layouts: 2.77 us -> 5.88 us
    ppermute x0 -> x3, starting transfers between devices: none -> 2.12 us  [summed(): lax.ppermute(array, axis, [(i, i ^ by) for i in range(count)])]
    pallas_call x1, Pallas kernels: 38.3 us -> 36.3 us  [per_device(): pl.pallas_call(functools.partial(near_kernel, rows), grid=(rows // 8,), o...]
  transfers between devices with their start and end apart: 15 -> 11, of which waited for: 5 -> 4; matrix products, arithmetic and copies ran while one was open for 4% -> 3% of each run, Pallas kernels for 20% -> 81%
where the time goes in v6:
time: 182 us
  Pallas kernels  148 us (81%)
  starting transfers between devices  13.3 us (7%)
  waiting for transfers between devices  9.26 us (5%)
  local copies, waits for them, and re-layouts  6.6 us (4%)
  other arithmetic  4.38 us (2%)
    pallas_call x1, Pallas kernels, per_device(): pl.pallas_call(functools.partial(force_kernel, rows), grid=(rows // 8,),...  102 us
    pallas_call x1, Pallas kernels, per_device(): pl.pallas_call(functools.partial(near_kernel, rows), grid=(rows // 8,), o...  36.3 us
    ppermute x8, starting transfers between devices, turned(): lax.ppermute(array, axis, [(i, (i + by) % count) for i in range(count)])  11.2 us
    pallas_call x1, Pallas kernels, per_device(): pl.pallas_call(relax_kernel, grid=(rows // 8,), out_shape=whole(3, rows,...  8 us
    ppermute x3, waiting for transfers between devices, summed(): lax.ppermute(array, axis, [(i, i ^ by) for i in range(count)])  7.4 us
    unnamed x15, local copies, waits for them, and re-layouts  5.88 us
  transfers between devices with their start and end apart: 11, of which 4 were waited for; matrix products, arithmetic and copies ran while one was open for 3% of the time, Pallas kernels for 81%

profile of v6, /device:TPU:0, one launch (start us, length us, event | category | flops | bytes accessed | tf_op | source)
XLA Modules:
  0.0 182.0 jit_solution(17296229103251811318)
XLA Ops:
  0.0 0.7 slice.26.refs_4_
  0.7 0.5 collective-permute-start.5
  1.2 2.5 %collective-permute-start.6 = (f32[3,8,128]{2,1,0:T(8,128)S(1)}, f32[3,8,128]{2,1,0:T(8,128)S(1)}, u32[]{:S(2)}, u32[]{:S(2)}) collective-permute-start(f32[3,8,128]{2,1,0:T(8,128)S(1)} %slice.26.refs_4_), channel_id=1, source_target_pairs={{0,16},{8,24},{16,0},{24,8},{1,17},{9,25},{17,1},{25,9},{2,18},{10... | collective-permute-start | bytes 36872 | tf_op jit(solution)/shard_map/ppermute | solution.py:372
  3.7 1.4 collective-permute-start.7
  5.8 0.9 convert_element_type.15
  6.8 0.9 fusion
  7.7 1.0 pad_maximum_fusion.2.fields_ref
  8.7 0.0 copy-start.3
  8.7 0.1 pad_maximum_fusion
  8.8 4.6 %collective-permute-start.1 = (f32[880,128]{1,0:T(8,128)S(1)}, f32[880,128]{1,0:T(8,128)S(1)}, u32[]{:S(2)}, u32[]{:S(2)}) collective-permute-start(f32[880,128]{1,0:T(8,128)S(1)} %get-tuple-element.20), channel_id=1, source_target_pairs={{0,7},{1,0},{2,1},{3,2},{4,3},{5,4},{6,5},{7,6},{8,15},{9,8},{10,9... | collective-permute-start | bytes 1351688 | tf_op jit(solution)/shard_map/ppermute | solution.py:372
  13.4 0.0 collective-permute-start
  13.4 0.6 fusion.2.eye_ref
  14.0 0.0 copy-done.3
  14.0 0.0 copy-start.4
  14.0 36.3 %shard_map.82 = (f32[20480,128]{1,0:T(8,128)}, bf16[160,384,128]{2,1,0:T(8,128)(2,1)}) custom-call(s32[20480]{0:T(1024)} %bitcast.27, f32[5,160,128]{2,1,0:T(8,128)} %copy-done.3, bf16[128,384]{1,0:T(8,128)(2,1)} %constant.15.clone.select_ref, bf16[128,128]{1,0:T(8,128)(2,1)} %fusion.2.eye_ref), custom_call_target="tpu_custom_call" | custom-call | flops 24999999488 | bytes 30000000 | tf_op jit(solution)/shard_map/pallas_call | solution.py:419
  50.3 0.0 copy-done.4
  50.3 0.8 copy.12
  51.1 0.0 collective-permute-done.1.upper_ref
  51.1 0.0 copy-start.5
  51.1 0.0 collective-permute-done.lower_ref
  51.2 0.0 copy-start.6
  51.2 0.8 pad_add_fusion.entry_ref
  52.0 0.0 copy-done.5
  52.0 0.1 copy-done.6
  52.1 0.0 copy-start.1
  52.1 102.5 %shard_map.83 = (f32[22528,128]{1,0:T(8,128)}, f32[3,8,128]{2,1,0:T(8,128)}) custom-call(s32[40960]{0:T(1024)} %bitcast.26, s32[40960]{0:T(1024)} %pad_add_fusion.entry_ref, s32[20480]{0:T(1024)} %bitcast.28, f32[880,128]{1,0:T(8,128)} %copy-done.6, f32[880,128]{1,0:T(8,128)} %copy-done.5, f32[3,160,128]{2,1,0:T(8,128)} %bitcast.20, ...), custom_call_target="tpu_custom_call" | custom-call | flops 24999999488 | bytes 30000000 | tf_op jit(solution)/shard_map/pallas_call | solution.py:436
  154.6 0.1 collective-permute-start.2
  154.7 0.7 collective-permute-start.3
  155.4 0.0 collective-permute-done.5.refs_5_
  155.4 1.4 collective-permute-start.4
  156.8 0.0 collective-permute-done.6.refs_6_
  156.8 0.0 collective-permute-done.7.refs_7_
  156.8 1.2 collective-permute-done.2.refs_1_
  158.0 0.7 collective-permute-done.3.refs_2_
  158.6 0.0 collective-permute-done.4.refs_3_
  158.6 0.0 copy-start.2
  158.7 0.7 copy-done.2
  159.4 0.1 shard_map.84
  159.4 0.1 collective-permute-start.8
  159.6 3.7 %collective-permute-done.8 = f32[32,128]{1,0:T(8,128)S(1)} collective-permute-done((f32[32,128]{1,0:T(8,128)S(1)}, f32[32,128]{1,0:T(8,128)S(1)}, u32[]{:S(2)}, u32[]{:S(2)}) %collective-permute-start.8) | collective-permute-done | bytes 16416 | tf_op jit(solution)/shard_map/ppermute | solution.py:381
  163.2 0.0 collective-permute-start.9
  163.2 3.7 %collective-permute-done.9 = f32[32,128]{1,0:T(8,128)S(1)} collective-permute-done((f32[32,128]{1,0:T(8,128)S(1)}, f32[32,128]{1,0:T(8,128)S(1)}, u32[]{:S(2)}, u32[]{:S(2)}) %collective-permute-start.9) | collective-permute-done | bytes 16416 | tf_op jit(solution)/shard_map/ppermute | solution.py:381
  167.0 2.0 %collective-permute-start.10 = (f32[32,128]{1,0:T(8,128)S(1)}, f32[32,128]{1,0:T(8,128)S(1)}, u32[]{:S(2)}, u32[]{:S(2)}) collective-permute-start(f32[32,128]{1,0:T(8,128)S(1)} %add.30), channel_id=1, source_target_pairs={{0,4},{1,5},{2,6},{3,7},{4,0},{5,1},{6,2},{7,3},{8,12},{9,13},{10,... | collective-permute-start | bytes 49160 | tf_op jit(solution)/shard_map/ppermute | solution.py:381
  168.9 0.0 copy-done.1
  169.0 4.3 %copy-done = f32[22528,128]{1,0:T(8,128)S(1)} copy-done((f32[22528,128]{1,0:T(8,128)S(1)}, f32[22528,128]{1,0:T(8,128)}, u32[]{:S(2)}) %copy-start) | copy-done | bytes 11534360
  173.2 8.0 %shard_map.85.out_in = f32[3,160,128]{2,1,0:T(8,128)} custom-call(f32[3,160,128]{2,1,0:T(8,128)S(1)} %bitcast.21, f32[22528,128]{1,0:T(8,128)S(1)} %copy-done), custom_call_target="tpu_custom_call" | custom-call | flops 1000000000 | bytes 20000000 | tf_op jit(solution)/shard_map/pallas_call | solution.py:460
  181.2 0.0 collective-permute-done.10
  181.2 0.8 shard_map.86
  (8 shorter events, 0.0 us)
Async XLA Ops:
  0.7 154.7 %collective-permute-start.5 = (f32[3,8,128]{2,1,0:T(8,128)S(1)}, f32[3,8,128]{2,1,0:T(8,128)S(1)}, u32[]{:S(2)}, u32[]{:S(2)}) collective-permute-start(f32[3,8,128]{2,1,0:T(8,128)S(1)} %slice.26.refs_4_), channel_id=1, source_target_pairs={{0,8},{8,16},{16,24},{24,0},{1,9},{9,17},{17,25},{25,1},{2,10},{10... | collective-permute-start | bytes 36872 | tf_op jit(solution)/shard_map/ppermute | solution.py:372
  1.2 155.6 %collective-permute-start.6 = (f32[3,8,128]{2,1,0:T(8,128)S(1)}, f32[3,8,128]{2,1,0:T(8,128)S(1)}, u32[]{:S(2)}, u32[]{:S(2)}) collective-permute-start(f32[3,8,128]{2,1,0:T(8,128)S(1)} %slice.26.refs_4_), channel_id=1, source_target_pairs={{0,16},{8,24},{16,0},{24,8},{1,17},{9,25},{17,1},{25,9},{2,18},{10... | collective-permute-start | bytes 36872 | tf_op jit(solution)/shard_map/ppermute | solution.py:372
  3.7 153.1 %collective-permute-start.7 = (f32[3,8,128]{2,1,0:T(8,128)S(1)}, f32[3,8,128]{2,1,0:T(8,128)S(1)}, u32[]{:S(2)}, u32[]{:S(2)}) collective-permute-start(f32[3,8,128]{2,1,0:T(8,128)S(1)} %slice.26.refs_4_), channel_id=1, source_target_pairs={{0,24},{8,0},{16,8},{24,16},{1,25},{9,1},{17,9},{25,17},{2,26},{10... | collective-permute-start | bytes 36872 | tf_op jit(solution)/shard_map/ppermute | solution.py:372
  8.7 5.3 %copy-start.3 = (f32[5,160,128]{2,1,0:T(8,128)}, f32[5,160,128]{2,1,0:T(8,128)S(1)}, u32[]{:S(2)}) copy-start(f32[5,160,128]{2,1,0:T(8,128)S(1)} %pad_maximum_fusion.2.fields_ref) | copy-start | bytes 1228804
  8.8 42.3 %collective-permute-start.1 = (f32[880,128]{1,0:T(8,128)S(1)}, f32[880,128]{1,0:T(8,128)S(1)}, u32[]{:S(2)}, u32[]{:S(2)}) collective-permute-start(f32[880,128]{1,0:T(8,128)S(1)} %get-tuple-element.20), channel_id=1, source_target_pairs={{0,7},{1,0},{2,1},{3,2},{4,3},{5,4},{6,5},{7,6},{8,15},{9,8},{10,9... | collective-permute-start | bytes 1351688 | tf_op jit(solution)/shard_map/ppermute | solution.py:372
  13.4 37.8 %collective-permute-start = (f32[880,128]{1,0:T(8,128)S(1)}, f32[880,128]{1,0:T(8,128)S(1)}, u32[]{:S(2)}, u32[]{:S(2)}) collective-permute-start(f32[880,128]{1,0:T(8,128)S(1)} %get-tuple-element.19), channel_id=1, source_target_pairs={{0,1},{1,2},{2,3},{3,4},{4,5},{5,6},{6,7},{7,0},{8,9},{9,10},{10,1... | collective-permute-start | bytes 1351688 | tf_op jit(solution)/shard_map/ppermute | solution.py:372
  14.0 36.3 %copy-start.4 = (s32[1,160,256]{2,1,0:T(8,128)S(1)}, s32[1,160,256]{2,1,0:T(8,128)}, u32[]{:S(2)}) copy-start(s32[1,160,256]{2,1,0:T(8,128)} %param.14) | copy-start | bytes 491524
  51.1 0.9 copy-start.5
  51.2 1.0 copy-start.6
  52.1 116.8 %copy-start.1 = (f32[1,3,20480]{2,0,1:T(1,128)S(1)}, f32[1,3,20480]{2,0,1:T(1,128)}, u32[]{:S(2)}) copy-start(f32[1,3,20480]{2,0,1:T(1,128)} %param.8) | copy-start | bytes 737284
  154.6 3.4 %collective-permute-start.2 = (f32[3,8,128]{2,1,0:T(8,128)}, f32[3,8,128]{2,1,0:T(8,128)S(1)}, u32[]{:S(2)}, u32[]{:S(2)}) collective-permute-start(f32[3,8,128]{2,1,0:T(8,128)} %get-tuple-element.14.refs_0_), channel_id=1, source_target_pairs={{0,8},{8,16},{16,24},{24,0},{1,9},{9,17},{17,25},{25,1},{2,10},{10... | collective-permute-start | bytes 36872 | tf_op jit(solution)/shard_map/ppermute | solution.py:372
  154.7 4.0 %collective-permute-start.3 = (f32[3,8,128]{2,1,0:T(8,128)}, f32[3,8,128]{2,1,0:T(8,128)S(1)}, u32[]{:S(2)}, u32[]{:S(2)}) collective-permute-start(f32[3,8,128]{2,1,0:T(8,128)} %get-tuple-element.14.refs_0_), channel_id=1, source_target_pairs={{0,16},{8,24},{16,0},{24,8},{1,17},{9,25},{17,1},{25,9},{2,18},{10... | collective-permute-start | bytes 36872 | tf_op jit(solution)/shard_map/ppermute | solution.py:372
  155.4 3.2 %collective-permute-start.4 = (f32[3,8,128]{2,1,0:T(8,128)}, f32[3,8,128]{2,1,0:T(8,128)S(1)}, u32[]{:S(2)}, u32[]{:S(2)}) collective-permute-start(f32[3,8,128]{2,1,0:T(8,128)} %get-tuple-element.14.refs_0_), channel_id=1, source_target_pairs={{0,24},{8,0},{16,8},{24,16},{1,25},{9,1},{17,9},{25,17},{2,26},{10... | collective-permute-start | bytes 36872 | tf_op jit(solution)/shard_map/ppermute | solution.py:372
  158.6 0.7 copy-start.2
  159.4 3.8 %collective-permute-start.8 = (f32[32,128]{1,0:T(8,128)S(1)}, f32[32,128]{1,0:T(8,128)S(1)}, u32[]{:S(2)}, u32[]{:S(2)}) collective-permute-start(f32[32,128]{1,0:T(8,128)S(1)} %get-tuple-element.15), channel_id=1, source_target_pairs={{0,1},{1,0},{2,3},{3,2},{4,5},{5,4},{6,7},{7,6},{8,9},{9,8},{10,11... | collective-permute-start | bytes 49160 | tf_op jit(solution)/shard_map/ppermute | solution.py:381
  163.2 3.7 %collective-permute-start.9 = (f32[32,128]{1,0:T(8,128)S(1)}, f32[32,128]{1,0:T(8,128)S(1)}, u32[]{:S(2)}, u32[]{:S(2)}) collective-permute-start(f32[32,128]{1,0:T(8,128)S(1)} %add.29), channel_id=1, source_target_pairs={{0,2},{1,3},{2,0},{3,1},{4,6},{5,7},{6,4},{7,5},{8,10},{9,11},{10,... | collective-permute-start | bytes 49160 | tf_op jit(solution)/shard_map/ppermute | solution.py:381
  167.0 14.3 %collective-permute-start.10 = (f32[32,128]{1,0:T(8,128)S(1)}, f32[32,128]{1,0:T(8,128)S(1)}, u32[]{:S(2)}, u32[]{:S(2)}) collective-permute-start(f32[32,128]{1,0:T(8,128)S(1)} %add.30), channel_id=1, source_target_pairs={{0,4},{1,5},{2,6},{3,7},{4,0},{5,1},{6,2},{7,3},{8,12},{9,13},{10,... | collective-permute-start | bytes 49160 | tf_op jit(solution)/shard_map/ppermute | solution.py:381
  168.9 4.3 %copy-start = (f32[22528,128]{1,0:T(8,128)S(1)}, f32[22528,128]{1,0:T(8,128)}, u32[]{:S(2)}) copy-start(f32[22528,128]{1,0:T(8,128)} %get-tuple-element.18.force_ref) | copy-start | bytes 34603012

commit v7 on v6

--- a/solution.py
+++ b/solution.py
@@ -86,22 +86,17 @@
     return lax.dot_general(left, right, (((1,), (1,)), ((), ())), preferred_element_type=F32)
 
 
-def fill_blocks(fields, eye, planes, table, first):
+def fill_blocks(fields, planes, table, first):
     fields = [field - CENTRE for field in fields[:3]] + fields[3:]
     fields[3] = fields[3] * LJ_COEF**0.5
     fields[4] = fields[4] * CHARGE_COEF**0.5
     for k, row in enumerate(features(fields)):
         planes[pl.ds(k, 8, stride=STRIDE), :] = row
-    blank = jnp.zeros((LANES - STRIDE, LANES), BF16)
-    for block in range(0, 8, 2):
-        parts = []
-        for side in range(2):
-            start = (block + side) * STRIDE
-            parts += [planes[start : start + STRIDE, :].astype(BF16), blank]
-        both = nt_dot(eye, jnp.concatenate(parts, axis=0))
-        for side in range(2):
-            start = pl.multiple_of(first + (block + side) * LANES + PAD, PAD)
-            table[pl.ds(start, LANES), :] = both[:, side * LANES : (side + 1) * LANES]
+    blank = jnp.zeros((LANES - STRIDE, LANES), F32)
+    for block in range(8):
+        part = jnp.concatenate([planes[block * STRIDE : (block + 1) * STRIDE, :], blank], axis=0)
+        start = pl.multiple_of(first + block * LANES + PAD, PAD)
+        table[pl.ds(start, LANES), :] = part.T
 
 
 def sublane_masks():
@@ -121,7 +116,7 @@
     stage[start : start + 16, :] = jnp.concatenate(parts, axis=0).astype(BF16)
 
 
-def near_kernel(rows, order_ref, fields_ref, select_ref, eye_ref, table_ref, left_ref, table, planes, stage):
+def near_kernel(rows, order_ref, fields_ref, select_ref, table_ref, left_ref, table, planes, stage):
     turn = pl.program_id(0)
 
     @pl.when(turn == 0)
@@ -133,7 +128,7 @@
                 group = turn * 2 + side
                 spot = pl.ds(pl.multiple_of(group * 8, 8), 8)
                 fields = [fields_ref[field, spot, :] for field in range(FIELDS)]
-                fill_blocks(fields, eye_ref[...], planes.at[side], table, group * 8 * LANES)
+                fill_blocks(fields, planes.at[side], table, group * 8 * LANES)
             return carry
 
         lax.fori_loop(0, rows // 16, fill, 0)
@@ -189,7 +184,7 @@
 
 
 def force_kernel(
-    rows, partner_ref, entry_ref, order_ref, lower_ref, upper_ref, place_ref, eye_ref, left_ref, own_ref,
+    rows, partner_ref, entry_ref, order_ref, lower_ref, upper_ref, place_ref, left_ref, own_ref,
     force_ref, solute_ref, table, forces, planes, far_a, far_b, sum_a, sum_b, arrival,
 ):
     turn = pl.program_id(0)
@@ -228,7 +223,7 @@
                     ref[pl.ds(pl.multiple_of(field * rows + group * 8, 8), 8), :] for field in range(FIELDS)
                 ]
                 fields[0] = fields[0] + shift
-                fill_blocks(fields, eye_ref[...], planes.at[side], table, first + group * 8 * LANES)
+                fill_blocks(fields, planes.at[side], table, first + group * 8 * LANES)
             return carry
 
         lax.fori_loop(0, rows // 8, fill, 0)
@@ -412,7 +407,6 @@
         ]
     )
     order = cell_order.reshape(atoms)
-    eye = jnp.eye(LANES, dtype=BF16)
     scalar = pl.BlockSpec(memory_space=pltpu.SMEM)
     vector = pl.BlockSpec(memory_space=pltpu.VMEM)
     params = pltpu.CompilerParams(vmem_limit_bytes=VMEM_LIMIT)
@@ -420,7 +414,7 @@
         functools.partial(near_kernel, rows),
         grid=(rows // 8,),
         out_shape=[whole(atoms, LANES), whole(rows, 3 * TILE, LANES, dtype=BF16)],
-        in_specs=[scalar] + [vector] * 3,
+        in_specs=[scalar] + [vector] * 2,
         out_specs=[
             pl.BlockSpec((8 * LANES, LANES), lambda i: (i, 0)),
             pl.BlockSpec((8, 3 * TILE, LANES), lambda i: (i, 0, 0)),
@@ -432,13 +426,13 @@
         ],
         compiler_params=params,
         cost_estimate=pl.CostEstimate(flops=25 * 10**9, bytes_accessed=3 * 10**7, transcendentals=0),
-    )(order, fields, near_selector(), eye)
+    )(order, fields, near_selector())
     forces, solute = pl.pallas_call(
         functools.partial(force_kernel, rows),
         grid=(rows // 8,),
         out_shape=[whole(atoms + 2 * FORCE_PAD, LANES), whole(3, SOL_DEV // LANES, LANES)],
         in_specs=[scalar] * 3
-        + [vector] * 4
+        + [vector] * 3
         + [pl.BlockSpec((8, 3 * TILE, LANES), lambda i: (i, 0, 0)), pl.BlockSpec(memory_space=pl.ANY)],
         out_specs=[pl.BlockSpec(memory_space=pl.ANY), vector],
         scratch_shapes=[
@@ -453,7 +447,7 @@
         ],
         compiler_params=params,
         cost_estimate=pl.CostEstimate(flops=25 * 10**9, bytes_accessed=3 * 10**7, transcendentals=0),
-    )(tile_atoms.reshape(rows * partners), entries, order, lower, upper, places, eye, left, table)
+    )(tile_atoms.reshape(rows * partners), entries, order, lower, upper, places, left, table)
     solutes = round_trip(solute, "image")
     block = pl.BlockSpec((3, 8, LANES), lambda i: (0, i, 0))
     small = pltpu.CompilerParams(vmem_limit_bytes=8 * 1024 * 1024)

time: 182 us -> 180 us (0.989)
  Pallas kernels: 148 us -> 146 us
where the time goes in v7:
time: 180 us
  Pallas kernels  146 us (81%)
  starting transfers between devices  12.9 us (7%)
  waiting for transfers between devices  9.46 us (5%)
  local copies, waits for them, and re-layouts  6.6 us (4%)
  other arithmetic  3.76 us (2%)
    pallas_call x1, Pallas kernels, per_device(): pl.pallas_call(functools.partial(force_kernel, rows), grid=(rows // 8,),...  102 us
    pallas_call x1, Pallas kernels, per_device(): pl.pallas_call(functools.partial(near_kernel, rows), grid=(rows // 8,), o...  35.9 us
    ppermute x8, starting transfers between devices, turned(): lax.ppermute(array, axis, [(i, (i + by) % count) for i in range(count)])  11 us
    pallas_call x1, Pallas kernels, per_device(): pl.pallas_call(relax_kernel, grid=(rows // 8,), out_shape=whole(3, rows,...  8 us
    ppermute x3, waiting for transfers between devices, summed(): lax.ppermute(array, axis, [(i, i ^ by) for i in range(count)])  7.46 us
    unnamed x15, local copies, waits for them, and re-layouts  5.88 us
  transfers between devices with their start and end apart: 11, of which 4 were waited for; matrix products, arithmetic and copies ran while one was open for 3% of the time, Pallas kernels for 81%

profile of v7, /device:TPU:0, one launch (start us, length us, event | category | flops | bytes accessed | tf_op | source)
XLA Modules:
  0.0 179.9 jit_solution(7848769334209001370)
XLA Ops:
  0.0 0.7 slice.26.refs_4_
  0.7 0.5 collective-permute-start.5
  1.2 2.5 %collective-permute-start.6 = (f32[3,8,128]{2,1,0:T(8,128)S(1)}, f32[3,8,128]{2,1,0:T(8,128)S(1)}, u32[]{:S(2)}, u32[]{:S(2)}) collective-permute-start(f32[3,8,128]{2,1,0:T(8,128)S(1)} %slice.26.refs_4_), channel_id=1, source_target_pairs={{0,16},{8,24},{16,0},{24,8},{1,17},{9,25},{17,1},{25,9},{2,18},{10... | collective-permute-start | bytes 36872 | tf_op jit(solution)/shard_map/ppermute | solution.py:367
  3.7 1.4 collective-permute-start.7
  5.8 0.9 convert_element_type.10
  6.8 0.9 fusion
  7.7 1.0 pad_maximum_fusion.2.fields_ref
  8.7 0.0 copy-start.3
  8.7 0.1 pad_maximum_fusion
  8.8 4.6 %collective-permute-start.1 = (f32[880,128]{1,0:T(8,128)S(1)}, f32[880,128]{1,0:T(8,128)S(1)}, u32[]{:S(2)}, u32[]{:S(2)}) collective-permute-start(f32[880,128]{1,0:T(8,128)S(1)} %get-tuple-element.20), channel_id=1, source_target_pairs={{0,7},{1,0},{2,1},{3,2},{4,3},{5,4},{6,5},{7,6},{8,15},{9,8},{10,9... | collective-permute-start | bytes 1351688 | tf_op jit(solution)/shard_map/ppermute | solution.py:367
  13.4 0.0 collective-permute-start
  13.4 0.0 copy-done.3
  13.4 0.0 copy-start.4
  13.4 35.9 %shard_map.82 = (f32[20480,128]{1,0:T(8,128)}, bf16[160,384,128]{2,1,0:T(8,128)(2,1)}) custom-call(s32[20480]{0:T(1024)} %bitcast.27, f32[5,160,128]{2,1,0:T(8,128)} %copy-done.3, bf16[128,384]{1,0:T(8,128)(2,1)} %constant.15.clone.select_ref), custom_call_target="tpu_custom_call" | custom-call | flops 24999999488 | bytes 30000000 | tf_op jit(solution)/shard_map/pallas_call | solution.py:413
  49.3 0.0 copy-done.4
  49.3 0.8 copy.12
  50.1 0.0 collective-permute-done.1.upper_ref
  50.1 0.0 copy-start.5
  50.1 0.0 collective-permute-done.lower_ref
  50.1 0.0 copy-start.6
  50.1 0.8 pad_add_fusion.entry_ref
  50.9 0.0 copy-done.5
  50.9 0.1 copy-done.6
  51.1 0.0 copy-start.1
  51.1 101.6 %shard_map.83 = (f32[22528,128]{1,0:T(8,128)}, f32[3,8,128]{2,1,0:T(8,128)}) custom-call(s32[40960]{0:T(1024)} %bitcast.26, s32[40960]{0:T(1024)} %pad_add_fusion.entry_ref, s32[20480]{0:T(1024)} %bitcast.28, f32[880,128]{1,0:T(8,128)} %copy-done.6, f32[880,128]{1,0:T(8,128)} %copy-done.5, f32[3,160,128]{2,1,0:T(8,128)} %bitcast.20, ...), custom_call_target="tpu_custom_call" | custom-call | flops 24999999488 | bytes 30000000 | tf_op jit(solution)/shard_map/pallas_call | solution.py:430
  152.7 0.1 collective-permute-start.2
  152.8 0.6 collective-permute-start.3
  153.3 0.0 collective-permute-done.5.refs_5_
  153.3 1.4 collective-permute-start.4
  154.7 0.0 collective-permute-done.6.refs_6_
  154.7 0.0 collective-permute-done.7.refs_7_
  154.7 1.3 collective-permute-done.2.refs_1_
  156.1 0.7 collective-permute-done.3.refs_2_
  156.7 0.0 collective-permute-done.4.refs_3_
  156.7 0.0 copy-start.2
  156.7 0.7 copy-done.2
  157.4 0.1 shard_map.84
  157.5 0.1 collective-permute-start.8
  157.6 3.7 %collective-permute-done.8 = f32[32,128]{1,0:T(8,128)S(1)} collective-permute-done((f32[32,128]{1,0:T(8,128)S(1)}, f32[32,128]{1,0:T(8,128)S(1)}, u32[]{:S(2)}, u32[]{:S(2)}) %collective-permute-start.8) | collective-permute-done | bytes 16416 | tf_op jit(solution)/shard_map/ppermute | solution.py:376
  161.3 0.0 collective-permute-start.9
  161.3 3.7 %collective-permute-done.9 = f32[32,128]{1,0:T(8,128)S(1)} collective-permute-done((f32[32,128]{1,0:T(8,128)S(1)}, f32[32,128]{1,0:T(8,128)S(1)}, u32[]{:S(2)}, u32[]{:S(2)}) %collective-permute-start.9) | collective-permute-done | bytes 16416 | tf_op jit(solution)/shard_map/ppermute | solution.py:376
  165.1 1.8 %collective-permute-start.10 = (f32[32,128]{1,0:T(8,128)S(1)}, f32[32,128]{1,0:T(8,128)S(1)}, u32[]{:S(2)}, u32[]{:S(2)}) collective-permute-start(f32[32,128]{1,0:T(8,128)S(1)} %add.30), channel_id=1, source_target_pairs={{0,4},{1,5},{2,6},{3,7},{4,0},{5,1},{6,2},{7,3},{8,12},{9,13},{10,... | collective-permute-start | bytes 49160 | tf_op jit(solution)/shard_map/ppermute | solution.py:376
  166.9 0.0 copy-done.1
  166.9 0.0 copy-start
  166.9 4.3 %copy-done = f32[22528,128]{1,0:T(8,128)S(1)} copy-done((f32[22528,128]{1,0:T(8,128)S(1)}, f32[22528,128]{1,0:T(8,128)}, u32[]{:S(2)}) %copy-start) | copy-done | bytes 11534360
  171.1 8.0 %shard_map.85.out_in = f32[3,160,128]{2,1,0:T(8,128)} custom-call(f32[3,160,128]{2,1,0:T(8,128)S(1)} %bitcast.21, f32[22528,128]{1,0:T(8,128)S(1)} %copy-done), custom_call_target="tpu_custom_call" | custom-call | flops 1000000000 | bytes 20000000 | tf_op jit(solution)/shard_map/pallas_call | solution.py:454
  179.1 0.0 collective-permute-done.10
  179.2 0.8 shard_map.86
  (7 shorter events, 0.0 us)
Async XLA Ops:
  0.7 152.6 %collective-permute-start.5 = (f32[3,8,128]{2,1,0:T(8,128)S(1)}, f32[3,8,128]{2,1,0:T(8,128)S(1)}, u32[]{:S(2)}, u32[]{:S(2)}) collective-permute-start(f32[3,8,128]{2,1,0:T(8,128)S(1)} %slice.26.refs_4_), channel_id=1, source_target_pairs={{0,8},{8,16},{16,24},{24,0},{1,9},{9,17},{17,25},{25,1},{2,10},{10... | collective-permute-start | bytes 36872 | tf_op jit(solution)/shard_map/ppermute | solution.py:367
  1.2 153.6 %collective-permute-start.6 = (f32[3,8,128]{2,1,0:T(8,128)S(1)}, f32[3,8,128]{2,1,0:T(8,128)S(1)}, u32[]{:S(2)}, u32[]{:S(2)}) collective-permute-start(f32[3,8,128]{2,1,0:T(8,128)S(1)} %slice.26.refs_4_), channel_id=1, source_target_pairs={{0,16},{8,24},{16,0},{24,8},{1,17},{9,25},{17,1},{25,9},{2,18},{10... | collective-permute-start | bytes 36872 | tf_op jit(solution)/shard_map/ppermute | solution.py:367
  3.7 151.0 %collective-permute-start.7 = (f32[3,8,128]{2,1,0:T(8,128)S(1)}, f32[3,8,128]{2,1,0:T(8,128)S(1)}, u32[]{:S(2)}, u32[]{:S(2)}) collective-permute-start(f32[3,8,128]{2,1,0:T(8,128)S(1)} %slice.26.refs_4_), channel_id=1, source_target_pairs={{0,24},{8,0},{16,8},{24,16},{1,25},{9,1},{17,9},{25,17},{2,26},{10... | collective-permute-start | bytes 36872 | tf_op jit(solution)/shard_map/ppermute | solution.py:367
  8.7 4.7 %copy-start.3 = (f32[5,160,128]{2,1,0:T(8,128)}, f32[5,160,128]{2,1,0:T(8,128)S(1)}, u32[]{:S(2)}) copy-start(f32[5,160,128]{2,1,0:T(8,128)S(1)} %pad_maximum_fusion.2.fields_ref) | copy-start | bytes 1228804
  8.8 41.3 %collective-permute-start.1 = (f32[880,128]{1,0:T(8,128)S(1)}, f32[880,128]{1,0:T(8,128)S(1)}, u32[]{:S(2)}, u32[]{:S(2)}) collective-permute-start(f32[880,128]{1,0:T(8,128)S(1)} %get-tuple-element.20), channel_id=1, source_target_pairs={{0,7},{1,0},{2,1},{3,2},{4,3},{5,4},{6,5},{7,6},{8,15},{9,8},{10,9... | collective-permute-start | bytes 1351688 | tf_op jit(solution)/shard_map/ppermute | solution.py:367
  13.4 36.7 %collective-permute-start = (f32[880,128]{1,0:T(8,128)S(1)}, f32[880,128]{1,0:T(8,128)S(1)}, u32[]{:S(2)}, u32[]{:S(2)}) collective-permute-start(f32[880,128]{1,0:T(8,128)S(1)} %get-tuple-element.19), channel_id=1, source_target_pairs={{0,1},{1,2},{2,3},{3,4},{4,5},{5,6},{6,7},{7,0},{8,9},{9,10},{10,1... | collective-permute-start | bytes 1351688 | tf_op jit(solution)/shard_map/ppermute | solution.py:367
  13.4 35.9 %copy-start.4 = (s32[1,160,256]{2,1,0:T(8,128)S(1)}, s32[1,160,256]{2,1,0:T(8,128)}, u32[]{:S(2)}) copy-start(s32[1,160,256]{2,1,0:T(8,128)} %param.14) | copy-start | bytes 491524
  50.1 0.9 copy-start.5
  50.1 1.0 copy-start.6
  51.1 115.8 %copy-start.1 = (f32[1,3,20480]{2,0,1:T(1,128)S(1)}, f32[1,3,20480]{2,0,1:T(1,128)}, u32[]{:S(2)}) copy-start(f32[1,3,20480]{2,0,1:T(1,128)} %param.8) | copy-start | bytes 737284
  152.7 3.4 %collective-permute-start.2 = (f32[3,8,128]{2,1,0:T(8,128)}, f32[3,8,128]{2,1,0:T(8,128)S(1)}, u32[]{:S(2)}, u32[]{:S(2)}) collective-permute-start(f32[3,8,128]{2,1,0:T(8,128)} %get-tuple-element.14.refs_0_), channel_id=1, source_target_pairs={{0,8},{8,16},{16,24},{24,0},{1,9},{9,17},{17,25},{25,1},{2,10},{10... | collective-permute-start | bytes 36872 | tf_op jit(solution)/shard_map/ppermute | solution.py:367
  152.8 4.0 %collective-permute-start.3 = (f32[3,8,128]{2,1,0:T(8,128)}, f32[3,8,128]{2,1,0:T(8,128)S(1)}, u32[]{:S(2)}, u32[]{:S(2)}) collective-permute-start(f32[3,8,128]{2,1,0:T(8,128)} %get-tuple-element.14.refs_0_), channel_id=1, source_target_pairs={{0,16},{8,24},{16,0},{24,8},{1,17},{9,25},{17,1},{25,9},{2,18},{10... | collective-permute-start | bytes 36872 | tf_op jit(solution)/shard_map/ppermute | solution.py:367
  153.3 3.4 %collective-permute-start.4 = (f32[3,8,128]{2,1,0:T(8,128)}, f32[3,8,128]{2,1,0:T(8,128)S(1)}, u32[]{:S(2)}, u32[]{:S(2)}) collective-permute-start(f32[3,8,128]{2,1,0:T(8,128)} %get-tuple-element.14.refs_0_), channel_id=1, source_target_pairs={{0,24},{8,0},{16,8},{24,16},{1,25},{9,1},{17,9},{25,17},{2,26},{10... | collective-permute-start | bytes 36872 | tf_op jit(solution)/shard_map/ppermute | solution.py:367
  156.7 0.7 copy-start.2
  157.5 3.8 %collective-permute-start.8 = (f32[32,128]{1,0:T(8,128)S(1)}, f32[32,128]{1,0:T(8,128)S(1)}, u32[]{:S(2)}, u32[]{:S(2)}) collective-permute-start(f32[32,128]{1,0:T(8,128)S(1)} %get-tuple-element.15), channel_id=1, source_target_pairs={{0,1},{1,0},{2,3},{3,2},{4,5},{5,4},{6,7},{7,6},{8,9},{9,8},{10,11... | collective-permute-start | bytes 49160 | tf_op jit(solution)/shard_map/ppermute | solution.py:376
  161.3 3.7 %collective-permute-start.9 = (f32[32,128]{1,0:T(8,128)S(1)}, f32[32,128]{1,0:T(8,128)S(1)}, u32[]{:S(2)}, u32[]{:S(2)}) collective-permute-start(f32[32,128]{1,0:T(8,128)S(1)} %add.29), channel_id=1, source_target_pairs={{0,2},{1,3},{2,0},{3,1},{4,6},{5,7},{6,4},{7,5},{8,10},{9,11},{10,... | collective-permute-start | bytes 49160 | tf_op jit(solution)/shard_map/ppermute | solution.py:376
  165.1 14.1 %collective-permute-start.10 = (f32[32,128]{1,0:T(8,128)S(1)}, f32[32,128]{1,0:T(8,128)S(1)}, u32[]{:S(2)}, u32[]{:S(2)}) collective-permute-start(f32[32,128]{1,0:T(8,128)S(1)} %add.30), channel_id=1, source_target_pairs={{0,4},{1,5},{2,6},{3,7},{4,0},{5,1},{6,2},{7,3},{8,12},{9,13},{10,... | collective-permute-start | bytes 49160 | tf_op jit(solution)/shard_map/ppermute | solution.py:376
  166.9 4.3 %copy-start = (f32[22528,128]{1,0:T(8,128)S(1)}, f32[22528,128]{1,0:T(8,128)}, u32[]{:S(2)}) copy-start(f32[22528,128]{1,0:T(8,128)} %get-tuple-element.18.force_ref) | copy-start | bytes 34603012

commit v8 on v7

--- a/solution.py
+++ b/solution.py
@@ -13,8 +13,6 @@
 LANES = 128
 FIELDS = 5
 STRIDE = 48
-FORCE_PAD = 1024
-PAD = 8
 
 LJ_COEF = 0.5
 CHARGE_COEF = 0.1
@@ -95,25 +93,12 @@
     blank = jnp.zeros((LANES - STRIDE, LANES), F32)
     for block in range(8):
         part = jnp.concatenate([planes[block * STRIDE : (block + 1) * STRIDE, :], blank], axis=0)
-        start = pl.multiple_of(first + block * LANES + PAD, PAD)
-        table[pl.ds(start, LANES), :] = part.T
-
-
-def sublane_masks():
-    sublane = lax.broadcasted_iota(I32, (8, LANES), 0)
-    return [sublane == k for k in range(8)]
-
-
-def merged(table, entries, masks):
-    result = table[pl.ds(entries[0] + PAD, 8), :]
-    for k in range(1, 8):
-        result = jnp.where(masks[k], table[pl.ds(entries[k] + (PAD - k), 8), :], result)
-    return result
-
-
-def copy_rows(table, entry_of, stage, start, masks):
-    parts = [merged(table, [entry_of(start + half + k) for k in range(8)], masks) for half in (0, 8)]
-    stage[start : start + 16, :] = jnp.concatenate(parts, axis=0).astype(BF16)
+        start = pl.multiple_of(first + block * LANES, LANES)
+        flat(table)[pl.ds(start, LANES), :] = part.T
+
+
+def flat(ref):
+    return ref.reshape(ref.shape[0], LANES)
 
 
 def near_kernel(rows, order_ref, fields_ref, select_ref, table_ref, left_ref, table, planes, stage):
@@ -133,15 +118,13 @@
 
         lax.fori_loop(0, rows // 16, fill, 0)
 
-    masks = sublane_masks()
-
     def tile_step(local, carry):
         for side in range(2):
             tile = turn * 8 + local * 2 + side
-            for start in range(0, TILE, 16):
-                copy_rows(table, lambda k: order_ref[tile * TILE + k], stage.at[side], start, masks)
+            for k in range(TILE):
+                stage[side, k : k + 1, :] = table[order_ref[tile * TILE + k]]
         for side in range(2):
-            left = jnp.dot(stage[side], select_ref[...], preferred_element_type=F32).astype(BF16)
+            left = jnp.dot(stage[side].astype(BF16), select_ref[...], preferred_element_type=F32).astype(BF16)
             for block in range(3):
                 left_ref[local * 2 + side, block * TILE : (block + 1) * TILE, :] = left[
                     :, block * LANES : (block + 1) * LANES
@@ -149,11 +132,11 @@
         return carry
 
     lax.fori_loop(0, 4, tile_step, 0)
-    table_ref[...] = table[pl.ds(pl.multiple_of(turn * 8 * LANES + PAD, PAD), 8 * LANES), :]
+    table_ref[...] = flat(table)[pl.ds(pl.multiple_of(turn * 8 * LANES, 8 * LANES), 8 * LANES), :]
 
 
 def tile_sums(left_ref, place, far, sums):
-    others = far[...]
+    others = far[...].astype(BF16)
     yield
     grams = nt_dot(left_ref[place], others)
     yield
@@ -191,29 +174,21 @@
     partners = far_a.shape[0]
     own = rows * LANES
 
-    masks = sublane_masks()
-
     def load(tile, far):
-        def entry_of(k):
-            return entry_ref[partner_ref[tile * partners + k]]
-
-        return [
-            functools.partial(copy_rows, table, entry_of, far, start, masks)
-            for start in range(0, partners, 16)
-        ]
+        def copy(k):
+            far[k : k + 1, :] = table[entry_ref[partner_ref[tile * partners + k]]]
+
+        return [functools.partial(copy, k) for k in range(partners)]
 
     def save(tile, sums):
-        def copy(block):
-            value = sums[block * 8 : block * 8 + 8, :]
-            for k in range(8):
-                place = order_ref[tile * TILE + block * 8 + k] + (FORCE_PAD - k)
-                pltpu.store(forces.at[pl.ds(place, 8), :], value, mask=masks[k])
-
-        return [functools.partial(copy, block) for block in range(TILE // 8)]
+        def copy(k):
+            forces[order_ref[tile * TILE + k]] = sums[k : k + 1, :]
+
+        return [functools.partial(copy, k) for k in range(TILE)]
 
     @pl.when(turn == 0)
     def _():
-        own_copy = pltpu.make_async_copy(own_ref, table.at[pl.ds(own + PAD, own), :], arrival)
+        own_copy = pltpu.make_async_copy(own_ref, flat(table).at[pl.ds(own, own), :], arrival)
         own_copy.start()
         planes[...] = jnp.zeros_like(planes)
 
@@ -247,11 +222,11 @@
         for copy in save(rows - 1, sum_b):
             copy()
 
-        send = pltpu.make_async_copy(forces, force_ref, arrival)
+        send = pltpu.make_async_copy(flat(forces), force_ref, arrival)
         send.start()
         for row in range(SOL_DEV // LANES):
-            start = FORCE_PAD + row * LANES
-            force = row_forces(forces[start : start + LANES, :], [place_ref[axis, row : row + 1, :] for axis in range(3)])
+            sums = flat(forces)[row * LANES : (row + 1) * LANES, :]
+            force = row_forces(sums, [place_ref[axis, row : row + 1, :] for axis in range(3)])
             for axis in range(3):
                 solute_ref[axis, row : row + 1, :] = place_ref[axis, row : row + 1, :] + STEP_SIZE * force[axis]
         send.wait()
@@ -420,9 +395,9 @@
             pl.BlockSpec((8, 3 * TILE, LANES), lambda i: (i, 0, 0)),
         ],
         scratch_shapes=[
-            pltpu.VMEM((atoms + 2 * PAD, LANES), F32),
+            pltpu.VMEM((atoms, 1, LANES), F32),
             pltpu.VMEM((2, 8 * STRIDE, LANES), F32),
-            pltpu.VMEM((2, TILE, LANES), BF16),
+            pltpu.VMEM((2, TILE, LANES), F32),
         ],
         compiler_params=params,
         cost_estimate=pl.CostEstimate(flops=25 * 10**9, bytes_accessed=3 * 10**7, transcendentals=0),
@@ -430,17 +405,17 @@
     forces, solute = pl.pallas_call(
         functools.partial(force_kernel, rows),
         grid=(rows // 8,),
-        out_shape=[whole(atoms + 2 * FORCE_PAD, LANES), whole(3, SOL_DEV // LANES, LANES)],
+        out_shape=[whole(atoms, LANES), whole(3, SOL_DEV // LANES, LANES)],
         in_specs=[scalar] * 3
         + [vector] * 3
         + [pl.BlockSpec((8, 3 * TILE, LANES), lambda i: (i, 0, 0)), pl.BlockSpec(memory_space=pl.ANY)],
         out_specs=[pl.BlockSpec(memory_space=pl.ANY), vector],
         scratch_shapes=[
-            pltpu.VMEM((3 * atoms + 2 * PAD, LANES), F32),
-            pltpu.VMEM((atoms + 2 * FORCE_PAD, LANES), F32),
+            pltpu.VMEM((3 * atoms, 1, LANES), F32),
+            pltpu.VMEM((atoms, 1, LANES), F32),
             pltpu.VMEM((2, 8 * STRIDE, LANES), F32),
-            pltpu.VMEM((partners, LANES), BF16),
-            pltpu.VMEM((partners, LANES), BF16),
+            pltpu.VMEM((partners, LANES), F32),
+            pltpu.VMEM((partners, LANES), F32),
             pltpu.VMEM((TILE, LANES), F32),
             pltpu.VMEM((TILE, LANES), F32),
             pltpu.SemaphoreType.DMA,
@@ -455,7 +430,7 @@
         relax_kernel,
         grid=(rows // 8,),
         out_shape=whole(3, rows, LANES),
-        in_specs=[block, pl.BlockSpec((8 * LANES, LANES), lambda i: (i + FORCE_PAD // (8 * LANES), 0))],
+        in_specs=[block, pl.BlockSpec((8 * LANES, LANES), lambda i: (i, 0))],
         out_specs=block,
         compiler_params=small,
         cost_estimate=pl.CostEstimate(flops=10**9, bytes_accessed=2 * 10**7, transcendentals=0),

time: 180 us -> 182 us (1.011)
  Pallas kernels: 146 us -> 149 us
    pallas_call x1, Pallas kernels: 35.9 us -> 38.2 us  [per_device(): pl.pallas_call(functools.partial(near_kernel, rows), grid=(rows // 8,), o...]
  transfers between devices with their start and end apart: 11 -> 11, of which waited for: 4 -> 4; matrix products, arithmetic and copies ran while one was open for 3% -> 2% of each run, Pallas kernels for 81% -> 81%
where the time goes in v8:
time: 182 us
  Pallas kernels  149 us (82%)
  starting transfers between devices  12.9 us (7%)
  waiting for transfers between devices  9.5 us (5%)
  local copies, waits for them, and re-layouts  6.36 us (3%)
  other arithmetic  3.73 us (2%)
    pallas_call x1, Pallas kernels, per_device(): pl.pallas_call(functools.partial(force_kernel, rows), grid=(rows // 8,),...  102 us
    pallas_call x1, Pallas kernels, per_device(): pl.pallas_call(functools.partial(near_kernel, rows), grid=(rows // 8,), o...  38.2 us
    ppermute x8, starting transfers between devices, turned(): lax.ppermute(array, axis, [(i, (i + by) % count) for i in range(count)])  11 us
    pallas_call x1, Pallas kernels, per_device(): pl.pallas_call(relax_kernel, grid=(rows // 8,), out_shape=whole(3, rows,...  8 us
    ppermute x3, waiting for transfers between devices, summed(): lax.ppermute(array, axis, [(i, i ^ by) for i in range(count)])  7.46 us
    unnamed x15, local copies, waits for them, and re-layouts  5.64 us
  transfers between devices with their start and end apart: 11, of which 4 were waited for; matrix products, arithmetic and copies ran while one was open for 2% of the time, Pallas kernels for 81%

profile of v8, /device:TPU:0, one launch (start us, length us, event | category | flops | bytes accessed | tf_op | source)
XLA Modules:
  0.0 181.8 jit_solution(862192107600473900)
XLA Ops:
  0.0 0.7 slice.26.refs_4_
  0.7 0.5 collective-permute-start.5
  1.2 2.5 %collective-permute-start.6 = (f32[3,8,128]{2,1,0:T(8,128)S(1)}, f32[3,8,128]{2,1,0:T(8,128)S(1)}, u32[]{:S(2)}, u32[]{:S(2)}) collective-permute-start(f32[3,8,128]{2,1,0:T(8,128)S(1)} %slice.26.refs_4_), channel_id=1, source_target_pairs={{0,16},{8,24},{16,0},{24,8},{1,17},{9,25},{17,1},{25,9},{2,18},{10... | collective-permute-start | bytes 36872 | tf_op jit(solution)/shard_map/ppermute | solution.py:342
  3.7 1.4 collective-permute-start.7
  5.8 0.9 convert_element_type.10
  6.8 0.9 fusion
  7.7 1.0 pad_maximum_fusion.2.fields_ref
  8.7 0.0 copy-start.3
  8.7 0.1 pad_maximum_fusion
  8.8 4.6 %collective-permute-start.1 = (f32[880,128]{1,0:T(8,128)S(1)}, f32[880,128]{1,0:T(8,128)S(1)}, u32[]{:S(2)}, u32[]{:S(2)}) collective-permute-start(f32[880,128]{1,0:T(8,128)S(1)} %get-tuple-element.20), channel_id=1, source_target_pairs={{0,7},{1,0},{2,1},{3,2},{4,3},{5,4},{6,5},{7,6},{8,15},{9,8},{10,9... | collective-permute-start | bytes 1351688 | tf_op jit(solution)/shard_map/ppermute | solution.py:342
  13.4 0.0 collective-permute-start
  13.4 0.0 copy-done.3
  13.4 0.0 copy-start.4
  13.4 38.2 %shard_map.82 = (f32[20480,128]{1,0:T(8,128)}, bf16[160,384,128]{2,1,0:T(8,128)(2,1)}) custom-call(s32[20480]{0:T(1024)} %bitcast.27, f32[5,160,128]{2,1,0:T(8,128)} %copy-done.3, bf16[128,384]{1,0:T(8,128)(2,1)} %constant.15.clone.select_ref), custom_call_target="tpu_custom_call" | custom-call | flops 24999999488 | bytes 30000000 | tf_op jit(solution)/shard_map/pallas_call | solution.py:388
  51.6 0.0 copy-done.4
  51.6 0.8 copy.12
  52.4 0.0 collective-permute-done.1.upper_ref
  52.4 0.0 copy-start.5
  52.4 0.0 collective-permute-done.lower_ref
  52.4 0.0 copy-start.6
  52.5 0.8 pad_add_fusion.entry_ref
  53.2 0.0 copy-done.5
  53.2 0.2 copy-done.6
  53.4 0.0 copy-start.1
  53.4 101.5 %shard_map.83 = (f32[20480,128]{1,0:T(8,128)}, f32[3,8,128]{2,1,0:T(8,128)}) custom-call(s32[40960]{0:T(1024)} %bitcast.26, s32[40960]{0:T(1024)} %pad_add_fusion.entry_ref, s32[20480]{0:T(1024)} %bitcast.28, f32[880,128]{1,0:T(8,128)} %copy-done.6, f32[880,128]{1,0:T(8,128)} %copy-done.5, f32[3,160,128]{2,1,0:T(8,128)} %bitcast.20, ...), custom_call_target="tpu_custom_call" | custom-call | flops 24999999488 | bytes 30000000 | tf_op jit(solution)/shard_map/pallas_call | solution.py:405
  154.9 0.1 collective-permute-start.2
  155.0 0.5 collective-permute-start.3
  155.6 0.0 collective-permute-done.5.refs_5_
  155.6 1.4 collective-permute-start.4
  156.9 0.0 collective-permute-done.6.refs_6_
  157.0 0.0 collective-permute-done.7.refs_7_
  157.0 1.4 collective-permute-done.2.refs_1_
  158.3 0.7 collective-permute-done.3.refs_2_
  159.0 0.0 collective-permute-done.4.refs_3_
  159.0 0.0 copy-start.2
  159.0 0.7 copy-done.2
  159.7 0.1 shard_map.84
  159.8 0.1 collective-permute-start.8
  159.8 3.7 %collective-permute-done.8 = f32[32,128]{1,0:T(8,128)S(1)} collective-permute-done((f32[32,128]{1,0:T(8,128)S(1)}, f32[32,128]{1,0:T(8,128)S(1)}, u32[]{:S(2)}, u32[]{:S(2)}) %collective-permute-start.8) | collective-permute-done | bytes 16416 | tf_op jit(solution)/shard_map/ppermute | solution.py:351
  163.6 0.0 collective-permute-start.9
  163.6 3.7 %collective-permute-done.9 = f32[32,128]{1,0:T(8,128)S(1)} collective-permute-done((f32[32,128]{1,0:T(8,128)S(1)}, f32[32,128]{1,0:T(8,128)S(1)}, u32[]{:S(2)}, u32[]{:S(2)}) %collective-permute-start.9) | collective-permute-done | bytes 16416 | tf_op jit(solution)/shard_map/ppermute | solution.py:351
  167.3 1.8 collective-permute-start.10
  169.1 0.0 copy-done.1
  169.1 0.0 copy-start
  169.1 4.0 %copy-done = f32[20480,128]{1,0:T(8,128)S(1)} copy-done((f32[20480,128]{1,0:T(8,128)S(1)}, f32[20480,128]{1,0:T(8,128)}, u32[]{:S(2)}) %copy-start) | copy-done | bytes 10485784
  173.1 8.0 %shard_map.85.out_in = f32[3,160,128]{2,1,0:T(8,128)} custom-call(f32[3,160,128]{2,1,0:T(8,128)S(1)} %bitcast.21, f32[20480,128]{1,0:T(8,128)S(1)} %copy-done), custom_call_target="tpu_custom_call" | custom-call | flops 1000000000 | bytes 20000000 | tf_op jit(solution)/shard_map/pallas_call | solution.py:429
  181.1 0.0 collective-permute-done.10
  181.1 0.8 shard_map.86
  (7 shorter events, 0.0 us)
Async XLA Ops:
  0.7 154.9 %collective-permute-start.5 = (f32[3,8,128]{2,1,0:T(8,128)S(1)}, f32[3,8,128]{2,1,0:T(8,128)S(1)}, u32[]{:S(2)}, u32[]{:S(2)}) collective-permute-start(f32[3,8,128]{2,1,0:T(8,128)S(1)} %slice.26.refs_4_), channel_id=1, source_target_pairs={{0,8},{8,16},{16,24},{24,0},{1,9},{9,17},{17,25},{25,1},{2,10},{10... | collective-permute-start | bytes 36872 | tf_op jit(solution)/shard_map/ppermute | solution.py:342
  1.2 155.8 %collective-permute-start.6 = (f32[3,8,128]{2,1,0:T(8,128)S(1)}, f32[3,8,128]{2,1,0:T(8,128)S(1)}, u32[]{:S(2)}, u32[]{:S(2)}) collective-permute-start(f32[3,8,128]{2,1,0:T(8,128)S(1)} %slice.26.refs_4_), channel_id=1, source_target_pairs={{0,16},{8,24},{16,0},{24,8},{1,17},{9,25},{17,1},{25,9},{2,18},{10... | collective-permute-start | bytes 36872 | tf_op jit(solution)/shard_map/ppermute | solution.py:342
  3.7 153.2 %collective-permute-start.7 = (f32[3,8,128]{2,1,0:T(8,128)S(1)}, f32[3,8,128]{2,1,0:T(8,128)S(1)}, u32[]{:S(2)}, u32[]{:S(2)}) collective-permute-start(f32[3,8,128]{2,1,0:T(8,128)S(1)} %slice.26.refs_4_), channel_id=1, source_target_pairs={{0,24},{8,0},{16,8},{24,16},{1,25},{9,1},{17,9},{25,17},{2,26},{10... | collective-permute-start | bytes 36872 | tf_op jit(solution)/shard_map/ppermute | solution.py:342
  8.7 4.7 %copy-start.3 = (f32[5,160,128]{2,1,0:T(8,128)}, f32[5,160,128]{2,1,0:T(8,128)S(1)}, u32[]{:S(2)}) copy-start(f32[5,160,128]{2,1,0:T(8,128)S(1)} %pad_maximum_fusion.2.fields_ref) | copy-start | bytes 1228804
  8.8 43.6 %collective-permute-start.1 = (f32[880,128]{1,0:T(8,128)S(1)}, f32[880,128]{1,0:T(8,128)S(1)}, u32[]{:S(2)}, u32[]{:S(2)}) collective-permute-start(f32[880,128]{1,0:T(8,128)S(1)} %get-tuple-element.20), channel_id=1, source_target_pairs={{0,7},{1,0},{2,1},{3,2},{4,3},{5,4},{6,5},{7,6},{8,15},{9,8},{10,9... | collective-permute-start | bytes 1351688 | tf_op jit(solution)/shard_map/ppermute | solution.py:342
  13.4 39.0 %collective-permute-start = (f32[880,128]{1,0:T(8,128)S(1)}, f32[880,128]{1,0:T(8,128)S(1)}, u32[]{:S(2)}, u32[]{:S(2)}) collective-permute-start(f32[880,128]{1,0:T(8,128)S(1)} %get-tuple-element.19), channel_id=1, source_target_pairs={{0,1},{1,2},{2,3},{3,4},{4,5},{5,6},{6,7},{7,0},{8,9},{9,10},{10,1... | collective-permute-start | bytes 1351688 | tf_op jit(solution)/shard_map/ppermute | solution.py:342
  13.4 38.2 %copy-start.4 = (s32[1,160,256]{2,1,0:T(8,128)S(1)}, s32[1,160,256]{2,1,0:T(8,128)}, u32[]{:S(2)}) copy-start(s32[1,160,256]{2,1,0:T(8,128)} %param.14) | copy-start | bytes 491524
  52.4 0.8 copy-start.5
  52.4 1.0 copy-start.6
  53.4 115.7 %copy-start.1 = (f32[1,3,20480]{2,0,1:T(1,128)S(1)}, f32[1,3,20480]{2,0,1:T(1,128)}, u32[]{:S(2)}) copy-start(f32[1,3,20480]{2,0,1:T(1,128)} %param.8) | copy-start | bytes 737284
  154.9 3.4 %collective-permute-start.2 = (f32[3,8,128]{2,1,0:T(8,128)}, f32[3,8,128]{2,1,0:T(8,128)S(1)}, u32[]{:S(2)}, u32[]{:S(2)}) collective-permute-start(f32[3,8,128]{2,1,0:T(8,128)} %get-tuple-element.14.refs_0_), channel_id=1, source_target_pairs={{0,8},{8,16},{16,24},{24,0},{1,9},{9,17},{17,25},{25,1},{2,10},{10... | collective-permute-start | bytes 36872 | tf_op jit(solution)/shard_map/ppermute | solution.py:342
  155.0 4.0 %collective-permute-start.3 = (f32[3,8,128]{2,1,0:T(8,128)}, f32[3,8,128]{2,1,0:T(8,128)S(1)}, u32[]{:S(2)}, u32[]{:S(2)}) collective-permute-start(f32[3,8,128]{2,1,0:T(8,128)} %get-tuple-element.14.refs_0_), channel_id=1, source_target_pairs={{0,16},{8,24},{16,0},{24,8},{1,17},{9,25},{17,1},{25,9},{2,18},{10... | collective-permute-start | bytes 36872 | tf_op jit(solution)/shard_map/ppermute | solution.py:342
  155.6 3.4 %collective-permute-start.4 = (f32[3,8,128]{2,1,0:T(8,128)}, f32[3,8,128]{2,1,0:T(8,128)S(1)}, u32[]{:S(2)}, u32[]{:S(2)}) collective-permute-start(f32[3,8,128]{2,1,0:T(8,128)} %get-tuple-element.14.refs_0_), channel_id=1, source_target_pairs={{0,24},{8,0},{16,8},{24,16},{1,25},{9,1},{17,9},{25,17},{2,26},{10... | collective-permute-start | bytes 36872 | tf_op jit(solution)/shard_map/ppermute | solution.py:342
  159.0 0.7 copy-start.2
  159.8 3.8 %collective-permute-start.8 = (f32[32,128]{1,0:T(8,128)S(1)}, f32[32,128]{1,0:T(8,128)S(1)}, u32[]{:S(2)}, u32[]{:S(2)}) collective-permute-start(f32[32,128]{1,0:T(8,128)S(1)} %get-tuple-element.15), channel_id=1, source_target_pairs={{0,1},{1,0},{2,3},{3,2},{4,5},{5,4},{6,7},{7,6},{8,9},{9,8},{10,11... | collective-permute-start | bytes 49160 | tf_op jit(solution)/shard_map/ppermute | solution.py:351
  163.6 3.7 %collective-permute-start.9 = (f32[32,128]{1,0:T(8,128)S(1)}, f32[32,128]{1,0:T(8,128)S(1)}, u32[]{:S(2)}, u32[]{:S(2)}) collective-permute-start(f32[32,128]{1,0:T(8,128)S(1)} %add.29), channel_id=1, source_target_pairs={{0,2},{1,3},{2,0},{3,1},{4,6},{5,7},{6,4},{7,5},{8,10},{9,11},{10,... | collective-permute-start | bytes 49160 | tf_op jit(solution)/shard_map/ppermute | solution.py:351
  167.3 13.8 %collective-permute-start.10 = (f32[32,128]{1,0:T(8,128)S(1)}, f32[32,128]{1,0:T(8,128)S(1)}, u32[]{:S(2)}, u32[]{:S(2)}) collective-permute-start(f32[32,128]{1,0:T(8,128)S(1)} %add.30), channel_id=1, source_target_pairs={{0,4},{1,5},{2,6},{3,7},{4,0},{5,1},{6,2},{7,3},{8,12},{9,13},{10,... | collective-permute-start | bytes 49160 | tf_op jit(solution)/shard_map/ppermute | solution.py:351
  169.1 4.0 %copy-start = (f32[20480,128]{1,0:T(8,128)S(1)}, f32[20480,128]{1,0:T(8,128)}, u32[]{:S(2)}) copy-start(f32[20480,128]{1,0:T(8,128)} %get-tuple-element.18.force_ref) | copy-start | bytes 31457284

commit v9 on v7

--- a/solution.py
+++ b/solution.py
@@ -12,7 +12,6 @@
 TILE = 128
 LANES = 128
 FIELDS = 5
-STRIDE = 48
 FORCE_PAD = 1024
 PAD = 8
 
@@ -30,50 +29,23 @@
 I32 = jnp.int32
 VMEM_LIMIT = 58 * 1024 * 1024
 
-ONES = 18
-NORM = 21
-DEPTH = 24
-CHARGE = 28
-LAST = 32
+DEPTH, CHARGE, ONE, NORM, LAST = 3, 4, 5, 6, 7
+FAR_PIECES = (0, 1, 2, 0, 1, 0)
+NEAR_PIECES = (0, 0, 0, 1, 1, 2)
 
 
 def near_selector():
     chosen = np.zeros((LANES, 3 * LANES), np.float32)
-    for axis in range(3):
-        high, middle, low = 6 * axis, 6 * axis + 1, 6 * axis + 3
-        for k, source in enumerate((high, high, middle, high, low, middle)):
-            chosen[source, 6 * axis + k] = 2.0
-    for k in range(3):
-        chosen[NORM + k, ONES + k] = 1.0
-        chosen[ONES, NORM + k] = 1.0
-    chosen[ONES, LAST] = 1.0
-    for block, first in ((1, DEPTH), (2, CHARGE)):
-        for k, source in enumerate((first, first, first + 1, first + 1)):
-            chosen[source, block * LANES + first + k] = 1.0
+    for group, piece in enumerate(NEAR_PIECES):
+        for axis in range(3):
+            chosen[piece * 8 + axis, group * 8 + axis] = 2.0
+        for block, field in ((1, DEPTH), (2, CHARGE)):
+            chosen[piece * 8 + field, block * LANES + group * 8 + field] = 1.0
+    for piece, group in ((0, 0), (1, 3), (2, 5)):
+        chosen[piece * 8 + NORM, group * 8 + ONE] = 1.0
+        chosen[ONE, piece * 8 + NORM] = 1.0
+    chosen[ONE, LAST] = 1.0
     return jnp.asarray(chosen, BF16)
-
-
-def pieces(value, count):
-    result = []
-    for _ in range(count - 1):
-        part = value.astype(BF16).astype(F32)
-        result.append(part)
-        value = value - part
-    return result + [value]
-
-
-def features(fields):
-    rows = []
-    for axis in range(3):
-        high, middle, low = pieces(fields[axis], 3)
-        rows += [high, middle, high, low, high, middle]
-    one = jnp.ones_like(fields[0])
-    rows += [one] * 3
-    rows += pieces(-(fields[0] * fields[0] + fields[1] * fields[1] + fields[2] * fields[2]), 3)
-    for value in fields[3:]:
-        high, low = pieces(value, 2)
-        rows += [high, low, high, low]
-    return rows + [one]
 
 
 def two_pieces(values):
@@ -86,17 +58,22 @@
     return lax.dot_general(left, right, (((1,), (1,)), ((), ())), preferred_element_type=F32)
 
 
-def fill_blocks(fields, planes, table, first):
-    fields = [field - CENTRE for field in fields[:3]] + fields[3:]
-    fields[3] = fields[3] * LJ_COEF**0.5
-    fields[4] = fields[4] * CHARGE_COEF**0.5
-    for k, row in enumerate(features(fields)):
-        planes[pl.ds(k, 8, stride=STRIDE), :] = row
-    blank = jnp.zeros((LANES - STRIDE, LANES), F32)
-    for block in range(8):
-        part = jnp.concatenate([planes[block * STRIDE : (block + 1) * STRIDE, :], blank], axis=0)
+def fill_blocks(block_at, count, shift, table, first):
+    sublane = lax.broadcasted_iota(I32, (8, LANES), 0)
+    move = jnp.where(sublane < 3, jnp.where(sublane == 0, shift - CENTRE, -CENTRE), 0.0)
+    blank = jnp.zeros((LANES - 8 * len(FAR_PIECES), LANES), F32)
+    for block in range(count):
+        values = block_at(block) + move
+        norm = jnp.sum(jnp.where(sublane < 3, values * values, 0.0), axis=0, keepdims=True)
+        rest = jnp.where(sublane == NORM, -norm, values)
+        parts = []
+        for _ in range(2):
+            parts.append(rest.astype(BF16).astype(F32))
+            rest = rest - parts[-1]
+        parts.append(rest)
+        rows = jnp.concatenate([parts[piece] for piece in FAR_PIECES] + [blank], axis=0)
         start = pl.multiple_of(first + block * LANES + PAD, PAD)
-        table[pl.ds(start, LANES), :] = part.T
+        table[pl.ds(start, LANES), :] = rows.T
 
 
 def sublane_masks():
@@ -116,22 +93,16 @@
     stage[start : start + 16, :] = jnp.concatenate(parts, axis=0).astype(BF16)
 
 
-def near_kernel(rows, order_ref, fields_ref, select_ref, table_ref, left_ref, table, planes, stage):
+def near_kernel(rows, order_ref, fields_ref, select_ref, table_ref, left_ref, table, stage):
     turn = pl.program_id(0)
 
     @pl.when(turn == 0)
     def _():
-        planes[...] = jnp.zeros_like(planes)
-
-        def fill(turn, carry):
-            for side in range(2):
-                group = turn * 2 + side
-                spot = pl.ds(pl.multiple_of(group * 8, 8), 8)
-                fields = [fields_ref[field, spot, :] for field in range(FIELDS)]
-                fill_blocks(fields, planes.at[side], table, group * 8 * LANES)
+        def fill(group, carry):
+            fill_blocks(lambda block: fields_ref[group * 8 + block], 8, 0.0, table, group * 8 * LANES)
             return carry
 
-        lax.fori_loop(0, rows // 16, fill, 0)
+        lax.fori_loop(0, rows // 8, fill, 0)
 
     masks = sublane_masks()
 
@@ -185,7 +156,7 @@
 
 def force_kernel(
     rows, partner_ref, entry_ref, order_ref, lower_ref, upper_ref, place_ref, left_ref, own_ref,
-    force_ref, solute_ref, table, forces, planes, far_a, far_b, sum_a, sum_b, arrival,
+    force_ref, solute_ref, table, forces, far_a, far_b, sum_a, sum_b, arrival,
 ):
     turn = pl.program_id(0)
     partners = far_a.shape[0]
@@ -215,18 +186,13 @@
     def _():
         own_copy = pltpu.make_async_copy(own_ref, table.at[pl.ds(own + PAD, own), :], arrival)
         own_copy.start()
-        planes[...] = jnp.zeros_like(planes)
 
         def fill(group, carry):
-            for side, ref, first, shift in ((0, lower_ref, 0, -SLAB_WIDTH), (1, upper_ref, 2 * own, SLAB_WIDTH)):
-                fields = [
-                    ref[pl.ds(pl.multiple_of(field * rows + group * 8, 8), 8), :] for field in range(FIELDS)
-                ]
-                fields[0] = fields[0] + shift
-                fill_blocks(fields, planes.at[side], table, first + group * 8 * LANES)
+            for ref, first, shift in ((lower_ref, 0, -SLAB_WIDTH), (upper_ref, 2 * own, SLAB_WIDTH)):
+                fill_blocks(lambda block: ref[group * 4 + block], 4, shift, table, first + group * 4 * LANES)
             return carry
 
-        lax.fori_loop(0, rows // 8, fill, 0)
+        lax.fori_loop(0, rows // 4, fill, 0)
         own_copy.wait()
         sum_b[...] = jnp.zeros_like(sum_b)
         for copy in load(0, far_a):
@@ -261,9 +227,8 @@
     across = sums.T
     result = []
     for axis, place in enumerate(places):
-        first = 6 * axis
-        moment = across[first : first + 1] + across[first + 1 : first + 2] + across[first + 3 : first + 4]
-        result.append((place - CENTRE) * across[ONES : ONES + 1] - moment)
+        moment = sum(across[first + axis : first + axis + 1] for first in (0, 8, 16))
+        result.append((place - CENTRE) * across[ONE : ONE + 1] - moment)
     return result
 
 
@@ -391,9 +356,14 @@
     index = lax.axis_index("image").reshape(1)
 
     factor = jnp.where(jnp.arange(atoms) < SOL_DEV, jnp.sqrt(rest_scale[0]), 1.0)
-    scaled = jnp.stack([strength * factor, charge * factor]).reshape(2, rows, LANES)
+    scaled = jnp.stack([strength * factor * LJ_COEF**0.5, charge * factor * CHARGE_COEF**0.5])
     places = positions.reshape(3, rows, LANES)
-    fields = jnp.concatenate([places, scaled])
+    fields = jnp.concatenate([places, scaled.reshape(2, rows, LANES)])
+    constant = jnp.stack([jnp.full((rows, LANES), value, F32) for value in (1.0, 0.0, 1.0)])
+
+    def blocks(planes):
+        return jnp.concatenate([planes, constant]).transpose(1, 0, 2)
+
     paths = round_trip(places[:, : SOL_DEV // LANES], "image")
     shell = ghost_index.reshape(2, rows // 2, LANES).astype(F32)
     planes = fields.reshape(FIELDS * rows, LANES)
@@ -406,6 +376,7 @@
             upper[FIELDS * rows :].astype(I32).reshape(half) + 2 * atoms,
         ]
     )
+    lower, upper = (blocks(side[: FIELDS * rows].reshape(FIELDS, rows, LANES)) for side in (lower, upper))
     order = cell_order.reshape(atoms)
     scalar = pl.BlockSpec(memory_space=pltpu.SMEM)
     vector = pl.BlockSpec(memory_space=pltpu.VMEM)
@@ -421,12 +392,11 @@
         ],
         scratch_shapes=[
             pltpu.VMEM((atoms + 2 * PAD, LANES), F32),
-            pltpu.VMEM((2, 8 * STRIDE, LANES), F32),
             pltpu.VMEM((2, TILE, LANES), BF16),
         ],
         compiler_params=params,
         cost_estimate=pl.CostEstimate(flops=25 * 10**9, bytes_accessed=3 * 10**7, transcendentals=0),
-    )(order, fields, near_selector())
+    )(order, blocks(fields), near_selector())
     forces, solute = pl.pallas_call(
         functools.partial(force_kernel, rows),
         grid=(rows // 8,),
@@ -438,7 +408,6 @@
         scratch_shapes=[
             pltpu.VMEM((3 * atoms + 2 * PAD, LANES), F32),
             pltpu.VMEM((atoms + 2 * FORCE_PAD, LANES), F32),
-            pltpu.VMEM((2, 8 * STRIDE, LANES), F32),
             pltpu.VMEM((partners, LANES), BF16),
             pltpu.VMEM((partners, LANES), BF16),
             pltpu.VMEM((TILE, LANES), F32),

time: 180 us -> 185 us (1.028)
  other arithmetic: 3.76 us -> 6.01 us
  Pallas kernels: 146 us -> 148 us
    transpose x0 -> x2, other arithmetic: none -> 2.37 us  [blocks(): return jnp.concatenate([planes, constant]).transpose(1, 0, 2)]
    unnamed x15 -> x11, local copies, waits for them, and re-layouts: 5.88 us -> 5.75 us
  transfers between devices with their start and end apart: 11 -> 11, of which waited for: 4 -> 4; matrix products, arithmetic and copies ran while one was open for 3% -> 5% of each run, Pallas kernels for 81% -> 80%
where the time goes in v9:
time: 185 us
  Pallas kernels  148 us (80%)
  starting transfers between devices  12 us (6%)
  waiting for transfers between devices  9.58 us (5%)
  local copies, waits for them, and re-layouts  8.27 us (4%)
  other arithmetic  6.01 us (3%)
    pallas_call x1, Pallas kernels, per_device(): pl.pallas_call(functools.partial(force_kernel, rows), grid=(rows // 8,),...  103 us
    pallas_call x1, Pallas kernels, per_device(): pl.pallas_call(functools.partial(near_kernel, rows), grid=(rows // 8,), o...  36.4 us
    ppermute x8, starting transfers between devices, turned(): lax.ppermute(array, axis, [(i, (i + by) % count) for i in range(count)])  11.1 us
    pallas_call x1, Pallas kernels, per_device(): pl.pallas_call(relax_kernel, grid=(rows // 8,), out_shape=whole(3, rows,...  7.99 us
    ppermute x3, waiting for transfers between devices, summed(): lax.ppermute(array, axis, [(i, i ^ by) for i in range(count)])  7.46 us
    unnamed x11, local copies, waits for them, and re-layouts  5.75 us
  transfers between devices with their start and end apart: 11, of which 4 were waited for; matrix products, arithmetic and copies ran while one was open for 5% of the time, Pallas kernels for 80%

profile of v9, /device:TPU:0, one launch (start us, length us, event | category | flops | bytes accessed | tf_op | source)
XLA Modules:
  0.0 184.6 jit_solution(8721892488435408349)
XLA Ops:
  0.0 0.7 slice.36.refs_4_
  0.7 0.5 collective-permute-start.5
  1.2 2.5 %collective-permute-start.6 = (f32[3,8,128]{2,1,0:T(8,128)S(1)}, f32[3,8,128]{2,1,0:T(8,128)S(1)}, u32[]{:S(2)}, u32[]{:S(2)}) collective-permute-start(f32[3,8,128]{2,1,0:T(8,128)S(1)} %slice.36.refs_4_), channel_id=1, source_target_pairs={{0,16},{8,24},{16,0},{24,8},{1,17},{9,25},{17,1},{25,9},{2,18},{10... | collective-permute-start | bytes 36872 | tf_op jit(solution)/shard_map/ppermute | solution.py:332
  3.7 1.4 collective-permute-start.7
  5.8 0.9 convert_element_type.10
  6.8 0.9 fusion.3
  7.8 1.0 pad_maximum_fusion.4
  8.7 0.1 pad_maximum_fusion.2
  8.8 1.5 collective-permute-start
  10.3 3.2 %collective-permute-start.1 = (f32[880,128]{1,0:T(8,128)S(1)}, f32[880,128]{1,0:T(8,128)S(1)}, u32[]{:S(2)}, u32[]{:S(2)}) collective-permute-start(f32[880,128]{1,0:T(8,128)S(1)} %get-tuple-element.20), channel_id=1, source_target_pairs={{0,7},{1,0},{2,1},{3,2},{4,3},{5,4},{6,5},{7,6},{8,15},{9,8},{10,9... | collective-permute-start | bytes 1351688 | tf_op jit(solution)/shard_map/ppermute | solution.py:332
  13.6 1.1 maximum_bitcast_fusion
  14.7 1.2 copy.18.fields_ref
  15.9 0.0 copy-start.3
  15.9 36.4 %shard_map.82 = (f32[20480,128]{1,0:T(8,128)}, bf16[160,384,128]{2,1,0:T(8,128)(2,1)}) custom-call(s32[20480]{0:T(1024)} %bitcast.38, f32[160,8,128]{2,1,0:T(8,128)} %copy.18.fields_ref, bf16[128,384]{1,0:T(8,128)(2,1)} %constant.21.clone.select_ref), custom_call_target="tpu_custom_call" | custom-call | flops 24999999488 | bytes 30000000 | tf_op jit(solution)/shard_map/pallas_call | solution.py:384
  52.4 0.0 copy-done.4
  52.4 0.8 copy.20
  53.1 0.0 collective-permute-done
  53.2 0.3 copy.14
  53.4 0.0 collective-permute-done.1
  53.5 0.3 copy.16
  53.7 0.0 copy-done.3
  53.8 1.3 fusion.1
  55.0 0.7 pad_add_fusion.entry_ref
  55.7 0.0 copy-start.1
  55.7 102.6 %shard_map.83 = (f32[22528,128]{1,0:T(8,128)}, f32[3,8,128]{2,1,0:T(8,128)}) custom-call(s32[40960]{0:T(1024)} %bitcast.37, s32[40960]{0:T(1024)} %pad_add_fusion.entry_ref, s32[20480]{0:T(1024)} %bitcast.39, f32[160,8,128]{2,1,0:T(8,128)} %get-tuple-element.22.lower_ref, f32[160,8,128]{2,1,0:T(8,128)} %get-tuple-element.21.upper_ref, ...), custom_call_target="tpu_custom_call" | custom-call | flops 24999999488 | bytes 30000000 | tf_op jit(solution)/shard_map/pallas_call | solution.py:400
  158.4 0.1 collective-permute-start.2
  158.4 0.5 collective-permute-start.3
  158.9 0.0 collective-permute-done.5.refs_5_
  158.9 1.4 collective-permute-start.4
  160.3 0.0 collective-permute-done.6.refs_6_
  160.3 0.0 collective-permute-done.7.refs_7_
  160.3 1.5 collective-permute-done.2.refs_1_
  161.7 0.7 collective-permute-done.3.refs_2_
  162.4 0.0 collective-permute-done.4.refs_3_
  162.4 0.0 copy-start.2
  162.4 0.7 copy-done.2
  163.1 0.1 shard_map.84
  163.2 0.1 collective-permute-start.8
  163.2 3.7 %collective-permute-done.8 = f32[32,128]{1,0:T(8,128)S(1)} collective-permute-done((f32[32,128]{1,0:T(8,128)S(1)}, f32[32,128]{1,0:T(8,128)S(1)}, u32[]{:S(2)}, u32[]{:S(2)}) %collective-permute-start.8) | collective-permute-done | bytes 16416 | tf_op jit(solution)/shard_map/ppermute | solution.py:341
  167.0 0.0 collective-permute-start.9
  167.0 3.7 %collective-permute-done.9 = f32[32,128]{1,0:T(8,128)S(1)} collective-permute-done((f32[32,128]{1,0:T(8,128)S(1)}, f32[32,128]{1,0:T(8,128)S(1)}, u32[]{:S(2)}, u32[]{:S(2)}) %collective-permute-start.9) | collective-permute-done | bytes 16416 | tf_op jit(solution)/shard_map/ppermute | solution.py:341
  170.7 0.8 collective-permute-start.10
  171.6 0.0 copy-done.1
  171.6 0.0 copy-start
  171.6 4.3 %copy-done = f32[22528,128]{1,0:T(8,128)S(1)} copy-done((f32[22528,128]{1,0:T(8,128)S(1)}, f32[22528,128]{1,0:T(8,128)}, u32[]{:S(2)}) %copy-start) | copy-done | bytes 11534360
  175.8 8.0 %shard_map.85.out_in = f32[3,160,128]{2,1,0:T(8,128)} custom-call(f32[3,160,128]{2,1,0:T(8,128)S(1)} %bitcast.30, f32[22528,128]{1,0:T(8,128)S(1)} %copy-done), custom_call_target="tpu_custom_call" | custom-call | flops 1000000000 | bytes 20000000 | tf_op jit(solution)/shard_map/pallas_call | solution.py:423
  183.8 0.0 collective-permute-done.10
  183.8 0.8 shard_map.86
  (10 shorter events, 0.1 us)
Async XLA Ops:
  0.7 158.2 %collective-permute-start.5 = (f32[3,8,128]{2,1,0:T(8,128)S(1)}, f32[3,8,128]{2,1,0:T(8,128)S(1)}, u32[]{:S(2)}, u32[]{:S(2)}) collective-permute-start(f32[3,8,128]{2,1,0:T(8,128)S(1)} %slice.36.refs_4_), channel_id=1, source_target_pairs={{0,8},{8,16},{16,24},{24,0},{1,9},{9,17},{17,25},{25,1},{2,10},{10... | collective-permute-start | bytes 36872 | tf_op jit(solution)/shard_map/ppermute | solution.py:332
  1.2 159.1 %collective-permute-start.6 = (f32[3,8,128]{2,1,0:T(8,128)S(1)}, f32[3,8,128]{2,1,0:T(8,128)S(1)}, u32[]{:S(2)}, u32[]{:S(2)}) collective-permute-start(f32[3,8,128]{2,1,0:T(8,128)S(1)} %slice.36.refs_4_), channel_id=1, source_target_pairs={{0,16},{8,24},{16,0},{24,8},{1,17},{9,25},{17,1},{25,9},{2,18},{10... | collective-permute-start | bytes 36872 | tf_op jit(solution)/shard_map/ppermute | solution.py:332
  3.7 156.6 %collective-permute-start.7 = (f32[3,8,128]{2,1,0:T(8,128)S(1)}, f32[3,8,128]{2,1,0:T(8,128)S(1)}, u32[]{:S(2)}, u32[]{:S(2)}) collective-permute-start(f32[3,8,128]{2,1,0:T(8,128)S(1)} %slice.36.refs_4_), channel_id=1, source_target_pairs={{0,24},{8,0},{16,8},{24,16},{1,25},{9,1},{17,9},{25,17},{2,26},{10... | collective-permute-start | bytes 36872 | tf_op jit(solution)/shard_map/ppermute | solution.py:332
  8.8 44.3 %collective-permute-start = (f32[880,128]{1,0:T(8,128)S(1)}, f32[880,128]{1,0:T(8,128)S(1)}, u32[]{:S(2)}, u32[]{:S(2)}) collective-permute-start(f32[880,128]{1,0:T(8,128)S(1)} %get-tuple-element.19), channel_id=1, source_target_pairs={{0,1},{1,2},{2,3},{3,4},{4,5},{5,6},{6,7},{7,0},{8,9},{9,10},{10,1... | collective-permute-start | bytes 1351688 | tf_op jit(solution)/shard_map/ppermute | solution.py:332
  10.3 43.1 %collective-permute-start.1 = (f32[880,128]{1,0:T(8,128)S(1)}, f32[880,128]{1,0:T(8,128)S(1)}, u32[]{:S(2)}, u32[]{:S(2)}) collective-permute-start(f32[880,128]{1,0:T(8,128)S(1)} %get-tuple-element.20), channel_id=1, source_target_pairs={{0,7},{1,0},{2,1},{3,2},{4,3},{5,4},{6,5},{7,6},{8,15},{9,8},{10,9... | collective-permute-start | bytes 1351688 | tf_op jit(solution)/shard_map/ppermute | solution.py:332
  15.9 36.4 %copy-start.4 = (s32[1,160,256]{2,1,0:T(8,128)S(1)}, s32[1,160,256]{2,1,0:T(8,128)}, u32[]{:S(2)}) copy-start(s32[1,160,256]{2,1,0:T(8,128)} %param.14) | copy-start | bytes 491524
  15.9 37.8 %copy-start.3 = (f32[3,160,128]{2,0,1:T(4,128)S(1)}, f32[3,160,128]{2,0,1:T(4,128)}, u32[]{:S(2)}) copy-start(f32[3,160,128]{2,0,1:T(4,128)} %constant.27) | copy-start | bytes 737284
  55.7 115.8 %copy-start.1 = (f32[1,3,20480]{2,0,1:T(1,128)S(1)}, f32[1,3,20480]{2,0,1:T(1,128)}, u32[]{:S(2)}) copy-start(f32[1,3,20480]{2,0,1:T(1,128)} %param.8) | copy-start | bytes 737284
  158.4 3.4 %collective-permute-start.2 = (f32[3,8,128]{2,1,0:T(8,128)}, f32[3,8,128]{2,1,0:T(8,128)S(1)}, u32[]{:S(2)}, u32[]{:S(2)}) collective-permute-start(f32[3,8,128]{2,1,0:T(8,128)} %get-tuple-element.14.refs_0_), channel_id=1, source_target_pairs={{0,8},{8,16},{16,24},{24,0},{1,9},{9,17},{17,25},{25,1},{2,10},{10... | collective-permute-start | bytes 36872 | tf_op jit(solution)/shard_map/ppermute | solution.py:332
  158.4 4.0 %collective-permute-start.3 = (f32[3,8,128]{2,1,0:T(8,128)}, f32[3,8,128]{2,1,0:T(8,128)S(1)}, u32[]{:S(2)}, u32[]{:S(2)}) collective-permute-start(f32[3,8,128]{2,1,0:T(8,128)} %get-tuple-element.14.refs_0_), channel_id=1, source_target_pairs={{0,16},{8,24},{16,0},{24,8},{1,17},{9,25},{17,1},{25,9},{2,18},{10... | collective-permute-start | bytes 36872 | tf_op jit(solution)/shard_map/ppermute | solution.py:332
  158.9 3.5 %collective-permute-start.4 = (f32[3,8,128]{2,1,0:T(8,128)}, f32[3,8,128]{2,1,0:T(8,128)S(1)}, u32[]{:S(2)}, u32[]{:S(2)}) collective-permute-start(f32[3,8,128]{2,1,0:T(8,128)} %get-tuple-element.14.refs_0_), channel_id=1, source_target_pairs={{0,24},{8,0},{16,8},{24,16},{1,25},{9,1},{17,9},{25,17},{2,26},{10... | collective-permute-start | bytes 36872 | tf_op jit(solution)/shard_map/ppermute | solution.py:332
  162.4 0.7 copy-start.2
  163.2 3.8 %collective-permute-start.8 = (f32[32,128]{1,0:T(8,128)S(1)}, f32[32,128]{1,0:T(8,128)S(1)}, u32[]{:S(2)}, u32[]{:S(2)}) collective-permute-start(f32[32,128]{1,0:T(8,128)S(1)} %get-tuple-element.15), channel_id=1, source_target_pairs={{0,1},{1,0},{2,3},{3,2},{4,5},{5,4},{6,7},{7,6},{8,9},{9,8},{10,11... | collective-permute-start | bytes 49160 | tf_op jit(solution)/shard_map/ppermute | solution.py:341
  167.0 3.7 %collective-permute-start.9 = (f32[32,128]{1,0:T(8,128)S(1)}, f32[32,128]{1,0:T(8,128)S(1)}, u32[]{:S(2)}, u32[]{:S(2)}) collective-permute-start(f32[32,128]{1,0:T(8,128)S(1)} %add.29), channel_id=1, source_target_pairs={{0,2},{1,3},{2,0},{3,1},{4,6},{5,7},{6,4},{7,5},{8,10},{9,11},{10,... | collective-permute-start | bytes 49160 | tf_op jit(solution)/shard_map/ppermute | solution.py:341
  170.7 13.1 %collective-permute-start.10 = (f32[32,128]{1,0:T(8,128)S(1)}, f32[32,128]{1,0:T(8,128)S(1)}, u32[]{:S(2)}, u32[]{:S(2)}) collective-permute-start(f32[32,128]{1,0:T(8,128)S(1)} %add.30), channel_id=1, source_target_pairs={{0,4},{1,5},{2,6},{3,7},{4,0},{5,1},{6,2},{7,3},{8,12},{9,13},{10,... | collective-permute-start | bytes 49160 | tf_op jit(solution)/shard_map/ppermute | solution.py:341
  171.6 4.3 %copy-start = (f32[22528,128]{1,0:T(8,128)S(1)}, f32[22528,128]{1,0:T(8,128)}, u32[]{:S(2)}) copy-start(f32[22528,128]{1,0:T(8,128)} %get-tuple-element.18.force_ref) | copy-start | bytes 34603012

commit v10 on v9

--- a/solution.py
+++ b/solution.py
@@ -35,17 +35,23 @@
 
 
 def near_selector():
-    chosen = np.zeros((LANES, 3 * LANES), np.float32)
+    chosen = np.zeros((LANES, LANES), np.float32)
     for group, piece in enumerate(NEAR_PIECES):
         for axis in range(3):
             chosen[piece * 8 + axis, group * 8 + axis] = 2.0
-        for block, field in ((1, DEPTH), (2, CHARGE)):
-            chosen[piece * 8 + field, block * LANES + group * 8 + field] = 1.0
+        for field in (DEPTH, CHARGE):
+            chosen[piece * 8 + field, group * 8 + field] = 1.0
     for piece, group in ((0, 0), (1, 3), (2, 5)):
         chosen[piece * 8 + NORM, group * 8 + ONE] = 1.0
         chosen[ONE, piece * 8 + NORM] = 1.0
     chosen[ONE, LAST] = 1.0
     return jnp.asarray(chosen, BF16)
+
+
+def near_masks():
+    field = np.arange(LANES) % 8
+    kinds = [(field != DEPTH) & (field != CHARGE), field == DEPTH, field == CHARGE]
+    return jnp.asarray(np.stack([np.tile(kind, (TILE, 1)) for kind in kinds]), BF16)
 
 
 def two_pieces(values):
@@ -93,7 +99,7 @@
     stage[start : start + 16, :] = jnp.concatenate(parts, axis=0).astype(BF16)
 
 
-def near_kernel(rows, order_ref, fields_ref, select_ref, table_ref, left_ref, table, stage):
+def near_kernel(rows, order_ref, fields_ref, select_ref, table_ref, left_ref, table, stage_a, stage_b):
     turn = pl.program_id(0)
 
     @pl.when(turn == 0)
@@ -106,27 +112,50 @@
 
     masks = sublane_masks()
 
-    def tile_step(local, carry):
+    def load(tile, stage):
+        def entry_of(k):
+            return order_ref[tile * TILE + k]
+
+        return [
+            functools.partial(copy_rows, table, entry_of, stage, start, masks) for start in range(0, TILE, 16)
+        ]
+
+    def factors(place, stage):
+        left = jnp.dot(stage[...], select_ref[...], preferred_element_type=F32)
+        yield
+        left_ref[place] = left.astype(BF16)
+
+    @pl.when(turn == 0)
+    def _():
         for side in range(2):
-            tile = turn * 8 + local * 2 + side
-            for start in range(0, TILE, 16):
-                copy_rows(table, lambda k: order_ref[tile * TILE + k], stage.at[side], start, masks)
-        for side in range(2):
-            left = jnp.dot(stage[side], select_ref[...], preferred_element_type=F32).astype(BF16)
-            for block in range(3):
-                left_ref[local * 2 + side, block * TILE : (block + 1) * TILE, :] = left[
-                    :, block * LANES : (block + 1) * LANES
-                ]
+            for copy in load(side, stage_a.at[side]):
+                copy()
+
+    def step(part, carry):
+        tile = turn * 8 + part * 4
+        last = rows - 1
+        weave(
+            [factors(part * 4 + side, stage_a.at[side]) for side in range(2)],
+            load(tile + 2, stage_b.at[0]) + load(tile + 3, stage_b.at[1]),
+            1,
+        )
+        weave(
+            [factors(part * 4 + 2 + side, stage_b.at[side]) for side in range(2)],
+            load(jnp.minimum(tile + 4, last), stage_a.at[0]) + load(jnp.minimum(tile + 5, last), stage_a.at[1]),
+            1,
+        )
         return carry
 
-    lax.fori_loop(0, 4, tile_step, 0)
+    lax.fori_loop(0, 2, step, 0)
     table_ref[...] = table[pl.ds(pl.multiple_of(turn * 8 * LANES + PAD, PAD), 8 * LANES), :]
 
 
-def tile_sums(left_ref, place, far, sums):
+def tile_sums(left_ref, kinds_ref, place, far, sums):
     others = far[...]
+    left = left_ref[place]
+    left = jnp.concatenate([left * kinds_ref[kind] for kind in range(3)], axis=0)
     yield
-    grams = nt_dot(left_ref[place], others)
+    grams = nt_dot(left, others)
     yield
     chunk = 32
     high, low = [], []
@@ -147,19 +176,22 @@
 
 def weave(stages, copies, parts):
     size = -(-len(copies) // parts)
-    for turn, _ in enumerate(stages):
+    for turn, _ in enumerate(zip(*stages)):
         for copy in copies[turn * size : (turn + 1) * size]:
             copy()
     for copy in copies[parts * size :]:
         copy()
+    for stage in stages:
+        for _ in stage:
+            pass
 
 
 def force_kernel(
-    rows, partner_ref, entry_ref, order_ref, lower_ref, upper_ref, place_ref, left_ref, own_ref,
+    rows, partner_ref, entry_ref, order_ref, lower_ref, upper_ref, place_ref, kinds_ref, left_ref, own_ref,
     force_ref, solute_ref, table, forces, far_a, far_b, sum_a, sum_b, arrival,
 ):
     turn = pl.program_id(0)
-    partners = far_a.shape[0]
+    partners = far_a.shape[1]
     own = rows * LANES
 
     masks = sublane_masks()
@@ -195,23 +227,36 @@
         lax.fori_loop(0, rows // 4, fill, 0)
         own_copy.wait()
         sum_b[...] = jnp.zeros_like(sum_b)
-        for copy in load(0, far_a):
-            copy()
-
-    def step(pair, carry):
-        tile = turn * 8 + pair * 2
-        copies = save(jnp.maximum(tile - 1, 0), sum_b) + load(tile + 1, far_b)
-        weave(tile_sums(left_ref, pair * 2, far_a, sum_a), copies, 7)
-        copies = save(tile, sum_a) + load(jnp.minimum(tile + 2, rows - 1), far_a)
-        weave(tile_sums(left_ref, pair * 2 + 1, far_b, sum_b), copies, 7)
+        for side in range(2):
+            for copy in load(side, far_a.at[side]):
+                copy()
+
+    def step(part, carry):
+        tile = turn * 8 + part * 4
+        last = rows - 1
+        copies = save(jnp.maximum(tile - 2, 0), sum_b.at[0]) + save(jnp.maximum(tile - 1, 0), sum_b.at[1])
+        copies += load(tile + 2, far_b.at[0]) + load(tile + 3, far_b.at[1])
+        weave(
+            [tile_sums(left_ref, kinds_ref, part * 4 + side, far_a.at[side], sum_a.at[side]) for side in range(2)],
+            copies,
+            7,
+        )
+        copies = save(tile, sum_a.at[0]) + save(tile + 1, sum_a.at[1])
+        copies += load(jnp.minimum(tile + 4, last), far_a.at[0]) + load(jnp.minimum(tile + 5, last), far_a.at[1])
+        weave(
+            [tile_sums(left_ref, kinds_ref, part * 4 + 2 + side, far_b.at[side], sum_b.at[side]) for side in range(2)],
+            copies,
+            7,
+        )
         return carry
 
-    lax.fori_loop(0, 4, step, 0)
+    lax.fori_loop(0, 2, step, 0)
 
     @pl.when(turn == pl.num_programs(0) - 1)
     def _():
-        for copy in save(rows - 1, sum_b):
-            copy()
+        for side in range(2):
+            for copy in save(rows - 2 + side, sum_b.at[side]):
+                copy()
 
         send = pltpu.make_async_copy(forces, force_ref, arrival)
         send.start()
@@ -384,14 +429,15 @@
     table, left = pl.pallas_call(
         functools.partial(near_kernel, rows),
         grid=(rows // 8,),
-        out_shape=[whole(atoms, LANES), whole(rows, 3 * TILE, LANES, dtype=BF16)],
+        out_shape=[whole(atoms, LANES), whole(rows, TILE, LANES, dtype=BF16)],
         in_specs=[scalar] + [vector] * 2,
         out_specs=[
             pl.BlockSpec((8 * LANES, LANES), lambda i: (i, 0)),
-            pl.BlockSpec((8, 3 * TILE, LANES), lambda i: (i, 0, 0)),
+            pl.BlockSpec((8, TILE, LANES), lambda i: (i, 0, 0)),
         ],
         scratch_shapes=[
             pltpu.VMEM((atoms + 2 * PAD, LANES), F32),
+            pltpu.VMEM((2, TILE, LANES), BF16),
             pltpu.VMEM((2, TILE, LANES), BF16),
         ],
         compiler_params=params,
@@ -402,21 +448,21 @@
         grid=(rows // 8,),
         out_shape=[whole(atoms + 2 * FORCE_PAD, LANES), whole(3, SOL_DEV // LANES, LANES)],
         in_specs=[scalar] * 3
-        + [vector] * 3
-        + [pl.BlockSpec((8, 3 * TILE, LANES), lambda i: (i, 0, 0)), pl.BlockSpec(memory_space=pl.ANY)],
+        + [vector] * 4
+        + [pl.BlockSpec((8, TILE, LANES), lambda i: (i, 0, 0)), pl.BlockSpec(memory_space=pl.ANY)],
         out_specs=[pl.BlockSpec(memory_space=pl.ANY), vector],
         scratch_shapes=[
             pltpu.VMEM((3 * atoms + 2 * PAD, LANES), F32),
             pltpu.VMEM((atoms + 2 * FORCE_PAD, LANES), F32),
-            pltpu.VMEM((partners, LANES), BF16),
-            pltpu.VMEM((partners, LANES), BF16),
-            pltpu.VMEM((TILE, LANES), F32),
-            pltpu.VMEM((TILE, LANES), F32),
+            pltpu.VMEM((2, partners, LANES), BF16),
+            pltpu.VMEM((2, partners, LANES), BF16),
+            pltpu.VMEM((2, TILE, LANES), F32),
+            pltpu.VMEM((2, TILE, LANES), F32),
             pltpu.SemaphoreType.DMA,
         ],
         compiler_params=params,
         cost_estimate=pl.CostEstimate(flops=25 * 10**9, bytes_accessed=3 * 10**7, transcendentals=0),
-    )(tile_atoms.reshape(rows * partners), entries, order, lower, upper, places, left, table)
+    )(tile_atoms.reshape(rows * partners), entries, order, lower, upper, places, near_masks(), left, table)
     solutes = round_trip(solute, "image")
     block = pl.BlockSpec((3, 8, LANES), lambda i: (0, i, 0))
     small = pltpu.CompilerParams(vmem_limit_bytes=8 * 1024 * 1024)

time: 185 us -> 173 us (0.935)
  Pallas kernels: 148 us -> 135 us
    pallas_call x1, Pallas kernels: 103 us -> 96.1 us  [per_device(): pl.pallas_call(functools.partial(force_kernel, rows), grid=(rows // 8,),...]
    pallas_call x1, Pallas kernels: 36.4 us -> 30.6 us  [per_device(): pl.pallas_call(functools.partial(near_kernel, rows), grid=(rows // 8,), o...]
  transfers between devices with their start and end apart: 11 -> 11, of which waited for: 4 -> 4; matrix products, arithmetic and copies ran while one was open for 5% -> 5% of each run, Pallas kernels for 80% -> 78%
where the time goes in v10:
time: 173 us; the launch traced here: 172 us
  Pallas kernels  135 us (78%)
  starting transfers between devices  11.9 us (7%)
  waiting for transfers between devices  9.66 us (6%)
  local copies, waits for them, and re-layouts  8.29 us (5%)
  other arithmetic  5.99 us (3%)
    pallas_call x1, Pallas kernels, per_device(): pl.pallas_call(functools.partial(force_kernel, rows), grid=(rows // 8,),...  96.1 us
    pallas_call x1, Pallas kernels, per_device(): pl.pallas_call(functools.partial(near_kernel, rows), grid=(rows // 8,), o...  30.6 us
    ppermute x8, starting transfers between devices, turned(): lax.ppermute(array, axis, [(i, (i + by) % count) for i in range(count)])  11.1 us
    pallas_call x1, Pallas kernels, per_device(): pl.pallas_call(relax_kernel, grid=(rows // 8,), out_shape=whole(3, rows,...  7.99 us
    ppermute x3, waiting for transfers between devices, summed(): lax.ppermute(array, axis, [(i, i ^ by) for i in range(count)])  7.46 us
    unnamed x11, local copies, waits for them, and re-layouts  5.75 us
  transfers between devices with their start and end apart: 11, of which 4 were waited for; matrix products, arithmetic and copies ran while one was open for 5% of the time, Pallas kernels for 78%

profile of v10, /device:TPU:0, one launch (start us, length us, event | category | flops | bytes accessed | tf_op | source)
XLA Modules:
  0.0 172.2 jit_solution(10316155637993940408)
XLA Ops:
  0.0 0.7 slice.36.refs_4_
  0.7 0.5 collective-permute-start.5
  1.2 2.5 %collective-permute-start.6 = (f32[3,8,128]{2,1,0:T(8,128)S(1)}, f32[3,8,128]{2,1,0:T(8,128)S(1)}, u32[]{:S(2)}, u32[]{:S(2)}) collective-permute-start(f32[3,8,128]{2,1,0:T(8,128)S(1)} %slice.36.refs_4_), channel_id=1, source_target_pairs={{0,16},{8,24},{16,0},{24,8},{1,17},{9,25},{17,1},{25,9},{2,18},{10... | collective-permute-start | bytes 36872 | tf_op jit(solution)/shard_map/ppermute | solution.py:377
  3.7 1.4 collective-permute-start.7
  5.8 0.9 convert_element_type.10
  6.8 0.9 fusion.3
  7.8 1.0 pad_maximum_fusion.4
  8.7 0.1 pad_maximum_fusion.2
  8.8 1.5 collective-permute-start
  10.3 3.2 %collective-permute-start.1 = (f32[880,128]{1,0:T(8,128)S(1)}, f32[880,128]{1,0:T(8,128)S(1)}, u32[]{:S(2)}, u32[]{:S(2)}) collective-permute-start(f32[880,128]{1,0:T(8,128)S(1)} %get-tuple-element.20), channel_id=1, source_target_pairs={{0,7},{1,0},{2,1},{3,2},{4,3},{5,4},{6,5},{7,6},{8,15},{9,8},{10,9... | collective-permute-start | bytes 1351688 | tf_op jit(solution)/shard_map/ppermute | solution.py:377
  13.6 1.1 maximum_bitcast_fusion
  14.7 1.3 copy.19.fields_ref
  15.9 0.0 copy-start.3
  15.9 30.6 %shard_map.91 = (f32[20480,128]{1,0:T(8,128)}, bf16[160,128,128]{2,1,0:T(8,128)(2,1)}) custom-call(s32[20480]{0:T(1024)} %bitcast.38, f32[160,8,128]{2,1,0:T(8,128)} %copy.19.fields_ref, bf16[128,128]{1,0:T(8,128)(2,1)} %constant.23.clone.select_ref), custom_call_target="tpu_custom_call" | custom-call | flops 24999999488 | bytes 30000000 | tf_op jit(solution)/shard_map/pallas_call | solution.py:429
  46.6 0.0 copy-done.4
  46.6 0.8 copy.21
  47.3 0.0 collective-permute-done
  47.4 0.3 copy.15
  47.6 0.0 collective-permute-done.1
  47.7 0.3 copy.17
  48.0 0.0 copy-done.3
  48.0 1.2 fusion.1
  49.2 0.7 pad_add_fusion.entry_ref
  49.9 0.0 copy-start.1
  49.9 96.1 %shard_map.92 = (f32[22528,128]{1,0:T(8,128)}, f32[3,8,128]{2,1,0:T(8,128)}) custom-call(s32[40960]{0:T(1024)} %bitcast.37, s32[40960]{0:T(1024)} %pad_add_fusion.entry_ref, s32[20480]{0:T(1024)} %bitcast.39, f32[160,8,128]{2,1,0:T(8,128)} %get-tuple-element.22.lower_ref, f32[160,8,128]{2,1,0:T(8,128)} %get-tuple-element.21.upper_ref, ...), custom_call_target="tpu_custom_call" | custom-call | flops 24999999488 | bytes 30000000 | tf_op jit(solution)/shard_map/pallas_call | solution.py:446
  146.0 0.1 collective-permute-start.2
  146.0 0.4 collective-permute-start.3
  146.4 0.0 collective-permute-done.5.refs_5_
  146.4 1.4 collective-permute-start.4
  147.8 0.0 collective-permute-done.6.refs_6_
  147.8 0.0 collective-permute-done.7.refs_7_
  147.8 1.5 collective-permute-done.2.refs_1_
  149.4 0.7 collective-permute-done.3.refs_2_
  150.0 0.0 collective-permute-done.4.refs_3_
  150.0 0.0 copy-start.2
  150.0 0.7 copy-done.2
  150.7 0.1 shard_map.93
  150.8 0.1 collective-permute-start.8
  150.9 3.7 %collective-permute-done.8 = f32[32,128]{1,0:T(8,128)S(1)} collective-permute-done((f32[32,128]{1,0:T(8,128)S(1)}, f32[32,128]{1,0:T(8,128)S(1)}, u32[]{:S(2)}, u32[]{:S(2)}) %collective-permute-start.8) | collective-permute-done | bytes 16416 | tf_op jit(solution)/shard_map/ppermute | solution.py:386
  154.6 0.0 collective-permute-start.9
  154.6 3.7 %collective-permute-done.9 = f32[32,128]{1,0:T(8,128)S(1)} collective-permute-done((f32[32,128]{1,0:T(8,128)S(1)}, f32[32,128]{1,0:T(8,128)S(1)}, u32[]{:S(2)}, u32[]{:S(2)}) %collective-permute-start.9) | collective-permute-done | bytes 16416 | tf_op jit(solution)/shard_map/ppermute | solution.py:386
  158.4 0.8 collective-permute-start.10
  159.1 0.0 copy-done.1
  159.1 0.0 copy-start
  159.1 4.3 %copy-done = f32[22528,128]{1,0:T(8,128)S(1)} copy-done((f32[22528,128]{1,0:T(8,128)S(1)}, f32[22528,128]{1,0:T(8,128)}, u32[]{:S(2)}) %copy-start) | copy-done | bytes 11534360
  163.4 8.0 %shard_map.94.out_in = f32[3,160,128]{2,1,0:T(8,128)} custom-call(f32[3,160,128]{2,1,0:T(8,128)S(1)} %bitcast.30, f32[22528,128]{1,0:T(8,128)S(1)} %copy-done), custom_call_target="tpu_custom_call" | custom-call | flops 1000000000 | bytes 20000000 | tf_op jit(solution)/shard_map/pallas_call | solution.py:469
  171.4 0.0 collective-permute-done.10
  171.4 0.8 shard_map.95
  (10 shorter events, 0.1 us)
Async XLA Ops:
  0.7 145.7 %collective-permute-start.5 = (f32[3,8,128]{2,1,0:T(8,128)S(1)}, f32[3,8,128]{2,1,0:T(8,128)S(1)}, u32[]{:S(2)}, u32[]{:S(2)}) collective-permute-start(f32[3,8,128]{2,1,0:T(8,128)S(1)} %slice.36.refs_4_), channel_id=1, source_target_pairs={{0,8},{8,16},{16,24},{24,0},{1,9},{9,17},{17,25},{25,1},{2,10},{10... | collective-permute-start | bytes 36872 | tf_op jit(solution)/shard_map/ppermute | solution.py:377
  1.2 146.7 %collective-permute-start.6 = (f32[3,8,128]{2,1,0:T(8,128)S(1)}, f32[3,8,128]{2,1,0:T(8,128)S(1)}, u32[]{:S(2)}, u32[]{:S(2)}) collective-permute-start(f32[3,8,128]{2,1,0:T(8,128)S(1)} %slice.36.refs_4_), channel_id=1, source_target_pairs={{0,16},{8,24},{16,0},{24,8},{1,17},{9,25},{17,1},{25,9},{2,18},{10... | collective-permute-start | bytes 36872 | tf_op jit(solution)/shard_map/ppermute | solution.py:377
  3.7 144.1 %collective-permute-start.7 = (f32[3,8,128]{2,1,0:T(8,128)S(1)}, f32[3,8,128]{2,1,0:T(8,128)S(1)}, u32[]{:S(2)}, u32[]{:S(2)}) collective-permute-start(f32[3,8,128]{2,1,0:T(8,128)S(1)} %slice.36.refs_4_), channel_id=1, source_target_pairs={{0,24},{8,0},{16,8},{24,16},{1,25},{9,1},{17,9},{25,17},{2,26},{10... | collective-permute-start | bytes 36872 | tf_op jit(solution)/shard_map/ppermute | solution.py:377
  8.8 38.5 %collective-permute-start = (f32[880,128]{1,0:T(8,128)S(1)}, f32[880,128]{1,0:T(8,128)S(1)}, u32[]{:S(2)}, u32[]{:S(2)}) collective-permute-start(f32[880,128]{1,0:T(8,128)S(1)} %get-tuple-element.19), channel_id=1, source_target_pairs={{0,1},{1,2},{2,3},{3,4},{4,5},{5,6},{6,7},{7,0},{8,9},{9,10},{10,1... | collective-permute-start | bytes 1351688 | tf_op jit(solution)/shard_map/ppermute | solution.py:377
  10.3 37.3 %collective-permute-start.1 = (f32[880,128]{1,0:T(8,128)S(1)}, f32[880,128]{1,0:T(8,128)S(1)}, u32[]{:S(2)}, u32[]{:S(2)}) collective-permute-start(f32[880,128]{1,0:T(8,128)S(1)} %get-tuple-element.20), channel_id=1, source_target_pairs={{0,7},{1,0},{2,1},{3,2},{4,3},{5,4},{6,5},{7,6},{8,15},{9,8},{10,9... | collective-permute-start | bytes 1351688 | tf_op jit(solution)/shard_map/ppermute | solution.py:377
  15.9 30.6 %copy-start.4 = (s32[1,160,256]{2,1,0:T(8,128)S(1)}, s32[1,160,256]{2,1,0:T(8,128)}, u32[]{:S(2)}) copy-start(s32[1,160,256]{2,1,0:T(8,128)} %param.15) | copy-start | bytes 491524
  15.9 32.0 %copy-start.3 = (f32[3,160,128]{2,0,1:T(4,128)S(1)}, f32[3,160,128]{2,0,1:T(4,128)}, u32[]{:S(2)}) copy-start(f32[3,160,128]{2,0,1:T(4,128)} %constant.30) | copy-start | bytes 737284
  49.9 109.2 %copy-start.1 = (f32[1,3,20480]{2,0,1:T(1,128)S(1)}, f32[1,3,20480]{2,0,1:T(1,128)}, u32[]{:S(2)}) copy-start(f32[1,3,20480]{2,0,1:T(1,128)} %param.9) | copy-start | bytes 737284
  146.0 3.4 %collective-permute-start.2 = (f32[3,8,128]{2,1,0:T(8,128)}, f32[3,8,128]{2,1,0:T(8,128)S(1)}, u32[]{:S(2)}, u32[]{:S(2)}) collective-permute-start(f32[3,8,128]{2,1,0:T(8,128)} %get-tuple-element.14.refs_0_), channel_id=1, source_target_pairs={{0,8},{8,16},{16,24},{24,0},{1,9},{9,17},{17,25},{25,1},{2,10},{10... | collective-permute-start | bytes 36872 | tf_op jit(solution)/shard_map/ppermute | solution.py:377
  146.0 4.0 %collective-permute-start.3 = (f32[3,8,128]{2,1,0:T(8,128)}, f32[3,8,128]{2,1,0:T(8,128)S(1)}, u32[]{:S(2)}, u32[]{:S(2)}) collective-permute-start(f32[3,8,128]{2,1,0:T(8,128)} %get-tuple-element.14.refs_0_), channel_id=1, source_target_pairs={{0,16},{8,24},{16,0},{24,8},{1,17},{9,25},{17,1},{25,9},{2,18},{10... | collective-permute-start | bytes 36872 | tf_op jit(solution)/shard_map/ppermute | solution.py:377
  146.4 3.6 %collective-permute-start.4 = (f32[3,8,128]{2,1,0:T(8,128)}, f32[3,8,128]{2,1,0:T(8,128)S(1)}, u32[]{:S(2)}, u32[]{:S(2)}) collective-permute-start(f32[3,8,128]{2,1,0:T(8,128)} %get-tuple-element.14.refs_0_), channel_id=1, source_target_pairs={{0,24},{8,0},{16,8},{24,16},{1,25},{9,1},{17,9},{25,17},{2,26},{10... | collective-permute-start | bytes 36872 | tf_op jit(solution)/shard_map/ppermute | solution.py:377
  150.0 0.7 copy-start.2
  150.8 3.8 %collective-permute-start.8 = (f32[32,128]{1,0:T(8,128)S(1)}, f32[32,128]{1,0:T(8,128)S(1)}, u32[]{:S(2)}, u32[]{:S(2)}) collective-permute-start(f32[32,128]{1,0:T(8,128)S(1)} %get-tuple-element.15), channel_id=1, source_target_pairs={{0,1},{1,0},{2,3},{3,2},{4,5},{5,4},{6,7},{7,6},{8,9},{9,8},{10,11... | collective-permute-start | bytes 49160 | tf_op jit(solution)/shard_map/ppermute | solution.py:386
  154.6 3.7 %collective-permute-start.9 = (f32[32,128]{1,0:T(8,128)S(1)}, f32[32,128]{1,0:T(8,128)S(1)}, u32[]{:S(2)}, u32[]{:S(2)}) collective-permute-start(f32[32,128]{1,0:T(8,128)S(1)} %add.29), channel_id=1, source_target_pairs={{0,2},{1,3},{2,0},{3,1},{4,6},{5,7},{6,4},{7,5},{8,10},{9,11},{10,... | collective-permute-start | bytes 49160 | tf_op jit(solution)/shard_map/ppermute | solution.py:386
  158.4 13.0 %collective-permute-start.10 = (f32[32,128]{1,0:T(8,128)S(1)}, f32[32,128]{1,0:T(8,128)S(1)}, u32[]{:S(2)}, u32[]{:S(2)}) collective-permute-start(f32[32,128]{1,0:T(8,128)S(1)} %add.30), channel_id=1, source_target_pairs={{0,4},{1,5},{2,6},{3,7},{4,0},{5,1},{6,2},{7,3},{8,12},{9,13},{10,... | collective-permute-start | bytes 49160 | tf_op jit(solution)/shard_map/ppermute | solution.py:386
  159.1 4.3 %copy-start = (f32[22528,128]{1,0:T(8,128)S(1)}, f32[22528,128]{1,0:T(8,128)}, u32[]{:S(2)}) copy-start(f32[22528,128]{1,0:T(8,128)} %get-tuple-element.18.force_ref) | copy-start | bytes 34603012

commit v11 on v10

--- a/solution.py
+++ b/solution.py
@@ -31,6 +31,7 @@
 
 DEPTH, CHARGE, ONE, NORM, LAST = 3, 4, 5, 6, 7
 FAR_PIECES = (0, 1, 2, 0, 1, 0)
+USED = 8 * len(FAR_PIECES)
 NEAR_PIECES = (0, 0, 0, 1, 1, 2)
 
 
@@ -67,7 +68,6 @@
 def fill_blocks(block_at, count, shift, table, first):
     sublane = lax.broadcasted_iota(I32, (8, LANES), 0)
     move = jnp.where(sublane < 3, jnp.where(sublane == 0, shift - CENTRE, -CENTRE), 0.0)
-    blank = jnp.zeros((LANES - 8 * len(FAR_PIECES), LANES), F32)
     for block in range(count):
         values = block_at(block) + move
         norm = jnp.sum(jnp.where(sublane < 3, values * values, 0.0), axis=0, keepdims=True)
@@ -77,21 +77,22 @@
             parts.append(rest.astype(BF16).astype(F32))
             rest = rest - parts[-1]
         parts.append(rest)
-        rows = jnp.concatenate([parts[piece] for piece in FAR_PIECES] + [blank], axis=0)
+        rows = jnp.concatenate([parts[piece] for piece in FAR_PIECES], axis=0)
         start = pl.multiple_of(first + block * LANES + PAD, PAD)
-        table[pl.ds(start, LANES), :] = rows.T
+        table[pl.ds(start, LANES), 0:USED] = rows.T
 
 
 def sublane_masks():
     sublane = lax.broadcasted_iota(I32, (8, LANES), 0)
-    return [sublane == k for k in range(8)]
+    used = lax.broadcasted_iota(I32, (8, LANES), 1) < USED
+    return [sublane == k for k in range(8)] + [used]
 
 
 def merged(table, entries, masks):
     result = table[pl.ds(entries[0] + PAD, 8), :]
     for k in range(1, 8):
         result = jnp.where(masks[k], table[pl.ds(entries[k] + (PAD - k), 8), :], result)
-    return result
+    return jnp.where(masks[8], result, 0.0)
 
 
 def copy_rows(table, entry_of, stage, start, masks):
@@ -99,7 +100,7 @@
     stage[start : start + 16, :] = jnp.concatenate(parts, axis=0).astype(BF16)
 
 
-def near_kernel(rows, order_ref, fields_ref, select_ref, table_ref, left_ref, table, stage_a, stage_b):
+def near_kernel(rows, order_ref, next_ref, fields_ref, select_ref, table_ref, left_ref, table, stage_a, stage_b):
     turn = pl.program_id(0)
 
     @pl.when(turn == 0)
@@ -112,9 +113,11 @@
 
     masks = sublane_masks()
 
-    def load(tile, stage):
+    def load(local, stage):
+        ref, first = (order_ref, local) if local < 8 else (next_ref, local - 8)
+
         def entry_of(k):
-            return order_ref[tile * TILE + k]
+            return ref[first * TILE + k]
 
         return [
             functools.partial(copy_rows, table, entry_of, stage, start, masks) for start in range(0, TILE, 16)
@@ -131,22 +134,13 @@
             for copy in load(side, stage_a.at[side]):
                 copy()
 
-    def step(part, carry):
-        tile = turn * 8 + part * 4
-        last = rows - 1
+    for tile in range(0, 8, 2):
+        here, there = (stage_a, stage_b) if tile % 4 == 0 else (stage_b, stage_a)
         weave(
-            [factors(part * 4 + side, stage_a.at[side]) for side in range(2)],
-            load(tile + 2, stage_b.at[0]) + load(tile + 3, stage_b.at[1]),
+            [factors(tile + side, here.at[side]) for side in range(2)],
+            load(tile + 2, there.at[0]) + load(tile + 3, there.at[1]),
             1,
         )
-        weave(
-            [factors(part * 4 + 2 + side, stage_b.at[side]) for side in range(2)],
-            load(jnp.minimum(tile + 4, last), stage_a.at[0]) + load(jnp.minimum(tile + 5, last), stage_a.at[1]),
-            1,
-        )
-        return carry
-
-    lax.fori_loop(0, 2, step, 0)
     table_ref[...] = table[pl.ds(pl.multiple_of(turn * 8 * LANES + PAD, PAD), 8 * LANES), :]
 
 
@@ -187,7 +181,7 @@
 
 
 def force_kernel(
-    rows, partner_ref, entry_ref, order_ref, lower_ref, upper_ref, place_ref, kinds_ref, left_ref, own_ref,
+    rows, partner_ref, next_ref, entry_ref, order_ref, before_ref, lower_ref, upper_ref, place_ref, kinds_ref, left_ref, own_ref,
     force_ref, solute_ref, table, forces, far_a, far_b, sum_a, sum_b, arrival,
 ):
     turn = pl.program_id(0)
@@ -196,20 +190,24 @@
 
     masks = sublane_masks()
 
-    def load(tile, far):
+    def load(local, far):
+        ref, first = (partner_ref, local) if local < 8 else (next_ref, local - 8)
+
         def entry_of(k):
-            return entry_ref[partner_ref[tile * partners + k]]
+            return entry_ref[ref[first * partners + k]]
 
         return [
             functools.partial(copy_rows, table, entry_of, far, start, masks)
             for start in range(0, partners, 16)
         ]
 
-    def save(tile, sums):
+    def save(local, sums):
+        ref, first = (order_ref, local) if local >= 0 else (before_ref, local + 8)
+
         def copy(block):
             value = sums[block * 8 : block * 8 + 8, :]
             for k in range(8):
-                place = order_ref[tile * TILE + block * 8 + k] + (FORCE_PAD - k)
+                place = ref[first * TILE + block * 8 + k] + (FORCE_PAD - k)
                 pltpu.store(forces.at[pl.ds(place, 8), :], value, mask=masks[k])
 
         return [functools.partial(copy, block) for block in range(TILE // 8)]
@@ -231,31 +229,22 @@
             for copy in load(side, far_a.at[side]):
                 copy()
 
-    def step(part, carry):
-        tile = turn * 8 + part * 4
-        last = rows - 1
-        copies = save(jnp.maximum(tile - 2, 0), sum_b.at[0]) + save(jnp.maximum(tile - 1, 0), sum_b.at[1])
-        copies += load(tile + 2, far_b.at[0]) + load(tile + 3, far_b.at[1])
+    for tile in range(0, 8, 2):
+        far, far_next, sums, sums_before = (
+            (far_a, far_b, sum_a, sum_b) if tile % 4 == 0 else (far_b, far_a, sum_b, sum_a)
+        )
+        copies = save(tile - 2, sums_before.at[0]) + save(tile - 1, sums_before.at[1])
+        copies += load(tile + 2, far_next.at[0]) + load(tile + 3, far_next.at[1])
         weave(
-            [tile_sums(left_ref, kinds_ref, part * 4 + side, far_a.at[side], sum_a.at[side]) for side in range(2)],
+            [tile_sums(left_ref, kinds_ref, tile + side, far.at[side], sums.at[side]) for side in range(2)],
             copies,
             7,
         )
-        copies = save(tile, sum_a.at[0]) + save(tile + 1, sum_a.at[1])
-        copies += load(jnp.minimum(tile + 4, last), far_a.at[0]) + load(jnp.minimum(tile + 5, last), far_a.at[1])
-        weave(
-            [tile_sums(left_ref, kinds_ref, part * 4 + 2 + side, far_b.at[side], sum_b.at[side]) for side in range(2)],
-            copies,
-            7,
-        )
-        return carry
-
-    lax.fori_loop(0, 2, step, 0)
 
     @pl.when(turn == pl.num_programs(0) - 1)
     def _():
         for side in range(2):
-            for copy in save(rows - 2 + side, sum_b.at[side]):
+            for copy in save(6 + side, sum_b.at[side]):
                 copy()
 
         send = pltpu.make_async_copy(forces, force_ref, arrival)
@@ -423,14 +412,20 @@
     )
     lower, upper = (blocks(side[: FIELDS * rows].reshape(FIELDS, rows, LANES)) for side in (lower, upper))
     order = cell_order.reshape(atoms)
+    pairs = tile_atoms.reshape(rows * partners)
     scalar = pl.BlockSpec(memory_space=pltpu.SMEM)
     vector = pl.BlockSpec(memory_space=pltpu.VMEM)
     params = pltpu.CompilerParams(vmem_limit_bytes=VMEM_LIMIT)
+    last = rows // 8 - 1
+
+    def listed(size, by):
+        return pl.BlockSpec((8 * size,), lambda i: (jnp.clip(i + by, 0, last),), memory_space=pltpu.SMEM)
+
     table, left = pl.pallas_call(
         functools.partial(near_kernel, rows),
         grid=(rows // 8,),
         out_shape=[whole(atoms, LANES), whole(rows, TILE, LANES, dtype=BF16)],
-        in_specs=[scalar] + [vector] * 2,
+        in_specs=[listed(TILE, 0), listed(TILE, 1)] + [vector] * 2,
         out_specs=[
             pl.BlockSpec((8 * LANES, LANES), lambda i: (i, 0)),
             pl.BlockSpec((8, TILE, LANES), lambda i: (i, 0, 0)),
@@ -442,12 +437,12 @@
         ],
         compiler_params=params,
         cost_estimate=pl.CostEstimate(flops=25 * 10**9, bytes_accessed=3 * 10**7, transcendentals=0),
-    )(order, blocks(fields), near_selector())
+    )(order, order, blocks(fields), near_selector())
     forces, solute = pl.pallas_call(
         functools.partial(force_kernel, rows),
         grid=(rows // 8,),
         out_shape=[whole(atoms + 2 * FORCE_PAD, LANES), whole(3, SOL_DEV // LANES, LANES)],
-        in_specs=[scalar] * 3
+        in_specs=[listed(partners, 0), listed(partners, 1), scalar, listed(TILE, 0), listed(TILE, -1)]
         + [vector] * 4
         + [pl.BlockSpec((8, TILE, LANES), lambda i: (i, 0, 0)), pl.BlockSpec(memory_space=pl.ANY)],
         out_specs=[pl.BlockSpec(memory_space=pl.ANY), vector],
@@ -462,7 +457,7 @@
         ],
         compiler_params=params,
         cost_estimate=pl.CostEstimate(flops=25 * 10**9, bytes_accessed=3 * 10**7, transcendentals=0),
-    )(tile_atoms.reshape(rows * partners), entries, order, lower, upper, places, near_masks(), left, table)
+    )(pairs, pairs, entries, order, order, lower, upper, places, near_masks(), left, table)
     solutes = round_trip(solute, "image")
     block = pl.BlockSpec((3, 8, LANES), lambda i: (0, i, 0))
     small = pltpu.CompilerParams(vmem_limit_bytes=8 * 1024 * 1024)

time: 173 us -> 164 us (0.948)
  Pallas kernels: 135 us -> 126 us
    pallas_call x1, Pallas kernels: 30.6 us -> 25.3 us  [per_device(): pl.pallas_call(functools.partial(near_kernel, rows), grid=(rows // 8,), o...]
    pallas_call x1, Pallas kernels: 96.1 us -> 92.2 us  [per_device(): pl.pallas_call(functools.partial(force_kernel, rows), grid=(rows // 8,),...]
  transfers between devices with their start and end apart: 11 -> 11, of which waited for: 4 -> 4; matrix products, arithmetic and copies ran while one was open for 5% -> 5% of each run, Pallas kernels for 78% -> 77%
where the time goes in v11:
time: 164 us; the launch traced here: 163 us
  Pallas kernels  126 us (77%)
  starting transfers between devices  12 us (7%)
  waiting for transfers between devices  9.56 us (6%)
  local copies, waits for them, and re-layouts  8.29 us (5%)
  other arithmetic  5.99 us (4%)
    pallas_call x1, Pallas kernels, per_device(): pl.pallas_call(functools.partial(force_kernel, rows), grid=(rows // 8,),...  92.2 us
    pallas_call x1, Pallas kernels, per_device(): pl.pallas_call(functools.partial(near_kernel, rows), grid=(rows // 8,), o...  25.3 us
    ppermute x8, starting transfers between devices, turned(): lax.ppermute(array, axis, [(i, (i + by) % count) for i in range(count)])  11.1 us
    pallas_call x1, Pallas kernels, per_device(): pl.pallas_call(relax_kernel, grid=(rows // 8,), out_shape=whole(3, rows,...  7.99 us
    ppermute x3, waiting for transfers between devices, summed(): lax.ppermute(array, axis, [(i, i ^ by) for i in range(count)])  7.46 us
    unnamed x11, local copies, waits for them, and re-layouts  5.75 us
  transfers between devices with their start and end apart: 11, of which 4 were waited for; matrix products, arithmetic and copies ran while one was open for 5% of the time, Pallas kernels for 77%

profile of v11, /device:TPU:0, one launch (start us, length us, event | category | flops | bytes accessed | tf_op | source)
XLA Modules:
  0.0 163.1 jit_solution(17201421043330683048)
XLA Ops:
  0.0 0.7 slice.36.refs_4_
  0.7 0.5 collective-permute-start.5
  1.2 2.5 %collective-permute-start.6 = (f32[3,8,128]{2,1,0:T(8,128)S(1)}, f32[3,8,128]{2,1,0:T(8,128)S(1)}, u32[]{:S(2)}, u32[]{:S(2)}) collective-permute-start(f32[3,8,128]{2,1,0:T(8,128)S(1)} %slice.36.refs_4_), channel_id=1, source_target_pairs={{0,16},{8,24},{16,0},{24,8},{1,17},{9,25},{17,1},{25,9},{2,18},{10... | collective-permute-start | bytes 36872 | tf_op jit(solution)/shard_map/ppermute | solution.py:366
  3.7 1.4 collective-permute-start.7
  5.8 0.9 convert_element_type.10
  6.8 0.9 fusion.3
  7.8 1.0 pad_maximum_fusion.4
  8.7 0.1 pad_maximum_fusion.2
  8.8 1.5 collective-permute-start
  10.3 3.2 %collective-permute-start.1 = (f32[880,128]{1,0:T(8,128)S(1)}, f32[880,128]{1,0:T(8,128)S(1)}, u32[]{:S(2)}, u32[]{:S(2)}) collective-permute-start(f32[880,128]{1,0:T(8,128)S(1)} %get-tuple-element.20), channel_id=1, source_target_pairs={{0,7},{1,0},{2,1},{3,2},{4,3},{5,4},{6,5},{7,6},{8,15},{9,8},{10,9... | collective-permute-start | bytes 1351688 | tf_op jit(solution)/shard_map/ppermute | solution.py:366
  13.6 1.1 maximum_bitcast_fusion
  14.7 1.3 copy.19.fields_ref
  15.9 0.0 copy-start.4
  15.9 0.0 copy-start.3
  15.9 25.3 %shard_map.91 = (f32[20480,128]{1,0:T(8,128)}, bf16[160,128,128]{2,1,0:T(8,128)(2,1)}) custom-call(s32[20480]{0:T(1024)} %bitcast.39, s32[20480]{0:T(1024)} %bitcast.40, f32[160,8,128]{2,1,0:T(8,128)} %copy.19.fields_ref, bf16[128,128]{1,0:T(8,128)(2,1)} %constant.23.clone.select_ref), custom_call_target="tpu_custom_call" | custom-call | flops 24999999488 | bytes 30000000 | tf_op jit(solution)/shard_map/pallas_call | solution.py:424
  41.3 0.0 copy-done.4
  41.3 0.8 copy.21
  42.0 0.0 collective-permute-done
  42.1 0.3 copy.15
  42.4 0.0 collective-permute-done.1
  42.4 0.3 copy.17
  42.7 0.0 copy-done.3
  42.7 1.2 fusion.1
  43.9 0.7 pad_add_fusion.entry_ref
  44.6 0.0 copy-start.1
  44.6 92.2 %shard_map.92 = (f32[22528,128]{1,0:T(8,128)}, f32[3,8,128]{2,1,0:T(8,128)}) custom-call(s32[40960]{0:T(1024)} %bitcast.37, s32[40960]{0:T(1024)} %bitcast.38, s32[40960]{0:T(1024)} %pad_add_fusion.entry_ref, s32[20480]{0:T(1024)} %bitcast.41, s32[20480]{0:T(1024)} %bitcast.42, f32[160,8,128]{2,1,0:T(8,128)} %get-tuple-element.22.lower_ref, ...), custom_call_target="tpu_custom_call" | custom-call | flops 24999999488 | bytes 30000000 | tf_op jit(solution)/shard_map/pallas_call | solution.py:441
  136.8 0.1 collective-permute-start.2
  136.9 0.5 collective-permute-start.3
  137.4 0.0 collective-permute-done.5.refs_5_
  137.4 1.4 collective-permute-start.4
  138.8 0.0 collective-permute-done.6.refs_6_
  138.8 0.0 collective-permute-done.7.refs_7_
  138.8 1.4 collective-permute-done.2.refs_1_
  140.2 0.7 collective-permute-done.3.refs_2_
  140.9 0.0 collective-permute-done.4.refs_3_
  140.9 0.7 copy-done.2
  141.6 0.1 shard_map.93
  141.7 0.1 collective-permute-start.8
  141.7 3.7 %collective-permute-done.8 = f32[32,128]{1,0:T(8,128)S(1)} collective-permute-done((f32[32,128]{1,0:T(8,128)S(1)}, f32[32,128]{1,0:T(8,128)S(1)}, u32[]{:S(2)}, u32[]{:S(2)}) %collective-permute-start.8) | collective-permute-done | bytes 16416 | tf_op jit(solution)/shard_map/ppermute | solution.py:375
  145.5 0.0 collective-permute-start.9
  145.5 3.7 %collective-permute-done.9 = f32[32,128]{1,0:T(8,128)S(1)} collective-permute-done((f32[32,128]{1,0:T(8,128)S(1)}, f32[32,128]{1,0:T(8,128)S(1)}, u32[]{:S(2)}, u32[]{:S(2)}) %collective-permute-start.9) | collective-permute-done | bytes 16416 | tf_op jit(solution)/shard_map/ppermute | solution.py:375
  149.2 0.8 collective-permute-start.10
  150.0 0.0 copy-done.1
  150.0 0.0 copy-start
  150.0 4.3 %copy-done = f32[22528,128]{1,0:T(8,128)S(1)} copy-done((f32[22528,128]{1,0:T(8,128)S(1)}, f32[22528,128]{1,0:T(8,128)}, u32[]{:S(2)}) %copy-start) | copy-done | bytes 11534360
  154.3 8.0 %shard_map.94.out_in = f32[3,160,128]{2,1,0:T(8,128)} custom-call(f32[3,160,128]{2,1,0:T(8,128)S(1)} %bitcast.30, f32[22528,128]{1,0:T(8,128)S(1)} %copy-done), custom_call_target="tpu_custom_call" | custom-call | flops 1000000000 | bytes 20000000 | tf_op jit(solution)/shard_map/pallas_call | solution.py:464
  162.3 0.0 collective-permute-done.10
  162.3 0.8 shard_map.95
  (10 shorter events, 0.1 us)
Async XLA Ops:
  0.7 136.7 %collective-permute-start.5 = (f32[3,8,128]{2,1,0:T(8,128)S(1)}, f32[3,8,128]{2,1,0:T(8,128)S(1)}, u32[]{:S(2)}, u32[]{:S(2)}) collective-permute-start(f32[3,8,128]{2,1,0:T(8,128)S(1)} %slice.36.refs_4_), channel_id=1, source_target_pairs={{0,8},{8,16},{16,24},{24,0},{1,9},{9,17},{17,25},{25,1},{2,10},{10... | collective-permute-start | bytes 36872 | tf_op jit(solution)/shard_map/ppermute | solution.py:366
  1.2 137.6 %collective-permute-start.6 = (f32[3,8,128]{2,1,0:T(8,128)S(1)}, f32[3,8,128]{2,1,0:T(8,128)S(1)}, u32[]{:S(2)}, u32[]{:S(2)}) collective-permute-start(f32[3,8,128]{2,1,0:T(8,128)S(1)} %slice.36.refs_4_), channel_id=1, source_target_pairs={{0,16},{8,24},{16,0},{24,8},{1,17},{9,25},{17,1},{25,9},{2,18},{10... | collective-permute-start | bytes 36872 | tf_op jit(solution)/shard_map/ppermute | solution.py:366
  3.7 135.1 %collective-permute-start.7 = (f32[3,8,128]{2,1,0:T(8,128)S(1)}, f32[3,8,128]{2,1,0:T(8,128)S(1)}, u32[]{:S(2)}, u32[]{:S(2)}) collective-permute-start(f32[3,8,128]{2,1,0:T(8,128)S(1)} %slice.36.refs_4_), channel_id=1, source_target_pairs={{0,24},{8,0},{16,8},{24,16},{1,25},{9,1},{17,9},{25,17},{2,26},{10... | collective-permute-start | bytes 36872 | tf_op jit(solution)/shard_map/ppermute | solution.py:366
  8.8 33.2 %collective-permute-start = (f32[880,128]{1,0:T(8,128)S(1)}, f32[880,128]{1,0:T(8,128)S(1)}, u32[]{:S(2)}, u32[]{:S(2)}) collective-permute-start(f32[880,128]{1,0:T(8,128)S(1)} %get-tuple-element.19), channel_id=1, source_target_pairs={{0,1},{1,2},{2,3},{3,4},{4,5},{5,6},{6,7},{7,0},{8,9},{9,10},{10,1... | collective-permute-start | bytes 1351688 | tf_op jit(solution)/shard_map/ppermute | solution.py:366
  10.3 32.0 %collective-permute-start.1 = (f32[880,128]{1,0:T(8,128)S(1)}, f32[880,128]{1,0:T(8,128)S(1)}, u32[]{:S(2)}, u32[]{:S(2)}) collective-permute-start(f32[880,128]{1,0:T(8,128)S(1)} %get-tuple-element.20), channel_id=1, source_target_pairs={{0,7},{1,0},{2,1},{3,2},{4,3},{5,4},{6,5},{7,6},{8,15},{9,8},{10,9... | collective-permute-start | bytes 1351688 | tf_op jit(solution)/shard_map/ppermute | solution.py:366
  15.9 25.3 %copy-start.4 = (s32[1,160,256]{2,1,0:T(8,128)S(1)}, s32[1,160,256]{2,1,0:T(8,128)}, u32[]{:S(2)}) copy-start(s32[1,160,256]{2,1,0:T(8,128)} %param.15) | copy-start | bytes 491524
  15.9 26.7 %copy-start.3 = (f32[3,160,128]{2,0,1:T(4,128)S(1)}, f32[3,160,128]{2,0,1:T(4,128)}, u32[]{:S(2)}) copy-start(f32[3,160,128]{2,0,1:T(4,128)} %constant.30) | copy-start | bytes 737284
  44.6 105.4 %copy-start.1 = (f32[1,3,20480]{2,0,1:T(1,128)S(1)}, f32[1,3,20480]{2,0,1:T(1,128)}, u32[]{:S(2)}) copy-start(f32[1,3,20480]{2,0,1:T(1,128)} %param.9) | copy-start | bytes 737284
  136.8 3.4 %collective-permute-start.2 = (f32[3,8,128]{2,1,0:T(8,128)}, f32[3,8,128]{2,1,0:T(8,128)S(1)}, u32[]{:S(2)}, u32[]{:S(2)}) collective-permute-start(f32[3,8,128]{2,1,0:T(8,128)} %get-tuple-element.14.refs_0_), channel_id=1, source_target_pairs={{0,8},{8,16},{16,24},{24,0},{1,9},{9,17},{17,25},{25,1},{2,10},{10... | collective-permute-start | bytes 36872 | tf_op jit(solution)/shard_map/ppermute | solution.py:366
  136.9 4.0 %collective-permute-start.3 = (f32[3,8,128]{2,1,0:T(8,128)}, f32[3,8,128]{2,1,0:T(8,128)S(1)}, u32[]{:S(2)}, u32[]{:S(2)}) collective-permute-start(f32[3,8,128]{2,1,0:T(8,128)} %get-tuple-element.14.refs_0_), channel_id=1, source_target_pairs={{0,16},{8,24},{16,0},{24,8},{1,17},{9,25},{17,1},{25,9},{2,18},{10... | collective-permute-start | bytes 36872 | tf_op jit(solution)/shard_map/ppermute | solution.py:366
  137.4 3.5 %collective-permute-start.4 = (f32[3,8,128]{2,1,0:T(8,128)}, f32[3,8,128]{2,1,0:T(8,128)S(1)}, u32[]{:S(2)}, u32[]{:S(2)}) collective-permute-start(f32[3,8,128]{2,1,0:T(8,128)} %get-tuple-element.14.refs_0_), channel_id=1, source_target_pairs={{0,24},{8,0},{16,8},{24,16},{1,25},{9,1},{17,9},{25,17},{2,26},{10... | collective-permute-start | bytes 36872 | tf_op jit(solution)/shard_map/ppermute | solution.py:366
  140.9 0.7 copy-start.2
  141.7 3.8 %collective-permute-start.8 = (f32[32,128]{1,0:T(8,128)S(1)}, f32[32,128]{1,0:T(8,128)S(1)}, u32[]{:S(2)}, u32[]{:S(2)}) collective-permute-start(f32[32,128]{1,0:T(8,128)S(1)} %get-tuple-element.15), channel_id=1, source_target_pairs={{0,1},{1,0},{2,3},{3,2},{4,5},{5,4},{6,7},{7,6},{8,9},{9,8},{10,11... | collective-permute-start | bytes 49160 | tf_op jit(solution)/shard_map/ppermute | solution.py:375
  145.5 3.7 %collective-permute-start.9 = (f32[32,128]{1,0:T(8,128)S(1)}, f32[32,128]{1,0:T(8,128)S(1)}, u32[]{:S(2)}, u32[]{:S(2)}) collective-permute-start(f32[32,128]{1,0:T(8,128)S(1)} %add.29), channel_id=1, source_target_pairs={{0,2},{1,3},{2,0},{3,1},{4,6},{5,7},{6,4},{7,5},{8,10},{9,11},{10,... | collective-permute-start | bytes 49160 | tf_op jit(solution)/shard_map/ppermute | solution.py:375
  149.2 13.1 %collective-permute-start.10 = (f32[32,128]{1,0:T(8,128)S(1)}, f32[32,128]{1,0:T(8,128)S(1)}, u32[]{:S(2)}, u32[]{:S(2)}) collective-permute-start(f32[32,128]{1,0:T(8,128)S(1)} %add.30), channel_id=1, source_target_pairs={{0,4},{1,5},{2,6},{3,7},{4,0},{5,1},{6,2},{7,3},{8,12},{9,13},{10,... | collective-permute-start | bytes 49160 | tf_op jit(solution)/shard_map/ppermute | solution.py:375
  150.0 4.3 %copy-start = (f32[22528,128]{1,0:T(8,128)S(1)}, f32[22528,128]{1,0:T(8,128)}, u32[]{:S(2)}) copy-start(f32[22528,128]{1,0:T(8,128)} %get-tuple-element.18.force_ref) | copy-start | bytes 34603012

commit v12 on v11

--- a/solution.py
+++ b/solution.py
@@ -1,4 +1,5 @@
 import functools
+import itertools
 
 import jax
 import jax.numpy as jnp
@@ -12,7 +13,6 @@
 TILE = 128
 LANES = 128
 FIELDS = 5
-FORCE_PAD = 1024
 PAD = 8
 
 LJ_COEF = 0.5
@@ -65,11 +65,13 @@
     return lax.dot_general(left, right, (((1,), (1,)), ((), ())), preferred_element_type=F32)
 
 
-def fill_blocks(block_at, count, shift, table, first):
+def fill_blocks(fields_ref, rows, start_row, count, shift, table, first):
     sublane = lax.broadcasted_iota(I32, (8, LANES), 0)
     move = jnp.where(sublane < 3, jnp.where(sublane == 0, shift - CENTRE, -CENTRE), 0.0)
+    ones = jnp.ones((8 - FIELDS, LANES), F32)
     for block in range(count):
-        values = block_at(block) + move
+        values = fields_ref[pl.ds(start_row + block, FIELDS, stride=rows), :]
+        values = jnp.concatenate([values, ones], axis=0) + move
         norm = jnp.sum(jnp.where(sublane < 3, values * values, 0.0), axis=0, keepdims=True)
         rest = jnp.where(sublane == NORM, -norm, values)
         parts = []
@@ -77,9 +79,9 @@
             parts.append(rest.astype(BF16).astype(F32))
             rest = rest - parts[-1]
         parts.append(rest)
-        rows = jnp.concatenate([parts[piece] for piece in FAR_PIECES], axis=0)
-        start = pl.multiple_of(first + block * LANES + PAD, PAD)
-        table[pl.ds(start, LANES), 0:USED] = rows.T
+        used = jnp.concatenate([parts[piece] for piece in FAR_PIECES], axis=0)
+        start = pl.multiple_of(first + (start_row + block) * LANES + PAD, PAD)
+        table[pl.ds(start, LANES), 0:USED] = used.T
 
 
 def sublane_masks():
@@ -89,9 +91,9 @@
 
 
 def merged(table, entries, masks):
-    result = table[pl.ds(entries[0] + PAD, 8), :]
+    result = table[pl.ds(entries[0], 8), :]
     for k in range(1, 8):
-        result = jnp.where(masks[k], table[pl.ds(entries[k] + (PAD - k), 8), :], result)
+        result = jnp.where(masks[k], table[pl.ds(entries[k], 8), :], result)
     return jnp.where(masks[8], result, 0.0)
 
 
@@ -100,16 +102,47 @@
     stage[start : start + 16, :] = jnp.concatenate(parts, axis=0).astype(BF16)
 
 
-def near_kernel(rows, order_ref, next_ref, fields_ref, select_ref, table_ref, left_ref, table, stage_a, stage_b):
+def near_kernel(
+    rows, order_ref, next_ref, lower_ref, upper_ref, partner_ref, fields_ref, select_ref, left_ref, list_ref,
+    table, stage_a, stage_b, lists,
+):
     turn = pl.program_id(0)
+    half = rows // 2
 
     @pl.when(turn == 0)
     def _():
+        for side, ref in enumerate((lower_ref, upper_ref)):
+            spot = slice(side * half, (side + 1) * half)
+            low = ref[...] & 255
+            lists[spot, 0:LANES] = (ref[...] - low).astype(F32).astype(BF16)
+            lists[spot, LANES:] = low.astype(F32).astype(BF16)
+
         def fill(group, carry):
-            fill_blocks(lambda block: fields_ref[group * 8 + block], 8, 0.0, table, group * 8 * LANES)
+            fill_blocks(fields_ref, rows, group * 8, 8, 0.0, table, 0)
             return carry
 
         lax.fori_loop(0, rows // 8, fill, 0)
+
+    def compose(tile):
+        entries = partner_ref[0, tile : tile + 1, :]
+        width = entries.shape[1]
+        grid = lax.broadcasted_iota(I32, (LANES, width), 0)
+        hot = jnp.where(grid == (entries & (LANES - 1)), 1.0, 0.0).astype(BF16)
+        found = jnp.dot(lists[...], jnp.concatenate([hot, hot], axis=0), preferred_element_type=F32)
+        yield
+        block = entries >> 7
+        low, high = block < half, block >= half + rows
+        chosen = jnp.where(low, block, jnp.where(high, block - rows, -8)) - lax.broadcasted_iota(I32, (8, width), 0)
+        picked = jnp.zeros((8, width), F32)
+        for start in range(0, rows, 8):
+            picked = jnp.where(chosen == start, found[start : start + 8], picked)
+        atom = jnp.sum(picked, axis=0, keepdims=True).astype(I32)
+        yield
+        atom = jnp.where(low, atom, jnp.where(high, atom + 2 * rows * LANES, entries + half * LANES))
+        atom = atom + PAD - (lax.broadcasted_iota(I32, (1, width), 1) & 7)
+        for side in range(width // LANES):
+            row = tile * (width // LANES) + side
+            list_ref[row : row + 1, :] = atom[:, side * LANES : (side + 1) * LANES]
 
     masks = sublane_masks()
 
@@ -137,11 +170,10 @@
     for tile in range(0, 8, 2):
         here, there = (stage_a, stage_b) if tile % 4 == 0 else (stage_b, stage_a)
         weave(
-            [factors(tile + side, here.at[side]) for side in range(2)],
+            [factors(tile + side, here.at[side]) for side in range(2)] + [compose(tile + side) for side in range(2)],
             load(tile + 2, there.at[0]) + load(tile + 3, there.at[1]),
-            1,
+            2,
         )
-    table_ref[...] = table[pl.ds(pl.multiple_of(turn * 8 * LANES + PAD, PAD), 8 * LANES), :]
 
 
 def tile_sums(left_ref, kinds_ref, place, far, sums):
@@ -170,31 +202,25 @@
 
 def weave(stages, copies, parts):
     size = -(-len(copies) // parts)
-    for turn, _ in enumerate(zip(*stages)):
+    for turn, _ in enumerate(itertools.zip_longest(*stages)):
         for copy in copies[turn * size : (turn + 1) * size]:
             copy()
-    for copy in copies[parts * size :]:
-        copy()
-    for stage in stages:
-        for _ in stage:
-            pass
 
 
 def force_kernel(
-    rows, partner_ref, next_ref, entry_ref, order_ref, before_ref, lower_ref, upper_ref, place_ref, kinds_ref, left_ref, own_ref,
-    force_ref, solute_ref, table, forces, far_a, far_b, sum_a, sum_b, arrival,
+    rows, list_ref, next_ref, order_ref, before_ref, lower_ref, fields_ref, upper_ref, kinds_ref, left_ref,
+    out_ref, solute_ref, table, forces, far_a, far_b, sum_a, sum_b,
 ):
     turn = pl.program_id(0)
     partners = far_a.shape[1]
     own = rows * LANES
-
     masks = sublane_masks()
 
     def load(local, far):
-        ref, first = (partner_ref, local) if local < 8 else (next_ref, local - 8)
+        ref, first = (list_ref, local) if local < 8 else (next_ref, local - 8)
 
         def entry_of(k):
-            return entry_ref[ref[first * partners + k]]
+            return ref[first * partners + k]
 
         return [
             functools.partial(copy_rows, table, entry_of, far, start, masks)
@@ -207,23 +233,19 @@
         def copy(block):
             value = sums[block * 8 : block * 8 + 8, :]
             for k in range(8):
-                place = ref[first * TILE + block * 8 + k] + (FORCE_PAD - k)
+                place = ref[first * TILE + block * 8 + k]
                 pltpu.store(forces.at[pl.ds(place, 8), :], value, mask=masks[k])
 
         return [functools.partial(copy, block) for block in range(TILE // 8)]
 
     @pl.when(turn == 0)
     def _():
-        own_copy = pltpu.make_async_copy(own_ref, table.at[pl.ds(own + PAD, own), :], arrival)
-        own_copy.start()
-
         def fill(group, carry):
-            for ref, first, shift in ((lower_ref, 0, -SLAB_WIDTH), (upper_ref, 2 * own, SLAB_WIDTH)):
-                fill_blocks(lambda block: ref[group * 4 + block], 4, shift, table, first + group * 4 * LANES)
+            for domain, ref in enumerate((lower_ref, fields_ref, upper_ref)):
+                fill_blocks(ref, rows, group * 4, 4, (domain - 1) * SLAB_WIDTH, table, domain * own)
             return carry
 
         lax.fori_loop(0, rows // 4, fill, 0)
-        own_copy.wait()
         sum_b[...] = jnp.zeros_like(sum_b)
         for side in range(2):
             for copy in load(side, far_a.at[side]):
@@ -247,14 +269,20 @@
             for copy in save(6 + side, sum_b.at[side]):
                 copy()
 
-        send = pltpu.make_async_copy(forces, force_ref, arrival)
-        send.start()
-        for row in range(SOL_DEV // LANES):
-            start = FORCE_PAD + row * LANES
-            force = row_forces(forces[start : start + LANES, :], [place_ref[axis, row : row + 1, :] for axis in range(3)])
-            for axis in range(3):
-                solute_ref[axis, row : row + 1, :] = place_ref[axis, row : row + 1, :] + STEP_SIZE * force[axis]
-        send.wait()
+        def finish(group, carry):
+            for local in range(8):
+                row = group * 8 + local
+                sums = forces[pl.ds(pl.multiple_of(row * LANES + PAD, PAD), LANES), :]
+                places = [fields_ref[pl.ds(axis * rows + row, 1), :] for axis in range(3)]
+                for axis, force in enumerate(row_forces(sums, places)):
+                    out_ref[axis, pl.ds(row, 1), :] = places[axis] + STEP_SIZE * force
+            return carry
+
+        lax.fori_loop(0, rows // 8, finish, 0)
+        solute = SOL_DEV // LANES
+        solute_ref[0:3] = out_ref[:, 0:solute, :]
+        for axis in range(3):
+            solute_ref[3 + axis] = fields_ref[axis * rows : axis * rows + solute, :]
 
 
 def row_forces(sums, places):
@@ -266,21 +294,13 @@
     return result
 
 
-def relax_kernel(place_ref, force_ref, out_ref):
-    for row in range(8):
-        places = [place_ref[axis, row : row + 1, :] for axis in range(3)]
-        for axis, force in enumerate(row_forces(force_ref[row * LANES : (row + 1) * LANES, :], places)):
-            out_ref[axis, row : row + 1, :] = places[axis] + STEP_SIZE * force
-
-
 def product_kernel(images, index_ref, *refs):
-    pushed_refs, path_refs = refs[:images], refs[images : 2 * images]
-    sums_ref, pushed, path = refs[2 * images :]
+    solute_refs, (sums_ref, pushed, path) = refs[:images], refs[images:]
     index = index_ref[0]
     for by in range(images):
         place = lax.rem(index + images - by, images)
-        pushed[place] = pushed_refs[by][...]
-        path[place] = path_refs[by][...]
+        pushed[place] = solute_refs[by][0:3]
+        path[place] = solute_refs[by][3:6]
     sums_ref[...] = jnp.zeros_like(sums_ref)
     last = images - 1
     tangents = [path[min(k + 1, last)] - path[max(k - 1, 0)] for k in range(images)]
@@ -384,7 +404,6 @@
 def per_device(positions, strength, charge, rest_scale, cell_order, ghost_index, tile_atoms):
     atoms = positions.shape[2]
     rows = atoms // LANES
-    half = atoms // 2
     partners = tile_atoms.shape[2]
     images = lax.axis_size("image")
     index = lax.axis_index("image").reshape(1)
@@ -392,27 +411,11 @@
     factor = jnp.where(jnp.arange(atoms) < SOL_DEV, jnp.sqrt(rest_scale[0]), 1.0)
     scaled = jnp.stack([strength * factor * LJ_COEF**0.5, charge * factor * CHARGE_COEF**0.5])
     places = positions.reshape(3, rows, LANES)
-    fields = jnp.concatenate([places, scaled.reshape(2, rows, LANES)])
-    constant = jnp.stack([jnp.full((rows, LANES), value, F32) for value in (1.0, 0.0, 1.0)])
-
-    def blocks(planes):
-        return jnp.concatenate([planes, constant]).transpose(1, 0, 2)
-
-    paths = round_trip(places[:, : SOL_DEV // LANES], "image")
-    shell = ghost_index.reshape(2, rows // 2, LANES).astype(F32)
-    planes = fields.reshape(FIELDS * rows, LANES)
-    lower = turned(jnp.concatenate([planes, shell[1]]), "space", 1)
-    upper = turned(jnp.concatenate([planes, shell[0]]), "space", -1)
-    entries = jnp.concatenate(
-        [
-            lower[FIELDS * rows :].astype(I32).reshape(half),
-            jnp.arange(atoms, 2 * atoms, dtype=I32),
-            upper[FIELDS * rows :].astype(I32).reshape(half) + 2 * atoms,
-        ]
-    )
-    lower, upper = (blocks(side[: FIELDS * rows].reshape(FIELDS, rows, LANES)) for side in (lower, upper))
-    order = cell_order.reshape(atoms)
-    pairs = tile_atoms.reshape(rows * partners)
+    fields = jnp.concatenate([places, scaled.reshape(2, rows, LANES)]).reshape(FIELDS * rows, LANES)
+    shell = ghost_index.reshape(2, rows // 2, LANES)
+    lower_list, upper_list = turned(shell[1], "space", 1), turned(shell[0], "space", -1)
+    lower, upper = turned(fields, "space", 1), turned(fields, "space", -1)
+    order = cell_order.reshape(atoms) + (PAD - jnp.arange(atoms, dtype=I32) % 8)
     scalar = pl.BlockSpec(memory_space=pltpu.SMEM)
     vector = pl.BlockSpec(memory_space=pltpu.VMEM)
     params = pltpu.CompilerParams(vmem_limit_bytes=VMEM_LIMIT)
@@ -421,63 +424,58 @@
     def listed(size, by):
         return pl.BlockSpec((8 * size,), lambda i: (jnp.clip(i + by, 0, last),), memory_space=pltpu.SMEM)
 
-    table, left = pl.pallas_call(
+    table = (atoms + 2 * PAD, LANES)
+    left, partner_rows = pl.pallas_call(
         functools.partial(near_kernel, rows),
         grid=(rows // 8,),
-        out_shape=[whole(atoms, LANES), whole(rows, TILE, LANES, dtype=BF16)],
-        in_specs=[listed(TILE, 0), listed(TILE, 1)] + [vector] * 2,
+        out_shape=[whole(rows, TILE, LANES, dtype=BF16), whole(rows * partners // LANES, LANES, dtype=I32)],
+        in_specs=[listed(TILE, 0), listed(TILE, 1)]
+        + [vector] * 2
+        + [pl.BlockSpec((1, 8, partners), lambda i: (0, i, 0))]
+        + [vector] * 2,
         out_specs=[
-            pl.BlockSpec((8 * LANES, LANES), lambda i: (i, 0)),
             pl.BlockSpec((8, TILE, LANES), lambda i: (i, 0, 0)),
+            pl.BlockSpec((8 * partners // LANES, LANES), lambda i: (i, 0)),
         ],
         scratch_shapes=[
-            pltpu.VMEM((atoms + 2 * PAD, LANES), F32),
+            pltpu.VMEM(table, F32),
             pltpu.VMEM((2, TILE, LANES), BF16),
             pltpu.VMEM((2, TILE, LANES), BF16),
+            pltpu.VMEM((rows, 2 * LANES), BF16),
         ],
         compiler_params=params,
-        cost_estimate=pl.CostEstimate(flops=25 * 10**9, bytes_accessed=3 * 10**7, transcendentals=0),
-    )(order, order, blocks(fields), near_selector())
-    forces, solute = pl.pallas_call(
+        cost_estimate=pl.CostEstimate(flops=25 * 10**9, bytes_accessed=10**7, transcendentals=0),
+    )(order, order, lower_list, upper_list, tile_atoms, fields, near_selector())
+    pairs = partner_rows.reshape(rows * partners)
+    out, solute = pl.pallas_call(
         functools.partial(force_kernel, rows),
         grid=(rows // 8,),
-        out_shape=[whole(atoms + 2 * FORCE_PAD, LANES), whole(3, SOL_DEV // LANES, LANES)],
-        in_specs=[listed(partners, 0), listed(partners, 1), scalar, listed(TILE, 0), listed(TILE, -1)]
+        out_shape=[whole(3, rows, LANES), whole(6, SOL_DEV // LANES, LANES)],
+        in_specs=[listed(partners, 0), listed(partners, 1), listed(TILE, 0), listed(TILE, -1)]
         + [vector] * 4
-        + [pl.BlockSpec((8, TILE, LANES), lambda i: (i, 0, 0)), pl.BlockSpec(memory_space=pl.ANY)],
-        out_specs=[pl.BlockSpec(memory_space=pl.ANY), vector],
+        + [pl.BlockSpec((8, TILE, LANES), lambda i: (i, 0, 0))],
+        out_specs=[vector] * 2,
         scratch_shapes=[
             pltpu.VMEM((3 * atoms + 2 * PAD, LANES), F32),
-            pltpu.VMEM((atoms + 2 * FORCE_PAD, LANES), F32),
+            pltpu.VMEM(table, F32),
             pltpu.VMEM((2, partners, LANES), BF16),
             pltpu.VMEM((2, partners, LANES), BF16),
             pltpu.VMEM((2, TILE, LANES), F32),
             pltpu.VMEM((2, TILE, LANES), F32),
-            pltpu.SemaphoreType.DMA,
         ],
         compiler_params=params,
-        cost_estimate=pl.CostEstimate(flops=25 * 10**9, bytes_accessed=3 * 10**7, transcendentals=0),
-    )(pairs, pairs, entries, order, order, lower, upper, places, near_masks(), left, table)
+        cost_estimate=pl.CostEstimate(flops=25 * 10**9, bytes_accessed=10**7, transcendentals=0),
+    )(pairs, pairs, order, order, lower, fields, upper, near_masks(), left)
     solutes = round_trip(solute, "image")
-    block = pl.BlockSpec((3, 8, LANES), lambda i: (0, i, 0))
     small = pltpu.CompilerParams(vmem_limit_bytes=8 * 1024 * 1024)
-    out = pl.pallas_call(
-        relax_kernel,
-        grid=(rows // 8,),
-        out_shape=whole(3, rows, LANES),
-        in_specs=[block, pl.BlockSpec((8 * LANES, LANES), lambda i: (i + FORCE_PAD // (8 * LANES), 0))],
-        out_specs=block,
-        compiler_params=small,
-        cost_estimate=pl.CostEstimate(flops=10**9, bytes_accessed=2 * 10**7, transcendentals=0),
-    )(places, forces)
     solute_shape = whole(images, 3, SOL_DEV // LANES, LANES)
     sums, pushed, path = pl.pallas_call(
         functools.partial(product_kernel, images),
         out_shape=[whole(-(-7 * images // 8) * 8, LANES), solute_shape, solute_shape],
-        in_specs=[scalar] + [vector] * (2 * images),
+        in_specs=[scalar] + [vector] * images,
         out_specs=[vector] * 3,
         compiler_params=small,
-    )(index, *solutes, *paths)
+    )(index, *solutes)
     out = pl.pallas_call(
         functools.partial(blend_kernel, images),
         grid=(1,),

time: 164 us -> 156 us (0.951)
  Pallas kernels: 126 us -> 110 us
  waiting for transfers between devices: 9.56 us -> 20.9 us
  starting transfers between devices: 12 us -> 18.1 us
  local copies, waits for them, and re-layouts: 8.29 us -> 3.05 us
  other arithmetic: 5.99 us -> 3.47 us
    pallas_call x1, Pallas kernels: 92.2 us -> 80 us  [per_device(): pl.pallas_call(functools.partial(force_kernel, rows), grid=(rows // 8,),...]
    ppermute x8 -> x7, waiting for transfers between devices: 2.1 us -> 13 us  [turned(): lax.ppermute(array, axis, [(i, (i + by) % count) for i in range(count)])]
    pallas_call x1 -> x0, Pallas kernels: 7.99 us -> none  [per_device(): pl.pallas_call(relax_kernel, grid=(rows // 8,), out_shape=whole(3, rows,...]
    pallas_call x1, Pallas kernels: 25.3 us -> 28.9 us  [per_device(): pl.pallas_call(functools.partial(near_kernel, rows), grid=(rows // 8,), o...]
    unnamed x11 -> x12, local copies, waits for them, and re-layouts: 5.75 us -> 2.25 us
    ppermute x3, starting transfers between devices: 0.88 us -> 4.28 us  [summed(): lax.ppermute(array, axis, [(i, i ^ by) for i in range(count)])]
    ppermute x8 -> x7, starting transfers between devices: 11.1 us -> 13.8 us  [turned(): lax.ppermute(array, axis, [(i, (i + by) % count) for i in range(count)])]
    transpose x2 -> x0, other arithmetic: 2.35 us -> none  [blocks(): return jnp.concatenate([planes, constant]).transpose(1, 0, 2)]
  transfers between devices with their start and end apart: 11 -> 10, of which waited for: 4 -> 8; matrix products, arithmetic and copies ran while one was open for 5% -> 1% of each run, Pallas kernels for 77% -> 19%
where the time goes in v12:
time: 156 us
  Pallas kernels  110 us (71%)
  waiting for transfers between devices  20.9 us (13%)
  starting transfers between devices  18.1 us (12%)
  other arithmetic  3.47 us (2%)
  local copies, waits for them, and re-layouts  3.05 us (2%)
    pallas_call x1, Pallas kernels, per_device(): pl.pallas_call(functools.partial(force_kernel, rows), grid=(rows // 8,),...  80 us
    pallas_call x1, Pallas kernels, per_device(): pl.pallas_call(functools.partial(near_kernel, rows), grid=(rows // 8,), o...  28.9 us
    ppermute x7, starting transfers between devices, turned(): lax.ppermute(array, axis, [(i, (i + by) % count) for i in range(count)])  13.8 us
    ppermute x7, waiting for transfers between devices, turned(): lax.ppermute(array, axis, [(i, (i + by) % count) for i in range(count)])  13 us
    ppermute x3, waiting for transfers between devices, summed(): lax.ppermute(array, axis, [(i, i ^ by) for i in range(count)])  7.9 us
    ppermute x3, starting transfers between devices, summed(): lax.ppermute(array, axis, [(i, i ^ by) for i in range(count)])  4.28 us
  transfers between devices with their start and end apart: 10, of which 8 were waited for; matrix products, arithmetic and copies ran while one was open for 1% of the time, Pallas kernels for 19%

profile of v12, /device:TPU:0, one launch (start us, length us, event | category | flops | bytes accessed | tf_op | source)
XLA Modules:
  0.0 156.1 jit_solution(15792355935897829376)
XLA Ops:
  0.7 0.9 fusion.1
  1.6 1.0 pad_maximum_fusion
  2.6 0.0 copy-start.1
  2.6 3.0 %collective-permute-start.2 = (f32[800,128]{1,0:T(8,128)S(1)}, f32[800,128]{1,0:T(8,128)S(1)}, u32[]{:S(2)}, u32[]{:S(2)}) collective-permute-start(f32[800,128]{1,0:T(8,128)S(1)} %bitcast.13), channel_id=1, source_target_pairs={{0,1},{1,2},{2,3},{3,4},{4,5},{5,6},{6,7},{7,0},{8,9},{9,10},{10,1... | collective-permute-start | bytes 1228808 | tf_op jit(solution)/shard_map/ppermute | solution.py:386
  5.6 3.1 %collective-permute-start.3 = (f32[800,128]{1,0:T(8,128)S(1)}, f32[800,128]{1,0:T(8,128)S(1)}, u32[]{:S(2)}, u32[]{:S(2)}) collective-permute-start(f32[800,128]{1,0:T(8,128)S(1)} %bitcast.14), channel_id=1, source_target_pairs={{0,7},{1,0},{2,1},{3,2},{4,3},{5,4},{6,5},{7,6},{8,15},{9,8},{10,9... | collective-permute-start | bytes 1228808 | tf_op jit(solution)/shard_map/ppermute | solution.py:386
  8.7 0.8 fusion.9
  9.5 0.0 collective-permute-start
  9.5 4.7 %collective-permute-start.1 = (s32[80,128]{1,0:T(8,128)S(1)}, s32[80,128]{1,0:T(8,128)S(1)}, u32[]{:S(2)}, u32[]{:S(2)}) collective-permute-start(s32[80,128]{1,0:T(8,128)S(1)} %bitcast.19), channel_id=1, source_target_pairs={{0,7},{1,0},{2,1},{3,2},{4,3},{5,4},{6,5},{7,6},{8,15},{9,8},{10,9... | collective-permute-start | bytes 122888 | tf_op jit(solution)/shard_map/ppermute | solution.py:386
  14.3 1.5 fusion.5.order_ref.next_ref.before_ref
  15.8 9.1 %collective-permute-done.lower_ref = s32[80,128]{1,0:T(8,128)S(1)} collective-permute-done((s32[80,128]{1,0:T(8,128)S(1)}, s32[80,128]{1,0:T(8,128)S(1)}, u32[]{:S(2)}, u32[]{:S(2)}) %collective-permute-start) | collective-permute-done | bytes 40992 | tf_op jit(solution)/shard_map/ppermute | solution.py:386
  24.9 0.0 copy-start.4
  24.9 2.2 %collective-permute-done.1.upper_ref = s32[80,128]{1,0:T(8,128)S(1)} collective-permute-done((s32[80,128]{1,0:T(8,128)S(1)}, s32[80,128]{1,0:T(8,128)S(1)}, u32[]{:S(2)}, u32[]{:S(2)}) %collective-permute-start.1) | collective-permute-done | bytes 40992 | tf_op jit(solution)/shard_map/ppermute | solution.py:386
  27.1 0.0 copy-done.1
  27.1 0.0 copy-done.4
  27.1 0.0 copy-start.5
  27.1 0.6 copy-done.5
  27.7 28.9 %shard_map.91 = (bf16[160,128,128]{2,1,0:T(8,128)(2,1)}, s32[320,128]{1,0:T(8,128)}) custom-call(s32[20480]{0:T(1024)} %fusion.5.order_ref.next_ref.before_ref, s32[20480]{0:T(1024)} %fusion.5.order_ref.next_ref.before_ref, s32[80,128]{1,0:T(8,128)} %copy-done.4, s32[80,128]{1,0:T(8,128)} %copy-done.5, s32[1,160,256]{2,1,0:T(8,128)} %partner_ref.1, ...), custom_call_target="tpu_custom_call" | custom-call | flops 24999999488 | bytes 10000000 | tf_op jit(solution)/shard_map/pallas_call | solution.py:428
  56.6 0.0 collective-permute-done.2.lower_ref
  56.6 0.0 copy-start.2
  56.7 0.0 collective-permute-done.3.upper_ref
  56.7 0.0 copy-start.3
  56.7 0.7 copy-done.2
  57.4 0.2 copy-done.3
  57.6 80.0 %shard_map.92 = (f32[3,160,128]{2,1,0:T(8,128)}, f32[6,8,128]{2,1,0:T(8,128)}) custom-call(s32[40960]{0:T(1024)} %bitcast.21, s32[40960]{0:T(1024)} %bitcast.22, s32[20480]{0:T(1024)} %fusion.5.order_ref.next_ref.before_ref, s32[20480]{0:T(1024)} %fusion.5.order_ref.next_ref.before_ref, f32[800,128]{1,0:T(8,128)} %copy-done.2, f32[800,128]{1,0:T(8,128)} %bitcast.16, ...), custom_call_target="tpu_custom_call" | custom-call | flops 24999999488 | bytes 10000000 | tf_op jit(solution)/shard_map/pallas_call | solution.py:450
  137.6 0.0 collective-permute-start.4
  137.6 1.6 %collective-permute-start.5 = (f32[6,8,128]{2,1,0:T(8,128)}, f32[6,8,128]{2,1,0:T(8,128)S(1)}, u32[]{:S(2)}, u32[]{:S(2)}) collective-permute-start(f32[6,8,128]{2,1,0:T(8,128)} %get-tuple-element.14.refs_0_), channel_id=1, source_target_pairs={{0,16},{8,24},{16,0},{24,8},{1,17},{9,25},{17,1},{25,9},{2,18},{10... | collective-permute-start | bytes 73736 | tf_op jit(solution)/shard_map/ppermute | solution.py:386
  139.2 1.4 collective-permute-start.6
  140.6 0.4 collective-permute-done.4.refs_1_
  141.0 0.6 collective-permute-done.5.refs_2_
  141.7 0.6 collective-permute-done.6.refs_3_
  142.3 0.0 copy-start
  142.3 0.7 copy-done
  143.1 0.1 shard_map.93
  143.1 0.8 collective-permute-start.7
  144.0 3.0 %collective-permute-done.7 = f32[32,128]{1,0:T(8,128)S(1)} collective-permute-done((f32[32,128]{1,0:T(8,128)S(1)}, f32[32,128]{1,0:T(8,128)S(1)}, u32[]{:S(2)}, u32[]{:S(2)}) %collective-permute-start.7) | collective-permute-done | bytes 16416 | tf_op jit(solution)/shard_map/ppermute | solution.py:395
  146.9 1.3 collective-permute-start.8
  148.2 2.5 %collective-permute-done.8 = f32[32,128]{1,0:T(8,128)S(1)} collective-permute-done((f32[32,128]{1,0:T(8,128)S(1)}, f32[32,128]{1,0:T(8,128)S(1)}, u32[]{:S(2)}, u32[]{:S(2)}) %collective-permute-start.8) | collective-permute-done | bytes 16416 | tf_op jit(solution)/shard_map/ppermute | solution.py:395
  150.7 2.2 %collective-permute-start.9 = (f32[32,128]{1,0:T(8,128)S(1)}, f32[32,128]{1,0:T(8,128)S(1)}, u32[]{:S(2)}, u32[]{:S(2)}) collective-permute-start(f32[32,128]{1,0:T(8,128)S(1)} %add.21), channel_id=1, source_target_pairs={{0,4},{1,5},{2,6},{3,7},{4,0},{5,1},{6,2},{7,3},{8,12},{9,13},{10,... | collective-permute-start | bytes 49160 | tf_op jit(solution)/shard_map/ppermute | solution.py:395
  152.8 2.5 %collective-permute-done.9 = f32[32,128]{1,0:T(8,128)S(1)} collective-permute-done((f32[32,128]{1,0:T(8,128)S(1)}, f32[32,128]{1,0:T(8,128)S(1)}, u32[]{:S(2)}, u32[]{:S(2)}) %collective-permute-start.9) | collective-permute-done | bytes 16416 | tf_op jit(solution)/shard_map/ppermute | solution.py:395
  155.3 0.8 shard_map.94
  (3 shorter events, 0.0 us)
Async XLA Ops:
  2.6 24.5 %copy-start.1 = (f32[5,160,128]{2,1,0:T(8,128)}, f32[5,160,128]{2,1,0:T(8,128)S(1)}, u32[]{:S(2)}) copy-start(f32[5,160,128]{2,1,0:T(8,128)S(1)} %pad_maximum_fusion) | copy-start | bytes 1228804
  2.6 54.0 %collective-permute-start.2 = (f32[800,128]{1,0:T(8,128)S(1)}, f32[800,128]{1,0:T(8,128)S(1)}, u32[]{:S(2)}, u32[]{:S(2)}) collective-permute-start(f32[800,128]{1,0:T(8,128)S(1)} %bitcast.13), channel_id=1, source_target_pairs={{0,1},{1,2},{2,3},{3,4},{4,5},{5,6},{6,7},{7,0},{8,9},{9,10},{10,1... | collective-permute-start | bytes 1228808 | tf_op jit(solution)/shard_map/ppermute | solution.py:386
  5.6 51.0 %collective-permute-start.3 = (f32[800,128]{1,0:T(8,128)S(1)}, f32[800,128]{1,0:T(8,128)S(1)}, u32[]{:S(2)}, u32[]{:S(2)}) collective-permute-start(f32[800,128]{1,0:T(8,128)S(1)} %bitcast.14), channel_id=1, source_target_pairs={{0,7},{1,0},{2,1},{3,2},{4,3},{5,4},{6,5},{7,6},{8,15},{9,8},{10,9... | collective-permute-start | bytes 1228808 | tf_op jit(solution)/shard_map/ppermute | solution.py:386
  9.5 15.3 %collective-permute-start = (s32[80,128]{1,0:T(8,128)S(1)}, s32[80,128]{1,0:T(8,128)S(1)}, u32[]{:S(2)}, u32[]{:S(2)}) collective-permute-start(s32[80,128]{1,0:T(8,128)S(1)} %bitcast.20), channel_id=1, source_target_pairs={{0,1},{1,2},{2,3},{3,4},{4,5},{5,6},{6,7},{7,0},{8,9},{9,10},{10,1... | collective-permute-start | bytes 122888 | tf_op jit(solution)/shard_map/ppermute | solution.py:386
  9.5 17.5 %collective-permute-start.1 = (s32[80,128]{1,0:T(8,128)S(1)}, s32[80,128]{1,0:T(8,128)S(1)}, u32[]{:S(2)}, u32[]{:S(2)}) collective-permute-start(s32[80,128]{1,0:T(8,128)S(1)} %bitcast.19), channel_id=1, source_target_pairs={{0,7},{1,0},{2,1},{3,2},{4,3},{5,4},{6,5},{7,6},{8,15},{9,8},{10,9... | collective-permute-start | bytes 122888 | tf_op jit(solution)/shard_map/ppermute | solution.py:386
  24.9 2.2 %copy-start.4 = (s32[80,128]{1,0:T(8,128)}, s32[80,128]{1,0:T(8,128)S(1)}, u32[]{:S(2)}) copy-start(s32[80,128]{1,0:T(8,128)S(1)} %collective-permute-done.lower_ref) | copy-start | bytes 122884
  27.1 0.6 copy-start.5
  56.6 0.8 copy-start.2
  56.7 0.9 copy-start.3
  137.6 3.5 %collective-permute-start.4 = (f32[6,8,128]{2,1,0:T(8,128)}, f32[6,8,128]{2,1,0:T(8,128)S(1)}, u32[]{:S(2)}, u32[]{:S(2)}) collective-permute-start(f32[6,8,128]{2,1,0:T(8,128)} %get-tuple-element.14.refs_0_), channel_id=1, source_target_pairs={{0,8},{8,16},{16,24},{24,0},{1,9},{9,17},{17,25},{25,1},{2,10},{10... | collective-permute-start | bytes 73736 | tf_op jit(solution)/shard_map/ppermute | solution.py:386
  137.6 4.1 %collective-permute-start.5 = (f32[6,8,128]{2,1,0:T(8,128)}, f32[6,8,128]{2,1,0:T(8,128)S(1)}, u32[]{:S(2)}, u32[]{:S(2)}) collective-permute-start(f32[6,8,128]{2,1,0:T(8,128)} %get-tuple-element.14.refs_0_), channel_id=1, source_target_pairs={{0,16},{8,24},{16,0},{24,8},{1,17},{9,25},{17,1},{25,9},{2,18},{10... | collective-permute-start | bytes 73736 | tf_op jit(solution)/shard_map/ppermute | solution.py:386
  139.2 3.1 %collective-permute-start.6 = (f32[6,8,128]{2,1,0:T(8,128)}, f32[6,8,128]{2,1,0:T(8,128)S(1)}, u32[]{:S(2)}, u32[]{:S(2)}) collective-permute-start(f32[6,8,128]{2,1,0:T(8,128)} %get-tuple-element.14.refs_0_), channel_id=1, source_target_pairs={{0,24},{8,0},{16,8},{24,16},{1,25},{9,1},{17,9},{25,17},{2,26},{10... | collective-permute-start | bytes 73736 | tf_op jit(solution)/shard_map/ppermute | solution.py:386
  142.3 0.7 copy-start
  143.1 3.8 %collective-permute-start.7 = (f32[32,128]{1,0:T(8,128)S(1)}, f32[32,128]{1,0:T(8,128)S(1)}, u32[]{:S(2)}, u32[]{:S(2)}) collective-permute-start(f32[32,128]{1,0:T(8,128)S(1)} %get-tuple-element.15), channel_id=1, source_target_pairs={{0,1},{1,0},{2,3},{3,2},{4,5},{5,4},{6,7},{7,6},{8,9},{9,8},{10,11... | collective-permute-start | bytes 49160 | tf_op jit(solution)/shard_map/ppermute | solution.py:395
  146.9 3.7 %collective-permute-start.8 = (f32[32,128]{1,0:T(8,128)S(1)}, f32[32,128]{1,0:T(8,128)S(1)}, u32[]{:S(2)}, u32[]{:S(2)}) collective-permute-start(f32[32,128]{1,0:T(8,128)S(1)} %add.20), channel_id=1, source_target_pairs={{0,2},{1,3},{2,0},{3,1},{4,6},{5,7},{6,4},{7,5},{8,10},{9,11},{10,... | collective-permute-start | bytes 49160 | tf_op jit(solution)/shard_map/ppermute | solution.py:395
  150.7 4.6 %collective-permute-start.9 = (f32[32,128]{1,0:T(8,128)S(1)}, f32[32,128]{1,0:T(8,128)S(1)}, u32[]{:S(2)}, u32[]{:S(2)}) collective-permute-start(f32[32,128]{1,0:T(8,128)S(1)} %add.21), channel_id=1, source_target_pairs={{0,4},{1,5},{2,6},{3,7},{4,0},{5,1},{6,2},{7,3},{8,12},{9,13},{10,... | collective-permute-start | bytes 49160 | tf_op jit(solution)/shard_map/ppermute | solution.py:395

commit v13 on v12

--- a/solution.py
+++ b/solution.py
@@ -414,6 +414,7 @@
     fields = jnp.concatenate([places, scaled.reshape(2, rows, LANES)]).reshape(FIELDS * rows, LANES)
     shell = ghost_index.reshape(2, rows // 2, LANES)
     lower_list, upper_list = turned(shell[1], "space", 1), turned(shell[0], "space", -1)
+    fields, lower_list, upper_list = lax.optimization_barrier((fields, lower_list, upper_list))
     lower, upper = turned(fields, "space", 1), turned(fields, "space", -1)
     order = cell_order.reshape(atoms) + (PAD - jnp.arange(atoms, dtype=I32) % 8)
     scalar = pl.BlockSpec(memory_space=pltpu.SMEM)

time: 156 us -> 145 us (0.929)
  waiting for transfers between devices: 20.9 us -> 13.8 us
  starting transfers between devices: 18.1 us -> 13.9 us
    ppermute x7, waiting for transfers between devices: 13 us -> 1.74 us  [turned(): lax.ppermute(array, axis, [(i, (i + by) % count) for i in range(count)])]
    ppermute x3, starting transfers between devices: 4.28 us -> 0.08 us  [summed(): lax.ppermute(array, axis, [(i, i ^ by) for i in range(count)])]
    ppermute x3, waiting for transfers between devices: 7.9 us -> 12.1 us  [summed(): lax.ppermute(array, axis, [(i, i ^ by) for i in range(count)])]
  transfers between devices with their start and end apart: 10 -> 10, of which waited for: 8 -> 6; matrix products, arithmetic and copies ran while one was open for 1% -> 2% of each run, Pallas kernels for 19% -> 20%
where the time goes in v13:
time: 145 us; the launch traced here: 144 us
  Pallas kernels  110 us (76%)
  starting transfers between devices  13.9 us (10%)
  waiting for transfers between devices  13.8 us (10%)
  other arithmetic  3.47 us (2%)
  local copies, waits for them, and re-layouts  2.44 us (2%)
    pallas_call x1, Pallas kernels, per_device(): pl.pallas_call(functools.partial(force_kernel, rows), grid=(rows // 8,),...  80 us
    pallas_call x1, Pallas kernels, per_device(): pl.pallas_call(functools.partial(near_kernel, rows), grid=(rows // 8,), o...  29 us
    ppermute x7, starting transfers between devices, turned(): lax.ppermute(array, axis, [(i, (i + by) % count) for i in range(count)])  13.9 us
    ppermute x3, waiting for transfers between devices, summed(): lax.ppermute(array, axis, [(i, i ^ by) for i in range(count)])  12.1 us
  transfers between devices with their start and end apart: 10, of which 6 were waited for; matrix products, arithmetic and copies ran while one was open for 2% of the time, Pallas kernels for 20%

profile of v13, /device:TPU:0, one launch (start us, length us, event | category | flops | bytes accessed | tf_op | source)
XLA Modules:
  0.0 144.3 jit_solution(4083030451382457509)
XLA Ops:
  0.0 0.8 fusion.9
  0.8 2.9 %collective-permute-start = (s32[80,128]{1,0:T(8,128)S(1)}, s32[80,128]{1,0:T(8,128)S(1)}, u32[]{:S(2)}, u32[]{:S(2)}) collective-permute-start(s32[80,128]{1,0:T(8,128)S(1)} %bitcast.20), channel_id=1, source_target_pairs={{0,1},{1,2},{2,3},{3,4},{4,5},{5,6},{6,7},{7,0},{8,9},{9,10},{10,1... | collective-permute-start | bytes 122888 | tf_op jit(solution)/shard_map/ppermute | solution.py:386
  3.7 3.1 %collective-permute-start.1 = (s32[80,128]{1,0:T(8,128)S(1)}, s32[80,128]{1,0:T(8,128)S(1)}, u32[]{:S(2)}, u32[]{:S(2)}) collective-permute-start(s32[80,128]{1,0:T(8,128)S(1)} %bitcast.19), channel_id=1, source_target_pairs={{0,7},{1,0},{2,1},{3,2},{4,3},{5,4},{6,5},{7,6},{8,15},{9,8},{10,9... | collective-permute-start | bytes 122888 | tf_op jit(solution)/shard_map/ppermute | solution.py:386
  7.5 1.5 %fusion.5.order_ref.next_ref.before_ref = s32[20480]{0:T(1024)} fusion(s32[20480]{0:T(1024)} %bitcast.18), kind=kLoop, calls=%fused_computation.9 | loop fusion | flops 163840 | bytes 163840 | tf_op jit(solution)/shard_map/add | solution.py:419
  9.1 0.9 fusion.1
  10.0 1.0 pad_maximum_fusion
  11.0 0.0 copy-start.1
  11.0 0.0 collective-permute-done.lower_ref
  11.0 0.0 copy-start.4
  11.0 0.0 collective-permute-done.1.upper_ref
  11.0 0.0 copy-start.5
  11.0 0.1 collective-permute-start.2
  11.1 4.7 %collective-permute-start.3 = (f32[800,128]{1,0:T(8,128)S(1)}, f32[800,128]{1,0:T(8,128)S(1)}, u32[]{:S(2)}, u32[]{:S(2)}) collective-permute-start(f32[800,128]{1,0:T(8,128)S(1)} %bitcast.14), channel_id=1, source_target_pairs={{0,7},{1,0},{2,1},{3,2},{4,3},{5,4},{6,5},{7,6},{8,15},{9,8},{10,9... | collective-permute-start | bytes 1228808 | tf_op jit(solution)/shard_map/ppermute | solution.py:386
  15.8 0.0 copy-done.1
  15.8 0.0 copy-done.4
  15.8 0.0 copy-done.5
  15.8 29.0 %shard_map.91 = (bf16[160,128,128]{2,1,0:T(8,128)(2,1)}, s32[320,128]{1,0:T(8,128)}) custom-call(s32[20480]{0:T(1024)} %fusion.5.order_ref.next_ref.before_ref, s32[20480]{0:T(1024)} %fusion.5.order_ref.next_ref.before_ref, s32[80,128]{1,0:T(8,128)} %copy-done.4, s32[80,128]{1,0:T(8,128)} %copy-done.5, s32[1,160,256]{2,1,0:T(8,128)} %partner_ref.1, ...), custom_call_target="tpu_custom_call" | custom-call | flops 24999999488 | bytes 10000000 | tf_op jit(solution)/shard_map/pallas_call | solution.py:429
  44.8 0.0 collective-permute-done.2.lower_ref
  44.8 0.0 copy-start.2
  44.8 0.0 collective-permute-done.3.upper_ref
  44.8 0.0 copy-start.3
  44.8 0.7 copy-done.2
  45.6 0.2 copy-done.3
  45.7 80.0 %shard_map.92 = (f32[3,160,128]{2,1,0:T(8,128)}, f32[6,8,128]{2,1,0:T(8,128)}) custom-call(s32[40960]{0:T(1024)} %bitcast.21, s32[40960]{0:T(1024)} %bitcast.22, s32[20480]{0:T(1024)} %fusion.5.order_ref.next_ref.before_ref, s32[20480]{0:T(1024)} %fusion.5.order_ref.next_ref.before_ref, f32[800,128]{1,0:T(8,128)} %copy-done.2, f32[800,128]{1,0:T(8,128)} %bitcast.16, ...), custom_call_target="tpu_custom_call" | custom-call | flops 24999999488 | bytes 10000000 | tf_op jit(solution)/shard_map/pallas_call | solution.py:451
  125.8 0.0 collective-permute-start.4
  125.8 1.7 %collective-permute-start.5 = (f32[6,8,128]{2,1,0:T(8,128)}, f32[6,8,128]{2,1,0:T(8,128)S(1)}, u32[]{:S(2)}, u32[]{:S(2)}) collective-permute-start(f32[6,8,128]{2,1,0:T(8,128)} %get-tuple-element.20.refs_0_), channel_id=1, source_target_pairs={{0,16},{8,24},{16,0},{24,8},{1,17},{9,25},{17,1},{25,9},{2,18},{10... | collective-permute-start | bytes 73736 | tf_op jit(solution)/shard_map/ppermute | solution.py:386
  127.4 1.4 collective-permute-start.6
  128.8 0.4 collective-permute-done.4.refs_1_
  129.2 0.6 collective-permute-done.5.refs_2_
  129.9 0.7 collective-permute-done.6.refs_3_
  130.6 0.0 copy-start
  130.6 0.7 copy-done
  131.3 0.1 shard_map.93
  131.4 0.1 collective-permute-start.7
  131.5 3.7 %collective-permute-done.7 = f32[32,128]{1,0:T(8,128)S(1)} collective-permute-done((f32[32,128]{1,0:T(8,128)S(1)}, f32[32,128]{1,0:T(8,128)S(1)}, u32[]{:S(2)}, u32[]{:S(2)}) %collective-permute-start.7) | collective-permute-done | bytes 16416 | tf_op jit(solution)/shard_map/ppermute | solution.py:395
  135.2 0.0 collective-permute-start.8
  135.2 3.7 %collective-permute-done.8 = f32[32,128]{1,0:T(8,128)S(1)} collective-permute-done((f32[32,128]{1,0:T(8,128)S(1)}, f32[32,128]{1,0:T(8,128)S(1)}, u32[]{:S(2)}, u32[]{:S(2)}) %collective-permute-start.8) | collective-permute-done | bytes 16416 | tf_op jit(solution)/shard_map/ppermute | solution.py:395
  138.9 0.0 collective-permute-start.9
  138.9 4.6 %collective-permute-done.9 = f32[32,128]{1,0:T(8,128)S(1)} collective-permute-done((f32[32,128]{1,0:T(8,128)S(1)}, f32[32,128]{1,0:T(8,128)S(1)}, u32[]{:S(2)}, u32[]{:S(2)}) %collective-permute-start.9) | collective-permute-done | bytes 16416 | tf_op jit(solution)/shard_map/ppermute | solution.py:395
  143.6 0.8 shard_map.94
  (3 shorter events, 0.0 us)
Async XLA Ops:
  0.8 10.2 %collective-permute-start = (s32[80,128]{1,0:T(8,128)S(1)}, s32[80,128]{1,0:T(8,128)S(1)}, u32[]{:S(2)}, u32[]{:S(2)}) collective-permute-start(s32[80,128]{1,0:T(8,128)S(1)} %bitcast.20), channel_id=1, source_target_pairs={{0,1},{1,2},{2,3},{3,4},{4,5},{5,6},{6,7},{7,0},{8,9},{9,10},{10,1... | collective-permute-start | bytes 122888 | tf_op jit(solution)/shard_map/ppermute | solution.py:386
  3.7 7.3 %collective-permute-start.1 = (s32[80,128]{1,0:T(8,128)S(1)}, s32[80,128]{1,0:T(8,128)S(1)}, u32[]{:S(2)}, u32[]{:S(2)}) collective-permute-start(s32[80,128]{1,0:T(8,128)S(1)} %bitcast.19), channel_id=1, source_target_pairs={{0,7},{1,0},{2,1},{3,2},{4,3},{5,4},{6,5},{7,6},{8,15},{9,8},{10,9... | collective-permute-start | bytes 122888 | tf_op jit(solution)/shard_map/ppermute | solution.py:386
  11.0 4.8 %copy-start.1 = (f32[5,160,128]{2,1,0:T(8,128)}, f32[5,160,128]{2,1,0:T(8,128)S(1)}, u32[]{:S(2)}) copy-start(f32[5,160,128]{2,1,0:T(8,128)S(1)} %pad_maximum_fusion) | copy-start | bytes 1228804
  11.0 4.8 %copy-start.4 = (s32[80,128]{1,0:T(8,128)}, s32[80,128]{1,0:T(8,128)S(1)}, u32[]{:S(2)}) copy-start(s32[80,128]{1,0:T(8,128)S(1)} %collective-permute-done.lower_ref) | copy-start | bytes 122884
  11.0 4.8 %copy-start.5 = (s32[80,128]{1,0:T(8,128)}, s32[80,128]{1,0:T(8,128)S(1)}, u32[]{:S(2)}) copy-start(s32[80,128]{1,0:T(8,128)S(1)} %collective-permute-done.1.upper_ref) | copy-start | bytes 122884
  11.0 33.8 %collective-permute-start.2 = (f32[800,128]{1,0:T(8,128)S(1)}, f32[800,128]{1,0:T(8,128)S(1)}, u32[]{:S(2)}, u32[]{:S(2)}) collective-permute-start(f32[800,128]{1,0:T(8,128)S(1)} %bitcast.13), channel_id=1, source_target_pairs={{0,1},{1,2},{2,3},{3,4},{4,5},{5,6},{6,7},{7,0},{8,9},{9,10},{10,1... | collective-permute-start | bytes 1228808 | tf_op jit(solution)/shard_map/ppermute | solution.py:386
  11.1 33.7 %collective-permute-start.3 = (f32[800,128]{1,0:T(8,128)S(1)}, f32[800,128]{1,0:T(8,128)S(1)}, u32[]{:S(2)}, u32[]{:S(2)}) collective-permute-start(f32[800,128]{1,0:T(8,128)S(1)} %bitcast.14), channel_id=1, source_target_pairs={{0,7},{1,0},{2,1},{3,2},{4,3},{5,4},{6,5},{7,6},{8,15},{9,8},{10,9... | collective-permute-start | bytes 1228808 | tf_op jit(solution)/shard_map/ppermute | solution.py:386
  44.8 0.8 copy-start.2
  44.8 0.9 copy-start.3
  125.8 3.5 %collective-permute-start.4 = (f32[6,8,128]{2,1,0:T(8,128)}, f32[6,8,128]{2,1,0:T(8,128)S(1)}, u32[]{:S(2)}, u32[]{:S(2)}) collective-permute-start(f32[6,8,128]{2,1,0:T(8,128)} %get-tuple-element.20.refs_0_), channel_id=1, source_target_pairs={{0,8},{8,16},{16,24},{24,0},{1,9},{9,17},{17,25},{25,1},{2,10},{10... | collective-permute-start | bytes 73736 | tf_op jit(solution)/shard_map/ppermute | solution.py:386
  125.8 4.1 %collective-permute-start.5 = (f32[6,8,128]{2,1,0:T(8,128)}, f32[6,8,128]{2,1,0:T(8,128)S(1)}, u32[]{:S(2)}, u32[]{:S(2)}) collective-permute-start(f32[6,8,128]{2,1,0:T(8,128)} %get-tuple-element.20.refs_0_), channel_id=1, source_target_pairs={{0,16},{8,24},{16,0},{24,8},{1,17},{9,25},{17,1},{25,9},{2,18},{10... | collective-permute-start | bytes 73736 | tf_op jit(solution)/shard_map/ppermute | solution.py:386
  127.4 3.1 %collective-permute-start.6 = (f32[6,8,128]{2,1,0:T(8,128)}, f32[6,8,128]{2,1,0:T(8,128)S(1)}, u32[]{:S(2)}, u32[]{:S(2)}) collective-permute-start(f32[6,8,128]{2,1,0:T(8,128)} %get-tuple-element.20.refs_0_), channel_id=1, source_target_pairs={{0,24},{8,0},{16,8},{24,16},{1,25},{9,1},{17,9},{25,17},{2,26},{10... | collective-permute-start | bytes 73736 | tf_op jit(solution)/shard_map/ppermute | solution.py:386
  130.6 0.7 copy-start
  131.4 3.8 %collective-permute-start.7 = (f32[32,128]{1,0:T(8,128)S(1)}, f32[32,128]{1,0:T(8,128)S(1)}, u32[]{:S(2)}, u32[]{:S(2)}) collective-permute-start(f32[32,128]{1,0:T(8,128)S(1)} %get-tuple-element.21), channel_id=1, source_target_pairs={{0,1},{1,0},{2,3},{3,2},{4,5},{5,4},{6,7},{7,6},{8,9},{9,8},{10,11... | collective-permute-start | bytes 49160 | tf_op jit(solution)/shard_map/ppermute | solution.py:395
  135.2 3.7 %collective-permute-start.8 = (f32[32,128]{1,0:T(8,128)S(1)}, f32[32,128]{1,0:T(8,128)S(1)}, u32[]{:S(2)}, u32[]{:S(2)}) collective-permute-start(f32[32,128]{1,0:T(8,128)S(1)} %add.20), channel_id=1, source_target_pairs={{0,2},{1,3},{2,0},{3,1},{4,6},{5,7},{6,4},{7,5},{8,10},{9,11},{10,... | collective-permute-start | bytes 49160 | tf_op jit(solution)/shard_map/ppermute | solution.py:395
  138.9 4.6 %collective-permute-start.9 = (f32[32,128]{1,0:T(8,128)S(1)}, f32[32,128]{1,0:T(8,128)S(1)}, u32[]{:S(2)}, u32[]{:S(2)}) collective-permute-start(f32[32,128]{1,0:T(8,128)S(1)} %add.21), channel_id=1, source_target_pairs={{0,4},{1,5},{2,6},{3,7},{4,0},{5,1},{6,2},{7,3},{8,12},{9,13},{10,... | collective-permute-start | bytes 49160 | tf_op jit(solution)/shard_map/ppermute | solution.py:395

commit v14 on v13

--- a/solution.py
+++ b/solution.py
@@ -31,6 +31,8 @@
 
 DEPTH, CHARGE, ONE, NORM, LAST = 3, 4, 5, 6, 7
 FAR_PIECES = (0, 1, 2, 0, 1, 0)
+ROW = 256
+COPY = 64
 USED = 8 * len(FAR_PIECES)
 NEAR_PIECES = (0, 0, 0, 1, 1, 2)
 
@@ -42,6 +44,9 @@
             chosen[piece * 8 + axis, group * 8 + axis] = 2.0
         for field in (DEPTH, CHARGE):
             chosen[piece * 8 + field, group * 8 + field] = 1.0
+    for piece in range(3):
+        for axis in range(3):
+            chosen[piece * 8 + axis, COPY + piece * 8 + axis] = 1.0
     for piece, group in ((0, 0), (1, 3), (2, 5)):
         chosen[piece * 8 + NORM, group * 8 + ONE] = 1.0
         chosen[ONE, piece * 8 + NORM] = 1.0
@@ -50,8 +55,9 @@
 
 
 def near_masks():
-    field = np.arange(LANES) % 8
-    kinds = [(field != DEPTH) & (field != CHARGE), field == DEPTH, field == CHARGE]
+    lane = np.arange(LANES)
+    field = lane % 8
+    kinds = [(field != DEPTH) & (field != CHARGE), field == DEPTH, field == CHARGE, lane >= COPY]
     return jnp.asarray(np.stack([np.tile(kind, (TILE, 1)) for kind in kinds]), BF16)
 
 
@@ -197,7 +203,35 @@
         yield
     both = jnp.dot(jnp.concatenate(high + low, axis=0), others, preferred_element_type=F32)
     yield
-    sums[...] = both[0:TILE] + both[TILE:]
+    sums[...] = both[0:TILE] + both[TILE:] + (left_ref[place] * kinds_ref[3]).astype(F32)
+
+
+def pair_scatter(numbers, sums, total):
+    entries = jnp.concatenate(numbers, axis=1)
+    forces = [[], [], []]
+    for side in range(2):
+        across = sums[side].T
+        for axis in range(3):
+            moment, place = (
+                sum(across[first + axis + 8 * piece : first + axis + 8 * piece + 1] for piece in range(3))
+                for first in (0, COPY)
+            )
+            forces[axis].append(place * across[ONE : ONE + 1] - moment)
+    yield
+    grid = lax.broadcasted_iota(I32, (ROW, ROW), 0)
+    hot = jnp.where(grid == (entries & (ROW - 1)), 1.0, 0.0).astype(BF16)
+    yield
+    count = total.shape[0] // 3
+    mask = lax.broadcasted_iota(I32, (count, ROW), 0) == (entries >> 8)
+    high, low = [], []
+    for axis in range(3):
+        force = jnp.concatenate(forces[axis], axis=1)
+        part = force.astype(BF16).astype(F32)
+        high.append(jnp.where(mask, part, 0.0).astype(BF16))
+        low.append(jnp.where(mask, force - part, 0.0).astype(BF16))
+        yield
+    parts = [jnp.concatenate(piece, axis=0) for piece in (high, low)]
+    total[...] += nt_dot(jnp.concatenate(parts, axis=1), jnp.concatenate([hot, hot], axis=1))
 
 
 def weave(stages, copies, parts):
@@ -209,7 +243,7 @@
 
 def force_kernel(
     rows, list_ref, next_ref, order_ref, before_ref, lower_ref, fields_ref, upper_ref, kinds_ref, left_ref,
-    out_ref, solute_ref, table, forces, far_a, far_b, sum_a, sum_b,
+    out_ref, solute_ref, table, total, far_a, far_b, sum_a, sum_b,
 ):
     turn = pl.program_id(0)
     partners = far_a.shape[1]
@@ -227,16 +261,9 @@
             for start in range(0, partners, 16)
         ]
 
-    def save(local, sums):
+    def scatter(local, sums):
         ref, first = (order_ref, local) if local >= 0 else (before_ref, local + 8)
-
-        def copy(block):
-            value = sums[block * 8 : block * 8 + 8, :]
-            for k in range(8):
-                place = ref[first * TILE + block * 8 + k]
-                pltpu.store(forces.at[pl.ds(place, 8), :], value, mask=masks[k])
-
-        return [functools.partial(copy, block) for block in range(TILE // 8)]
+        return pair_scatter([ref[first + side : first + side + 1, :] for side in range(2)], sums, total)
 
     @pl.when(turn == 0)
     def _():
@@ -247,6 +274,7 @@
 
         lax.fori_loop(0, rows // 4, fill, 0)
         sum_b[...] = jnp.zeros_like(sum_b)
+        total[...] = jnp.zeros_like(total)
         for side in range(2):
             for copy in load(side, far_a.at[side]):
                 copy()
@@ -255,43 +283,27 @@
         far, far_next, sums, sums_before = (
             (far_a, far_b, sum_a, sum_b) if tile % 4 == 0 else (far_b, far_a, sum_b, sum_a)
         )
-        copies = save(tile - 2, sums_before.at[0]) + save(tile - 1, sums_before.at[1])
-        copies += load(tile + 2, far_next.at[0]) + load(tile + 3, far_next.at[1])
         weave(
-            [tile_sums(left_ref, kinds_ref, tile + side, far.at[side], sums.at[side]) for side in range(2)],
-            copies,
+            [tile_sums(left_ref, kinds_ref, tile + side, far.at[side], sums.at[side]) for side in range(2)]
+            + [scatter(tile - 2, sums_before)],
+            load(tile + 2, far_next.at[0]) + load(tile + 3, far_next.at[1]),
             7,
         )
 
     @pl.when(turn == pl.num_programs(0) - 1)
     def _():
-        for side in range(2):
-            for copy in save(6 + side, sum_b.at[side]):
-                copy()
-
-        def finish(group, carry):
-            for local in range(8):
-                row = group * 8 + local
-                sums = forces[pl.ds(pl.multiple_of(row * LANES + PAD, PAD), LANES), :]
-                places = [fields_ref[pl.ds(axis * rows + row, 1), :] for axis in range(3)]
-                for axis, force in enumerate(row_forces(sums, places)):
-                    out_ref[axis, pl.ds(row, 1), :] = places[axis] + STEP_SIZE * force
-            return carry
-
-        lax.fori_loop(0, rows // 8, finish, 0)
+        for _ in scatter(6, sum_b):
+            pass
+        count = rows * LANES // ROW
+        for axis in range(3):
+            force = total[axis * count : (axis + 1) * count, :]
+            for side in range(ROW // LANES):
+                spot = pl.ds(axis * rows + side, count, stride=ROW // LANES)
+                out_ref[spot, :] = fields_ref[spot, :] + STEP_SIZE * force[:, side * LANES : (side + 1) * LANES]
         solute = SOL_DEV // LANES
-        solute_ref[0:3] = out_ref[:, 0:solute, :]
         for axis in range(3):
+            solute_ref[axis] = out_ref[axis * rows : axis * rows + solute, :]
             solute_ref[3 + axis] = fields_ref[axis * rows : axis * rows + solute, :]
-
-
-def row_forces(sums, places):
-    across = sums.T
-    result = []
-    for axis, place in enumerate(places):
-        moment = sum(across[first + axis : first + axis + 1] for first in (0, 8, 16))
-        result.append((place - CENTRE) * across[ONE : ONE + 1] - moment)
-    return result
 
 
 def product_kernel(images, index_ref, *refs):
@@ -416,6 +428,7 @@
     lower_list, upper_list = turned(shell[1], "space", 1), turned(shell[0], "space", -1)
     fields, lower_list, upper_list = lax.optimization_barrier((fields, lower_list, upper_list))
     lower, upper = turned(fields, "space", 1), turned(fields, "space", -1)
+    tile_order = cell_order.reshape(rows, LANES)
     order = cell_order.reshape(atoms) + (PAD - jnp.arange(atoms, dtype=I32) % 8)
     scalar = pl.BlockSpec(memory_space=pltpu.SMEM)
     vector = pl.BlockSpec(memory_space=pltpu.VMEM)
@@ -451,14 +464,15 @@
     out, solute = pl.pallas_call(
         functools.partial(force_kernel, rows),
         grid=(rows // 8,),
-        out_shape=[whole(3, rows, LANES), whole(6, SOL_DEV // LANES, LANES)],
-        in_specs=[listed(partners, 0), listed(partners, 1), listed(TILE, 0), listed(TILE, -1)]
+        out_shape=[whole(3 * rows, LANES), whole(6, SOL_DEV // LANES, LANES)],
+        in_specs=[listed(partners, 0), listed(partners, 1)]
+        + [pl.BlockSpec((8, LANES), lambda i, by=by: (jnp.maximum(i - by, 0), 0)) for by in (0, 1)]
         + [vector] * 4
         + [pl.BlockSpec((8, TILE, LANES), lambda i: (i, 0, 0))],
         out_specs=[vector] * 2,
         scratch_shapes=[
             pltpu.VMEM((3 * atoms + 2 * PAD, LANES), F32),
-            pltpu.VMEM(table, F32),
+            pltpu.VMEM((3 * atoms // ROW, ROW), F32),
             pltpu.VMEM((2, partners, LANES), BF16),
             pltpu.VMEM((2, partners, LANES), BF16),
             pltpu.VMEM((2, TILE, LANES), F32),
@@ -466,7 +480,8 @@
         ],
         compiler_params=params,
         cost_estimate=pl.CostEstimate(flops=25 * 10**9, bytes_accessed=10**7, transcendentals=0),
-    )(pairs, pairs, order, order, lower, fields, upper, near_masks(), left)
+    )(pairs, pairs, tile_order, tile_order, lower, fields, upper, near_masks(), left)
+    out = out.reshape(3, rows, LANES)
     solutes = round_trip(solute, "image")
     small = pltpu.CompilerParams(vmem_limit_bytes=8 * 1024 * 1024)
     solute_shape = whole(images, 3, SOL_DEV // LANES, LANES)

time: 145 us -> 132 us (0.910)
  Pallas kernels: 110 us -> 96.8 us
    pallas_call x1, Pallas kernels: 80 us -> 67 us  [per_device(): pl.pallas_call(functools.partial(force_kernel, rows), grid=(rows // 8,),...]
  transfers between devices with their start and end apart: 10 -> 10, of which waited for: 6 -> 6; matrix products, arithmetic and copies ran while one was open for 2% -> 3% of each run, Pallas kernels for 20% -> 22%
where the time goes in v14:
time: 132 us; the launch traced here: 131 us
  Pallas kernels  96.8 us (73%)
  starting transfers between devices  14 us (11%)
  waiting for transfers between devices  13.8 us (10%)
  other arithmetic  3.47 us (3%)
  local copies, waits for them, and re-layouts  2.44 us (2%)
    pallas_call x1, Pallas kernels, per_device(): pl.pallas_call(functools.partial(force_kernel, rows), grid=(rows // 8,),...  67 us
    pallas_call x1, Pallas kernels, per_device(): pl.pallas_call(functools.partial(near_kernel, rows), grid=(rows // 8,), o...  29 us
    ppermute x7, starting transfers between devices, turned(): lax.ppermute(array, axis, [(i, (i + by) % count) for i in range(count)])  13.9 us
    ppermute x3, waiting for transfers between devices, summed(): lax.ppermute(array, axis, [(i, i ^ by) for i in range(count)])  12.1 us
  transfers between devices with their start and end apart: 10, of which 6 were waited for; matrix products, arithmetic and copies ran while one was open for 3% of the time, Pallas kernels for 22%

profile of v14, /device:TPU:0, one launch (start us, length us, event | category | flops | bytes accessed | tf_op | source)
XLA Modules:
  0.0 131.3 jit_solution(3846842373295609336)
XLA Ops:
  0.0 0.8 fusion.9
  0.8 2.9 %collective-permute-start = (s32[80,128]{1,0:T(8,128)S(1)}, s32[80,128]{1,0:T(8,128)S(1)}, u32[]{:S(2)}, u32[]{:S(2)}) collective-permute-start(s32[80,128]{1,0:T(8,128)S(1)} %bitcast.25), channel_id=1, source_target_pairs={{0,1},{1,2},{2,3},{3,4},{4,5},{5,6},{6,7},{7,0},{8,9},{9,10},{10,1... | collective-permute-start | bytes 122888 | tf_op jit(solution)/shard_map/ppermute | solution.py:398
  3.7 3.1 %collective-permute-start.1 = (s32[80,128]{1,0:T(8,128)S(1)}, s32[80,128]{1,0:T(8,128)S(1)}, u32[]{:S(2)}, u32[]{:S(2)}) collective-permute-start(s32[80,128]{1,0:T(8,128)S(1)} %bitcast.24), channel_id=1, source_target_pairs={{0,7},{1,0},{2,1},{3,2},{4,3},{5,4},{6,5},{7,6},{8,15},{9,8},{10,9... | collective-permute-start | bytes 122888 | tf_op jit(solution)/shard_map/ppermute | solution.py:398
  7.5 1.5 %fusion.5.order_ref.next_ref = s32[20480]{0:T(1024)} fusion(s32[20480]{0:T(1024)} %bitcast.21), kind=kLoop, calls=%fused_computation.9 | loop fusion | flops 163840 | bytes 163840 | tf_op jit(solution)/shard_map/add | solution.py:432
  9.1 0.9 fusion.1
  10.0 1.0 pad_maximum_fusion
  11.0 0.0 copy-start.1
  11.0 0.0 collective-permute-done.lower_ref
  11.0 0.0 copy-start.4
  11.0 0.0 collective-permute-done.1.upper_ref
  11.0 0.0 copy-start.5
  11.1 0.1 collective-permute-start.2
  11.1 4.7 %collective-permute-start.3 = (f32[800,128]{1,0:T(8,128)S(1)}, f32[800,128]{1,0:T(8,128)S(1)}, u32[]{:S(2)}, u32[]{:S(2)}) collective-permute-start(f32[800,128]{1,0:T(8,128)S(1)} %bitcast.16), channel_id=1, source_target_pairs={{0,7},{1,0},{2,1},{3,2},{4,3},{5,4},{6,5},{7,6},{8,15},{9,8},{10,9... | collective-permute-start | bytes 1228808 | tf_op jit(solution)/shard_map/ppermute | solution.py:398
  15.8 0.0 copy-done.1
  15.8 0.0 copy-done.4
  15.8 0.0 copy-done.5
  15.8 29.0 %shard_map.91 = (bf16[160,128,128]{2,1,0:T(8,128)(2,1)}, s32[320,128]{1,0:T(8,128)}) custom-call(s32[20480]{0:T(1024)} %fusion.5.order_ref.next_ref, s32[20480]{0:T(1024)} %fusion.5.order_ref.next_ref, s32[80,128]{1,0:T(8,128)} %copy-done.4, s32[80,128]{1,0:T(8,128)} %copy-done.5, s32[1,160,256]{2,1,0:T(8,128)} %partner_ref.1, f32[800,128]{1,0:T(8,128)} %bitcast.17, ...), custom_call_target="tpu_custom_call" | custom-call | flops 24999999488 | bytes 10000000 | tf_op jit(solution)/shard_map/pallas_call | solution.py:442
  44.8 0.0 collective-permute-done.2.lower_ref
  44.8 0.0 copy-start.2
  44.8 0.0 collective-permute-done.3.upper_ref
  44.8 0.0 copy-start.3
  44.8 0.7 copy-done.2
  45.6 0.2 copy-done.3
  45.7 67.0 %shard_map.92 = (f32[480,128]{1,0:T(8,128)}, f32[6,8,128]{2,1,0:T(8,128)}) custom-call(s32[40960]{0:T(1024)} %bitcast.26, s32[40960]{0:T(1024)} %bitcast.27, s32[160,128]{1,0:T(8,128)} %bitcast.22, s32[160,128]{1,0:T(8,128)} %bitcast.23, f32[800,128]{1,0:T(8,128)} %copy-done.2, f32[800,128]{1,0:T(8,128)} %bitcast.18, f32[800,128]{1,0:T(8,128)} %copy-done.3, ...), custom_call_target="tpu_custom_call" | custom-call | flops 24999999488 | bytes 10000000 | tf_op jit(solution)/shard_map/pallas_call | solution.py:464
  112.7 0.0 collective-permute-start.4
  112.7 1.7 %collective-permute-start.5 = (f32[6,8,128]{2,1,0:T(8,128)}, f32[6,8,128]{2,1,0:T(8,128)S(1)}, u32[]{:S(2)}, u32[]{:S(2)}) collective-permute-start(f32[6,8,128]{2,1,0:T(8,128)} %get-tuple-element.20.refs_0_), channel_id=1, source_target_pairs={{0,16},{8,24},{16,0},{24,8},{1,17},{9,25},{17,1},{25,9},{2,18},{10... | collective-permute-start | bytes 73736 | tf_op jit(solution)/shard_map/ppermute | solution.py:398
  114.4 1.4 %collective-permute-start.6 = (f32[6,8,128]{2,1,0:T(8,128)}, f32[6,8,128]{2,1,0:T(8,128)S(1)}, u32[]{:S(2)}, u32[]{:S(2)}) collective-permute-start(f32[6,8,128]{2,1,0:T(8,128)} %get-tuple-element.20.refs_0_), channel_id=1, source_target_pairs={{0,24},{8,0},{16,8},{24,16},{1,25},{9,1},{17,9},{25,17},{2,26},{10... | collective-permute-start | bytes 73736 | tf_op jit(solution)/shard_map/ppermute | solution.py:398
  115.8 0.3 collective-permute-done.4.refs_1_
  116.2 0.6 collective-permute-done.5.refs_2_
  116.8 0.7 collective-permute-done.6.refs_3_
  117.5 0.0 copy-start
  117.5 0.7 copy-done
  118.3 0.1 shard_map.93
  118.3 0.1 collective-permute-start.7
  118.4 3.7 %collective-permute-done.7 = f32[32,128]{1,0:T(8,128)S(1)} collective-permute-done((f32[32,128]{1,0:T(8,128)S(1)}, f32[32,128]{1,0:T(8,128)S(1)}, u32[]{:S(2)}, u32[]{:S(2)}) %collective-permute-start.7) | collective-permute-done | bytes 16416 | tf_op jit(solution)/shard_map/ppermute | solution.py:407
  122.2 0.0 collective-permute-start.8
  122.2 3.7 %collective-permute-done.8 = f32[32,128]{1,0:T(8,128)S(1)} collective-permute-done((f32[32,128]{1,0:T(8,128)S(1)}, f32[32,128]{1,0:T(8,128)S(1)}, u32[]{:S(2)}, u32[]{:S(2)}) %collective-permute-start.8) | collective-permute-done | bytes 16416 | tf_op jit(solution)/shard_map/ppermute | solution.py:407
  125.9 0.0 collective-permute-start.9
  125.9 4.6 %collective-permute-done.9 = f32[32,128]{1,0:T(8,128)S(1)} collective-permute-done((f32[32,128]{1,0:T(8,128)S(1)}, f32[32,128]{1,0:T(8,128)S(1)}, u32[]{:S(2)}, u32[]{:S(2)}) %collective-permute-start.9) | collective-permute-done | bytes 16416 | tf_op jit(solution)/shard_map/ppermute | solution.py:407
  130.5 0.8 shard_map.94
  (3 shorter events, 0.0 us)
Async XLA Ops:
  0.8 10.2 %collective-permute-start = (s32[80,128]{1,0:T(8,128)S(1)}, s32[80,128]{1,0:T(8,128)S(1)}, u32[]{:S(2)}, u32[]{:S(2)}) collective-permute-start(s32[80,128]{1,0:T(8,128)S(1)} %bitcast.25), channel_id=1, source_target_pairs={{0,1},{1,2},{2,3},{3,4},{4,5},{5,6},{6,7},{7,0},{8,9},{9,10},{10,1... | collective-permute-start | bytes 122888 | tf_op jit(solution)/shard_map/ppermute | solution.py:398
  3.7 7.3 %collective-permute-start.1 = (s32[80,128]{1,0:T(8,128)S(1)}, s32[80,128]{1,0:T(8,128)S(1)}, u32[]{:S(2)}, u32[]{:S(2)}) collective-permute-start(s32[80,128]{1,0:T(8,128)S(1)} %bitcast.24), channel_id=1, source_target_pairs={{0,7},{1,0},{2,1},{3,2},{4,3},{5,4},{6,5},{7,6},{8,15},{9,8},{10,9... | collective-permute-start | bytes 122888 | tf_op jit(solution)/shard_map/ppermute | solution.py:398
  11.0 4.8 %copy-start.1 = (f32[5,160,128]{2,1,0:T(8,128)}, f32[5,160,128]{2,1,0:T(8,128)S(1)}, u32[]{:S(2)}) copy-start(f32[5,160,128]{2,1,0:T(8,128)S(1)} %pad_maximum_fusion) | copy-start | bytes 1228804
  11.0 4.8 %copy-start.4 = (s32[80,128]{1,0:T(8,128)}, s32[80,128]{1,0:T(8,128)S(1)}, u32[]{:S(2)}) copy-start(s32[80,128]{1,0:T(8,128)S(1)} %collective-permute-done.lower_ref) | copy-start | bytes 122884
  11.0 4.8 %copy-start.5 = (s32[80,128]{1,0:T(8,128)}, s32[80,128]{1,0:T(8,128)S(1)}, u32[]{:S(2)}) copy-start(s32[80,128]{1,0:T(8,128)S(1)} %collective-permute-done.1.upper_ref) | copy-start | bytes 122884
  11.1 33.7 %collective-permute-start.2 = (f32[800,128]{1,0:T(8,128)S(1)}, f32[800,128]{1,0:T(8,128)S(1)}, u32[]{:S(2)}, u32[]{:S(2)}) collective-permute-start(f32[800,128]{1,0:T(8,128)S(1)} %bitcast.15), channel_id=1, source_target_pairs={{0,1},{1,2},{2,3},{3,4},{4,5},{5,6},{6,7},{7,0},{8,9},{9,10},{10,1... | collective-permute-start | bytes 1228808 | tf_op jit(solution)/shard_map/ppermute | solution.py:398
  11.1 33.7 %collective-permute-start.3 = (f32[800,128]{1,0:T(8,128)S(1)}, f32[800,128]{1,0:T(8,128)S(1)}, u32[]{:S(2)}, u32[]{:S(2)}) collective-permute-start(f32[800,128]{1,0:T(8,128)S(1)} %bitcast.16), channel_id=1, source_target_pairs={{0,7},{1,0},{2,1},{3,2},{4,3},{5,4},{6,5},{7,6},{8,15},{9,8},{10,9... | collective-permute-start | bytes 1228808 | tf_op jit(solution)/shard_map/ppermute | solution.py:398
  44.8 0.8 copy-start.2
  44.8 0.9 copy-start.3
  112.7 3.5 %collective-permute-start.4 = (f32[6,8,128]{2,1,0:T(8,128)}, f32[6,8,128]{2,1,0:T(8,128)S(1)}, u32[]{:S(2)}, u32[]{:S(2)}) collective-permute-start(f32[6,8,128]{2,1,0:T(8,128)} %get-tuple-element.20.refs_0_), channel_id=1, source_target_pairs={{0,8},{8,16},{16,24},{24,0},{1,9},{9,17},{17,25},{25,1},{2,10},{10... | collective-permute-start | bytes 73736 | tf_op jit(solution)/shard_map/ppermute | solution.py:398
  112.7 4.1 %collective-permute-start.5 = (f32[6,8,128]{2,1,0:T(8,128)}, f32[6,8,128]{2,1,0:T(8,128)S(1)}, u32[]{:S(2)}, u32[]{:S(2)}) collective-permute-start(f32[6,8,128]{2,1,0:T(8,128)} %get-tuple-element.20.refs_0_), channel_id=1, source_target_pairs={{0,16},{8,24},{16,0},{24,8},{1,17},{9,25},{17,1},{25,9},{2,18},{10... | collective-permute-start | bytes 73736 | tf_op jit(solution)/shard_map/ppermute | solution.py:398
  114.4 3.1 %collective-permute-start.6 = (f32[6,8,128]{2,1,0:T(8,128)}, f32[6,8,128]{2,1,0:T(8,128)S(1)}, u32[]{:S(2)}, u32[]{:S(2)}) collective-permute-start(f32[6,8,128]{2,1,0:T(8,128)} %get-tuple-element.20.refs_0_), channel_id=1, source_target_pairs={{0,24},{8,0},{16,8},{24,16},{1,25},{9,1},{17,9},{25,17},{2,26},{10... | collective-permute-start | bytes 73736 | tf_op jit(solution)/shard_map/ppermute | solution.py:398
  117.5 0.7 copy-start
  118.3 3.8 %collective-permute-start.7 = (f32[32,128]{1,0:T(8,128)S(1)}, f32[32,128]{1,0:T(8,128)S(1)}, u32[]{:S(2)}, u32[]{:S(2)}) collective-permute-start(f32[32,128]{1,0:T(8,128)S(1)} %get-tuple-element.21), channel_id=1, source_target_pairs={{0,1},{1,0},{2,3},{3,2},{4,5},{5,4},{6,7},{7,6},{8,9},{9,8},{10,11... | collective-permute-start | bytes 49160 | tf_op jit(solution)/shard_map/ppermute | solution.py:407
  122.2 3.7 %collective-permute-start.8 = (f32[32,128]{1,0:T(8,128)S(1)}, f32[32,128]{1,0:T(8,128)S(1)}, u32[]{:S(2)}, u32[]{:S(2)}) collective-permute-start(f32[32,128]{1,0:T(8,128)S(1)} %add.20), channel_id=1, source_target_pairs={{0,2},{1,3},{2,0},{3,1},{4,6},{5,7},{6,4},{7,5},{8,10},{9,11},{10,... | collective-permute-start | bytes 49160 | tf_op jit(solution)/shard_map/ppermute | solution.py:407
  125.9 4.6 %collective-permute-start.9 = (f32[32,128]{1,0:T(8,128)S(1)}, f32[32,128]{1,0:T(8,128)S(1)}, u32[]{:S(2)}, u32[]{:S(2)}) collective-permute-start(f32[32,128]{1,0:T(8,128)S(1)} %add.21), channel_id=1, source_target_pairs={{0,4},{1,5},{2,6},{3,7},{4,0},{5,1},{6,2},{7,3},{8,12},{9,13},{10,... | collective-permute-start | bytes 49160 | tf_op jit(solution)/shard_map/ppermute | solution.py:407

commit v15 on v14

--- a/solution.py
+++ b/solution.py
@@ -58,7 +58,7 @@
     lane = np.arange(LANES)
     field = lane % 8
     kinds = [(field != DEPTH) & (field != CHARGE), field == DEPTH, field == CHARGE, lane >= COPY]
-    return jnp.asarray(np.stack([np.tile(kind, (TILE, 1)) for kind in kinds]), BF16)
+    return jnp.asarray(np.stack([np.tile(kind, (16, 1)) for kind in kinds]), BF16)
 
 
 def two_pieces(values):
@@ -182,10 +182,15 @@
         )
 
 
+def masked(values, kind):
+    blocks = values.reshape(TILE // 16, 16, LANES) * kind[None]
+    return blocks.reshape(TILE, LANES)
+
+
 def tile_sums(left_ref, kinds_ref, place, far, sums):
     others = far[...]
     left = left_ref[place]
-    left = jnp.concatenate([left * kinds_ref[kind] for kind in range(3)], axis=0)
+    left = jnp.concatenate([masked(left, kinds_ref[kind]) for kind in range(3)], axis=0)
     yield
     grams = nt_dot(left, others)
     yield
@@ -203,7 +208,7 @@
         yield
     both = jnp.dot(jnp.concatenate(high + low, axis=0), others, preferred_element_type=F32)
     yield
-    sums[...] = both[0:TILE] + both[TILE:] + (left_ref[place] * kinds_ref[3]).astype(F32)
+    sums[...] = both[0:TILE] + both[TILE:] + masked(left_ref[place], kinds_ref[3]).astype(F32)
 
 
 def pair_scatter(numbers, sums, total):
@@ -230,8 +235,8 @@
         high.append(jnp.where(mask, part, 0.0).astype(BF16))
         low.append(jnp.where(mask, force - part, 0.0).astype(BF16))
         yield
-    parts = [jnp.concatenate(piece, axis=0) for piece in (high, low)]
-    total[...] += nt_dot(jnp.concatenate(parts, axis=1), jnp.concatenate([hot, hot], axis=1))
+    both = nt_dot(jnp.concatenate(high + low, axis=0), hot)
+    total[...] += both[0 : 3 * count] + both[3 * count :]
 
 
 def weave(stages, copies, parts):
@@ -402,11 +407,12 @@
     count = lax.axis_size(axis)
     if count & (count - 1):
         return lax.psum(array, axis)
-    by = 1
-    while by < count:
-        array = array + lax.ppermute(array, axis, [(i, i ^ by) for i in range(count)])
-        by *= 2
-    return array
+
+    def crossed(by):
+        return lax.ppermute(array, axis, [(i, i ^ by) for i in range(count)])
+
+    array = array + crossed(1)
+    return sum((crossed(by) for by in range(2, count, 2)), array)
 
 
 def round_trip(array, axis):

time: 132 us -> 128 us (0.970)
  waiting for transfers between devices: 13.8 us -> 7.36 us
  starting transfers between devices: 14 us -> 18.4 us
  Pallas kernels: 96.8 us -> 95.1 us
    ppermute x3 -> x4, waiting for transfers between devices: 12.1 us -> 5.62 us  [crossed(): return lax.ppermute(array, axis, [(i, i ^ by) for i in range(count)])]
    ppermute x3 -> x4, starting transfers between devices: 0.08 us -> 4.45 us  [crossed(): return lax.ppermute(array, axis, [(i, i ^ by) for i in range(count)])]
    pallas_call x1, Pallas kernels: 67 us -> 65.3 us  [per_device(): pl.pallas_call(functools.partial(force_kernel, rows), grid=(rows // 8,),...]
  transfers between devices with their start and end apart: 10 -> 11, of which waited for: 6 -> 6; matrix products, arithmetic and copies ran while one was open for 3% -> 3% of each run, Pallas kernels for 22% -> 23%
where the time goes in v15:
time: 128 us
  Pallas kernels  95.1 us (74%)
  starting transfers between devices  18.4 us (14%)
  waiting for transfers between devices  7.36 us (6%)
  other arithmetic  3.47 us (3%)
  local copies, waits for them, and re-layouts  2.44 us (2%)
    pallas_call x1, Pallas kernels, per_device(): pl.pallas_call(functools.partial(force_kernel, rows), grid=(rows // 8,),...  65.3 us
    pallas_call x1, Pallas kernels, per_device(): pl.pallas_call(functools.partial(near_kernel, rows), grid=(rows // 8,), o...  29 us
    ppermute x7, starting transfers between devices, turned(): lax.ppermute(array, axis, [(i, (i + by) % count) for i in range(count)])  13.9 us
    ppermute x4, waiting for transfers between devices, crossed(): return lax.ppermute(array, axis, [(i, i ^ by) for i in range(count)])  5.62 us
    ppermute x4, starting transfers between devices, crossed(): return lax.ppermute(array, axis, [(i, i ^ by) for i in range(count)])  4.45 us
  transfers between devices with their start and end apart: 11, of which 6 were waited for; matrix products, arithmetic and copies ran while one was open for 3% of the time, Pallas kernels for 23%

profile of v15, /device:TPU:0, one launch (start us, length us, event | category | flops | bytes accessed | tf_op | source)
XLA Modules:
  0.0 127.5 jit_solution(10251993070329521547)
XLA Ops:
  0.0 0.8 fusion.9
  0.8 2.9 %collective-permute-start = (s32[80,128]{1,0:T(8,128)S(1)}, s32[80,128]{1,0:T(8,128)S(1)}, u32[]{:S(2)}, u32[]{:S(2)}) collective-permute-start(s32[80,128]{1,0:T(8,128)S(1)} %bitcast.25), channel_id=1, source_target_pairs={{0,1},{1,2},{2,3},{3,4},{4,5},{5,6},{6,7},{7,0},{8,9},{9,10},{10,1... | collective-permute-start | bytes 122888 | tf_op jit(solution)/shard_map/ppermute | solution.py:403
  3.7 3.1 %collective-permute-start.1 = (s32[80,128]{1,0:T(8,128)S(1)}, s32[80,128]{1,0:T(8,128)S(1)}, u32[]{:S(2)}, u32[]{:S(2)}) collective-permute-start(s32[80,128]{1,0:T(8,128)S(1)} %bitcast.24), channel_id=1, source_target_pairs={{0,7},{1,0},{2,1},{3,2},{4,3},{5,4},{6,5},{7,6},{8,15},{9,8},{10,9... | collective-permute-start | bytes 122888 | tf_op jit(solution)/shard_map/ppermute | solution.py:403
  7.5 1.5 %fusion.5.order_ref.next_ref = s32[20480]{0:T(1024)} fusion(s32[20480]{0:T(1024)} %bitcast.21), kind=kLoop, calls=%fused_computation.9 | loop fusion | flops 163840 | bytes 163840 | tf_op jit(solution)/shard_map/add | solution.py:438
  9.1 0.9 fusion.1
  10.0 1.0 pad_maximum_fusion
  11.0 0.0 copy-start.1
  11.0 0.0 collective-permute-done.lower_ref
  11.0 0.0 copy-start.4
  11.0 0.0 collective-permute-done.1.upper_ref
  11.0 0.0 copy-start.5
  11.1 0.1 collective-permute-start.2
  11.1 4.7 %collective-permute-start.3 = (f32[800,128]{1,0:T(8,128)S(1)}, f32[800,128]{1,0:T(8,128)S(1)}, u32[]{:S(2)}, u32[]{:S(2)}) collective-permute-start(f32[800,128]{1,0:T(8,128)S(1)} %bitcast.16), channel_id=1, source_target_pairs={{0,7},{1,0},{2,1},{3,2},{4,3},{5,4},{6,5},{7,6},{8,15},{9,8},{10,9... | collective-permute-start | bytes 1228808 | tf_op jit(solution)/shard_map/ppermute | solution.py:403
  15.8 0.0 copy-done.1
  15.8 0.0 copy-done.4
  15.8 0.0 copy-done.5
  15.8 29.0 %shard_map.91 = (bf16[160,128,128]{2,1,0:T(8,128)(2,1)}, s32[320,128]{1,0:T(8,128)}) custom-call(s32[20480]{0:T(1024)} %fusion.5.order_ref.next_ref, s32[20480]{0:T(1024)} %fusion.5.order_ref.next_ref, s32[80,128]{1,0:T(8,128)} %copy-done.4, s32[80,128]{1,0:T(8,128)} %copy-done.5, s32[1,160,256]{2,1,0:T(8,128)} %partner_ref.1, f32[800,128]{1,0:T(8,128)} %bitcast.17, ...), custom_call_target="tpu_custom_call" | custom-call | flops 24999999488 | bytes 10000000 | tf_op jit(solution)/shard_map/pallas_call | solution.py:448
  44.8 0.0 collective-permute-done.2.lower_ref
  44.8 0.0 copy-start.2
  44.8 0.0 collective-permute-done.3.upper_ref
  44.8 0.0 copy-start.3
  44.8 0.7 copy-done.2
  45.5 0.2 copy-done.3
  45.7 65.3 %shard_map.92 = (f32[480,128]{1,0:T(8,128)}, f32[6,8,128]{2,1,0:T(8,128)}) custom-call(s32[40960]{0:T(1024)} %bitcast.26, s32[40960]{0:T(1024)} %bitcast.27, s32[160,128]{1,0:T(8,128)} %bitcast.22, s32[160,128]{1,0:T(8,128)} %bitcast.23, f32[800,128]{1,0:T(8,128)} %copy-done.2, f32[800,128]{1,0:T(8,128)} %bitcast.18, f32[800,128]{1,0:T(8,128)} %copy-done.3, ...), custom_call_target="tpu_custom_call" | custom-call | flops 24999999488 | bytes 10000000 | tf_op jit(solution)/shard_map/pallas_call | solution.py:470
  111.0 0.0 collective-permute-start.4
  111.0 1.7 %collective-permute-start.5 = (f32[6,8,128]{2,1,0:T(8,128)}, f32[6,8,128]{2,1,0:T(8,128)S(1)}, u32[]{:S(2)}, u32[]{:S(2)}) collective-permute-start(f32[6,8,128]{2,1,0:T(8,128)} %get-tuple-element.20.refs_0_), channel_id=1, source_target_pairs={{0,16},{8,24},{16,0},{24,8},{1,17},{9,25},{17,1},{25,9},{2,18},{10... | collective-permute-start | bytes 73736 | tf_op jit(solution)/shard_map/ppermute | solution.py:403
  112.7 1.4 %collective-permute-start.6 = (f32[6,8,128]{2,1,0:T(8,128)}, f32[6,8,128]{2,1,0:T(8,128)S(1)}, u32[]{:S(2)}, u32[]{:S(2)}) collective-permute-start(f32[6,8,128]{2,1,0:T(8,128)} %get-tuple-element.20.refs_0_), channel_id=1, source_target_pairs={{0,24},{8,0},{16,8},{24,16},{1,25},{9,1},{17,9},{25,17},{2,26},{10... | collective-permute-start | bytes 73736 | tf_op jit(solution)/shard_map/ppermute | solution.py:403
  114.1 0.3 collective-permute-done.4.refs_1_
  114.5 0.6 collective-permute-done.5.refs_2_
  115.1 0.7 collective-permute-done.6.refs_3_
  115.9 0.0 copy-start
  115.9 0.7 copy-done
  116.6 0.1 shard_map.93
  116.7 0.1 collective-permute-start.7
  116.7 3.7 %collective-permute-done.7 = f32[32,128]{1,0:T(8,128)S(1)} collective-permute-done((f32[32,128]{1,0:T(8,128)S(1)}, f32[32,128]{1,0:T(8,128)S(1)}, u32[]{:S(2)}, u32[]{:S(2)}) %collective-permute-start.7) | collective-permute-done | bytes 16416 | tf_op jit(solution)/shard_map/ppermute | solution.py:412
  120.5 0.0 collective-permute-start.10
  120.5 0.0 collective-permute-start.8
  120.6 4.3 %collective-permute-start.9 = (f32[32,128]{1,0:T(8,128)S(1)}, f32[32,128]{1,0:T(8,128)S(1)}, u32[]{:S(2)}, u32[]{:S(2)}) collective-permute-start(f32[32,128]{1,0:T(8,128)S(1)} %add.23), channel_id=1, source_target_pairs={{0,4},{1,5},{2,6},{3,7},{4,0},{5,1},{6,2},{7,3},{8,12},{9,13},{10,... | collective-permute-start | bytes 49160 | tf_op jit(solution)/shard_map/ppermute | solution.py:412
  124.9 1.1 collective-permute-done.10
  126.0 0.0 collective-permute-done.8
  126.0 0.7 collective-permute-done.9
  126.8 0.8 shard_map.94
  (2 shorter events, 0.0 us)
Async XLA Ops:
  0.8 10.2 %collective-permute-start = (s32[80,128]{1,0:T(8,128)S(1)}, s32[80,128]{1,0:T(8,128)S(1)}, u32[]{:S(2)}, u32[]{:S(2)}) collective-permute-start(s32[80,128]{1,0:T(8,128)S(1)} %bitcast.25), channel_id=1, source_target_pairs={{0,1},{1,2},{2,3},{3,4},{4,5},{5,6},{6,7},{7,0},{8,9},{9,10},{10,1... | collective-permute-start | bytes 122888 | tf_op jit(solution)/shard_map/ppermute | solution.py:403
  3.7 7.3 %collective-permute-start.1 = (s32[80,128]{1,0:T(8,128)S(1)}, s32[80,128]{1,0:T(8,128)S(1)}, u32[]{:S(2)}, u32[]{:S(2)}) collective-permute-start(s32[80,128]{1,0:T(8,128)S(1)} %bitcast.24), channel_id=1, source_target_pairs={{0,7},{1,0},{2,1},{3,2},{4,3},{5,4},{6,5},{7,6},{8,15},{9,8},{10,9... | collective-permute-start | bytes 122888 | tf_op jit(solution)/shard_map/ppermute | solution.py:403
  11.0 4.8 %copy-start.1 = (f32[5,160,128]{2,1,0:T(8,128)}, f32[5,160,128]{2,1,0:T(8,128)S(1)}, u32[]{:S(2)}) copy-start(f32[5,160,128]{2,1,0:T(8,128)S(1)} %pad_maximum_fusion) | copy-start | bytes 1228804
  11.0 4.8 %copy-start.4 = (s32[80,128]{1,0:T(8,128)}, s32[80,128]{1,0:T(8,128)S(1)}, u32[]{:S(2)}) copy-start(s32[80,128]{1,0:T(8,128)S(1)} %collective-permute-done.lower_ref) | copy-start | bytes 122884
  11.0 4.8 %copy-start.5 = (s32[80,128]{1,0:T(8,128)}, s32[80,128]{1,0:T(8,128)S(1)}, u32[]{:S(2)}) copy-start(s32[80,128]{1,0:T(8,128)S(1)} %collective-permute-done.1.upper_ref) | copy-start | bytes 122884
  11.1 33.7 %collective-permute-start.2 = (f32[800,128]{1,0:T(8,128)S(1)}, f32[800,128]{1,0:T(8,128)S(1)}, u32[]{:S(2)}, u32[]{:S(2)}) collective-permute-start(f32[800,128]{1,0:T(8,128)S(1)} %bitcast.15), channel_id=1, source_target_pairs={{0,1},{1,2},{2,3},{3,4},{4,5},{5,6},{6,7},{7,0},{8,9},{9,10},{10,1... | collective-permute-start | bytes 1228808 | tf_op jit(solution)/shard_map/ppermute | solution.py:403
  11.1 33.7 %collective-permute-start.3 = (f32[800,128]{1,0:T(8,128)S(1)}, f32[800,128]{1,0:T(8,128)S(1)}, u32[]{:S(2)}, u32[]{:S(2)}) collective-permute-start(f32[800,128]{1,0:T(8,128)S(1)} %bitcast.16), channel_id=1, source_target_pairs={{0,7},{1,0},{2,1},{3,2},{4,3},{5,4},{6,5},{7,6},{8,15},{9,8},{10,9... | collective-permute-start | bytes 1228808 | tf_op jit(solution)/shard_map/ppermute | solution.py:403
  44.8 0.8 copy-start.2
  44.8 0.9 copy-start.3
  111.0 3.5 %collective-permute-start.4 = (f32[6,8,128]{2,1,0:T(8,128)}, f32[6,8,128]{2,1,0:T(8,128)S(1)}, u32[]{:S(2)}, u32[]{:S(2)}) collective-permute-start(f32[6,8,128]{2,1,0:T(8,128)} %get-tuple-element.20.refs_0_), channel_id=1, source_target_pairs={{0,8},{8,16},{16,24},{24,0},{1,9},{9,17},{17,25},{25,1},{2,10},{10... | collective-permute-start | bytes 73736 | tf_op jit(solution)/shard_map/ppermute | solution.py:403
  111.0 4.1 %collective-permute-start.5 = (f32[6,8,128]{2,1,0:T(8,128)}, f32[6,8,128]{2,1,0:T(8,128)S(1)}, u32[]{:S(2)}, u32[]{:S(2)}) collective-permute-start(f32[6,8,128]{2,1,0:T(8,128)} %get-tuple-element.20.refs_0_), channel_id=1, source_target_pairs={{0,16},{8,24},{16,0},{24,8},{1,17},{9,25},{17,1},{25,9},{2,18},{10... | collective-permute-start | bytes 73736 | tf_op jit(solution)/shard_map/ppermute | solution.py:403
  112.7 3.1 %collective-permute-start.6 = (f32[6,8,128]{2,1,0:T(8,128)}, f32[6,8,128]{2,1,0:T(8,128)S(1)}, u32[]{:S(2)}, u32[]{:S(2)}) collective-permute-start(f32[6,8,128]{2,1,0:T(8,128)} %get-tuple-element.20.refs_0_), channel_id=1, source_target_pairs={{0,24},{8,0},{16,8},{24,16},{1,25},{9,1},{17,9},{25,17},{2,26},{10... | collective-permute-start | bytes 73736 | tf_op jit(solution)/shard_map/ppermute | solution.py:403
  115.9 0.7 copy-start
  116.7 3.8 %collective-permute-start.7 = (f32[32,128]{1,0:T(8,128)S(1)}, f32[32,128]{1,0:T(8,128)S(1)}, u32[]{:S(2)}, u32[]{:S(2)}) collective-permute-start(f32[32,128]{1,0:T(8,128)S(1)} %get-tuple-element.21), channel_id=1, source_target_pairs={{0,1},{1,0},{2,3},{3,2},{4,5},{5,4},{6,7},{7,6},{8,9},{9,8},{10,11... | collective-permute-start | bytes 49160 | tf_op jit(solution)/shard_map/ppermute | solution.py:412
  120.5 5.5 %collective-permute-start.10 = (f32[32,128]{1,0:T(8,128)S(1)}, f32[32,128]{1,0:T(8,128)S(1)}, u32[]{:S(2)}, u32[]{:S(2)}) collective-permute-start(f32[32,128]{1,0:T(8,128)S(1)} %add.23), channel_id=1, source_target_pairs={{0,6},{1,7},{2,4},{3,5},{4,2},{5,3},{6,0},{7,1},{8,14},{9,15},{10,... | collective-permute-start | bytes 49160 | tf_op jit(solution)/shard_map/ppermute | solution.py:412
  120.5 5.5 %collective-permute-start.8 = (f32[32,128]{1,0:T(8,128)S(1)}, f32[32,128]{1,0:T(8,128)S(1)}, u32[]{:S(2)}, u32[]{:S(2)}) collective-permute-start(f32[32,128]{1,0:T(8,128)S(1)} %add.23), channel_id=1, source_target_pairs={{0,2},{1,3},{2,0},{3,1},{4,6},{5,7},{6,4},{7,5},{8,10},{9,11},{10,... | collective-permute-start | bytes 49160 | tf_op jit(solution)/shard_map/ppermute | solution.py:412
  120.6 6.2 %collective-permute-start.9 = (f32[32,128]{1,0:T(8,128)S(1)}, f32[32,128]{1,0:T(8,128)S(1)}, u32[]{:S(2)}, u32[]{:S(2)}) collective-permute-start(f32[32,128]{1,0:T(8,128)S(1)} %add.23), channel_id=1, source_target_pairs={{0,4},{1,5},{2,6},{3,7},{4,0},{5,1},{6,2},{7,3},{8,12},{9,13},{10,... | collective-permute-start | bytes 49160 | tf_op jit(solution)/shard_map/ppermute | solution.py:412

commit v16 on v15

--- a/solution.py
+++ b/solution.py
@@ -75,7 +75,11 @@
     sublane = lax.broadcasted_iota(I32, (8, LANES), 0)
     move = jnp.where(sublane < 3, jnp.where(sublane == 0, shift - CENTRE, -CENTRE), 0.0)
     ones = jnp.ones((8 - FIELDS, LANES), F32)
-    for block in range(count):
+    corner = lax.broadcasted_iota(I32, (LANES, LANES), 0) == lax.broadcasted_iota(I32, (LANES, LANES), 1)
+    eye = jnp.where(corner, 1.0, 0.0).astype(BF16)
+    blank = jnp.zeros((LANES - USED, LANES), F32)
+
+    def pieces(block):
         values = fields_ref[pl.ds(start_row + block, FIELDS, stride=rows), :]
         values = jnp.concatenate([values, ones], axis=0) + move
         norm = jnp.sum(jnp.where(sublane < 3, values * values, 0.0), axis=0, keepdims=True)
@@ -85,9 +89,19 @@
             parts.append(rest.astype(BF16).astype(F32))
             rest = rest - parts[-1]
         parts.append(rest)
-        used = jnp.concatenate([parts[piece] for piece in FAR_PIECES], axis=0)
+        return [parts[piece] for piece in FAR_PIECES]
+
+    def put(block, value):
         start = pl.multiple_of(first + (start_row + block) * LANES + PAD, PAD)
-        table[pl.ds(start, LANES), 0:USED] = used.T
+        table[pl.ds(start, LANES), 0:USED] = value
+
+    for block in range(0, count, 4):
+        for side in range(2):
+            put(block + side, jnp.concatenate(pieces(block + side), axis=0).T)
+        both = jnp.concatenate(pieces(block + 2) + [blank] + pieces(block + 3) + [blank], axis=0)
+        both = nt_dot(eye, both.astype(BF16))
+        for side in range(2):
+            put(block + 2 + side, both[:, side * LANES : side * LANES + USED])
 
 
 def sublane_masks():

time: 128 us -> 127 us (level)
  no operation moved by 1% of the time
where the time goes in v16:
time: 127 us
  Pallas kernels  94.2 us (74%)
  starting transfers between devices  18.4 us (14%)
  waiting for transfers between devices  7.36 us (6%)
  other arithmetic  3.47 us (3%)
  local copies, waits for them, and re-layouts  2.44 us (2%)
    pallas_call x1, Pallas kernels, per_device(): pl.pallas_call(functools.partial(force_kernel, rows), grid=(rows // 8,),...  64.4 us
    pallas_call x1, Pallas kernels, per_device(): pl.pallas_call(functools.partial(near_kernel, rows), grid=(rows // 8,), o...  29 us
    ppermute x7, starting transfers between devices, turned(): lax.ppermute(array, axis, [(i, (i + by) % count) for i in range(count)])  13.9 us
    ppermute x4, waiting for transfers between devices, crossed(): return lax.ppermute(array, axis, [(i, i ^ by) for i in range(count)])  5.62 us
    ppermute x4, starting transfers between devices, crossed(): return lax.ppermute(array, axis, [(i, i ^ by) for i in range(count)])  4.45 us
  transfers between devices with their start and end apart: 11, of which 6 were waited for; matrix products, arithmetic and copies ran while one was open for 3% of the time, Pallas kernels for 23%

profile of v16, /device:TPU:0, one launch (start us, length us, event | category | flops | bytes accessed | tf_op | source)
XLA Modules:
  0.0 126.6 jit_solution(15461354713423795910)
XLA Ops:
  0.0 0.8 fusion.9
  0.8 2.9 %collective-permute-start = (s32[80,128]{1,0:T(8,128)S(1)}, s32[80,128]{1,0:T(8,128)S(1)}, u32[]{:S(2)}, u32[]{:S(2)}) collective-permute-start(s32[80,128]{1,0:T(8,128)S(1)} %bitcast.25), channel_id=1, source_target_pairs={{0,1},{1,2},{2,3},{3,4},{4,5},{5,6},{6,7},{7,0},{8,9},{9,10},{10,1... | collective-permute-start | bytes 122888 | tf_op jit(solution)/shard_map/ppermute | solution.py:417
  3.7 3.1 %collective-permute-start.1 = (s32[80,128]{1,0:T(8,128)S(1)}, s32[80,128]{1,0:T(8,128)S(1)}, u32[]{:S(2)}, u32[]{:S(2)}) collective-permute-start(s32[80,128]{1,0:T(8,128)S(1)} %bitcast.24), channel_id=1, source_target_pairs={{0,7},{1,0},{2,1},{3,2},{4,3},{5,4},{6,5},{7,6},{8,15},{9,8},{10,9... | collective-permute-start | bytes 122888 | tf_op jit(solution)/shard_map/ppermute | solution.py:417
  7.5 1.5 %fusion.5.order_ref.next_ref = s32[20480]{0:T(1024)} fusion(s32[20480]{0:T(1024)} %bitcast.21), kind=kLoop, calls=%fused_computation.9 | loop fusion | flops 163840 | bytes 163840 | tf_op jit(solution)/shard_map/add | solution.py:452
  9.1 0.9 fusion.1
  10.0 1.0 pad_maximum_fusion
  11.0 0.0 copy-start.1
  11.0 0.0 collective-permute-done.lower_ref
  11.0 0.0 copy-start.4
  11.0 0.0 collective-permute-done.1.upper_ref
  11.0 0.0 copy-start.5
  11.1 0.1 collective-permute-start.2
  11.1 4.7 %collective-permute-start.3 = (f32[800,128]{1,0:T(8,128)S(1)}, f32[800,128]{1,0:T(8,128)S(1)}, u32[]{:S(2)}, u32[]{:S(2)}) collective-permute-start(f32[800,128]{1,0:T(8,128)S(1)} %bitcast.16), channel_id=1, source_target_pairs={{0,7},{1,0},{2,1},{3,2},{4,3},{5,4},{6,5},{7,6},{8,15},{9,8},{10,9... | collective-permute-start | bytes 1228808 | tf_op jit(solution)/shard_map/ppermute | solution.py:417
  15.8 0.0 copy-done.1
  15.8 0.0 copy-done.4
  15.8 0.0 copy-done.5
  15.8 29.0 %shard_map.91 = (bf16[160,128,128]{2,1,0:T(8,128)(2,1)}, s32[320,128]{1,0:T(8,128)}) custom-call(s32[20480]{0:T(1024)} %fusion.5.order_ref.next_ref, s32[20480]{0:T(1024)} %fusion.5.order_ref.next_ref, s32[80,128]{1,0:T(8,128)} %copy-done.4, s32[80,128]{1,0:T(8,128)} %copy-done.5, s32[1,160,256]{2,1,0:T(8,128)} %partner_ref.1, f32[800,128]{1,0:T(8,128)} %bitcast.17, ...), custom_call_target="tpu_custom_call" | custom-call | flops 24999999488 | bytes 10000000 | tf_op jit(solution)/shard_map/pallas_call | solution.py:462
  44.8 0.0 collective-permute-done.2.lower_ref
  44.8 0.0 copy-start.2
  44.8 0.0 collective-permute-done.3.upper_ref
  44.8 0.0 copy-start.3
  44.8 0.7 copy-done.2
  45.6 0.2 copy-done.3
  45.7 64.4 %shard_map.92 = (f32[480,128]{1,0:T(8,128)}, f32[6,8,128]{2,1,0:T(8,128)}) custom-call(s32[40960]{0:T(1024)} %bitcast.26, s32[40960]{0:T(1024)} %bitcast.27, s32[160,128]{1,0:T(8,128)} %bitcast.22, s32[160,128]{1,0:T(8,128)} %bitcast.23, f32[800,128]{1,0:T(8,128)} %copy-done.2, f32[800,128]{1,0:T(8,128)} %bitcast.18, f32[800,128]{1,0:T(8,128)} %copy-done.3, ...), custom_call_target="tpu_custom_call" | custom-call | flops 24999999488 | bytes 10000000 | tf_op jit(solution)/shard_map/pallas_call | solution.py:484
  110.1 0.0 collective-permute-start.4
  110.1 1.7 %collective-permute-start.5 = (f32[6,8,128]{2,1,0:T(8,128)}, f32[6,8,128]{2,1,0:T(8,128)S(1)}, u32[]{:S(2)}, u32[]{:S(2)}) collective-permute-start(f32[6,8,128]{2,1,0:T(8,128)} %get-tuple-element.20.refs_0_), channel_id=1, source_target_pairs={{0,16},{8,24},{16,0},{24,8},{1,17},{9,25},{17,1},{25,9},{2,18},{10... | collective-permute-start | bytes 73736 | tf_op jit(solution)/shard_map/ppermute | solution.py:417
  111.8 1.4 %collective-permute-start.6 = (f32[6,8,128]{2,1,0:T(8,128)}, f32[6,8,128]{2,1,0:T(8,128)S(1)}, u32[]{:S(2)}, u32[]{:S(2)}) collective-permute-start(f32[6,8,128]{2,1,0:T(8,128)} %get-tuple-element.20.refs_0_), channel_id=1, source_target_pairs={{0,24},{8,0},{16,8},{24,16},{1,25},{9,1},{17,9},{25,17},{2,26},{10... | collective-permute-start | bytes 73736 | tf_op jit(solution)/shard_map/ppermute | solution.py:417
  113.2 0.4 collective-permute-done.4.refs_1_
  113.6 0.6 collective-permute-done.5.refs_2_
  114.2 0.7 collective-permute-done.6.refs_3_
  114.9 0.0 copy-start
  115.0 0.7 copy-done
  115.7 0.1 shard_map.93
  115.7 0.1 collective-permute-start.7
  115.8 3.7 %collective-permute-done.7 = f32[32,128]{1,0:T(8,128)S(1)} collective-permute-done((f32[32,128]{1,0:T(8,128)S(1)}, f32[32,128]{1,0:T(8,128)S(1)}, u32[]{:S(2)}, u32[]{:S(2)}) %collective-permute-start.7) | collective-permute-done | bytes 16416 | tf_op jit(solution)/shard_map/ppermute | solution.py:426
  119.6 0.0 collective-permute-start.10
  119.6 0.1 collective-permute-start.8
  119.6 4.3 %collective-permute-start.9 = (f32[32,128]{1,0:T(8,128)S(1)}, f32[32,128]{1,0:T(8,128)S(1)}, u32[]{:S(2)}, u32[]{:S(2)}) collective-permute-start(f32[32,128]{1,0:T(8,128)S(1)} %add.23), channel_id=1, source_target_pairs={{0,4},{1,5},{2,6},{3,7},{4,0},{5,1},{6,2},{7,3},{8,12},{9,13},{10,... | collective-permute-start | bytes 49160 | tf_op jit(solution)/shard_map/ppermute | solution.py:426
  123.9 1.1 collective-permute-done.10
  125.1 0.0 collective-permute-done.8
  125.1 0.7 collective-permute-done.9
  125.8 0.8 shard_map.94
  (2 shorter events, 0.0 us)
Async XLA Ops:
  0.8 10.2 %collective-permute-start = (s32[80,128]{1,0:T(8,128)S(1)}, s32[80,128]{1,0:T(8,128)S(1)}, u32[]{:S(2)}, u32[]{:S(2)}) collective-permute-start(s32[80,128]{1,0:T(8,128)S(1)} %bitcast.25), channel_id=1, source_target_pairs={{0,1},{1,2},{2,3},{3,4},{4,5},{5,6},{6,7},{7,0},{8,9},{9,10},{10,1... | collective-permute-start | bytes 122888 | tf_op jit(solution)/shard_map/ppermute | solution.py:417
  3.7 7.3 %collective-permute-start.1 = (s32[80,128]{1,0:T(8,128)S(1)}, s32[80,128]{1,0:T(8,128)S(1)}, u32[]{:S(2)}, u32[]{:S(2)}) collective-permute-start(s32[80,128]{1,0:T(8,128)S(1)} %bitcast.24), channel_id=1, source_target_pairs={{0,7},{1,0},{2,1},{3,2},{4,3},{5,4},{6,5},{7,6},{8,15},{9,8},{10,9... | collective-permute-start | bytes 122888 | tf_op jit(solution)/shard_map/ppermute | solution.py:417
  11.0 4.8 %copy-start.1 = (f32[5,160,128]{2,1,0:T(8,128)}, f32[5,160,128]{2,1,0:T(8,128)S(1)}, u32[]{:S(2)}) copy-start(f32[5,160,128]{2,1,0:T(8,128)S(1)} %pad_maximum_fusion) | copy-start | bytes 1228804
  11.0 4.8 %copy-start.4 = (s32[80,128]{1,0:T(8,128)}, s32[80,128]{1,0:T(8,128)S(1)}, u32[]{:S(2)}) copy-start(s32[80,128]{1,0:T(8,128)S(1)} %collective-permute-done.lower_ref) | copy-start | bytes 122884
  11.0 4.8 %copy-start.5 = (s32[80,128]{1,0:T(8,128)}, s32[80,128]{1,0:T(8,128)S(1)}, u32[]{:S(2)}) copy-start(s32[80,128]{1,0:T(8,128)S(1)} %collective-permute-done.1.upper_ref) | copy-start | bytes 122884
  11.1 33.8 %collective-permute-start.2 = (f32[800,128]{1,0:T(8,128)S(1)}, f32[800,128]{1,0:T(8,128)S(1)}, u32[]{:S(2)}, u32[]{:S(2)}) collective-permute-start(f32[800,128]{1,0:T(8,128)S(1)} %bitcast.15), channel_id=1, source_target_pairs={{0,1},{1,2},{2,3},{3,4},{4,5},{5,6},{6,7},{7,0},{8,9},{9,10},{10,1... | collective-permute-start | bytes 1228808 | tf_op jit(solution)/shard_map/ppermute | solution.py:417
  11.1 33.7 %collective-permute-start.3 = (f32[800,128]{1,0:T(8,128)S(1)}, f32[800,128]{1,0:T(8,128)S(1)}, u32[]{:S(2)}, u32[]{:S(2)}) collective-permute-start(f32[800,128]{1,0:T(8,128)S(1)} %bitcast.16), channel_id=1, source_target_pairs={{0,7},{1,0},{2,1},{3,2},{4,3},{5,4},{6,5},{7,6},{8,15},{9,8},{10,9... | collective-permute-start | bytes 1228808 | tf_op jit(solution)/shard_map/ppermute | solution.py:417
  44.8 0.8 copy-start.2
  44.8 0.9 copy-start.3
  110.1 3.5 %collective-permute-start.4 = (f32[6,8,128]{2,1,0:T(8,128)}, f32[6,8,128]{2,1,0:T(8,128)S(1)}, u32[]{:S(2)}, u32[]{:S(2)}) collective-permute-start(f32[6,8,128]{2,1,0:T(8,128)} %get-tuple-element.20.refs_0_), channel_id=1, source_target_pairs={{0,8},{8,16},{16,24},{24,0},{1,9},{9,17},{17,25},{25,1},{2,10},{10... | collective-permute-start | bytes 73736 | tf_op jit(solution)/shard_map/ppermute | solution.py:417
  110.1 4.1 %collective-permute-start.5 = (f32[6,8,128]{2,1,0:T(8,128)}, f32[6,8,128]{2,1,0:T(8,128)S(1)}, u32[]{:S(2)}, u32[]{:S(2)}) collective-permute-start(f32[6,8,128]{2,1,0:T(8,128)} %get-tuple-element.20.refs_0_), channel_id=1, source_target_pairs={{0,16},{8,24},{16,0},{24,8},{1,17},{9,25},{17,1},{25,9},{2,18},{10... | collective-permute-start | bytes 73736 | tf_op jit(solution)/shard_map/ppermute | solution.py:417
  111.8 3.1 %collective-permute-start.6 = (f32[6,8,128]{2,1,0:T(8,128)}, f32[6,8,128]{2,1,0:T(8,128)S(1)}, u32[]{:S(2)}, u32[]{:S(2)}) collective-permute-start(f32[6,8,128]{2,1,0:T(8,128)} %get-tuple-element.20.refs_0_), channel_id=1, source_target_pairs={{0,24},{8,0},{16,8},{24,16},{1,25},{9,1},{17,9},{25,17},{2,26},{10... | collective-permute-start | bytes 73736 | tf_op jit(solution)/shard_map/ppermute | solution.py:417
  114.9 0.7 copy-start
  115.7 3.8 %collective-permute-start.7 = (f32[32,128]{1,0:T(8,128)S(1)}, f32[32,128]{1,0:T(8,128)S(1)}, u32[]{:S(2)}, u32[]{:S(2)}) collective-permute-start(f32[32,128]{1,0:T(8,128)S(1)} %get-tuple-element.21), channel_id=1, source_target_pairs={{0,1},{1,0},{2,3},{3,2},{4,5},{5,4},{6,7},{7,6},{8,9},{9,8},{10,11... | collective-permute-start | bytes 49160 | tf_op jit(solution)/shard_map/ppermute | solution.py:426
  119.6 5.5 %collective-permute-start.10 = (f32[32,128]{1,0:T(8,128)S(1)}, f32[32,128]{1,0:T(8,128)S(1)}, u32[]{:S(2)}, u32[]{:S(2)}) collective-permute-start(f32[32,128]{1,0:T(8,128)S(1)} %add.23), channel_id=1, source_target_pairs={{0,6},{1,7},{2,4},{3,5},{4,2},{5,3},{6,0},{7,1},{8,14},{9,15},{10,... | collective-permute-start | bytes 49160 | tf_op jit(solution)/shard_map/ppermute | solution.py:426
  119.6 5.5 %collective-permute-start.8 = (f32[32,128]{1,0:T(8,128)S(1)}, f32[32,128]{1,0:T(8,128)S(1)}, u32[]{:S(2)}, u32[]{:S(2)}) collective-permute-start(f32[32,128]{1,0:T(8,128)S(1)} %add.23), channel_id=1, source_target_pairs={{0,2},{1,3},{2,0},{3,1},{4,6},{5,7},{6,4},{7,5},{8,10},{9,11},{10,... | collective-permute-start | bytes 49160 | tf_op jit(solution)/shard_map/ppermute | solution.py:426
  119.6 6.2 %collective-permute-start.9 = (f32[32,128]{1,0:T(8,128)S(1)}, f32[32,128]{1,0:T(8,128)S(1)}, u32[]{:S(2)}, u32[]{:S(2)}) collective-permute-start(f32[32,128]{1,0:T(8,128)S(1)} %add.23), channel_id=1, source_target_pairs={{0,4},{1,5},{2,6},{3,7},{4,0},{5,1},{6,2},{7,3},{8,12},{9,13},{10,... | collective-permute-start | bytes 49160 | tf_op jit(solution)/shard_map/ppermute | solution.py:426

commit v17 on v16

--- a/solution.py
+++ b/solution.py
@@ -61,6 +61,14 @@
     return jnp.asarray(np.stack([np.tile(kind, (16, 1)) for kind in kinds]), BF16)
 
 
+def sublane_numbers():
+    return jnp.asarray(np.arange(ROW)[:, None] * np.ones((1, ROW)), BF16)
+
+
+def equal_rows(numbers, row, value):
+    return jnp.where(numbers == row.astype(F32).astype(BF16), value, jnp.zeros((), BF16))
+
+
 def two_pieces(values):
     high = values.astype(BF16)
     low = (values - high.astype(F32)).astype(BF16)
@@ -123,7 +131,7 @@
 
 
 def near_kernel(
-    rows, order_ref, next_ref, lower_ref, upper_ref, partner_ref, fields_ref, select_ref, left_ref, list_ref,
+    rows, order_ref, next_ref, lower_ref, upper_ref, partner_ref, fields_ref, select_ref, numbers_ref, left_ref, list_ref,
     table, stage_a, stage_b, lists,
 ):
     turn = pl.program_id(0)
@@ -146,8 +154,7 @@
     def compose(tile):
         entries = partner_ref[0, tile : tile + 1, :]
         width = entries.shape[1]
-        grid = lax.broadcasted_iota(I32, (LANES, width), 0)
-        hot = jnp.where(grid == (entries & (LANES - 1)), 1.0, 0.0).astype(BF16)
+        hot = equal_rows(numbers_ref[0:LANES, 0:width], entries & (LANES - 1), jnp.ones((), BF16))
         found = jnp.dot(lists[...], jnp.concatenate([hot, hot], axis=0), preferred_element_type=F32)
         yield
         block = entries >> 7
@@ -225,8 +232,8 @@
     sums[...] = both[0:TILE] + both[TILE:] + masked(left_ref[place], kinds_ref[3]).astype(F32)
 
 
-def pair_scatter(numbers, sums, total):
-    entries = jnp.concatenate(numbers, axis=1)
+def pair_scatter(lists, numbers_ref, sums, total):
+    entries = jnp.concatenate(lists, axis=1)
     forces = [[], [], []]
     for side in range(2):
         across = sums[side].T
@@ -237,17 +244,14 @@
             )
             forces[axis].append(place * across[ONE : ONE + 1] - moment)
     yield
-    grid = lax.broadcasted_iota(I32, (ROW, ROW), 0)
-    hot = jnp.where(grid == (entries & (ROW - 1)), 1.0, 0.0).astype(BF16)
+    hot = equal_rows(numbers_ref[...], entries & (ROW - 1), jnp.ones((), BF16))
     yield
     count = total.shape[0] // 3
-    mask = lax.broadcasted_iota(I32, (count, ROW), 0) == (entries >> 8)
     high, low = [], []
     for axis in range(3):
-        force = jnp.concatenate(forces[axis], axis=1)
-        part = force.astype(BF16).astype(F32)
-        high.append(jnp.where(mask, part, 0.0).astype(BF16))
-        low.append(jnp.where(mask, force - part, 0.0).astype(BF16))
+        parts = two_pieces(jnp.concatenate(forces[axis], axis=1))
+        for part, kept in zip(parts, (high, low)):
+            kept.append(equal_rows(numbers_ref[0:count, :], entries >> 8, part))
         yield
     both = nt_dot(jnp.concatenate(high + low, axis=0), hot)
     total[...] += both[0 : 3 * count] + both[3 * count :]
@@ -261,7 +265,7 @@
 
 
 def force_kernel(
-    rows, list_ref, next_ref, order_ref, before_ref, lower_ref, fields_ref, upper_ref, kinds_ref, left_ref,
+    rows, list_ref, next_ref, order_ref, before_ref, lower_ref, fields_ref, upper_ref, kinds_ref, numbers_ref, left_ref,
     out_ref, solute_ref, table, total, far_a, far_b, sum_a, sum_b,
 ):
     turn = pl.program_id(0)
@@ -282,7 +286,7 @@
 
     def scatter(local, sums):
         ref, first = (order_ref, local) if local >= 0 else (before_ref, local + 8)
-        return pair_scatter([ref[first + side : first + side + 1, :] for side in range(2)], sums, total)
+        return pair_scatter([ref[first + side : first + side + 1, :] for side in range(2)], numbers_ref, sums, total)
 
     @pl.when(turn == 0)
     def _():
@@ -466,7 +470,7 @@
         in_specs=[listed(TILE, 0), listed(TILE, 1)]
         + [vector] * 2
         + [pl.BlockSpec((1, 8, partners), lambda i: (0, i, 0))]
-        + [vector] * 2,
+        + [vector] * 3,
         out_specs=[
             pl.BlockSpec((8, TILE, LANES), lambda i: (i, 0, 0)),
             pl.BlockSpec((8 * partners // LANES, LANES), lambda i: (i, 0)),
@@ -479,7 +483,7 @@
         ],
         compiler_params=params,
         cost_estimate=pl.CostEstimate(flops=25 * 10**9, bytes_accessed=10**7, transcendentals=0),
-    )(order, order, lower_list, upper_list, tile_atoms, fields, near_selector())
+    )(order, order, lower_list, upper_list, tile_atoms, fields, near_selector(), sublane_numbers())
     pairs = partner_rows.reshape(rows * partners)
     out, solute = pl.pallas_call(
         functools.partial(force_kernel, rows),
@@ -487,7 +491,7 @@
         out_shape=[whole(3 * rows, LANES), whole(6, SOL_DEV // LANES, LANES)],
         in_specs=[listed(partners, 0), listed(partners, 1)]
         + [pl.BlockSpec((8, LANES), lambda i, by=by: (jnp.maximum(i - by, 0), 0)) for by in (0, 1)]
-        + [vector] * 4
+        + [vector] * 5
         + [pl.BlockSpec((8, TILE, LANES), lambda i: (i, 0, 0))],
         out_specs=[vector] * 2,
         scratch_shapes=[
@@ -500,7 +504,7 @@
         ],
         compiler_params=params,
         cost_estimate=pl.CostEstimate(flops=25 * 10**9, bytes_accessed=10**7, transcendentals=0),
-    )(pairs, pairs, tile_order, tile_order, lower, fields, upper, near_masks(), left)
+    )(pairs, pairs, tile_order, tile_order, lower, fields, upper, near_masks(), sublane_numbers(), left)
     out = out.reshape(3, rows, LANES)
     solutes = round_trip(solute, "image")
     small = pltpu.CompilerParams(vmem_limit_bytes=8 * 1024 * 1024)

time: 127 us -> 127 us (level)
  no operation moved by 1% of the time
where the time goes in v17:
time: 127 us
  Pallas kernels  94.6 us (74%)
  starting transfers between devices  18.4 us (14%)
  waiting for transfers between devices  7.36 us (6%)
  other arithmetic  3.47 us (3%)
  local copies, waits for them, and re-layouts  2.44 us (2%)
    pallas_call x1, Pallas kernels, per_device(): pl.pallas_call(functools.partial(force_kernel, rows), grid=(rows // 8,),...  65.1 us
    pallas_call x1, Pallas kernels, per_device(): pl.pallas_call(functools.partial(near_kernel, rows), grid=(rows // 8,), o...  28.6 us
    ppermute x7, starting transfers between devices, turned(): lax.ppermute(array, axis, [(i, (i + by) % count) for i in range(count)])  14 us
    ppermute x4, waiting for transfers between devices, crossed(): return lax.ppermute(array, axis, [(i, i ^ by) for i in range(count)])  5.62 us
    ppermute x4, starting transfers between devices, crossed(): return lax.ppermute(array, axis, [(i, i ^ by) for i in range(count)])  4.45 us
  transfers between devices with their start and end apart: 11, of which 6 were waited for; matrix products, arithmetic and copies ran while one was open for 3% of the time, Pallas kernels for 23%

profile of v17, /device:TPU:0, one launch (start us, length us, event | category | flops | bytes accessed | tf_op | source)
XLA Modules:
  0.0 127.0 jit_solution(15816575057852637512)
XLA Ops:
  0.0 0.8 fusion.9
  0.8 2.9 %collective-permute-start = (s32[80,128]{1,0:T(8,128)S(1)}, s32[80,128]{1,0:T(8,128)S(1)}, u32[]{:S(2)}, u32[]{:S(2)}) collective-permute-start(s32[80,128]{1,0:T(8,128)S(1)} %bitcast.25), channel_id=1, source_target_pairs={{0,1},{1,2},{2,3},{3,4},{4,5},{5,6},{6,7},{7,0},{8,9},{9,10},{10,1... | collective-permute-start | bytes 122888 | tf_op jit(solution)/shard_map/ppermute | solution.py:421
  3.7 3.1 %collective-permute-start.1 = (s32[80,128]{1,0:T(8,128)S(1)}, s32[80,128]{1,0:T(8,128)S(1)}, u32[]{:S(2)}, u32[]{:S(2)}) collective-permute-start(s32[80,128]{1,0:T(8,128)S(1)} %bitcast.24), channel_id=1, source_target_pairs={{0,7},{1,0},{2,1},{3,2},{4,3},{5,4},{6,5},{7,6},{8,15},{9,8},{10,9... | collective-permute-start | bytes 122888 | tf_op jit(solution)/shard_map/ppermute | solution.py:421
  7.5 1.5 %fusion.5.order_ref.next_ref = s32[20480]{0:T(1024)} fusion(s32[20480]{0:T(1024)} %bitcast.21), kind=kLoop, calls=%fused_computation.9 | loop fusion | flops 163840 | bytes 163840 | tf_op jit(solution)/shard_map/add | solution.py:456
  9.1 0.9 fusion.1
  10.0 1.0 pad_maximum_fusion
  11.0 0.0 copy-start.1
  11.0 0.0 collective-permute-done.lower_ref
  11.0 0.0 copy-start.4
  11.0 0.0 collective-permute-done.1.upper_ref
  11.0 0.0 copy-start.5
  11.1 0.1 collective-permute-start.2
  11.1 4.7 %collective-permute-start.3 = (f32[800,128]{1,0:T(8,128)S(1)}, f32[800,128]{1,0:T(8,128)S(1)}, u32[]{:S(2)}, u32[]{:S(2)}) collective-permute-start(f32[800,128]{1,0:T(8,128)S(1)} %bitcast.16), channel_id=1, source_target_pairs={{0,7},{1,0},{2,1},{3,2},{4,3},{5,4},{6,5},{7,6},{8,15},{9,8},{10,9... | collective-permute-start | bytes 1228808 | tf_op jit(solution)/shard_map/ppermute | solution.py:421
  15.8 0.0 copy-done.1
  15.8 0.0 copy-done.4
  15.8 0.0 copy-done.5
  15.8 28.6 %shard_map.109 = (bf16[160,128,128]{2,1,0:T(8,128)(2,1)}, s32[320,128]{1,0:T(8,128)}) custom-call(s32[20480]{0:T(1024)} %fusion.5.order_ref.next_ref, s32[20480]{0:T(1024)} %fusion.5.order_ref.next_ref, s32[80,128]{1,0:T(8,128)} %copy-done.4, s32[80,128]{1,0:T(8,128)} %copy-done.5, s32[1,160,256]{2,1,0:T(8,128)} %partner_ref.1, f32[800,128]{1,0:T(8,128)} %bitcast.17, ...), custom_call_target="tpu_custom_call" | custom-call | flops 24999999488 | bytes 10000000 | tf_op jit(solution)/shard_map/pallas_call | solution.py:466
  44.4 0.0 collective-permute-done.2.lower_ref
  44.4 0.0 copy-start.2
  44.4 0.0 collective-permute-done.3.upper_ref
  44.4 0.0 copy-start.3
  44.4 0.7 copy-done.2
  45.2 0.2 copy-done.3
  45.3 65.1 %shard_map.110 = (f32[480,128]{1,0:T(8,128)}, f32[6,8,128]{2,1,0:T(8,128)}) custom-call(s32[40960]{0:T(1024)} %bitcast.26, s32[40960]{0:T(1024)} %bitcast.27, s32[160,128]{1,0:T(8,128)} %bitcast.22, s32[160,128]{1,0:T(8,128)} %bitcast.23, f32[800,128]{1,0:T(8,128)} %copy-done.2, f32[800,128]{1,0:T(8,128)} %bitcast.18, f32[800,128]{1,0:T(8,128)} %copy-done.3, ...), custom_call_target="tpu_custom_call" | custom-call | flops 24999999488 | bytes 10000000 | tf_op jit(solution)/shard_map/pallas_call | solution.py:488
  110.5 0.0 collective-permute-start.4
  110.5 1.8 %collective-permute-start.5 = (f32[6,8,128]{2,1,0:T(8,128)}, f32[6,8,128]{2,1,0:T(8,128)S(1)}, u32[]{:S(2)}, u32[]{:S(2)}) collective-permute-start(f32[6,8,128]{2,1,0:T(8,128)} %get-tuple-element.20.refs_0_), channel_id=1, source_target_pairs={{0,16},{8,24},{16,0},{24,8},{1,17},{9,25},{17,1},{25,9},{2,18},{10... | collective-permute-start | bytes 73736 | tf_op jit(solution)/shard_map/ppermute | solution.py:421
  112.3 1.4 %collective-permute-start.6 = (f32[6,8,128]{2,1,0:T(8,128)}, f32[6,8,128]{2,1,0:T(8,128)S(1)}, u32[]{:S(2)}, u32[]{:S(2)}) collective-permute-start(f32[6,8,128]{2,1,0:T(8,128)} %get-tuple-element.20.refs_0_), channel_id=1, source_target_pairs={{0,24},{8,0},{16,8},{24,16},{1,25},{9,1},{17,9},{25,17},{2,26},{10... | collective-permute-start | bytes 73736 | tf_op jit(solution)/shard_map/ppermute | solution.py:421
  113.6 0.3 collective-permute-done.4.refs_1_
  113.9 0.6 collective-permute-done.5.refs_2_
  114.6 0.8 collective-permute-done.6.refs_3_
  115.4 0.0 copy-start
  115.4 0.7 copy-done
  116.1 0.1 shard_map.111
  116.2 0.1 collective-permute-start.7
  116.3 3.7 %collective-permute-done.7 = f32[32,128]{1,0:T(8,128)S(1)} collective-permute-done((f32[32,128]{1,0:T(8,128)S(1)}, f32[32,128]{1,0:T(8,128)S(1)}, u32[]{:S(2)}, u32[]{:S(2)}) %collective-permute-start.7) | collective-permute-done | bytes 16416 | tf_op jit(solution)/shard_map/ppermute | solution.py:430
  120.0 0.0 collective-permute-start.10
  120.0 0.1 collective-permute-start.8
  120.1 4.3 %collective-permute-start.9 = (f32[32,128]{1,0:T(8,128)S(1)}, f32[32,128]{1,0:T(8,128)S(1)}, u32[]{:S(2)}, u32[]{:S(2)}) collective-permute-start(f32[32,128]{1,0:T(8,128)S(1)} %add.23), channel_id=1, source_target_pairs={{0,4},{1,5},{2,6},{3,7},{4,0},{5,1},{6,2},{7,3},{8,12},{9,13},{10,... | collective-permute-start | bytes 49160 | tf_op jit(solution)/shard_map/ppermute | solution.py:430
  124.4 1.1 collective-permute-done.10
  125.5 0.0 collective-permute-done.8
  125.5 0.7 collective-permute-done.9
  126.3 0.8 shard_map.112
  (2 shorter events, 0.0 us)
Async XLA Ops:
  0.8 10.2 %collective-permute-start = (s32[80,128]{1,0:T(8,128)S(1)}, s32[80,128]{1,0:T(8,128)S(1)}, u32[]{:S(2)}, u32[]{:S(2)}) collective-permute-start(s32[80,128]{1,0:T(8,128)S(1)} %bitcast.25), channel_id=1, source_target_pairs={{0,1},{1,2},{2,3},{3,4},{4,5},{5,6},{6,7},{7,0},{8,9},{9,10},{10,1... | collective-permute-start | bytes 122888 | tf_op jit(solution)/shard_map/ppermute | solution.py:421
  3.7 7.3 %collective-permute-start.1 = (s32[80,128]{1,0:T(8,128)S(1)}, s32[80,128]{1,0:T(8,128)S(1)}, u32[]{:S(2)}, u32[]{:S(2)}) collective-permute-start(s32[80,128]{1,0:T(8,128)S(1)} %bitcast.24), channel_id=1, source_target_pairs={{0,7},{1,0},{2,1},{3,2},{4,3},{5,4},{6,5},{7,6},{8,15},{9,8},{10,9... | collective-permute-start | bytes 122888 | tf_op jit(solution)/shard_map/ppermute | solution.py:421
  11.0 4.8 %copy-start.1 = (f32[5,160,128]{2,1,0:T(8,128)}, f32[5,160,128]{2,1,0:T(8,128)S(1)}, u32[]{:S(2)}) copy-start(f32[5,160,128]{2,1,0:T(8,128)S(1)} %pad_maximum_fusion) | copy-start | bytes 1228804
  11.0 4.8 %copy-start.4 = (s32[80,128]{1,0:T(8,128)}, s32[80,128]{1,0:T(8,128)S(1)}, u32[]{:S(2)}) copy-start(s32[80,128]{1,0:T(8,128)S(1)} %collective-permute-done.lower_ref) | copy-start | bytes 122884
  11.0 4.8 %copy-start.5 = (s32[80,128]{1,0:T(8,128)}, s32[80,128]{1,0:T(8,128)S(1)}, u32[]{:S(2)}) copy-start(s32[80,128]{1,0:T(8,128)S(1)} %collective-permute-done.1.upper_ref) | copy-start | bytes 122884
  11.1 33.4 %collective-permute-start.2 = (f32[800,128]{1,0:T(8,128)S(1)}, f32[800,128]{1,0:T(8,128)S(1)}, u32[]{:S(2)}, u32[]{:S(2)}) collective-permute-start(f32[800,128]{1,0:T(8,128)S(1)} %bitcast.15), channel_id=1, source_target_pairs={{0,1},{1,2},{2,3},{3,4},{4,5},{5,6},{6,7},{7,0},{8,9},{9,10},{10,1... | collective-permute-start | bytes 1228808 | tf_op jit(solution)/shard_map/ppermute | solution.py:421
  11.1 33.3 %collective-permute-start.3 = (f32[800,128]{1,0:T(8,128)S(1)}, f32[800,128]{1,0:T(8,128)S(1)}, u32[]{:S(2)}, u32[]{:S(2)}) collective-permute-start(f32[800,128]{1,0:T(8,128)S(1)} %bitcast.16), channel_id=1, source_target_pairs={{0,7},{1,0},{2,1},{3,2},{4,3},{5,4},{6,5},{7,6},{8,15},{9,8},{10,9... | collective-permute-start | bytes 1228808 | tf_op jit(solution)/shard_map/ppermute | solution.py:421
  44.4 0.8 copy-start.2
  44.4 0.9 copy-start.3
  110.5 3.5 %collective-permute-start.4 = (f32[6,8,128]{2,1,0:T(8,128)}, f32[6,8,128]{2,1,0:T(8,128)S(1)}, u32[]{:S(2)}, u32[]{:S(2)}) collective-permute-start(f32[6,8,128]{2,1,0:T(8,128)} %get-tuple-element.20.refs_0_), channel_id=1, source_target_pairs={{0,8},{8,16},{16,24},{24,0},{1,9},{9,17},{17,25},{25,1},{2,10},{10... | collective-permute-start | bytes 73736 | tf_op jit(solution)/shard_map/ppermute | solution.py:421
  110.5 4.1 %collective-permute-start.5 = (f32[6,8,128]{2,1,0:T(8,128)}, f32[6,8,128]{2,1,0:T(8,128)S(1)}, u32[]{:S(2)}, u32[]{:S(2)}) collective-permute-start(f32[6,8,128]{2,1,0:T(8,128)} %get-tuple-element.20.refs_0_), channel_id=1, source_target_pairs={{0,16},{8,24},{16,0},{24,8},{1,17},{9,25},{17,1},{25,9},{2,18},{10... | collective-permute-start | bytes 73736 | tf_op jit(solution)/shard_map/ppermute | solution.py:421
  112.3 3.1 %collective-permute-start.6 = (f32[6,8,128]{2,1,0:T(8,128)}, f32[6,8,128]{2,1,0:T(8,128)S(1)}, u32[]{:S(2)}, u32[]{:S(2)}) collective-permute-start(f32[6,8,128]{2,1,0:T(8,128)} %get-tuple-element.20.refs_0_), channel_id=1, source_target_pairs={{0,24},{8,0},{16,8},{24,16},{1,25},{9,1},{17,9},{25,17},{2,26},{10... | collective-permute-start | bytes 73736 | tf_op jit(solution)/shard_map/ppermute | solution.py:421
  115.4 0.7 copy-start
  116.2 3.8 %collective-permute-start.7 = (f32[32,128]{1,0:T(8,128)S(1)}, f32[32,128]{1,0:T(8,128)S(1)}, u32[]{:S(2)}, u32[]{:S(2)}) collective-permute-start(f32[32,128]{1,0:T(8,128)S(1)} %get-tuple-element.21), channel_id=1, source_target_pairs={{0,1},{1,0},{2,3},{3,2},{4,5},{5,4},{6,7},{7,6},{8,9},{9,8},{10,11... | collective-permute-start | bytes 49160 | tf_op jit(solution)/shard_map/ppermute | solution.py:430
  120.0 5.5 %collective-permute-start.10 = (f32[32,128]{1,0:T(8,128)S(1)}, f32[32,128]{1,0:T(8,128)S(1)}, u32[]{:S(2)}, u32[]{:S(2)}) collective-permute-start(f32[32,128]{1,0:T(8,128)S(1)} %add.23), channel_id=1, source_target_pairs={{0,6},{1,7},{2,4},{3,5},{4,2},{5,3},{6,0},{7,1},{8,14},{9,15},{10,... | collective-permute-start | bytes 49160 | tf_op jit(solution)/shard_map/ppermute | solution.py:430
  120.0 5.5 %collective-permute-start.8 = (f32[32,128]{1,0:T(8,128)S(1)}, f32[32,128]{1,0:T(8,128)S(1)}, u32[]{:S(2)}, u32[]{:S(2)}) collective-permute-start(f32[32,128]{1,0:T(8,128)S(1)} %add.23), channel_id=1, source_target_pairs={{0,2},{1,3},{2,0},{3,1},{4,6},{5,7},{6,4},{7,5},{8,10},{9,11},{10,... | collective-permute-start | bytes 49160 | tf_op jit(solution)/shard_map/ppermute | solution.py:430
  120.1 6.2 %collective-permute-start.9 = (f32[32,128]{1,0:T(8,128)S(1)}, f32[32,128]{1,0:T(8,128)S(1)}, u32[]{:S(2)}, u32[]{:S(2)}) collective-permute-start(f32[32,128]{1,0:T(8,128)S(1)} %add.23), channel_id=1, source_target_pairs={{0,4},{1,5},{2,6},{3,7},{4,0},{5,1},{6,2},{7,3},{8,12},{9,13},{10,... | collective-permute-start | bytes 49160 | tf_op jit(solution)/shard_map/ppermute | solution.py:430

commit v18 on v17

--- a/solution.py
+++ b/solution.py
@@ -13,7 +13,6 @@
 TILE = 128
 LANES = 128
 FIELDS = 5
-PAD = 8
 
 LJ_COEF = 0.5
 CHARGE_COEF = 0.1
@@ -100,8 +99,8 @@
         return [parts[piece] for piece in FAR_PIECES]
 
     def put(block, value):
-        start = pl.multiple_of(first + (start_row + block) * LANES + PAD, PAD)
-        table[pl.ds(start, LANES), 0:USED] = value
+        start = pl.multiple_of(first + (start_row + block) * LANES, LANES)
+        flat(table)[pl.ds(start, LANES), 0:USED] = value
 
     for block in range(0, count, 4):
         for side in range(2):
@@ -112,22 +111,18 @@
             put(block + 2 + side, both[:, side * LANES : side * LANES + USED])
 
 
-def sublane_masks():
-    sublane = lax.broadcasted_iota(I32, (8, LANES), 0)
-    used = lax.broadcasted_iota(I32, (8, LANES), 1) < USED
-    return [sublane == k for k in range(8)] + [used]
-
-
-def merged(table, entries, masks):
-    result = table[pl.ds(entries[0], 8), :]
-    for k in range(1, 8):
-        result = jnp.where(masks[k], table[pl.ds(entries[k], 8), :], result)
-    return jnp.where(masks[8], result, 0.0)
-
-
-def copy_rows(table, entry_of, stage, start, masks):
-    parts = [merged(table, [entry_of(start + half + k) for k in range(8)], masks) for half in (0, 8)]
-    stage[start : start + 16, :] = jnp.concatenate(parts, axis=0).astype(BF16)
+def flat(table):
+    return table.reshape(table.shape[0], LANES)
+
+
+def copy_rows(table, entry_of, stage, start):
+    for k in range(start, start + 16):
+        stage[k : k + 1, :] = table[entry_of(k)]
+
+
+def used_lanes(stage):
+    used = lax.broadcasted_iota(I32, stage.shape, 1) < USED
+    return jnp.where(used, stage[...], 0.0).astype(BF16)
 
 
 def near_kernel(
@@ -166,13 +161,10 @@
         atom = jnp.sum(picked, axis=0, keepdims=True).astype(I32)
         yield
         atom = jnp.where(low, atom, jnp.where(high, atom + 2 * rows * LANES, entries + half * LANES))
-        atom = atom + PAD - (lax.broadcasted_iota(I32, (1, width), 1) & 7)
         for side in range(width // LANES):
             row = tile * (width // LANES) + side
             list_ref[row : row + 1, :] = atom[:, side * LANES : (side + 1) * LANES]
 
-    masks = sublane_masks()
-
     def load(local, stage):
         ref, first = (order_ref, local) if local < 8 else (next_ref, local - 8)
 
@@ -180,11 +172,11 @@
             return ref[first * TILE + k]
 
         return [
-            functools.partial(copy_rows, table, entry_of, stage, start, masks) for start in range(0, TILE, 16)
+            functools.partial(copy_rows, table, entry_of, stage, start) for start in range(0, TILE, 16)
         ]
 
     def factors(place, stage):
-        left = jnp.dot(stage[...], select_ref[...], preferred_element_type=F32)
+        left = jnp.dot(used_lanes(stage), select_ref[...], preferred_element_type=F32)
         yield
         left_ref[place] = left.astype(BF16)
 
@@ -209,7 +201,7 @@
 
 
 def tile_sums(left_ref, kinds_ref, place, far, sums):
-    others = far[...]
+    others = used_lanes(far)
     left = left_ref[place]
     left = jnp.concatenate([masked(left, kinds_ref[kind]) for kind in range(3)], axis=0)
     yield
@@ -271,8 +263,6 @@
     turn = pl.program_id(0)
     partners = far_a.shape[1]
     own = rows * LANES
-    masks = sublane_masks()
-
     def load(local, far):
         ref, first = (list_ref, local) if local < 8 else (next_ref, local - 8)
 
@@ -280,7 +270,7 @@
             return ref[first * partners + k]
 
         return [
-            functools.partial(copy_rows, table, entry_of, far, start, masks)
+            functools.partial(copy_rows, table, entry_of, far, start)
             for start in range(0, partners, 16)
         ]
 
@@ -453,7 +443,7 @@
     fields, lower_list, upper_list = lax.optimization_barrier((fields, lower_list, upper_list))
     lower, upper = turned(fields, "space", 1), turned(fields, "space", -1)
     tile_order = cell_order.reshape(rows, LANES)
-    order = cell_order.reshape(atoms) + (PAD - jnp.arange(atoms, dtype=I32) % 8)
+    order = cell_order.reshape(atoms)
     scalar = pl.BlockSpec(memory_space=pltpu.SMEM)
     vector = pl.BlockSpec(memory_space=pltpu.VMEM)
     params = pltpu.CompilerParams(vmem_limit_bytes=VMEM_LIMIT)
@@ -462,7 +452,6 @@
     def listed(size, by):
         return pl.BlockSpec((8 * size,), lambda i: (jnp.clip(i + by, 0, last),), memory_space=pltpu.SMEM)
 
-    table = (atoms + 2 * PAD, LANES)
     left, partner_rows = pl.pallas_call(
         functools.partial(near_kernel, rows),
         grid=(rows // 8,),
@@ -476,9 +465,9 @@
             pl.BlockSpec((8 * partners // LANES, LANES), lambda i: (i, 0)),
         ],
         scratch_shapes=[
-            pltpu.VMEM(table, F32),
-            pltpu.VMEM((2, TILE, LANES), BF16),
-            pltpu.VMEM((2, TILE, LANES), BF16),
+            pltpu.VMEM((atoms, 1, LANES), F32),
+            pltpu.VMEM((2, TILE, LANES), F32),
+            pltpu.VMEM((2, TILE, LANES), F32),
             pltpu.VMEM((rows, 2 * LANES), BF16),
         ],
         compiler_params=params,
@@ -495,10 +484,10 @@
         + [pl.BlockSpec((8, TILE, LANES), lambda i: (i, 0, 0))],
         out_specs=[vector] * 2,
         scratch_shapes=[
-            pltpu.VMEM((3 * atoms + 2 * PAD, LANES), F32),
+            pltpu.VMEM((3 * atoms, 1, LANES), F32),
             pltpu.VMEM((3 * atoms // ROW, ROW), F32),
-            pltpu.VMEM((2, partners, LANES), BF16),
-            pltpu.VMEM((2, partners, LANES), BF16),
+            pltpu.VMEM((2, partners, LANES), F32),
+            pltpu.VMEM((2, partners, LANES), F32),
             pltpu.VMEM((2, TILE, LANES), F32),
             pltpu.VMEM((2, TILE, LANES), F32),
         ],

time: 127 us -> 136 us (1.071)
  Pallas kernels: 94.6 us -> 105 us
  other arithmetic: 3.47 us -> 1.94 us
    pallas_call x1, Pallas kernels: 65.1 us -> 72.5 us  [per_device(): pl.pallas_call(functools.partial(force_kernel, rows), grid=(rows // 8,),...]
    pallas_call x1, Pallas kernels: 28.6 us -> 31.6 us  [per_device(): pl.pallas_call(functools.partial(near_kernel, rows), grid=(rows // 8,), o...]
    add x1 -> x0, other arithmetic: 1.54 us -> none  [per_device(): order = cell_order.reshape(atoms) + (PAD - jnp.arange(atoms, dtype=I32) % 8)]
  transfers between devices with their start and end apart: 11 -> 11, of which waited for: 6 -> 6; matrix products, arithmetic and copies ran while one was open for 3% -> 1% of each run, Pallas kernels for 23% -> 23%
where the time goes in v18:
time: 136 us
  Pallas kernels  105 us (77%)
  starting transfers between devices  18.3 us (13%)
  waiting for transfers between devices  7.36 us (5%)
  local copies, waits for them, and re-layouts  2.44 us (2%)
  other arithmetic  1.94 us (1%)
    pallas_call x1, Pallas kernels, per_device(): pl.pallas_call(functools.partial(force_kernel, rows), grid=(rows // 8,),...  72.5 us
    pallas_call x1, Pallas kernels, per_device(): pl.pallas_call(functools.partial(near_kernel, rows), grid=(rows // 8,), o...  31.6 us
    ppermute x7, starting transfers between devices, turned(): lax.ppermute(array, axis, [(i, (i + by) % count) for i in range(count)])  13.9 us
    ppermute x4, waiting for transfers between devices, crossed(): return lax.ppermute(array, axis, [(i, i ^ by) for i in range(count)])  5.62 us
    ppermute x4, starting transfers between devices, crossed(): return lax.ppermute(array, axis, [(i, i ^ by) for i in range(count)])  4.45 us
  transfers between devices with their start and end apart: 11, of which 6 were waited for; matrix products, arithmetic and copies ran while one was open for 1% of the time, Pallas kernels for 23%

profile of v18, /device:TPU:0, one launch (start us, length us, event | category | flops | bytes accessed | tf_op | source)
XLA Modules:
  0.0 135.7 jit_solution(7262791002057894322)
XLA Ops:
  0.0 0.8 fusion.4
  0.8 2.9 %collective-permute-start = (s32[80,128]{1,0:T(8,128)S(1)}, s32[80,128]{1,0:T(8,128)S(1)}, u32[]{:S(2)}, u32[]{:S(2)}) collective-permute-start(s32[80,128]{1,0:T(8,128)S(1)} %bitcast.22), channel_id=1, source_target_pairs={{0,1},{1,2},{2,3},{3,4},{4,5},{5,6},{6,7},{7,0},{8,9},{9,10},{10,1... | collective-permute-start | bytes 122888 | tf_op jit(solution)/shard_map/ppermute | solution.py:411
  3.7 3.1 %collective-permute-start.1 = (s32[80,128]{1,0:T(8,128)S(1)}, s32[80,128]{1,0:T(8,128)S(1)}, u32[]{:S(2)}, u32[]{:S(2)}) collective-permute-start(s32[80,128]{1,0:T(8,128)S(1)} %bitcast.21), channel_id=1, source_target_pairs={{0,7},{1,0},{2,1},{3,2},{4,3},{5,4},{6,5},{7,6},{8,15},{9,8},{10,9... | collective-permute-start | bytes 122888 | tf_op jit(solution)/shard_map/ppermute | solution.py:411
  7.5 0.9 fusion.1
  8.5 1.0 pad_maximum_fusion
  9.5 0.0 copy-start.1
  9.5 0.0 collective-permute-done.lower_ref
  9.5 0.0 copy-start.4
  9.5 0.0 collective-permute-done.1.upper_ref
  9.5 0.0 copy-start.5
  9.5 0.7 collective-permute-start.2
  10.2 4.1 %collective-permute-start.3 = (f32[800,128]{1,0:T(8,128)S(1)}, f32[800,128]{1,0:T(8,128)S(1)}, u32[]{:S(2)}, u32[]{:S(2)}) collective-permute-start(f32[800,128]{1,0:T(8,128)S(1)} %bitcast.16), channel_id=1, source_target_pairs={{0,7},{1,0},{2,1},{3,2},{4,3},{5,4},{6,5},{7,6},{8,15},{9,8},{10,9... | collective-permute-start | bytes 1228808 | tf_op jit(solution)/shard_map/ppermute | solution.py:411
  14.3 0.0 copy-done.1
  14.3 0.0 copy-done.4
  14.3 0.0 copy-done.5
  14.3 31.6 %shard_map.109 = (bf16[160,128,128]{2,1,0:T(8,128)(2,1)}, s32[320,128]{1,0:T(8,128)}) custom-call(s32[20480]{0:T(1024)} %bitcast.23, s32[20480]{0:T(1024)} %bitcast.24, s32[80,128]{1,0:T(8,128)} %copy-done.4, s32[80,128]{1,0:T(8,128)} %copy-done.5, s32[1,160,256]{2,1,0:T(8,128)} %partner_ref.1, f32[800,128]{1,0:T(8,128)} %bitcast.17, ...), custom_call_target="tpu_custom_call" | custom-call | flops 24999999488 | bytes 10000000 | tf_op jit(solution)/shard_map/pallas_call | solution.py:455
  45.9 0.0 collective-permute-done.2.lower_ref
  45.9 0.0 copy-start.2
  45.9 0.0 collective-permute-done.3.upper_ref
  45.9 0.0 copy-start.3
  45.9 0.7 copy-done.2
  46.6 0.2 copy-done.3
  46.8 72.5 %shard_map.110 = (f32[480,128]{1,0:T(8,128)}, f32[6,8,128]{2,1,0:T(8,128)}) custom-call(s32[40960]{0:T(1024)} %bitcast.27, s32[40960]{0:T(1024)} %bitcast.28, s32[160,128]{1,0:T(8,128)} %bitcast.25, s32[160,128]{1,0:T(8,128)} %bitcast.26, f32[800,128]{1,0:T(8,128)} %copy-done.2, f32[800,128]{1,0:T(8,128)} %bitcast.18, f32[800,128]{1,0:T(8,128)} %copy-done.3, ...), custom_call_target="tpu_custom_call" | custom-call | flops 24999999488 | bytes 10000000 | tf_op jit(solution)/shard_map/pallas_call | solution.py:477
  119.2 0.0 collective-permute-start.4
  119.3 1.7 %collective-permute-start.5 = (f32[6,8,128]{2,1,0:T(8,128)}, f32[6,8,128]{2,1,0:T(8,128)S(1)}, u32[]{:S(2)}, u32[]{:S(2)}) collective-permute-start(f32[6,8,128]{2,1,0:T(8,128)} %get-tuple-element.20.refs_0_), channel_id=1, source_target_pairs={{0,16},{8,24},{16,0},{24,8},{1,17},{9,25},{17,1},{25,9},{2,18},{10... | collective-permute-start | bytes 73736 | tf_op jit(solution)/shard_map/ppermute | solution.py:411
  120.9 1.4 %collective-permute-start.6 = (f32[6,8,128]{2,1,0:T(8,128)}, f32[6,8,128]{2,1,0:T(8,128)S(1)}, u32[]{:S(2)}, u32[]{:S(2)}) collective-permute-start(f32[6,8,128]{2,1,0:T(8,128)} %get-tuple-element.20.refs_0_), channel_id=1, source_target_pairs={{0,24},{8,0},{16,8},{24,16},{1,25},{9,1},{17,9},{25,17},{2,26},{10... | collective-permute-start | bytes 73736 | tf_op jit(solution)/shard_map/ppermute | solution.py:411
  122.3 0.4 collective-permute-done.4.refs_1_
  122.7 0.6 collective-permute-done.5.refs_2_
  123.4 0.7 collective-permute-done.6.refs_3_
  124.1 0.0 copy-start
  124.1 0.7 copy-done
  124.8 0.1 shard_map.111
  124.9 0.1 collective-permute-start.7
  124.9 3.7 %collective-permute-done.7 = f32[32,128]{1,0:T(8,128)S(1)} collective-permute-done((f32[32,128]{1,0:T(8,128)S(1)}, f32[32,128]{1,0:T(8,128)S(1)}, u32[]{:S(2)}, u32[]{:S(2)}) %collective-permute-start.7) | collective-permute-done | bytes 16416 | tf_op jit(solution)/shard_map/ppermute | solution.py:420
  128.7 0.0 collective-permute-start.10
  128.7 0.1 collective-permute-start.8
  128.8 4.3 %collective-permute-start.9 = (f32[32,128]{1,0:T(8,128)S(1)}, f32[32,128]{1,0:T(8,128)S(1)}, u32[]{:S(2)}, u32[]{:S(2)}) collective-permute-start(f32[32,128]{1,0:T(8,128)S(1)} %add.12), channel_id=1, source_target_pairs={{0,4},{1,5},{2,6},{3,7},{4,0},{5,1},{6,2},{7,3},{8,12},{9,13},{10,... | collective-permute-start | bytes 49160 | tf_op jit(solution)/shard_map/ppermute | solution.py:420
  133.1 1.1 collective-permute-done.10
  134.2 0.0 collective-permute-done.8
  134.2 0.7 collective-permute-done.9
  135.0 0.8 shard_map.112
  (2 shorter events, 0.0 us)
Async XLA Ops:
  0.8 8.7 %collective-permute-start = (s32[80,128]{1,0:T(8,128)S(1)}, s32[80,128]{1,0:T(8,128)S(1)}, u32[]{:S(2)}, u32[]{:S(2)}) collective-permute-start(s32[80,128]{1,0:T(8,128)S(1)} %bitcast.22), channel_id=1, source_target_pairs={{0,1},{1,2},{2,3},{3,4},{4,5},{5,6},{6,7},{7,0},{8,9},{9,10},{10,1... | collective-permute-start | bytes 122888 | tf_op jit(solution)/shard_map/ppermute | solution.py:411
  3.7 5.8 %collective-permute-start.1 = (s32[80,128]{1,0:T(8,128)S(1)}, s32[80,128]{1,0:T(8,128)S(1)}, u32[]{:S(2)}, u32[]{:S(2)}) collective-permute-start(s32[80,128]{1,0:T(8,128)S(1)} %bitcast.21), channel_id=1, source_target_pairs={{0,7},{1,0},{2,1},{3,2},{4,3},{5,4},{6,5},{7,6},{8,15},{9,8},{10,9... | collective-permute-start | bytes 122888 | tf_op jit(solution)/shard_map/ppermute | solution.py:411
  9.5 4.8 %copy-start.1 = (f32[5,160,128]{2,1,0:T(8,128)}, f32[5,160,128]{2,1,0:T(8,128)S(1)}, u32[]{:S(2)}) copy-start(f32[5,160,128]{2,1,0:T(8,128)S(1)} %pad_maximum_fusion) | copy-start | bytes 1228804
  9.5 4.8 %copy-start.4 = (s32[80,128]{1,0:T(8,128)}, s32[80,128]{1,0:T(8,128)S(1)}, u32[]{:S(2)}) copy-start(s32[80,128]{1,0:T(8,128)S(1)} %collective-permute-done.lower_ref) | copy-start | bytes 122884
  9.5 4.8 %copy-start.5 = (s32[80,128]{1,0:T(8,128)}, s32[80,128]{1,0:T(8,128)S(1)}, u32[]{:S(2)}) copy-start(s32[80,128]{1,0:T(8,128)S(1)} %collective-permute-done.1.upper_ref) | copy-start | bytes 122884
  9.5 36.4 %collective-permute-start.2 = (f32[800,128]{1,0:T(8,128)S(1)}, f32[800,128]{1,0:T(8,128)S(1)}, u32[]{:S(2)}, u32[]{:S(2)}) collective-permute-start(f32[800,128]{1,0:T(8,128)S(1)} %bitcast.15), channel_id=1, source_target_pairs={{0,1},{1,2},{2,3},{3,4},{4,5},{5,6},{6,7},{7,0},{8,9},{9,10},{10,1... | collective-permute-start | bytes 1228808 | tf_op jit(solution)/shard_map/ppermute | solution.py:411
  10.2 35.7 %collective-permute-start.3 = (f32[800,128]{1,0:T(8,128)S(1)}, f32[800,128]{1,0:T(8,128)S(1)}, u32[]{:S(2)}, u32[]{:S(2)}) collective-permute-start(f32[800,128]{1,0:T(8,128)S(1)} %bitcast.16), channel_id=1, source_target_pairs={{0,7},{1,0},{2,1},{3,2},{4,3},{5,4},{6,5},{7,6},{8,15},{9,8},{10,9... | collective-permute-start | bytes 1228808 | tf_op jit(solution)/shard_map/ppermute | solution.py:411
  45.9 0.8 copy-start.2
  45.9 0.9 copy-start.3
  119.2 3.5 %collective-permute-start.4 = (f32[6,8,128]{2,1,0:T(8,128)}, f32[6,8,128]{2,1,0:T(8,128)S(1)}, u32[]{:S(2)}, u32[]{:S(2)}) collective-permute-start(f32[6,8,128]{2,1,0:T(8,128)} %get-tuple-element.20.refs_0_), channel_id=1, source_target_pairs={{0,8},{8,16},{16,24},{24,0},{1,9},{9,17},{17,25},{25,1},{2,10},{10... | collective-permute-start | bytes 73736 | tf_op jit(solution)/shard_map/ppermute | solution.py:411
  119.3 4.1 %collective-permute-start.5 = (f32[6,8,128]{2,1,0:T(8,128)}, f32[6,8,128]{2,1,0:T(8,128)S(1)}, u32[]{:S(2)}, u32[]{:S(2)}) collective-permute-start(f32[6,8,128]{2,1,0:T(8,128)} %get-tuple-element.20.refs_0_), channel_id=1, source_target_pairs={{0,16},{8,24},{16,0},{24,8},{1,17},{9,25},{17,1},{25,9},{2,18},{10... | collective-permute-start | bytes 73736 | tf_op jit(solution)/shard_map/ppermute | solution.py:411
  120.9 3.1 %collective-permute-start.6 = (f32[6,8,128]{2,1,0:T(8,128)}, f32[6,8,128]{2,1,0:T(8,128)S(1)}, u32[]{:S(2)}, u32[]{:S(2)}) collective-permute-start(f32[6,8,128]{2,1,0:T(8,128)} %get-tuple-element.20.refs_0_), channel_id=1, source_target_pairs={{0,24},{8,0},{16,8},{24,16},{1,25},{9,1},{17,9},{25,17},{2,26},{10... | collective-permute-start | bytes 73736 | tf_op jit(solution)/shard_map/ppermute | solution.py:411
  124.1 0.7 copy-start
  124.9 3.8 %collective-permute-start.7 = (f32[32,128]{1,0:T(8,128)S(1)}, f32[32,128]{1,0:T(8,128)S(1)}, u32[]{:S(2)}, u32[]{:S(2)}) collective-permute-start(f32[32,128]{1,0:T(8,128)S(1)} %get-tuple-element.21), channel_id=1, source_target_pairs={{0,1},{1,0},{2,3},{3,2},{4,5},{5,4},{6,7},{7,6},{8,9},{9,8},{10,11... | collective-permute-start | bytes 49160 | tf_op jit(solution)/shard_map/ppermute | solution.py:420
  128.7 5.5 %collective-permute-start.10 = (f32[32,128]{1,0:T(8,128)S(1)}, f32[32,128]{1,0:T(8,128)S(1)}, u32[]{:S(2)}, u32[]{:S(2)}) collective-permute-start(f32[32,128]{1,0:T(8,128)S(1)} %add.12), channel_id=1, source_target_pairs={{0,6},{1,7},{2,4},{3,5},{4,2},{5,3},{6,0},{7,1},{8,14},{9,15},{10,... | collective-permute-start | bytes 49160 | tf_op jit(solution)/shard_map/ppermute | solution.py:420
  128.7 5.5 %collective-permute-start.8 = (f32[32,128]{1,0:T(8,128)S(1)}, f32[32,128]{1,0:T(8,128)S(1)}, u32[]{:S(2)}, u32[]{:S(2)}) collective-permute-start(f32[32,128]{1,0:T(8,128)S(1)} %add.12), channel_id=1, source_target_pairs={{0,2},{1,3},{2,0},{3,1},{4,6},{5,7},{6,4},{7,5},{8,10},{9,11},{10,... | collective-permute-start | bytes 49160 | tf_op jit(solution)/shard_map/ppermute | solution.py:420
  128.8 6.2 %collective-permute-start.9 = (f32[32,128]{1,0:T(8,128)S(1)}, f32[32,128]{1,0:T(8,128)S(1)}, u32[]{:S(2)}, u32[]{:S(2)}) collective-permute-start(f32[32,128]{1,0:T(8,128)S(1)} %add.12), channel_id=1, source_target_pairs={{0,4},{1,5},{2,6},{3,7},{4,0},{5,1},{6,2},{7,3},{8,12},{9,13},{10,... | collective-permute-start | bytes 49160 | tf_op jit(solution)/shard_map/ppermute | solution.py:420

commit v19 on v16

--- a/solution.py
+++ b/solution.py
@@ -31,6 +31,7 @@
 
 DEPTH, CHARGE, ONE, NORM, LAST = 3, 4, 5, 6, 7
 FAR_PIECES = (0, 1, 2, 0, 1, 0)
+STEP = 16
 ROW = 256
 COPY = 64
 USED = 8 * len(FAR_PIECES)
@@ -167,7 +168,7 @@
     masks = sublane_masks()
 
     def load(local, stage):
-        ref, first = (order_ref, local) if local < 8 else (next_ref, local - 8)
+        ref, first = (order_ref, local) if local < STEP else (next_ref, local - STEP)
 
         def entry_of(k):
             return ref[first * TILE + k]
@@ -187,7 +188,7 @@
             for copy in load(side, stage_a.at[side]):
                 copy()
 
-    for tile in range(0, 8, 2):
+    for tile in range(0, STEP, 2):
         here, there = (stage_a, stage_b) if tile % 4 == 0 else (stage_b, stage_a)
         weave(
             [factors(tile + side, here.at[side]) for side in range(2)] + [compose(tile + side) for side in range(2)],
@@ -270,7 +271,7 @@
     masks = sublane_masks()
 
     def load(local, far):
-        ref, first = (list_ref, local) if local < 8 else (next_ref, local - 8)
+        ref, first = (list_ref, local) if local < STEP else (next_ref, local - STEP)
 
         def entry_of(k):
             return ref[first * partners + k]
@@ -281,7 +282,7 @@
         ]
 
     def scatter(local, sums):
-        ref, first = (order_ref, local) if local >= 0 else (before_ref, local + 8)
+        ref, first = (order_ref, local) if local >= 0 else (before_ref, local + STEP)
         return pair_scatter([ref[first + side : first + side + 1, :] for side in range(2)], sums, total)
 
     @pl.when(turn == 0)
@@ -298,7 +299,7 @@
             for copy in load(side, far_a.at[side]):
                 copy()
 
-    for tile in range(0, 8, 2):
+    for tile in range(0, STEP, 2):
         far, far_next, sums, sums_before = (
             (far_a, far_b, sum_a, sum_b) if tile % 4 == 0 else (far_b, far_a, sum_b, sum_a)
         )
@@ -311,7 +312,7 @@
 
     @pl.when(turn == pl.num_programs(0) - 1)
     def _():
-        for _ in scatter(6, sum_b):
+        for _ in scatter(STEP - 2, sum_b):
             pass
         count = rows * LANES // ROW
         for axis in range(3):
@@ -453,23 +454,23 @@
     scalar = pl.BlockSpec(memory_space=pltpu.SMEM)
     vector = pl.BlockSpec(memory_space=pltpu.VMEM)
     params = pltpu.CompilerParams(vmem_limit_bytes=VMEM_LIMIT)
-    last = rows // 8 - 1
+    last = rows // STEP - 1
 
     def listed(size, by):
-        return pl.BlockSpec((8 * size,), lambda i: (jnp.clip(i + by, 0, last),), memory_space=pltpu.SMEM)
+        return pl.BlockSpec((STEP * size,), lambda i: (jnp.clip(i + by, 0, last),), memory_space=pltpu.SMEM)
 
     table = (atoms + 2 * PAD, LANES)
     left, partner_rows = pl.pallas_call(
         functools.partial(near_kernel, rows),
-        grid=(rows // 8,),
+        grid=(rows // STEP,),
         out_shape=[whole(rows, TILE, LANES, dtype=BF16), whole(rows * partners // LANES, LANES, dtype=I32)],
         in_specs=[listed(TILE, 0), listed(TILE, 1)]
         + [vector] * 2
-        + [pl.BlockSpec((1, 8, partners), lambda i: (0, i, 0))]
+        + [pl.BlockSpec((1, STEP, partners), lambda i: (0, i, 0))]
         + [vector] * 2,
         out_specs=[
-            pl.BlockSpec((8, TILE, LANES), lambda i: (i, 0, 0)),
-            pl.BlockSpec((8 * partners // LANES, LANES), lambda i: (i, 0)),
+            pl.BlockSpec((STEP, TILE, LANES), lambda i: (i, 0, 0)),
+            pl.BlockSpec((STEP * partners // LANES, LANES), lambda i: (i, 0)),
         ],
         scratch_shapes=[
             pltpu.VMEM(table, F32),
@@ -483,12 +484,12 @@
     pairs = partner_rows.reshape(rows * partners)
     out, solute = pl.pallas_call(
         functools.partial(force_kernel, rows),
-        grid=(rows // 8,),
+        grid=(rows // STEP,),
         out_shape=[whole(3 * rows, LANES), whole(6, SOL_DEV // LANES, LANES)],
         in_specs=[listed(partners, 0), listed(partners, 1)]
-        + [pl.BlockSpec((8, LANES), lambda i, by=by: (jnp.maximum(i - by, 0), 0)) for by in (0, 1)]
+        + [pl.BlockSpec((STEP, LANES), lambda i, by=by: (jnp.maximum(i - by, 0), 0)) for by in (0, 1)]
         + [vector] * 4
-        + [pl.BlockSpec((8, TILE, LANES), lambda i: (i, 0, 0))],
+        + [pl.BlockSpec((STEP, TILE, LANES), lambda i: (i, 0, 0))],
         out_specs=[vector] * 2,
         scratch_shapes=[
             pltpu.VMEM((3 * atoms + 2 * PAD, LANES), F32),

time: 127 us -> 117 us (0.921)
  Pallas kernels: 94.2 us -> 84.1 us
    pallas_call x2, Pallas kernels: 93.4 us -> 83.2 us  [the longest x1 56.3 us: per_device(): pl.pallas_call(functools.partial(force_kernel, rows), grid=(rows // STEP,...]
where the time goes in v19:
time: 117 us; the launch traced here: 116 us
  Pallas kernels  84.1 us (72%)
  starting transfers between devices  18.3 us (16%)
  waiting for transfers between devices  7.36 us (6%)
  other arithmetic  3.47 us (3%)
  local copies, waits for them, and re-layouts  2.44 us (2%)
    pallas_call x1, Pallas kernels, per_device(): pl.pallas_call(functools.partial(force_kernel, rows), grid=(rows // STEP,...  56.3 us
    pallas_call x1, Pallas kernels, per_device(): pl.pallas_call(functools.partial(near_kernel, rows), grid=(rows // STEP,)...  27 us
    ppermute x7, starting transfers between devices, turned(): lax.ppermute(array, axis, [(i, (i + by) % count) for i in range(count)])  13.8 us
    ppermute x4, waiting for transfers between devices, crossed(): return lax.ppermute(array, axis, [(i, i ^ by) for i in range(count)])  5.62 us
    ppermute x4, starting transfers between devices, crossed(): return lax.ppermute(array, axis, [(i, i ^ by) for i in range(count)])  4.45 us
  transfers between devices with their start and end apart: 11, of which 6 were waited for; matrix products, arithmetic and copies ran while one was open for 3% of the time, Pallas kernels for 23%

profile of v19, /device:TPU:0, one launch (start us, length us, event | category | flops | bytes accessed | tf_op | source)
XLA Modules:
  0.0 116.4 jit_solution(10275608701779941522)
XLA Ops:
  0.0 0.8 fusion.9
  0.8 2.9 %collective-permute-start = (s32[80,128]{1,0:T(8,128)S(1)}, s32[80,128]{1,0:T(8,128)S(1)}, u32[]{:S(2)}, u32[]{:S(2)}) collective-permute-start(s32[80,128]{1,0:T(8,128)S(1)} %bitcast.25), channel_id=1, source_target_pairs={{0,1},{1,2},{2,3},{3,4},{4,5},{5,6},{6,7},{7,0},{8,9},{9,10},{10,1... | collective-permute-start | bytes 122888 | tf_op jit(solution)/shard_map/ppermute | solution.py:418
  3.7 3.1 %collective-permute-start.1 = (s32[80,128]{1,0:T(8,128)S(1)}, s32[80,128]{1,0:T(8,128)S(1)}, u32[]{:S(2)}, u32[]{:S(2)}) collective-permute-start(s32[80,128]{1,0:T(8,128)S(1)} %bitcast.24), channel_id=1, source_target_pairs={{0,7},{1,0},{2,1},{3,2},{4,3},{5,4},{6,5},{7,6},{8,15},{9,8},{10,9... | collective-permute-start | bytes 122888 | tf_op jit(solution)/shard_map/ppermute | solution.py:418
  7.5 1.5 %fusion.5.order_ref.next_ref = s32[20480]{0:T(1024)} fusion(s32[20480]{0:T(1024)} %bitcast.21), kind=kLoop, calls=%fused_computation.9 | loop fusion | flops 163840 | bytes 163840 | tf_op jit(solution)/shard_map/add | solution.py:453
  9.1 0.9 fusion.1
  10.0 1.0 pad_maximum_fusion
  11.0 0.0 copy-start.1
  11.0 0.0 collective-permute-done.lower_ref
  11.0 0.0 copy-start.4
  11.0 0.0 collective-permute-done.1.upper_ref
  11.0 0.0 copy-start.5
  11.1 0.1 collective-permute-start.2
  11.1 4.7 %collective-permute-start.3 = (f32[800,128]{1,0:T(8,128)S(1)}, f32[800,128]{1,0:T(8,128)S(1)}, u32[]{:S(2)}, u32[]{:S(2)}) collective-permute-start(f32[800,128]{1,0:T(8,128)S(1)} %bitcast.16), channel_id=1, source_target_pairs={{0,7},{1,0},{2,1},{3,2},{4,3},{5,4},{6,5},{7,6},{8,15},{9,8},{10,9... | collective-permute-start | bytes 1228808 | tf_op jit(solution)/shard_map/ppermute | solution.py:418
  15.8 0.0 copy-done.1
  15.8 0.0 copy-done.4
  15.8 0.0 copy-done.5
  15.8 27.0 %shard_map.91 = (bf16[160,128,128]{2,1,0:T(8,128)(2,1)}, s32[320,128]{1,0:T(8,128)}) custom-call(s32[20480]{0:T(1024)} %fusion.5.order_ref.next_ref, s32[20480]{0:T(1024)} %fusion.5.order_ref.next_ref, s32[80,128]{1,0:T(8,128)} %copy-done.4, s32[80,128]{1,0:T(8,128)} %copy-done.5, s32[1,160,256]{2,1,0:T(8,128)} %partner_ref.1, f32[800,128]{1,0:T(8,128)} %bitcast.17, ...), custom_call_target="tpu_custom_call" | custom-call | flops 24999999488 | bytes 10000000 | tf_op jit(solution)/shard_map/pallas_call | solution.py:463
  42.8 0.0 collective-permute-done.2.lower_ref
  42.8 0.0 copy-start.2
  42.8 0.0 collective-permute-done.3.upper_ref
  42.8 0.0 copy-start.3
  42.8 0.7 copy-done.2
  43.5 0.2 copy-done.3
  43.7 56.3 %shard_map.92 = (f32[480,128]{1,0:T(8,128)}, f32[6,8,128]{2,1,0:T(8,128)}) custom-call(s32[40960]{0:T(1024)} %bitcast.26, s32[40960]{0:T(1024)} %bitcast.27, s32[160,128]{1,0:T(8,128)} %bitcast.22, s32[160,128]{1,0:T(8,128)} %bitcast.23, f32[800,128]{1,0:T(8,128)} %copy-done.2, f32[800,128]{1,0:T(8,128)} %bitcast.18, f32[800,128]{1,0:T(8,128)} %copy-done.3, ...), custom_call_target="tpu_custom_call" | custom-call | flops 24999999488 | bytes 10000000 | tf_op jit(solution)/shard_map/pallas_call | solution.py:485
  100.0 0.0 collective-permute-start.4
  100.0 1.6 %collective-permute-start.5 = (f32[6,8,128]{2,1,0:T(8,128)}, f32[6,8,128]{2,1,0:T(8,128)S(1)}, u32[]{:S(2)}, u32[]{:S(2)}) collective-permute-start(f32[6,8,128]{2,1,0:T(8,128)} %get-tuple-element.20.refs_0_), channel_id=1, source_target_pairs={{0,16},{8,24},{16,0},{24,8},{1,17},{9,25},{17,1},{25,9},{2,18},{10... | collective-permute-start | bytes 73736 | tf_op jit(solution)/shard_map/ppermute | solution.py:418
  101.6 1.4 %collective-permute-start.6 = (f32[6,8,128]{2,1,0:T(8,128)}, f32[6,8,128]{2,1,0:T(8,128)S(1)}, u32[]{:S(2)}, u32[]{:S(2)}) collective-permute-start(f32[6,8,128]{2,1,0:T(8,128)} %get-tuple-element.20.refs_0_), channel_id=1, source_target_pairs={{0,24},{8,0},{16,8},{24,16},{1,25},{9,1},{17,9},{25,17},{2,26},{10... | collective-permute-start | bytes 73736 | tf_op jit(solution)/shard_map/ppermute | solution.py:418
  103.0 0.5 collective-permute-done.4.refs_1_
  103.4 0.6 collective-permute-done.5.refs_2_
  104.1 0.6 collective-permute-done.6.refs_3_
  104.7 0.0 copy-start
  104.7 0.7 copy-done
  105.5 0.1 shard_map.93
  105.5 0.1 collective-permute-start.7
  105.6 3.7 %collective-permute-done.7 = f32[32,128]{1,0:T(8,128)S(1)} collective-permute-done((f32[32,128]{1,0:T(8,128)S(1)}, f32[32,128]{1,0:T(8,128)S(1)}, u32[]{:S(2)}, u32[]{:S(2)}) %collective-permute-start.7) | collective-permute-done | bytes 16416 | tf_op jit(solution)/shard_map/ppermute | solution.py:427
  109.3 0.0 collective-permute-start.10
  109.4 0.1 collective-permute-start.8
  109.4 4.3 %collective-permute-start.9 = (f32[32,128]{1,0:T(8,128)S(1)}, f32[32,128]{1,0:T(8,128)S(1)}, u32[]{:S(2)}, u32[]{:S(2)}) collective-permute-start(f32[32,128]{1,0:T(8,128)S(1)} %add.23), channel_id=1, source_target_pairs={{0,4},{1,5},{2,6},{3,7},{4,0},{5,1},{6,2},{7,3},{8,12},{9,13},{10,... | collective-permute-start | bytes 49160 | tf_op jit(solution)/shard_map/ppermute | solution.py:427
  113.7 1.1 collective-permute-done.10
  114.9 0.0 collective-permute-done.8
  114.9 0.7 collective-permute-done.9
  115.6 0.8 shard_map.94
  (2 shorter events, 0.0 us)
Async XLA Ops:
  0.8 10.2 %collective-permute-start = (s32[80,128]{1,0:T(8,128)S(1)}, s32[80,128]{1,0:T(8,128)S(1)}, u32[]{:S(2)}, u32[]{:S(2)}) collective-permute-start(s32[80,128]{1,0:T(8,128)S(1)} %bitcast.25), channel_id=1, source_target_pairs={{0,1},{1,2},{2,3},{3,4},{4,5},{5,6},{6,7},{7,0},{8,9},{9,10},{10,1... | collective-permute-start | bytes 122888 | tf_op jit(solution)/shard_map/ppermute | solution.py:418
  3.7 7.3 %collective-permute-start.1 = (s32[80,128]{1,0:T(8,128)S(1)}, s32[80,128]{1,0:T(8,128)S(1)}, u32[]{:S(2)}, u32[]{:S(2)}) collective-permute-start(s32[80,128]{1,0:T(8,128)S(1)} %bitcast.24), channel_id=1, source_target_pairs={{0,7},{1,0},{2,1},{3,2},{4,3},{5,4},{6,5},{7,6},{8,15},{9,8},{10,9... | collective-permute-start | bytes 122888 | tf_op jit(solution)/shard_map/ppermute | solution.py:418
  11.0 4.8 %copy-start.1 = (f32[5,160,128]{2,1,0:T(8,128)}, f32[5,160,128]{2,1,0:T(8,128)S(1)}, u32[]{:S(2)}) copy-start(f32[5,160,128]{2,1,0:T(8,128)S(1)} %pad_maximum_fusion) | copy-start | bytes 1228804
  11.0 4.8 %copy-start.4 = (s32[80,128]{1,0:T(8,128)}, s32[80,128]{1,0:T(8,128)S(1)}, u32[]{:S(2)}) copy-start(s32[80,128]{1,0:T(8,128)S(1)} %collective-permute-done.lower_ref) | copy-start | bytes 122884
  11.0 4.8 %copy-start.5 = (s32[80,128]{1,0:T(8,128)}, s32[80,128]{1,0:T(8,128)S(1)}, u32[]{:S(2)}) copy-start(s32[80,128]{1,0:T(8,128)S(1)} %collective-permute-done.1.upper_ref) | copy-start | bytes 122884
  11.1 31.7 %collective-permute-start.2 = (f32[800,128]{1,0:T(8,128)S(1)}, f32[800,128]{1,0:T(8,128)S(1)}, u32[]{:S(2)}, u32[]{:S(2)}) collective-permute-start(f32[800,128]{1,0:T(8,128)S(1)} %bitcast.15), channel_id=1, source_target_pairs={{0,1},{1,2},{2,3},{3,4},{4,5},{5,6},{6,7},{7,0},{8,9},{9,10},{10,1... | collective-permute-start | bytes 1228808 | tf_op jit(solution)/shard_map/ppermute | solution.py:418
  11.1 31.7 %collective-permute-start.3 = (f32[800,128]{1,0:T(8,128)S(1)}, f32[800,128]{1,0:T(8,128)S(1)}, u32[]{:S(2)}, u32[]{:S(2)}) collective-permute-start(f32[800,128]{1,0:T(8,128)S(1)} %bitcast.16), channel_id=1, source_target_pairs={{0,7},{1,0},{2,1},{3,2},{4,3},{5,4},{6,5},{7,6},{8,15},{9,8},{10,9... | collective-permute-start | bytes 1228808 | tf_op jit(solution)/shard_map/ppermute | solution.py:418
  42.8 0.8 copy-start.2
  42.8 0.9 copy-start.3
  100.0 3.5 %collective-permute-start.4 = (f32[6,8,128]{2,1,0:T(8,128)}, f32[6,8,128]{2,1,0:T(8,128)S(1)}, u32[]{:S(2)}, u32[]{:S(2)}) collective-permute-start(f32[6,8,128]{2,1,0:T(8,128)} %get-tuple-element.20.refs_0_), channel_id=1, source_target_pairs={{0,8},{8,16},{16,24},{24,0},{1,9},{9,17},{17,25},{25,1},{2,10},{10... | collective-permute-start | bytes 73736 | tf_op jit(solution)/shard_map/ppermute | solution.py:418
  100.0 4.1 %collective-permute-start.5 = (f32[6,8,128]{2,1,0:T(8,128)}, f32[6,8,128]{2,1,0:T(8,128)S(1)}, u32[]{:S(2)}, u32[]{:S(2)}) collective-permute-start(f32[6,8,128]{2,1,0:T(8,128)} %get-tuple-element.20.refs_0_), channel_id=1, source_target_pairs={{0,16},{8,24},{16,0},{24,8},{1,17},{9,25},{17,1},{25,9},{2,18},{10... | collective-permute-start | bytes 73736 | tf_op jit(solution)/shard_map/ppermute | solution.py:418
  101.6 3.1 %collective-permute-start.6 = (f32[6,8,128]{2,1,0:T(8,128)}, f32[6,8,128]{2,1,0:T(8,128)S(1)}, u32[]{:S(2)}, u32[]{:S(2)}) collective-permute-start(f32[6,8,128]{2,1,0:T(8,128)} %get-tuple-element.20.refs_0_), channel_id=1, source_target_pairs={{0,24},{8,0},{16,8},{24,16},{1,25},{9,1},{17,9},{25,17},{2,26},{10... | collective-permute-start | bytes 73736 | tf_op jit(solution)/shard_map/ppermute | solution.py:418
  104.7 0.7 copy-start
  105.5 3.8 %collective-permute-start.7 = (f32[32,128]{1,0:T(8,128)S(1)}, f32[32,128]{1,0:T(8,128)S(1)}, u32[]{:S(2)}, u32[]{:S(2)}) collective-permute-start(f32[32,128]{1,0:T(8,128)S(1)} %get-tuple-element.21), channel_id=1, source_target_pairs={{0,1},{1,0},{2,3},{3,2},{4,5},{5,4},{6,7},{7,6},{8,9},{9,8},{10,11... | collective-permute-start | bytes 49160 | tf_op jit(solution)/shard_map/ppermute | solution.py:427
  109.3 5.5 %collective-permute-start.10 = (f32[32,128]{1,0:T(8,128)S(1)}, f32[32,128]{1,0:T(8,128)S(1)}, u32[]{:S(2)}, u32[]{:S(2)}) collective-permute-start(f32[32,128]{1,0:T(8,128)S(1)} %add.23), channel_id=1, source_target_pairs={{0,6},{1,7},{2,4},{3,5},{4,2},{5,3},{6,0},{7,1},{8,14},{9,15},{10,... | collective-permute-start | bytes 49160 | tf_op jit(solution)/shard_map/ppermute | solution.py:427
  109.4 5.5 %collective-permute-start.8 = (f32[32,128]{1,0:T(8,128)S(1)}, f32[32,128]{1,0:T(8,128)S(1)}, u32[]{:S(2)}, u32[]{:S(2)}) collective-permute-start(f32[32,128]{1,0:T(8,128)S(1)} %add.23), channel_id=1, source_target_pairs={{0,2},{1,3},{2,0},{3,1},{4,6},{5,7},{6,4},{7,5},{8,10},{9,11},{10,... | collective-permute-start | bytes 49160 | tf_op jit(solution)/shard_map/ppermute | solution.py:427
  109.4 6.2 %collective-permute-start.9 = (f32[32,128]{1,0:T(8,128)S(1)}, f32[32,128]{1,0:T(8,128)S(1)}, u32[]{:S(2)}, u32[]{:S(2)}) collective-permute-start(f32[32,128]{1,0:T(8,128)S(1)} %add.23), channel_id=1, source_target_pairs={{0,4},{1,5},{2,6},{3,7},{4,0},{5,1},{6,2},{7,3},{8,12},{9,13},{10,... | collective-permute-start | bytes 49160 | tf_op jit(solution)/shard_map/ppermute | solution.py:427

commit v20 on v19

--- a/solution.py
+++ b/solution.py
@@ -31,7 +31,7 @@
 
 DEPTH, CHARGE, ONE, NORM, LAST = 3, 4, 5, 6, 7
 FAR_PIECES = (0, 1, 2, 0, 1, 0)
-STEP = 16
+STEP = 40
 ROW = 256
 COPY = 64
 USED = 8 * len(FAR_PIECES)

time: 117 us -> 116 us (level)
  no operation moved by 1% of the time
where the time goes in v20:
time: 116 us
  Pallas kernels  83.5 us (72%)
  starting transfers between devices  18.4 us (16%)
  waiting for transfers between devices  7.36 us (6%)
  other arithmetic  3.47 us (3%)
  local copies, waits for them, and re-layouts  2.44 us (2%)
    pallas_call x1, Pallas kernels, per_device(): pl.pallas_call(functools.partial(force_kernel, rows), grid=(rows // STEP,...  55.8 us
    pallas_call x1, Pallas kernels, per_device(): pl.pallas_call(functools.partial(near_kernel, rows), grid=(rows // STEP,)...  26.9 us
    ppermute x7, starting transfers between devices, turned(): lax.ppermute(array, axis, [(i, (i + by) % count) for i in range(count)])  13.9 us
    ppermute x4, waiting for transfers between devices, crossed(): return lax.ppermute(array, axis, [(i, i ^ by) for i in range(count)])  5.62 us
    ppermute x4, starting transfers between devices, crossed(): return lax.ppermute(array, axis, [(i, i ^ by) for i in range(count)])  4.45 us
  transfers between devices with their start and end apart: 11, of which 6 were waited for; matrix products, arithmetic and copies ran while one was open for 3% of the time, Pallas kernels for 23%

profile of v20, /device:TPU:0, one launch (start us, length us, event | category | flops | bytes accessed | tf_op | source)
XLA Modules:
  0.0 116.0 jit_solution(11538446845464983475)
XLA Ops:
  0.0 0.8 fusion.9
  0.8 2.9 %collective-permute-start = (s32[80,128]{1,0:T(8,128)S(1)}, s32[80,128]{1,0:T(8,128)S(1)}, u32[]{:S(2)}, u32[]{:S(2)}) collective-permute-start(s32[80,128]{1,0:T(8,128)S(1)} %bitcast.25), channel_id=1, source_target_pairs={{0,1},{1,2},{2,3},{3,4},{4,5},{5,6},{6,7},{7,0},{8,9},{9,10},{10,1... | collective-permute-start | bytes 122888 | tf_op jit(solution)/shard_map/ppermute | solution.py:418
  3.7 3.1 %collective-permute-start.1 = (s32[80,128]{1,0:T(8,128)S(1)}, s32[80,128]{1,0:T(8,128)S(1)}, u32[]{:S(2)}, u32[]{:S(2)}) collective-permute-start(s32[80,128]{1,0:T(8,128)S(1)} %bitcast.24), channel_id=1, source_target_pairs={{0,7},{1,0},{2,1},{3,2},{4,3},{5,4},{6,5},{7,6},{8,15},{9,8},{10,9... | collective-permute-start | bytes 122888 | tf_op jit(solution)/shard_map/ppermute | solution.py:418
  7.5 1.5 %fusion.5.order_ref.next_ref = s32[20480]{0:T(1024)} fusion(s32[20480]{0:T(1024)} %bitcast.21), kind=kLoop, calls=%fused_computation.9 | loop fusion | flops 163840 | bytes 163840 | tf_op jit(solution)/shard_map/add | solution.py:453
  9.1 0.9 fusion.1
  10.0 1.0 pad_maximum_fusion
  11.0 0.0 copy-start.1
  11.0 0.0 collective-permute-done.lower_ref
  11.0 0.0 copy-start.4
  11.0 0.0 collective-permute-done.1.upper_ref
  11.0 0.0 copy-start.5
  11.1 0.1 collective-permute-start.2
  11.1 4.7 %collective-permute-start.3 = (f32[800,128]{1,0:T(8,128)S(1)}, f32[800,128]{1,0:T(8,128)S(1)}, u32[]{:S(2)}, u32[]{:S(2)}) collective-permute-start(f32[800,128]{1,0:T(8,128)S(1)} %bitcast.16), channel_id=1, source_target_pairs={{0,7},{1,0},{2,1},{3,2},{4,3},{5,4},{6,5},{7,6},{8,15},{9,8},{10,9... | collective-permute-start | bytes 1228808 | tf_op jit(solution)/shard_map/ppermute | solution.py:418
  15.8 0.0 copy-done.1
  15.8 0.0 copy-done.4
  15.8 0.0 copy-done.5
  15.8 26.9 %shard_map.91 = (bf16[160,128,128]{2,1,0:T(8,128)(2,1)}, s32[320,128]{1,0:T(8,128)}) custom-call(s32[20480]{0:T(1024)} %fusion.5.order_ref.next_ref, s32[20480]{0:T(1024)} %fusion.5.order_ref.next_ref, s32[80,128]{1,0:T(8,128)} %copy-done.4, s32[80,128]{1,0:T(8,128)} %copy-done.5, s32[1,160,256]{2,1,0:T(8,128)} %partner_ref.1, f32[800,128]{1,0:T(8,128)} %bitcast.17, ...), custom_call_target="tpu_custom_call" | custom-call | flops 24999999488 | bytes 10000000 | tf_op jit(solution)/shard_map/pallas_call | solution.py:463
  42.7 0.0 collective-permute-done.2.lower_ref
  42.7 0.0 copy-start.2
  42.8 0.0 collective-permute-done.3.upper_ref
  42.8 0.0 copy-start.3
  42.8 0.7 copy-done.2
  43.5 0.2 copy-done.3
  43.7 55.8 %shard_map.92 = (f32[480,128]{1,0:T(8,128)}, f32[6,8,128]{2,1,0:T(8,128)}) custom-call(s32[40960]{0:T(1024)} %bitcast.26, s32[40960]{0:T(1024)} %bitcast.27, s32[160,128]{1,0:T(8,128)} %bitcast.22, s32[160,128]{1,0:T(8,128)} %bitcast.23, f32[800,128]{1,0:T(8,128)} %copy-done.2, f32[800,128]{1,0:T(8,128)} %bitcast.18, f32[800,128]{1,0:T(8,128)} %copy-done.3, ...), custom_call_target="tpu_custom_call" | custom-call | flops 24999999488 | bytes 10000000 | tf_op jit(solution)/shard_map/pallas_call | solution.py:485
  99.5 0.0 collective-permute-start.4
  99.5 1.7 %collective-permute-start.5 = (f32[6,8,128]{2,1,0:T(8,128)}, f32[6,8,128]{2,1,0:T(8,128)S(1)}, u32[]{:S(2)}, u32[]{:S(2)}) collective-permute-start(f32[6,8,128]{2,1,0:T(8,128)} %get-tuple-element.20.refs_0_), channel_id=1, source_target_pairs={{0,16},{8,24},{16,0},{24,8},{1,17},{9,25},{17,1},{25,9},{2,18},{10... | collective-permute-start | bytes 73736 | tf_op jit(solution)/shard_map/ppermute | solution.py:418
  101.2 1.4 %collective-permute-start.6 = (f32[6,8,128]{2,1,0:T(8,128)}, f32[6,8,128]{2,1,0:T(8,128)S(1)}, u32[]{:S(2)}, u32[]{:S(2)}) collective-permute-start(f32[6,8,128]{2,1,0:T(8,128)} %get-tuple-element.20.refs_0_), channel_id=1, source_target_pairs={{0,24},{8,0},{16,8},{24,16},{1,25},{9,1},{17,9},{25,17},{2,26},{10... | collective-permute-start | bytes 73736 | tf_op jit(solution)/shard_map/ppermute | solution.py:418
  102.6 0.3 collective-permute-done.4.refs_1_
  102.9 0.6 collective-permute-done.5.refs_2_
  103.6 0.7 collective-permute-done.6.refs_3_
  104.3 0.0 copy-start
  104.3 0.7 copy-done
  105.1 0.1 shard_map.93
  105.1 0.1 collective-permute-start.7
  105.2 3.7 %collective-permute-done.7 = f32[32,128]{1,0:T(8,128)S(1)} collective-permute-done((f32[32,128]{1,0:T(8,128)S(1)}, f32[32,128]{1,0:T(8,128)S(1)}, u32[]{:S(2)}, u32[]{:S(2)}) %collective-permute-start.7) | collective-permute-done | bytes 16416 | tf_op jit(solution)/shard_map/ppermute | solution.py:427
  108.9 0.0 collective-permute-start.10
  108.9 0.1 collective-permute-start.8
  109.0 4.3 %collective-permute-start.9 = (f32[32,128]{1,0:T(8,128)S(1)}, f32[32,128]{1,0:T(8,128)S(1)}, u32[]{:S(2)}, u32[]{:S(2)}) collective-permute-start(f32[32,128]{1,0:T(8,128)S(1)} %add.23), channel_id=1, source_target_pairs={{0,4},{1,5},{2,6},{3,7},{4,0},{5,1},{6,2},{7,3},{8,12},{9,13},{10,... | collective-permute-start | bytes 49160 | tf_op jit(solution)/shard_map/ppermute | solution.py:427
  113.3 1.1 collective-permute-done.10
  114.5 0.0 collective-permute-done.8
  114.5 0.7 collective-permute-done.9
  115.2 0.8 shard_map.94
  (2 shorter events, 0.0 us)
Async XLA Ops:
  0.8 10.2 %collective-permute-start = (s32[80,128]{1,0:T(8,128)S(1)}, s32[80,128]{1,0:T(8,128)S(1)}, u32[]{:S(2)}, u32[]{:S(2)}) collective-permute-start(s32[80,128]{1,0:T(8,128)S(1)} %bitcast.25), channel_id=1, source_target_pairs={{0,1},{1,2},{2,3},{3,4},{4,5},{5,6},{6,7},{7,0},{8,9},{9,10},{10,1... | collective-permute-start | bytes 122888 | tf_op jit(solution)/shard_map/ppermute | solution.py:418
  3.7 7.3 %collective-permute-start.1 = (s32[80,128]{1,0:T(8,128)S(1)}, s32[80,128]{1,0:T(8,128)S(1)}, u32[]{:S(2)}, u32[]{:S(2)}) collective-permute-start(s32[80,128]{1,0:T(8,128)S(1)} %bitcast.24), channel_id=1, source_target_pairs={{0,7},{1,0},{2,1},{3,2},{4,3},{5,4},{6,5},{7,6},{8,15},{9,8},{10,9... | collective-permute-start | bytes 122888 | tf_op jit(solution)/shard_map/ppermute | solution.py:418
  11.0 4.8 %copy-start.1 = (f32[5,160,128]{2,1,0:T(8,128)}, f32[5,160,128]{2,1,0:T(8,128)S(1)}, u32[]{:S(2)}) copy-start(f32[5,160,128]{2,1,0:T(8,128)S(1)} %pad_maximum_fusion) | copy-start | bytes 1228804
  11.0 4.8 %copy-start.4 = (s32[80,128]{1,0:T(8,128)}, s32[80,128]{1,0:T(8,128)S(1)}, u32[]{:S(2)}) copy-start(s32[80,128]{1,0:T(8,128)S(1)} %collective-permute-done.lower_ref) | copy-start | bytes 122884
  11.0 4.8 %copy-start.5 = (s32[80,128]{1,0:T(8,128)}, s32[80,128]{1,0:T(8,128)S(1)}, u32[]{:S(2)}) copy-start(s32[80,128]{1,0:T(8,128)S(1)} %collective-permute-done.1.upper_ref) | copy-start | bytes 122884
  11.1 31.7 %collective-permute-start.2 = (f32[800,128]{1,0:T(8,128)S(1)}, f32[800,128]{1,0:T(8,128)S(1)}, u32[]{:S(2)}, u32[]{:S(2)}) collective-permute-start(f32[800,128]{1,0:T(8,128)S(1)} %bitcast.15), channel_id=1, source_target_pairs={{0,1},{1,2},{2,3},{3,4},{4,5},{5,6},{6,7},{7,0},{8,9},{9,10},{10,1... | collective-permute-start | bytes 1228808 | tf_op jit(solution)/shard_map/ppermute | solution.py:418
  11.1 31.6 %collective-permute-start.3 = (f32[800,128]{1,0:T(8,128)S(1)}, f32[800,128]{1,0:T(8,128)S(1)}, u32[]{:S(2)}, u32[]{:S(2)}) collective-permute-start(f32[800,128]{1,0:T(8,128)S(1)} %bitcast.16), channel_id=1, source_target_pairs={{0,7},{1,0},{2,1},{3,2},{4,3},{5,4},{6,5},{7,6},{8,15},{9,8},{10,9... | collective-permute-start | bytes 1228808 | tf_op jit(solution)/shard_map/ppermute | solution.py:418
  42.7 0.8 copy-start.2
  42.8 0.9 copy-start.3
  99.5 3.5 %collective-permute-start.4 = (f32[6,8,128]{2,1,0:T(8,128)}, f32[6,8,128]{2,1,0:T(8,128)S(1)}, u32[]{:S(2)}, u32[]{:S(2)}) collective-permute-start(f32[6,8,128]{2,1,0:T(8,128)} %get-tuple-element.20.refs_0_), channel_id=1, source_target_pairs={{0,8},{8,16},{16,24},{24,0},{1,9},{9,17},{17,25},{25,1},{2,10},{10... | collective-permute-start | bytes 73736 | tf_op jit(solution)/shard_map/ppermute | solution.py:418
  99.5 4.1 %collective-permute-start.5 = (f32[6,8,128]{2,1,0:T(8,128)}, f32[6,8,128]{2,1,0:T(8,128)S(1)}, u32[]{:S(2)}, u32[]{:S(2)}) collective-permute-start(f32[6,8,128]{2,1,0:T(8,128)} %get-tuple-element.20.refs_0_), channel_id=1, source_target_pairs={{0,16},{8,24},{16,0},{24,8},{1,17},{9,25},{17,1},{25,9},{2,18},{10... | collective-permute-start | bytes 73736 | tf_op jit(solution)/shard_map/ppermute | solution.py:418
  101.2 3.1 %collective-permute-start.6 = (f32[6,8,128]{2,1,0:T(8,128)}, f32[6,8,128]{2,1,0:T(8,128)S(1)}, u32[]{:S(2)}, u32[]{:S(2)}) collective-permute-start(f32[6,8,128]{2,1,0:T(8,128)} %get-tuple-element.20.refs_0_), channel_id=1, source_target_pairs={{0,24},{8,0},{16,8},{24,16},{1,25},{9,1},{17,9},{25,17},{2,26},{10... | collective-permute-start | bytes 73736 | tf_op jit(solution)/shard_map/ppermute | solution.py:418
  104.3 0.7 copy-start
  105.1 3.8 %collective-permute-start.7 = (f32[32,128]{1,0:T(8,128)S(1)}, f32[32,128]{1,0:T(8,128)S(1)}, u32[]{:S(2)}, u32[]{:S(2)}) collective-permute-start(f32[32,128]{1,0:T(8,128)S(1)} %get-tuple-element.21), channel_id=1, source_target_pairs={{0,1},{1,0},{2,3},{3,2},{4,5},{5,4},{6,7},{7,6},{8,9},{9,8},{10,11... | collective-permute-start | bytes 49160 | tf_op jit(solution)/shard_map/ppermute | solution.py:427
  108.9 5.5 %collective-permute-start.10 = (f32[32,128]{1,0:T(8,128)S(1)}, f32[32,128]{1,0:T(8,128)S(1)}, u32[]{:S(2)}, u32[]{:S(2)}) collective-permute-start(f32[32,128]{1,0:T(8,128)S(1)} %add.23), channel_id=1, source_target_pairs={{0,6},{1,7},{2,4},{3,5},{4,2},{5,3},{6,0},{7,1},{8,14},{9,15},{10,... | collective-permute-start | bytes 49160 | tf_op jit(solution)/shard_map/ppermute | solution.py:427
  108.9 5.5 %collective-permute-start.8 = (f32[32,128]{1,0:T(8,128)S(1)}, f32[32,128]{1,0:T(8,128)S(1)}, u32[]{:S(2)}, u32[]{:S(2)}) collective-permute-start(f32[32,128]{1,0:T(8,128)S(1)} %add.23), channel_id=1, source_target_pairs={{0,2},{1,3},{2,0},{3,1},{4,6},{5,7},{6,4},{7,5},{8,10},{9,11},{10,... | collective-permute-start | bytes 49160 | tf_op jit(solution)/shard_map/ppermute | solution.py:427
  109.0 6.2 %collective-permute-start.9 = (f32[32,128]{1,0:T(8,128)S(1)}, f32[32,128]{1,0:T(8,128)S(1)}, u32[]{:S(2)}, u32[]{:S(2)}) collective-permute-start(f32[32,128]{1,0:T(8,128)S(1)} %add.23), channel_id=1, source_target_pairs={{0,4},{1,5},{2,6},{3,7},{4,0},{5,1},{6,2},{7,3},{8,12},{9,13},{10,... | collective-permute-start | bytes 49160 | tf_op jit(solution)/shard_map/ppermute | solution.py:427

commit v21 on v19

--- a/solution.py
+++ b/solution.py
@@ -32,6 +32,7 @@
 DEPTH, CHARGE, ONE, NORM, LAST = 3, 4, 5, 6, 7
 FAR_PIECES = (0, 1, 2, 0, 1, 0)
 STEP = 16
+FLIGHT = 4
 ROW = 256
 COPY = 64
 USED = 8 * len(FAR_PIECES)
@@ -171,7 +172,7 @@
         ref, first = (order_ref, local) if local < STEP else (next_ref, local - STEP)
 
         def entry_of(k):
-            return ref[first * TILE + k]
+            return ref[first * TILE + k] + (PAD - k % 8)
 
         return [
             functools.partial(copy_rows, table, entry_of, stage, start, masks) for start in range(0, TILE, 16)
@@ -295,25 +296,27 @@
         lax.fori_loop(0, rows // 4, fill, 0)
         sum_b[...] = jnp.zeros_like(sum_b)
         total[...] = jnp.zeros_like(total)
-        for side in range(2):
+        for side in range(FLIGHT):
             for copy in load(side, far_a.at[side]):
                 copy()
 
-    for tile in range(0, STEP, 2):
+    flight = range(FLIGHT)
+    for tile in range(0, STEP, FLIGHT):
         far, far_next, sums, sums_before = (
-            (far_a, far_b, sum_a, sum_b) if tile % 4 == 0 else (far_b, far_a, sum_b, sum_a)
+            (far_a, far_b, sum_a, sum_b) if tile % (2 * FLIGHT) == 0 else (far_b, far_a, sum_b, sum_a)
         )
         weave(
-            [tile_sums(left_ref, kinds_ref, tile + side, far.at[side], sums.at[side]) for side in range(2)]
-            + [scatter(tile - 2, sums_before)],
-            load(tile + 2, far_next.at[0]) + load(tile + 3, far_next.at[1]),
+            [tile_sums(left_ref, kinds_ref, tile + side, far.at[side], sums.at[side]) for side in flight]
+            + [scatter(tile - FLIGHT + side, sums_before.at[pl.ds(side, 2)]) for side in flight[::2]],
+            [copy for side in flight for copy in load(tile + FLIGHT + side, far_next.at[side])],
             7,
         )
 
     @pl.when(turn == pl.num_programs(0) - 1)
     def _():
-        for _ in scatter(STEP - 2, sum_b):
-            pass
+        for side in range(0, FLIGHT, 2):
+            for _ in scatter(STEP - FLIGHT + side, sum_b.at[pl.ds(side, 2)]):
+                pass
         count = rows * LANES // ROW
         for axis in range(3):
             force = total[axis * count : (axis + 1) * count, :]
@@ -450,7 +453,7 @@
     fields, lower_list, upper_list = lax.optimization_barrier((fields, lower_list, upper_list))
     lower, upper = turned(fields, "space", 1), turned(fields, "space", -1)
     tile_order = cell_order.reshape(rows, LANES)
-    order = cell_order.reshape(atoms) + (PAD - jnp.arange(atoms, dtype=I32) % 8)
+    order = cell_order.reshape(atoms)
     scalar = pl.BlockSpec(memory_space=pltpu.SMEM)
     vector = pl.BlockSpec(memory_space=pltpu.VMEM)
     params = pltpu.CompilerParams(vmem_limit_bytes=VMEM_LIMIT)
@@ -494,10 +497,10 @@
         scratch_shapes=[
             pltpu.VMEM((3 * atoms + 2 * PAD, LANES), F32),
             pltpu.VMEM((3 * atoms // ROW, ROW), F32),
-            pltpu.VMEM((2, partners, LANES), BF16),
-            pltpu.VMEM((2, partners, LANES), BF16),
-            pltpu.VMEM((2, TILE, LANES), F32),
-            pltpu.VMEM((2, TILE, LANES), F32),
+            pltpu.VMEM((FLIGHT, partners, LANES), BF16),
+            pltpu.VMEM((FLIGHT, partners, LANES), BF16),
+            pltpu.VMEM((FLIGHT, TILE, LANES), F32),
+            pltpu.VMEM((FLIGHT, TILE, LANES), F32),
         ],
         compiler_params=params,
         cost_estimate=pl.CostEstimate(flops=25 * 10**9, bytes_accessed=10**7, transcendentals=0),

time: 117 us -> 119 us (1.017)
  Pallas kernels: 84.1 us -> 87.9 us
  other arithmetic: 3.47 us -> 1.94 us
    pallas_call x1, Pallas kernels: 56.3 us -> 60.1 us  [per_device(): pl.pallas_call(functools.partial(force_kernel, rows), grid=(rows // STEP,...]
    add x1 -> x0, other arithmetic: 1.54 us -> none  [per_device(): order = cell_order.reshape(atoms) + (PAD - jnp.arange(atoms, dtype=I32) % 8)]
  transfers between devices with their start and end apart: 11 -> 11, of which waited for: 6 -> 6; matrix products, arithmetic and copies ran while one was open for 3% -> 2% of each run, Pallas kernels for 23% -> 23%
where the time goes in v21:
time: 119 us
  Pallas kernels  87.9 us (74%)
  starting transfers between devices  18.4 us (15%)
  waiting for transfers between devices  7.36 us (6%)
  local copies, waits for them, and re-layouts  2.44 us (2%)
  other arithmetic  1.94 us (2%)
    pallas_call x1, Pallas kernels, per_device(): pl.pallas_call(functools.partial(force_kernel, rows), grid=(rows // STEP,...  60.1 us
    pallas_call x1, Pallas kernels, per_device(): pl.pallas_call(functools.partial(near_kernel, rows), grid=(rows // STEP,)...  26.9 us
    ppermute x7, starting transfers between devices, turned(): lax.ppermute(array, axis, [(i, (i + by) % count) for i in range(count)])  13.9 us
    ppermute x4, waiting for transfers between devices, crossed(): return lax.ppermute(array, axis, [(i, i ^ by) for i in range(count)])  5.62 us
    ppermute x4, starting transfers between devices, crossed(): return lax.ppermute(array, axis, [(i, i ^ by) for i in range(count)])  4.45 us
  transfers between devices with their start and end apart: 11, of which 6 were waited for; matrix products, arithmetic and copies ran while one was open for 2% of the time, Pallas kernels for 23%

profile of v21, /device:TPU:0, one launch (start us, length us, event | category | flops | bytes accessed | tf_op | source)
XLA Modules:
  0.0 118.8 jit_solution(1411210144970072806)
XLA Ops:
  0.0 0.8 fusion.4
  0.8 2.9 %collective-permute-start = (s32[80,128]{1,0:T(8,128)S(1)}, s32[80,128]{1,0:T(8,128)S(1)}, u32[]{:S(2)}, u32[]{:S(2)}) collective-permute-start(s32[80,128]{1,0:T(8,128)S(1)} %bitcast.22), channel_id=1, source_target_pairs={{0,1},{1,2},{2,3},{3,4},{4,5},{5,6},{6,7},{7,0},{8,9},{9,10},{10,1... | collective-permute-start | bytes 122888 | tf_op jit(solution)/shard_map/ppermute | solution.py:421
  3.7 3.1 %collective-permute-start.1 = (s32[80,128]{1,0:T(8,128)S(1)}, s32[80,128]{1,0:T(8,128)S(1)}, u32[]{:S(2)}, u32[]{:S(2)}) collective-permute-start(s32[80,128]{1,0:T(8,128)S(1)} %bitcast.21), channel_id=1, source_target_pairs={{0,7},{1,0},{2,1},{3,2},{4,3},{5,4},{6,5},{7,6},{8,15},{9,8},{10,9... | collective-permute-start | bytes 122888 | tf_op jit(solution)/shard_map/ppermute | solution.py:421
  7.5 0.9 fusion.1
  8.5 1.0 pad_maximum_fusion
  9.5 0.0 copy-start.1
  9.5 0.0 collective-permute-done.lower_ref
  9.5 0.0 copy-start.4
  9.5 0.0 collective-permute-done.1.upper_ref
  9.5 0.0 copy-start.5
  9.5 0.7 collective-permute-start.2
  10.2 4.1 %collective-permute-start.3 = (f32[800,128]{1,0:T(8,128)S(1)}, f32[800,128]{1,0:T(8,128)S(1)}, u32[]{:S(2)}, u32[]{:S(2)}) collective-permute-start(f32[800,128]{1,0:T(8,128)S(1)} %bitcast.16), channel_id=1, source_target_pairs={{0,7},{1,0},{2,1},{3,2},{4,3},{5,4},{6,5},{7,6},{8,15},{9,8},{10,9... | collective-permute-start | bytes 1228808 | tf_op jit(solution)/shard_map/ppermute | solution.py:421
  14.3 0.0 copy-done.1
  14.3 0.0 copy-done.4
  14.3 0.0 copy-done.5
  14.3 26.9 %shard_map.91 = (bf16[160,128,128]{2,1,0:T(8,128)(2,1)}, s32[320,128]{1,0:T(8,128)}) custom-call(s32[20480]{0:T(1024)} %bitcast.23, s32[20480]{0:T(1024)} %bitcast.24, s32[80,128]{1,0:T(8,128)} %copy-done.4, s32[80,128]{1,0:T(8,128)} %copy-done.5, s32[1,160,256]{2,1,0:T(8,128)} %partner_ref.1, f32[800,128]{1,0:T(8,128)} %bitcast.17, ...), custom_call_target="tpu_custom_call" | custom-call | flops 24999999488 | bytes 10000000 | tf_op jit(solution)/shard_map/pallas_call | solution.py:466
  41.2 0.0 collective-permute-done.2.lower_ref
  41.2 0.0 copy-start.2
  41.2 0.0 collective-permute-done.3.upper_ref
  41.2 0.0 copy-start.3
  41.2 0.7 copy-done.2
  42.0 0.2 copy-done.3
  42.1 60.1 %shard_map.92 = (f32[480,128]{1,0:T(8,128)}, f32[6,8,128]{2,1,0:T(8,128)}) custom-call(s32[40960]{0:T(1024)} %bitcast.27, s32[40960]{0:T(1024)} %bitcast.28, s32[160,128]{1,0:T(8,128)} %bitcast.25, s32[160,128]{1,0:T(8,128)} %bitcast.26, f32[800,128]{1,0:T(8,128)} %copy-done.2, f32[800,128]{1,0:T(8,128)} %bitcast.18, f32[800,128]{1,0:T(8,128)} %copy-done.3, ...), custom_call_target="tpu_custom_call" | custom-call | flops 24999999488 | bytes 10000000 | tf_op jit(solution)/shard_map/pallas_call | solution.py:488
  102.2 0.0 collective-permute-start.4
  102.3 1.7 %collective-permute-start.5 = (f32[6,8,128]{2,1,0:T(8,128)}, f32[6,8,128]{2,1,0:T(8,128)S(1)}, u32[]{:S(2)}, u32[]{:S(2)}) collective-permute-start(f32[6,8,128]{2,1,0:T(8,128)} %get-tuple-element.20.refs_0_), channel_id=1, source_target_pairs={{0,16},{8,24},{16,0},{24,8},{1,17},{9,25},{17,1},{25,9},{2,18},{10... | collective-permute-start | bytes 73736 | tf_op jit(solution)/shard_map/ppermute | solution.py:421
  104.0 1.4 %collective-permute-start.6 = (f32[6,8,128]{2,1,0:T(8,128)}, f32[6,8,128]{2,1,0:T(8,128)S(1)}, u32[]{:S(2)}, u32[]{:S(2)}) collective-permute-start(f32[6,8,128]{2,1,0:T(8,128)} %get-tuple-element.20.refs_0_), channel_id=1, source_target_pairs={{0,24},{8,0},{16,8},{24,16},{1,25},{9,1},{17,9},{25,17},{2,26},{10... | collective-permute-start | bytes 73736 | tf_op jit(solution)/shard_map/ppermute | solution.py:421
  105.4 0.3 collective-permute-done.4.refs_1_
  105.7 0.6 collective-permute-done.5.refs_2_
  106.4 0.7 collective-permute-done.6.refs_3_
  107.1 0.0 copy-start
  107.1 0.7 copy-done
  107.8 0.1 shard_map.93
  107.9 0.1 collective-permute-start.7
  108.0 3.7 %collective-permute-done.7 = f32[32,128]{1,0:T(8,128)S(1)} collective-permute-done((f32[32,128]{1,0:T(8,128)S(1)}, f32[32,128]{1,0:T(8,128)S(1)}, u32[]{:S(2)}, u32[]{:S(2)}) %collective-permute-start.7) | collective-permute-done | bytes 16416 | tf_op jit(solution)/shard_map/ppermute | solution.py:430
  111.7 0.0 collective-permute-start.10
  111.7 0.0 collective-permute-start.8
  111.8 4.3 %collective-permute-start.9 = (f32[32,128]{1,0:T(8,128)S(1)}, f32[32,128]{1,0:T(8,128)S(1)}, u32[]{:S(2)}, u32[]{:S(2)}) collective-permute-start(f32[32,128]{1,0:T(8,128)S(1)} %add.12), channel_id=1, source_target_pairs={{0,4},{1,5},{2,6},{3,7},{4,0},{5,1},{6,2},{7,3},{8,12},{9,13},{10,... | collective-permute-start | bytes 49160 | tf_op jit(solution)/shard_map/ppermute | solution.py:430
  116.1 1.1 collective-permute-done.10
  117.2 0.0 collective-permute-done.8
  117.2 0.7 collective-permute-done.9
  118.0 0.8 shard_map.94
  (2 shorter events, 0.0 us)
Async XLA Ops:
  0.8 8.7 %collective-permute-start = (s32[80,128]{1,0:T(8,128)S(1)}, s32[80,128]{1,0:T(8,128)S(1)}, u32[]{:S(2)}, u32[]{:S(2)}) collective-permute-start(s32[80,128]{1,0:T(8,128)S(1)} %bitcast.22), channel_id=1, source_target_pairs={{0,1},{1,2},{2,3},{3,4},{4,5},{5,6},{6,7},{7,0},{8,9},{9,10},{10,1... | collective-permute-start | bytes 122888 | tf_op jit(solution)/shard_map/ppermute | solution.py:421
  3.7 5.8 %collective-permute-start.1 = (s32[80,128]{1,0:T(8,128)S(1)}, s32[80,128]{1,0:T(8,128)S(1)}, u32[]{:S(2)}, u32[]{:S(2)}) collective-permute-start(s32[80,128]{1,0:T(8,128)S(1)} %bitcast.21), channel_id=1, source_target_pairs={{0,7},{1,0},{2,1},{3,2},{4,3},{5,4},{6,5},{7,6},{8,15},{9,8},{10,9... | collective-permute-start | bytes 122888 | tf_op jit(solution)/shard_map/ppermute | solution.py:421
  9.5 4.8 %copy-start.1 = (f32[5,160,128]{2,1,0:T(8,128)}, f32[5,160,128]{2,1,0:T(8,128)S(1)}, u32[]{:S(2)}) copy-start(f32[5,160,128]{2,1,0:T(8,128)S(1)} %pad_maximum_fusion) | copy-start | bytes 1228804
  9.5 4.8 %copy-start.4 = (s32[80,128]{1,0:T(8,128)}, s32[80,128]{1,0:T(8,128)S(1)}, u32[]{:S(2)}) copy-start(s32[80,128]{1,0:T(8,128)S(1)} %collective-permute-done.lower_ref) | copy-start | bytes 122884
  9.5 4.8 %copy-start.5 = (s32[80,128]{1,0:T(8,128)}, s32[80,128]{1,0:T(8,128)S(1)}, u32[]{:S(2)}) copy-start(s32[80,128]{1,0:T(8,128)S(1)} %collective-permute-done.1.upper_ref) | copy-start | bytes 122884
  9.5 31.7 %collective-permute-start.2 = (f32[800,128]{1,0:T(8,128)S(1)}, f32[800,128]{1,0:T(8,128)S(1)}, u32[]{:S(2)}, u32[]{:S(2)}) collective-permute-start(f32[800,128]{1,0:T(8,128)S(1)} %bitcast.15), channel_id=1, source_target_pairs={{0,1},{1,2},{2,3},{3,4},{4,5},{5,6},{6,7},{7,0},{8,9},{9,10},{10,1... | collective-permute-start | bytes 1228808 | tf_op jit(solution)/shard_map/ppermute | solution.py:421
  10.2 31.0 %collective-permute-start.3 = (f32[800,128]{1,0:T(8,128)S(1)}, f32[800,128]{1,0:T(8,128)S(1)}, u32[]{:S(2)}, u32[]{:S(2)}) collective-permute-start(f32[800,128]{1,0:T(8,128)S(1)} %bitcast.16), channel_id=1, source_target_pairs={{0,7},{1,0},{2,1},{3,2},{4,3},{5,4},{6,5},{7,6},{8,15},{9,8},{10,9... | collective-permute-start | bytes 1228808 | tf_op jit(solution)/shard_map/ppermute | solution.py:421
  41.2 0.8 copy-start.2
  41.2 0.9 copy-start.3
  102.2 3.5 %collective-permute-start.4 = (f32[6,8,128]{2,1,0:T(8,128)}, f32[6,8,128]{2,1,0:T(8,128)S(1)}, u32[]{:S(2)}, u32[]{:S(2)}) collective-permute-start(f32[6,8,128]{2,1,0:T(8,128)} %get-tuple-element.20.refs_0_), channel_id=1, source_target_pairs={{0,8},{8,16},{16,24},{24,0},{1,9},{9,17},{17,25},{25,1},{2,10},{10... | collective-permute-start | bytes 73736 | tf_op jit(solution)/shard_map/ppermute | solution.py:421
  102.3 4.1 %collective-permute-start.5 = (f32[6,8,128]{2,1,0:T(8,128)}, f32[6,8,128]{2,1,0:T(8,128)S(1)}, u32[]{:S(2)}, u32[]{:S(2)}) collective-permute-start(f32[6,8,128]{2,1,0:T(8,128)} %get-tuple-element.20.refs_0_), channel_id=1, source_target_pairs={{0,16},{8,24},{16,0},{24,8},{1,17},{9,25},{17,1},{25,9},{2,18},{10... | collective-permute-start | bytes 73736 | tf_op jit(solution)/shard_map/ppermute | solution.py:421
  104.0 3.1 %collective-permute-start.6 = (f32[6,8,128]{2,1,0:T(8,128)}, f32[6,8,128]{2,1,0:T(8,128)S(1)}, u32[]{:S(2)}, u32[]{:S(2)}) collective-permute-start(f32[6,8,128]{2,1,0:T(8,128)} %get-tuple-element.20.refs_0_), channel_id=1, source_target_pairs={{0,24},{8,0},{16,8},{24,16},{1,25},{9,1},{17,9},{25,17},{2,26},{10... | collective-permute-start | bytes 73736 | tf_op jit(solution)/shard_map/ppermute | solution.py:421
  107.1 0.7 copy-start
  107.9 3.8 %collective-permute-start.7 = (f32[32,128]{1,0:T(8,128)S(1)}, f32[32,128]{1,0:T(8,128)S(1)}, u32[]{:S(2)}, u32[]{:S(2)}) collective-permute-start(f32[32,128]{1,0:T(8,128)S(1)} %get-tuple-element.21), channel_id=1, source_target_pairs={{0,1},{1,0},{2,3},{3,2},{4,5},{5,4},{6,7},{7,6},{8,9},{9,8},{10,11... | collective-permute-start | bytes 49160 | tf_op jit(solution)/shard_map/ppermute | solution.py:430
  111.7 5.5 %collective-permute-start.10 = (f32[32,128]{1,0:T(8,128)S(1)}, f32[32,128]{1,0:T(8,128)S(1)}, u32[]{:S(2)}, u32[]{:S(2)}) collective-permute-start(f32[32,128]{1,0:T(8,128)S(1)} %add.12), channel_id=1, source_target_pairs={{0,6},{1,7},{2,4},{3,5},{4,2},{5,3},{6,0},{7,1},{8,14},{9,15},{10,... | collective-permute-start | bytes 49160 | tf_op jit(solution)/shard_map/ppermute | solution.py:430
  111.7 5.5 %collective-permute-start.8 = (f32[32,128]{1,0:T(8,128)S(1)}, f32[32,128]{1,0:T(8,128)S(1)}, u32[]{:S(2)}, u32[]{:S(2)}) collective-permute-start(f32[32,128]{1,0:T(8,128)S(1)} %add.12), channel_id=1, source_target_pairs={{0,2},{1,3},{2,0},{3,1},{4,6},{5,7},{6,4},{7,5},{8,10},{9,11},{10,... | collective-permute-start | bytes 49160 | tf_op jit(solution)/shard_map/ppermute | solution.py:430
  111.8 6.2 %collective-permute-start.9 = (f32[32,128]{1,0:T(8,128)S(1)}, f32[32,128]{1,0:T(8,128)S(1)}, u32[]{:S(2)}, u32[]{:S(2)}) collective-permute-start(f32[32,128]{1,0:T(8,128)S(1)} %add.12), channel_id=1, source_target_pairs={{0,4},{1,5},{2,6},{3,7},{4,0},{5,1},{6,2},{7,3},{8,12},{9,13},{10,... | collective-permute-start | bytes 49160 | tf_op jit(solution)/shard_map/ppermute | solution.py:430

commit v22 on v21

--- a/solution.py
+++ b/solution.py
@@ -32,7 +32,7 @@
 DEPTH, CHARGE, ONE, NORM, LAST = 3, 4, 5, 6, 7
 FAR_PIECES = (0, 1, 2, 0, 1, 0)
 STEP = 16
-FLIGHT = 4
+FLIGHT = 2
 ROW = 256
 COPY = 64
 USED = 8 * len(FAR_PIECES)

time: 119 us -> 115 us (0.966)
  Pallas kernels: 87.9 us -> 84 us
    pallas_call x1, Pallas kernels: 60.1 us -> 56.3 us  [per_device(): pl.pallas_call(functools.partial(force_kernel, rows), grid=(rows // STEP,...]
where the time goes in v22:
time: 115 us
  Pallas kernels  84 us (73%)
  starting transfers between devices  18.4 us (16%)
  waiting for transfers between devices  7.36 us (6%)
  local copies, waits for them, and re-layouts  2.44 us (2%)
  other arithmetic  1.94 us (2%)
    pallas_call x1, Pallas kernels, per_device(): pl.pallas_call(functools.partial(force_kernel, rows), grid=(rows // STEP,...  56.3 us
    pallas_call x1, Pallas kernels, per_device(): pl.pallas_call(functools.partial(near_kernel, rows), grid=(rows // STEP,)...  26.9 us
    ppermute x7, starting transfers between devices, turned(): lax.ppermute(array, axis, [(i, (i + by) % count) for i in range(count)])  13.9 us
    ppermute x4, waiting for transfers between devices, crossed(): return lax.ppermute(array, axis, [(i, i ^ by) for i in range(count)])  5.62 us
    ppermute x4, starting transfers between devices, crossed(): return lax.ppermute(array, axis, [(i, i ^ by) for i in range(count)])  4.45 us
  transfers between devices with their start and end apart: 11, of which 6 were waited for; matrix products, arithmetic and copies ran while one was open for 2% of the time, Pallas kernels for 23%

profile of v22, /device:TPU:0, one launch (start us, length us, event | category | flops | bytes accessed | tf_op | source)
XLA Modules:
  0.0 114.9 jit_solution(8928101943639392452)
XLA Ops:
  0.0 0.8 fusion.4
  0.8 2.9 %collective-permute-start = (s32[80,128]{1,0:T(8,128)S(1)}, s32[80,128]{1,0:T(8,128)S(1)}, u32[]{:S(2)}, u32[]{:S(2)}) collective-permute-start(s32[80,128]{1,0:T(8,128)S(1)} %bitcast.22), channel_id=1, source_target_pairs={{0,1},{1,2},{2,3},{3,4},{4,5},{5,6},{6,7},{7,0},{8,9},{9,10},{10,1... | collective-permute-start | bytes 122888 | tf_op jit(solution)/shard_map/ppermute | solution.py:421
  3.7 3.1 %collective-permute-start.1 = (s32[80,128]{1,0:T(8,128)S(1)}, s32[80,128]{1,0:T(8,128)S(1)}, u32[]{:S(2)}, u32[]{:S(2)}) collective-permute-start(s32[80,128]{1,0:T(8,128)S(1)} %bitcast.21), channel_id=1, source_target_pairs={{0,7},{1,0},{2,1},{3,2},{4,3},{5,4},{6,5},{7,6},{8,15},{9,8},{10,9... | collective-permute-start | bytes 122888 | tf_op jit(solution)/shard_map/ppermute | solution.py:421
  7.5 0.9 fusion.1
  8.5 1.0 pad_maximum_fusion
  9.5 0.0 copy-start.1
  9.5 0.0 collective-permute-done.lower_ref
  9.5 0.0 copy-start.4
  9.5 0.0 collective-permute-done.1.upper_ref
  9.5 0.0 copy-start.5
  9.5 0.7 collective-permute-start.2
  10.2 4.1 %collective-permute-start.3 = (f32[800,128]{1,0:T(8,128)S(1)}, f32[800,128]{1,0:T(8,128)S(1)}, u32[]{:S(2)}, u32[]{:S(2)}) collective-permute-start(f32[800,128]{1,0:T(8,128)S(1)} %bitcast.16), channel_id=1, source_target_pairs={{0,7},{1,0},{2,1},{3,2},{4,3},{5,4},{6,5},{7,6},{8,15},{9,8},{10,9... | collective-permute-start | bytes 1228808 | tf_op jit(solution)/shard_map/ppermute | solution.py:421
  14.3 0.0 copy-done.1
  14.3 0.0 copy-done.4
  14.3 0.0 copy-done.5
  14.3 26.9 %shard_map.91 = (bf16[160,128,128]{2,1,0:T(8,128)(2,1)}, s32[320,128]{1,0:T(8,128)}) custom-call(s32[20480]{0:T(1024)} %bitcast.23, s32[20480]{0:T(1024)} %bitcast.24, s32[80,128]{1,0:T(8,128)} %copy-done.4, s32[80,128]{1,0:T(8,128)} %copy-done.5, s32[1,160,256]{2,1,0:T(8,128)} %partner_ref.1, f32[800,128]{1,0:T(8,128)} %bitcast.17, ...), custom_call_target="tpu_custom_call" | custom-call | flops 24999999488 | bytes 10000000 | tf_op jit(solution)/shard_map/pallas_call | solution.py:466
  41.2 0.0 collective-permute-done.2.lower_ref
  41.2 0.0 copy-start.2
  41.2 0.0 collective-permute-done.3.upper_ref
  41.2 0.0 copy-start.3
  41.2 0.7 copy-done.2
  42.0 0.2 copy-done.3
  42.1 56.3 %shard_map.92 = (f32[480,128]{1,0:T(8,128)}, f32[6,8,128]{2,1,0:T(8,128)}) custom-call(s32[40960]{0:T(1024)} %bitcast.27, s32[40960]{0:T(1024)} %bitcast.28, s32[160,128]{1,0:T(8,128)} %bitcast.25, s32[160,128]{1,0:T(8,128)} %bitcast.26, f32[800,128]{1,0:T(8,128)} %copy-done.2, f32[800,128]{1,0:T(8,128)} %bitcast.18, f32[800,128]{1,0:T(8,128)} %copy-done.3, ...), custom_call_target="tpu_custom_call" | custom-call | flops 24999999488 | bytes 10000000 | tf_op jit(solution)/shard_map/pallas_call | solution.py:488
  98.4 0.0 collective-permute-start.4
  98.4 1.7 %collective-permute-start.5 = (f32[6,8,128]{2,1,0:T(8,128)}, f32[6,8,128]{2,1,0:T(8,128)S(1)}, u32[]{:S(2)}, u32[]{:S(2)}) collective-permute-start(f32[6,8,128]{2,1,0:T(8,128)} %get-tuple-element.20.refs_0_), channel_id=1, source_target_pairs={{0,16},{8,24},{16,0},{24,8},{1,17},{9,25},{17,1},{25,9},{2,18},{10... | collective-permute-start | bytes 73736 | tf_op jit(solution)/shard_map/ppermute | solution.py:421
  100.1 1.4 %collective-permute-start.6 = (f32[6,8,128]{2,1,0:T(8,128)}, f32[6,8,128]{2,1,0:T(8,128)S(1)}, u32[]{:S(2)}, u32[]{:S(2)}) collective-permute-start(f32[6,8,128]{2,1,0:T(8,128)} %get-tuple-element.20.refs_0_), channel_id=1, source_target_pairs={{0,24},{8,0},{16,8},{24,16},{1,25},{9,1},{17,9},{25,17},{2,26},{10... | collective-permute-start | bytes 73736 | tf_op jit(solution)/shard_map/ppermute | solution.py:421
  101.5 0.3 collective-permute-done.4.refs_1_
  101.8 0.6 collective-permute-done.5.refs_2_
  102.5 0.7 collective-permute-done.6.refs_3_
  103.2 0.0 copy-start
  103.2 0.7 copy-done
  104.0 0.1 shard_map.93
  104.0 0.1 collective-permute-start.7
  104.1 3.7 %collective-permute-done.7 = f32[32,128]{1,0:T(8,128)S(1)} collective-permute-done((f32[32,128]{1,0:T(8,128)S(1)}, f32[32,128]{1,0:T(8,128)S(1)}, u32[]{:S(2)}, u32[]{:S(2)}) %collective-permute-start.7) | collective-permute-done | bytes 16416 | tf_op jit(solution)/shard_map/ppermute | solution.py:430
  107.8 0.0 collective-permute-start.10
  107.8 0.1 collective-permute-start.8
  107.9 4.3 %collective-permute-start.9 = (f32[32,128]{1,0:T(8,128)S(1)}, f32[32,128]{1,0:T(8,128)S(1)}, u32[]{:S(2)}, u32[]{:S(2)}) collective-permute-start(f32[32,128]{1,0:T(8,128)S(1)} %add.12), channel_id=1, source_target_pairs={{0,4},{1,5},{2,6},{3,7},{4,0},{5,1},{6,2},{7,3},{8,12},{9,13},{10,... | collective-permute-start | bytes 49160 | tf_op jit(solution)/shard_map/ppermute | solution.py:430
  112.2 1.1 collective-permute-done.10
  113.4 0.0 collective-permute-done.8
  113.4 0.7 collective-permute-done.9
  114.1 0.8 shard_map.94
  (2 shorter events, 0.0 us)
Async XLA Ops:
  0.8 8.7 %collective-permute-start = (s32[80,128]{1,0:T(8,128)S(1)}, s32[80,128]{1,0:T(8,128)S(1)}, u32[]{:S(2)}, u32[]{:S(2)}) collective-permute-start(s32[80,128]{1,0:T(8,128)S(1)} %bitcast.22), channel_id=1, source_target_pairs={{0,1},{1,2},{2,3},{3,4},{4,5},{5,6},{6,7},{7,0},{8,9},{9,10},{10,1... | collective-permute-start | bytes 122888 | tf_op jit(solution)/shard_map/ppermute | solution.py:421
  3.7 5.8 %collective-permute-start.1 = (s32[80,128]{1,0:T(8,128)S(1)}, s32[80,128]{1,0:T(8,128)S(1)}, u32[]{:S(2)}, u32[]{:S(2)}) collective-permute-start(s32[80,128]{1,0:T(8,128)S(1)} %bitcast.21), channel_id=1, source_target_pairs={{0,7},{1,0},{2,1},{3,2},{4,3},{5,4},{6,5},{7,6},{8,15},{9,8},{10,9... | collective-permute-start | bytes 122888 | tf_op jit(solution)/shard_map/ppermute | solution.py:421
  9.5 4.8 %copy-start.1 = (f32[5,160,128]{2,1,0:T(8,128)}, f32[5,160,128]{2,1,0:T(8,128)S(1)}, u32[]{:S(2)}) copy-start(f32[5,160,128]{2,1,0:T(8,128)S(1)} %pad_maximum_fusion) | copy-start | bytes 1228804
  9.5 4.8 %copy-start.4 = (s32[80,128]{1,0:T(8,128)}, s32[80,128]{1,0:T(8,128)S(1)}, u32[]{:S(2)}) copy-start(s32[80,128]{1,0:T(8,128)S(1)} %collective-permute-done.lower_ref) | copy-start | bytes 122884
  9.5 4.8 %copy-start.5 = (s32[80,128]{1,0:T(8,128)}, s32[80,128]{1,0:T(8,128)S(1)}, u32[]{:S(2)}) copy-start(s32[80,128]{1,0:T(8,128)S(1)} %collective-permute-done.1.upper_ref) | copy-start | bytes 122884
  9.5 31.7 %collective-permute-start.2 = (f32[800,128]{1,0:T(8,128)S(1)}, f32[800,128]{1,0:T(8,128)S(1)}, u32[]{:S(2)}, u32[]{:S(2)}) collective-permute-start(f32[800,128]{1,0:T(8,128)S(1)} %bitcast.15), channel_id=1, source_target_pairs={{0,1},{1,2},{2,3},{3,4},{4,5},{5,6},{6,7},{7,0},{8,9},{9,10},{10,1... | collective-permute-start | bytes 1228808 | tf_op jit(solution)/shard_map/ppermute | solution.py:421
  10.2 31.0 %collective-permute-start.3 = (f32[800,128]{1,0:T(8,128)S(1)}, f32[800,128]{1,0:T(8,128)S(1)}, u32[]{:S(2)}, u32[]{:S(2)}) collective-permute-start(f32[800,128]{1,0:T(8,128)S(1)} %bitcast.16), channel_id=1, source_target_pairs={{0,7},{1,0},{2,1},{3,2},{4,3},{5,4},{6,5},{7,6},{8,15},{9,8},{10,9... | collective-permute-start | bytes 1228808 | tf_op jit(solution)/shard_map/ppermute | solution.py:421
  41.2 0.8 copy-start.2
  41.2 0.9 copy-start.3
  98.4 3.5 %collective-permute-start.4 = (f32[6,8,128]{2,1,0:T(8,128)}, f32[6,8,128]{2,1,0:T(8,128)S(1)}, u32[]{:S(2)}, u32[]{:S(2)}) collective-permute-start(f32[6,8,128]{2,1,0:T(8,128)} %get-tuple-element.20.refs_0_), channel_id=1, source_target_pairs={{0,8},{8,16},{16,24},{24,0},{1,9},{9,17},{17,25},{25,1},{2,10},{10... | collective-permute-start | bytes 73736 | tf_op jit(solution)/shard_map/ppermute | solution.py:421
  98.4 4.1 %collective-permute-start.5 = (f32[6,8,128]{2,1,0:T(8,128)}, f32[6,8,128]{2,1,0:T(8,128)S(1)}, u32[]{:S(2)}, u32[]{:S(2)}) collective-permute-start(f32[6,8,128]{2,1,0:T(8,128)} %get-tuple-element.20.refs_0_), channel_id=1, source_target_pairs={{0,16},{8,24},{16,0},{24,8},{1,17},{9,25},{17,1},{25,9},{2,18},{10... | collective-permute-start | bytes 73736 | tf_op jit(solution)/shard_map/ppermute | solution.py:421
  100.1 3.1 %collective-permute-start.6 = (f32[6,8,128]{2,1,0:T(8,128)}, f32[6,8,128]{2,1,0:T(8,128)S(1)}, u32[]{:S(2)}, u32[]{:S(2)}) collective-permute-start(f32[6,8,128]{2,1,0:T(8,128)} %get-tuple-element.20.refs_0_), channel_id=1, source_target_pairs={{0,24},{8,0},{16,8},{24,16},{1,25},{9,1},{17,9},{25,17},{2,26},{10... | collective-permute-start | bytes 73736 | tf_op jit(solution)/shard_map/ppermute | solution.py:421
  103.2 0.7 copy-start
  104.0 3.8 %collective-permute-start.7 = (f32[32,128]{1,0:T(8,128)S(1)}, f32[32,128]{1,0:T(8,128)S(1)}, u32[]{:S(2)}, u32[]{:S(2)}) collective-permute-start(f32[32,128]{1,0:T(8,128)S(1)} %get-tuple-element.21), channel_id=1, source_target_pairs={{0,1},{1,0},{2,3},{3,2},{4,5},{5,4},{6,7},{7,6},{8,9},{9,8},{10,11... | collective-permute-start | bytes 49160 | tf_op jit(solution)/shard_map/ppermute | solution.py:430
  107.8 5.5 %collective-permute-start.10 = (f32[32,128]{1,0:T(8,128)S(1)}, f32[32,128]{1,0:T(8,128)S(1)}, u32[]{:S(2)}, u32[]{:S(2)}) collective-permute-start(f32[32,128]{1,0:T(8,128)S(1)} %add.12), channel_id=1, source_target_pairs={{0,6},{1,7},{2,4},{3,5},{4,2},{5,3},{6,0},{7,1},{8,14},{9,15},{10,... | collective-permute-start | bytes 49160 | tf_op jit(solution)/shard_map/ppermute | solution.py:430
  107.8 5.5 %collective-permute-start.8 = (f32[32,128]{1,0:T(8,128)S(1)}, f32[32,128]{1,0:T(8,128)S(1)}, u32[]{:S(2)}, u32[]{:S(2)}) collective-permute-start(f32[32,128]{1,0:T(8,128)S(1)} %add.12), channel_id=1, source_target_pairs={{0,2},{1,3},{2,0},{3,1},{4,6},{5,7},{6,4},{7,5},{8,10},{9,11},{10,... | collective-permute-start | bytes 49160 | tf_op jit(solution)/shard_map/ppermute | solution.py:430
  107.9 6.2 %collective-permute-start.9 = (f32[32,128]{1,0:T(8,128)S(1)}, f32[32,128]{1,0:T(8,128)S(1)}, u32[]{:S(2)}, u32[]{:S(2)}) collective-permute-start(f32[32,128]{1,0:T(8,128)S(1)} %add.12), channel_id=1, source_target_pairs={{0,4},{1,5},{2,6},{3,7},{4,0},{5,1},{6,2},{7,3},{8,12},{9,13},{10,... | collective-permute-start | bytes 49160 | tf_op jit(solution)/shard_map/ppermute | solution.py:430
